TPU v7x, 32 devices: a whole 2x2x4 slice. The times are simulated.
32 devices in a mesh: leaf: 4 (over y, x), grp: 8 (over z, core).
Axes of the slice: x: 2, y: 2, z: 4, core: 2. Of those that a mesh axis runs over, the one named last changes fastest.
Arguments:
- rhs_leaf: float32 [4, 8192, 256], P('leaf', 'grp'), may hold values from -6 to 6
- rhs_group: float32 [4, 512, 256], P('leaf'), may hold values from -6 to 6
- rhs_middle: float32 [1024, 256], replicated, may hold values from -6 to 6
- rhs_top: float32 [1024, 256], replicated, may hold values from -6 to 6
- inv_leaf: bfloat16 [4, 64, 128, 128], P('leaf', 'grp')
- inv_group: bfloat16 [4, 512, 512], P('leaf')
- inv_middle: bfloat16 [1024, 1024], replicated
- inv_top: bfloat16 [1024, 1024], replicated
- leaf_tiles: bfloat16 [4, 2048, 128, 128], P('leaf', 'grp'), may hold values from -0.03125 to 0.03125
- tile_column: int32 [4, 2048], P('leaf', 'grp'), may hold values from 0 to 7
- tile_target: int32 [4, 2048], P('leaf', 'grp'), may hold values from 0 to 19
- tile_count: int32 [4, 8], P('leaf', 'grp'), may hold values from 64 to 256, as said below
- group_panel: bfloat16 [4, 2048, 512], P('leaf', 'grp'), may hold values from -0.125 to 0.125
- middle_panel: bfloat16 [1024, 1024], P(('leaf', 'grp')), may hold values from -0.1875 to 0.1875
Outputs:
- leaf_out: float32 [4, 8192, 256], P('leaf', 'grp')
- group_out: float32 [4, 512, 256], P('leaf')
- mid_out: float32 [1024, 256], replicated
- top_out: float32 [1024, 256], replicated
Inputs may be any that keep to these rules, and one draw needn't show every extreme that they name: Only the first tile_count slots of a device hold blocks of the factor; the other slots are ignored. Some device has all 256 slots live.
All inputs are finite; a program needn't handle non-finite values.
Results may differ from a plain program's by a relative error of at most 0.018.
Values may be sent and summed in bfloat16 or wider, within the bound.
No kernel may reach another device: no remote copies, remote signals or barrier semaphores. Data moves between devices by JAX's collectives and lax.ppermute only.
A program may use at most 128 MiB of HBM per device.

v0:
```python
import jax
import jax.numpy as jnp
from jax import lax
from jax.sharding import PartitionSpec as P

BLOCK = 128
GROUP_COLS = 512
MID_COLS = 1024
LEAF_SN = 8
UPPER_BLOCKS = 20


tile_step = 16


def upper_forward(inverse, residual):
    return jnp.dot(
        inverse, residual.astype(jnp.bfloat16), preferred_element_type=jnp.float32
    ).astype(jnp.bfloat16)


def upper_backward(inverse, vector):
    return jnp.einsum("ji,jr->ir", inverse, vector, preferred_element_type=jnp.float32)


def solve_columns(
    rhs_leaf,
    rhs_group,
    rhs_middle,
    rhs_top,
    inv_leaf,
    inv_group,
    inv_middle,
    inv_top,
    leaf_tiles,
    tile_column,
    tile_target,
    tile_count,
    group_panel,
    middle_panel,
    whole_panels,
):
    width = rhs_top.shape[-1]
    tiles_here = leaf_tiles[0]
    columns_here = tile_column[0]
    targets_here = tile_target[0]
    live_count = tile_count[0, 0]
    trips = (live_count + tile_step - 1) // tile_step
    leaf_rhs = rhs_leaf[0].reshape(LEAF_SN, BLOCK, width).astype(jnp.bfloat16)
    leaf_solved = jnp.einsum(
        "sij,sjr->sir", inv_leaf[0], leaf_rhs, preferred_element_type=jnp.float32
    ).astype(jnp.bfloat16)

    def slot_block(step_index):
        begin = step_index * tile_step
        tile_block = lax.dynamic_slice_in_dim(tiles_here, begin, tile_step, 0)
        column_block = lax.dynamic_slice_in_dim(columns_here, begin, tile_step, 0)
        target_block = lax.dynamic_slice_in_dim(targets_here, begin, tile_step, 0)
        live_block = begin + jnp.arange(tile_step, dtype=jnp.int32) < live_count
        return (tile_block, column_block, target_block, live_block)

    def forward_step(step_index, totals):
        tile_block, column_block, target_block, live_block = slot_block(step_index)
        picked = leaf_solved[column_block]
        terms = jnp.einsum("pij,pjr->pir", tile_block, picked, preferred_element_type=jnp.float32)
        terms = jnp.where(live_block[:, None, None], terms, 0.0)
        return totals.at[target_block].add(terms)

    totals = lax.fori_loop(
        0, trips, forward_step, jnp.zeros((UPPER_BLOCKS, BLOCK, width), jnp.float32)
    )
    flat = totals.reshape(UPPER_BLOCKS * BLOCK, width)
    group_sum = lax.psum(flat[:GROUP_COLS], "grp")
    group_solved = upper_forward(inv_group[0], rhs_group[0] - group_sum)
    panel_rows = group_panel.shape[1]
    panel_begin = lax.axis_index("grp") * panel_rows
    panel_terms = jnp.dot(group_panel[0], group_solved, preferred_element_type=jnp.float32)
    upper = flat[GROUP_COLS:]
    section = lax.dynamic_slice_in_dim(upper, panel_begin, panel_rows, 0) + panel_terms
    upper = lax.dynamic_update_slice_in_dim(upper, section, panel_begin, 0)
    mid_sum = lax.psum(upper[:MID_COLS], ("leaf", "grp"))
    mid_solved = upper_forward(inv_middle, rhs_middle - mid_sum)
    middle_rows = middle_panel.shape[0]
    middle_begin = lax.axis_index(("leaf", "grp")) * middle_rows
    top_part = upper[MID_COLS:]
    top_section = lax.dynamic_slice_in_dim(top_part, middle_begin, middle_rows, 0) + jnp.dot(
        middle_panel, mid_solved, preferred_element_type=jnp.float32
    )
    top_part = lax.dynamic_update_slice_in_dim(top_part, top_section, middle_begin, 0)
    top_sum = lax.psum(top_part, ("leaf", "grp"))
    top_solved = upper_forward(inv_top, rhs_top - top_sum)
    top_out = upper_backward(inv_top, top_solved)
    top_round = top_out.astype(jnp.bfloat16)
    my_top = lax.dynamic_slice_in_dim(top_round, middle_begin, middle_rows, 0)
    mid_terms = jnp.einsum("ji,jr->ir", middle_panel, my_top, preferred_element_type=jnp.float32)
    mid_back = mid_solved.astype(jnp.float32) - lax.psum(mid_terms, ("leaf", "grp"))
    mid_out = upper_backward(inv_middle, mid_back.astype(jnp.bfloat16))
    upper_round = jnp.concatenate([mid_out.astype(jnp.bfloat16), top_round], axis=0)
    my_upper = lax.dynamic_slice_in_dim(upper_round, panel_begin, panel_rows, 0)
    group_terms = jnp.einsum(
        "ji,jr->ir", group_panel[0], my_upper, preferred_element_type=jnp.float32
    )
    group_back = group_solved.astype(jnp.float32) - lax.psum(
        group_terms.astype(jnp.bfloat16), "grp"
    ).astype(jnp.float32)
    group_out = upper_backward(inv_group[0], group_back.astype(jnp.bfloat16))
    above = jnp.concatenate([group_out.astype(jnp.bfloat16), upper_round], axis=0).reshape(
        UPPER_BLOCKS, BLOCK, width
    )

    def backward_step(step_index, totals_back):
        tile_block, column_block, target_block, live_block = slot_block(step_index)
        picked = above[target_block]
        terms = jnp.einsum("pji,pjr->pir", tile_block, picked, preferred_element_type=jnp.float32)
        terms = jnp.where(live_block[:, None, None], terms, 0.0)
        return totals_back.at[column_block].add(terms)

    leaf_terms = lax.fori_loop(
        0, trips, backward_step, jnp.zeros((LEAF_SN, BLOCK, width), jnp.float32)
    )
    leaf_back = (leaf_solved.astype(jnp.float32) - leaf_terms).astype(jnp.bfloat16)
    leaf_out = jnp.einsum(
        "sji,sjr->sir", inv_leaf[0], leaf_back, preferred_element_type=jnp.float32
    )
    return (leaf_out.reshape(1, LEAF_SN * BLOCK, width), group_out[None], mid_out, top_out)


def body(
    rhs_leaf,
    rhs_group,
    rhs_middle,
    rhs_top,
    inv_leaf,
    inv_group,
    inv_middle,
    inv_top,
    leaf_tiles,
    tile_column,
    tile_target,
    tile_count,
    group_panel,
    middle_panel,
):
    fixed_parts = (
        inv_leaf,
        inv_group,
        inv_middle,
        inv_top,
        leaf_tiles,
        tile_column,
        tile_target,
        tile_count,
        group_panel,
        middle_panel,
        None,
    )
    return solve_columns(rhs_leaf, rhs_group, rhs_middle, rhs_top, *fixed_parts)


def solution(mesh):
    placed = (
        P("leaf", "grp", None),
        P("leaf", None, None),
        P(),
        P(),
        P("leaf", "grp", None, None),
        P("leaf", None, None),
        P(),
        P(),
        P("leaf", "grp", None, None),
        P("leaf", "grp"),
        P("leaf", "grp"),
        P("leaf", "grp"),
        P("leaf", "grp", None),
        P(("leaf", "grp"), None),
    )
    return jax.shard_map(
        body,
        mesh=mesh,
        in_specs=placed,
        out_specs=(P("leaf", "grp", None), P("leaf", None, None), P(), P()),
        check_vma=False,
    )
```

profile of v0, /device:TPU:14, one launch (start us, length us, event | category | flops | bytes accessed | tf_op | source)
XLA Modules:
  0.0 882.3 jit_solution(8995844514969525255)
XLA Ops:
  13.2 166.1 %while.20 = (s32[]{:T(128)}, f32[20,128,256]{2,1,0:T(8,128)}, s32[]{:T(128)}, s32[256]{0:T(256)S(1)}, s32[]{:T(128)}, /*index=5*/bf16[256,128,128]{2,1,0:T(8,128...) while((s32[]{:T(128)}, f32[20,128,256]{2,1,0:T(8,128)}, ...), condition=%wide.region_2.3_spmd, body=%wide.region_0.2_spmd.sunk | while | flops 135267456 | bytes 12063379 | solution.py:69
  18.4 5.2 scatter_fusion
  28.8 5.2 scatter_fusion
  39.2 5.2 scatter_fusion
  49.6 5.2 scatter_fusion
  60.0 5.2 scatter_fusion
  70.4 5.1 scatter_fusion
  80.7 5.2 scatter_fusion
  91.1 5.2 scatter_fusion
  101.5 5.2 scatter_fusion
  111.9 5.1 scatter_fusion
  132.5 5.3 scatter_fusion
  143.0 5.1 scatter_fusion
  153.4 5.2 scatter_fusion
  163.8 5.1 scatter_fusion
  174.1 5.2 scatter_fusion
  184.4 52.1 %all-reduce.6.cloned.1.call-done = f32[512,256]{1,0:T(8,128)} async-done(((f32[512,256]{1,0:T(8,128)}), f32[512,256]{1,0:T(8,128)}) %all-reduce.6.cloned.1.call-update) | async-done | bytes 524304 | tf_op jit(solution)/shard_map/psum | solution.py:73
  243.0 129.0 %all-reduce.8.cloned.1.call-done = f32[1024,256]{1,0:T(8,128)} async-done(((f32[1024,256]{1,0:T(8,128)}), f32[1024,256]{1,0:T(8,128)}) %all-reduce.8.cloned.1.call-update) | async-done | bytes 1048592 | tf_op jit(solution)/shard_map/psum | solution.py:81
  376.0 130.5 %all-reduce.10.cloned.1.call-done = f32[1024,256]{1,0:T(8,128)} async-done(((f32[1024,256]{1,0:T(8,128)}), f32[1024,256]{1,0:T(8,128)}) %all-reduce.10.cloned.1.call-update) | async-done | bytes 1048592 | tf_op jit(solution)/shard_map/psum | solution.py:90
  506.5 5.1 fusion.30
  513.1 128.9 %all-reduce.12.cloned.1.call-done = f32[1024,256]{0,1:T(8,128)} async-done(((f32[1024,256]{0,1:T(8,128)}), f32[1024,256]{0,1:T(8,128)}) %all-reduce.12.cloned.1.call-update) | async-done | bytes 1048592 | tf_op jit(solution)/shard_map/psum | solution.py:96
  646.7 12.1 %copy.25 = bf16[1,256,128,128]{2,3,1,0:T(8,128)(2,1)} copy(bf16[1,256,128,128]{3,2,1,0:T(8,128)(2,1)} %bitcast.90) | data formatting | bytes 16777216 | tf_op args[8]
  662.7 38.0 %all-reduce.14.cloned.1.call-done = bf16[512,256]{0,1:T(8,128)(2,1)} async-done(((bf16[512,256]{0,1:T(8,128)(2,1)}), bf16[512,256]{0,1:T(8,128)(2,1)}) %all-reduce.14.cloned.1.call-update) | async-done | bytes 262160 | tf_op jit(solution)/shard_map/psum | solution.py:103
  707.6 165.8 %while.21 = (s32[]{:T(128)}, f32[8,128,256]{2,1,0:T(8,128)S(1)}, s32[]{:T(128)}, s32[256]{0:T(256)S(1)}, s32[]{:T(128)}, /*index=5*/bf16[256,128,128]{1,2,0:T(8,...) while((s32[]{:T(128)}, f32[8,128,256]{2,1,0:T(8,128)S(1)}, ...), condition=%wide.region_10.11_spmd, body=%wide.region_8.10_spmd.sunk | while | flops 135267456 | bytes 12063379 | solution.py:118
  (232 shorter events, 293.4 us)
Async XLA Ops:
  7.2 364.8 %copy-start = (bf16[1024,1024]{1,0:T(8,128)(2,1)S(1)}, bf16[1024,1024]{1,0:T(8,128)(2,1)}, u32[]{:S(2)}) copy-start(bf16[1024,1024]{1,0:T(8,128)(2,1)} %param.24) | copy-start | bytes 6291460
  7.2 229.3 %all-reduce.6.cloned.1.call-start = ((), (), s32[]{:S(2)}) async-start(), calls=%async_computation | async-start | bytes 1048576 | tf_op jit(solution)/shard_map/psum | solution.py:73
  9.3 3.9 copy-start.10
  9.3 3.9 copy-start.11
  181.1 190.8 %all-reduce.8.cloned.1.call-start = ((), (), s32[]{:S(2)}) async-start(), calls=%async_computation.1 | async-start | bytes 2097152 | tf_op jit(solution)/shard_map/psum | solution.py:81
  181.2 55.3 %copy-start.4 = (bf16[1,512,512]{2,1,0:T(8,128)(2,1)S(1)}, bf16[1,512,512]{2,1,0:T(8,128)(2,1)}, u32[]{:S(2)}) copy-start(bf16[1,512,512]{2,1,0:T(8,128)(2,1)} %param.23) | copy-start | bytes 1572868
  181.2 56.8 %copy-start.6 = (bf16[1,256,512]{2,1,0:T(8,128)(2,1)S(1)}, bf16[1,256,512]{2,1,0:T(8,128)(2,1)}, u32[]{:S(2)}) copy-start(bf16[1,256,512]{2,1,0:T(8,128)(2,1)} %param.30) | copy-start | bytes 786436
  243.0 263.6 %all-reduce.10.cloned.1.call-start = ((), (), s32[]{:S(2)}) async-start(), calls=%async_computation.2 | async-start | bytes 2097152 | tf_op jit(solution)/shard_map/psum | solution.py:90
  243.0 131.3 %copy-start.9 = (bf16[32,1024]{1,0:T(8,128)(2,1)S(1)}, bf16[32,1024]{1,0:T(8,128)(2,1)}, u32[]{:S(2)}) copy-start(bf16[32,1024]{1,0:T(8,128)(2,1)} %param.31) | copy-start | bytes 196612
  376.0 266.0 %all-reduce.12.cloned.1.call-start = ((), (), s32[]{:S(2)}) async-start(), calls=%async_computation.3 | async-start | bytes 2097152 | tf_op jit(solution)/shard_map/psum | solution.py:96
  511.7 133.2 %copy-start.1 = (bf16[1024,256]{0,1:T(8,128)(2,1)}, bf16[1024,256]{0,1:T(8,128)(2,1)S(1)}, u32[]{:S(2)}) copy-start(bf16[1024,256]{0,1:T(8,128)(2,1)S(1)} %get-tuple-element.162) | copy-start | bytes 1572868
  513.0 187.7 %all-reduce.14.cloned.1.call-start = ((), (), s32[]{:S(2)}) async-start(), calls=%async_computation.4 | async-start | bytes 524288 | tf_op jit(solution)/shard_map/psum | solution.py:103
  642.0 3.8 copy-start.7
  644.9 0.8 copy-start.2
  646.7 12.1 %copy-start.3 = (f32[1024,256]{0,1:T(8,128)S(1)}, f32[1024,256]{0,1:T(8,128)}, u32[]{:S(2)}) copy-start(f32[1024,256]{0,1:T(8,128)} %get-tuple-element.163) | copy-start | bytes 3145732
  660.1 40.6 %copy-start.5 = (bf16[1,512,512]{2,1,0:T(8,128)(2,1)S(1)}, bf16[1,512,512]{2,1,0:T(8,128)(2,1)}, u32[]{:S(2)}) copy-start(bf16[1,512,512]{2,1,0:T(8,128)(2,1)} %param.23) | copy-start | bytes 1572868
  707.6 165.8 %copy-start.8 = (bf16[1,8,128,128]{3,2,1,0:T(8,128)(2,1)S(1)}, bf16[1,8,128,128]{3,2,1,0:T(8,128)(2,1)}, u32[]{:S(2)}) copy-start(bf16[1,8,128,128]{3,2,1,0:T(8,128)(2,1)} %param.22) | copy-start | bytes 786436
Sparse Core Ops, SparseCore 0:
  181.3 55.1 all-reduce.5
  243.1 128.8 all-reduce.7
  377.7 128.7 all-reduce.9
  513.2 128.7 all-reduce.11
  646.8 53.8 all-reduce.13
where the time goes:
time: 886 us; the launch traced here: 882 us
  waiting for transfers between devices  479 us (54%)
  other arithmetic  165 us (19%)
  matrix products  120 us (14%)
  local copies, waits for them, and re-layouts  103 us (12%)
  between operations  14.7 us (2%)
    psum x1, waiting for transfers between devices, solve_columns(): top_sum = lax.psum(top_part, ('leaf', 'grp'))  131 us
    psum x1, waiting for transfers between devices, solve_columns(): mid_sum = lax.psum(upper[:MID_COLS], ('leaf', 'grp'))  129 us
    psum x1, waiting for transfers between devices, solve_columns(): lax.psum(mid_terms, ('leaf', 'grp'))  129 us
    scatter-add x16, other arithmetic, forward_step(): return totals.at[target_block].add(terms)  82.7 us
    scatter-add x16, other arithmetic, backward_step(): return totals_back.at[column_block].add(terms)  55.9 us
    psum x1, waiting for transfers between devices, solve_columns(): group_sum = lax.psum(flat[:GROUP_COLS], 'grp')  52.1 us
    dot_general x16, matrix products, backward_step(): jnp.einsum('pji,pjr->pir', tile_block, picked, preferred_element_type=jnp...  51 us
    gather x16, local copies, waits for them, and re-layouts, backward_step(): picked = above[target_block]  46.4 us
  transfers between devices with their start and end apart: 5, of which 5 were waited for; matrix products, arithmetic and copies ran while one was open for 2% of the time, Pallas kernels for 0%

commit v1 on v0

v1 whole, which is shorter than its diff:
```python
import functools

import jax
import jax.numpy as jnp
from jax import lax
from jax.experimental import pallas as pl
from jax.experimental.pallas import tpu as pltpu
from jax.sharding import PartitionSpec as P

BF = jnp.bfloat16
F32 = jnp.float32
MIB = 1024 * 1024
CHUNKS = 16


def dot(a, b):
    return jnp.dot(a, b, preferred_element_type=F32)


def forward_kernel(
    group_cols,
    cols,
    tgts,
    count,
    rhs_ref,
    inv_ref,
    tiles_hbm,
    out_ref,
    solved_ref,
    dense_hbm,
    tiles,
    acc,
    dense,
    tile_sems,
    dense_sems,
):
    slots, block, _ = tiles_hbm.shape
    supernodes = inv_ref.shape[0]
    targets = acc.shape[0]
    chunks = tile_sems.shape[0]
    step = slots // chunks
    parts, part_rows, _ = out_ref.shape
    group_rows = group_cols // parts
    upper_rows = part_rows - group_rows

    def tile_copy(k):
        span = pl.ds(k * step, step)
        return pltpu.make_async_copy(tiles_hbm.at[span], tiles.at[span], tile_sems.at[k])

    for k in range(chunks):
        tile_copy(k).start()

    acc[...] = jnp.zeros_like(acc)
    for s in range(supernodes):
        rows = pl.ds(s * block, block)
        solved_ref[rows, :] = dot(inv_ref[s], rhs_ref[rows, :].astype(BF)).astype(BF)

    live = count[0]
    for k in range(chunks):
        tile_copy(k).wait()

        def add(p, carry):
            t = tgts[p]
            c = cols[p]
            acc[t, c] = acc[t, c] + tiles[p].astype(F32)
            return carry

        lax.fori_loop(k * step, jnp.clip(live, k * step, (k + 1) * step), add, 0)

    def dense_copy(t):
        rows = pl.ds(t * block, block)
        return pltpu.make_async_copy(dense.at[rows], dense_hbm.at[rows], dense_sems.at[t])

    group_blocks = group_cols // block
    for t in range(targets):
        rows = pl.ds(t * block, block)
        for c in range(supernodes):
            dense[rows, c * block : (c + 1) * block] = acc[t, c].astype(BF)
        dense_copy(t).start()
        total = dot(dense[rows, :], solved_ref[...]).astype(BF)
        if t < group_blocks:
            first, per, shift = t * block, group_rows, 0
        else:
            first, per, shift = (t - group_blocks) * block, upper_rows, group_rows
        piece = min(per, block)
        for q in range(0, block, piece):
            row = first + q
            place = shift + row % per
            out_ref[row // per, place : place + piece, :] = total[q : q + piece, :]
    for t in range(targets):
        dense_copy(t).wait()


def leaf_forward(rhs, inverse, tiles, cols, tgts, count, parts, group_cols, upper_cols):
    slots, block, _ = tiles.shape
    supernodes = inverse.shape[0]
    targets = (group_cols + upper_cols) // block
    width = rhs.shape[-1]
    any_space = pl.BlockSpec(memory_space=pl.ANY)
    vmem = pl.BlockSpec(memory_space=pltpu.VMEM)
    smem = pl.BlockSpec(memory_space=pltpu.SMEM)
    return pl.pallas_call(
        functools.partial(forward_kernel, group_cols),
        out_shape=(
            jax.ShapeDtypeStruct((parts, (group_cols + upper_cols) // parts, width), BF),
            jax.ShapeDtypeStruct((supernodes * block, width), BF),
            jax.ShapeDtypeStruct((targets * block, supernodes * block), BF),
        ),
        in_specs=[smem, smem, smem, vmem, vmem, any_space],
        out_specs=(vmem, vmem, any_space),
        scratch_shapes=[
            pltpu.VMEM((slots, block, block), BF),
            pltpu.VMEM((targets, supernodes, block, block), F32),
            pltpu.VMEM((targets * block, supernodes * block), BF),
            pltpu.SemaphoreType.DMA((CHUNKS,)),
            pltpu.SemaphoreType.DMA((targets,)),
        ],
        compiler_params=pltpu.CompilerParams(vmem_limit_bytes=40 * MIB),
        name="leaf_forward",
    )(cols, tgts, count, rhs, inverse, tiles)


def group_kernel(residual_ref, inv_ref, panel_ref, section_ref, solved_ref, out_ref):
    solved_ref[...] = dot(inv_ref[...], residual_ref[...]).astype(BF)
    out_ref[...] = (section_ref[...] + dot(panel_ref[...], solved_ref[...])).astype(BF)


def group_forward(residual, inverse, panel, section):
    vmem = pl.BlockSpec(memory_space=pltpu.VMEM)
    return pl.pallas_call(
        group_kernel,
        out_shape=(
            jax.ShapeDtypeStruct(residual.shape, BF),
            jax.ShapeDtypeStruct(section.shape, BF),
        ),
        in_specs=[vmem] * 4,
        out_specs=(vmem, vmem),
        compiler_params=pltpu.CompilerParams(vmem_limit_bytes=16 * MIB),
        name="group_forward",
    )(residual, inverse, panel, section)


def backward_kernel(
    upper_ref,
    group_solved_ref,
    leaf_solved_ref,
    inv_leaf_ref,
    inv_mid_hbm,
    panel_mid_hbm,
    inv_top_hbm,
    panel_group_hbm,
    inv_group_hbm,
    dense_hbm,
    leaf_hbm,
    group_hbm,
    mid_hbm,
    top_hbm,
    inv_mid,
    panel_mid,
    inv_top,
    panel_group,
    inv_group,
    dense,
    leaf_out,
    group_out,
    mid_out,
    top_out,
    above,
    sems,
    out_sems,
):
    pairs = (
        (inv_mid_hbm, inv_mid),
        (panel_mid_hbm, panel_mid),
        (inv_top_hbm, inv_top),
        (panel_group_hbm, panel_group),
        (inv_group_hbm, inv_group),
        (dense_hbm, dense),
    )
    loads = [pltpu.make_async_copy(a, b, sems.at[i]) for i, (a, b) in enumerate(pairs)]
    for load in loads:
        load.start()
    mid_rows = inv_mid.shape[0]
    top_rows = inv_top.shape[0]
    group_rows = inv_group.shape[0]
    supernodes, block, _ = inv_leaf_ref.shape
    upper_cols = pl.ds(group_rows, mid_rows + top_rows)
    mid_cols = pl.ds(group_rows, mid_rows)
    top_cols = pl.ds(group_rows + mid_rows, top_rows)

    loads[0].wait()
    mid_solved = dot(inv_mid[...], upper_ref[0:mid_rows, :]).astype(BF)
    loads[1].wait()
    top_residual = upper_ref[mid_rows:, :].astype(F32) - dot(panel_mid[...], mid_solved)
    loads[2].wait()
    top_solved = dot(inv_top[...], top_residual.astype(BF))
    top_t = dot(top_solved.T.astype(BF), inv_top[...])
    above[:, top_cols] = top_t.astype(BF)
    top_out[...] = top_t.T
    stores = [pltpu.make_async_copy(top_out, top_hbm, out_sems.at[0])]
    stores[0].start()
    mid_back = mid_solved.astype(F32).T - dot(above[:, top_cols], panel_mid[...])
    mid_t = dot(mid_back.astype(BF), inv_mid[...])
    above[:, mid_cols] = mid_t.astype(BF)
    mid_out[...] = mid_t.T
    stores.append(pltpu.make_async_copy(mid_out, mid_hbm, out_sems.at[1]))
    stores[1].start()
    loads[3].wait()
    group_back = group_solved_ref[...].astype(F32).T - dot(above[:, upper_cols], panel_group[...])
    loads[4].wait()
    group_t = dot(group_back.astype(BF), inv_group[...])
    above[:, 0:group_rows] = group_t.astype(BF)
    group_out[...] = group_t.T
    stores.append(pltpu.make_async_copy(group_out, group_hbm, out_sems.at[2]))
    stores[2].start()
    loads[5].wait()
    for s in range(supernodes):
        cols = pl.ds(s * block, block)
        terms = dot(above[...], dense[:, cols])
        back = (leaf_solved_ref[cols, :].astype(F32).T - terms).astype(BF)
        leaf_out[cols, :] = dot(back, inv_leaf_ref[s]).T
    stores.append(pltpu.make_async_copy(leaf_out, leaf_hbm, out_sems.at[3]))
    stores[3].start()
    for store in stores:
        store.wait()


def backward(
    upper, group_solved, leaf_solved, inv_leaf, inv_mid, panel_mid, inv_top, panel_group, inv_group, dense
):
    width = upper.shape[-1]
    any_space = pl.BlockSpec(memory_space=pl.ANY)
    vmem = pl.BlockSpec(memory_space=pltpu.VMEM)
    heavy = (inv_mid, panel_mid, inv_top, panel_group, inv_group, dense)
    outs = (
        jax.ShapeDtypeStruct(leaf_solved.shape, F32),
        jax.ShapeDtypeStruct(group_solved.shape, F32),
        jax.ShapeDtypeStruct((inv_mid.shape[0], width), F32),
        jax.ShapeDtypeStruct((inv_top.shape[0], width), F32),
    )
    return pl.pallas_call(
        backward_kernel,
        out_shape=outs,
        in_specs=[vmem] * 4 + [any_space] * 6,
        out_specs=(any_space,) * 4,
        scratch_shapes=[pltpu.VMEM(a.shape, a.dtype) for a in heavy]
        + [pltpu.VMEM(a.shape, a.dtype) for a in outs]
        + [
            pltpu.VMEM((width, dense.shape[0]), BF),
            pltpu.SemaphoreType.DMA((len(heavy),)),
            pltpu.SemaphoreType.DMA((len(outs),)),
        ],
        compiler_params=pltpu.CompilerParams(vmem_limit_bytes=48 * MIB),
        name="backward",
    )(upper, group_solved, leaf_solved, inv_leaf, *heavy)


def body(
    n_leaf,
    n_grp,
    rhs_leaf,
    rhs_group,
    rhs_middle,
    rhs_top,
    inv_leaf,
    inv_group,
    inv_middle,
    inv_top,
    leaf_tiles,
    tile_column,
    tile_target,
    tile_count,
    group_panel,
    middle_panel,
):
    group_cols = rhs_group.shape[1]
    upper_cols = rhs_middle.shape[0] + rhs_top.shape[0]
    width = rhs_top.shape[-1]
    group_rows = group_cols // n_grp
    upper_rows = upper_cols // n_grp
    mine = lax.axis_index("grp")

    with jax.named_scope("gather_panels"):
        panel_mid = lax.all_gather(middle_panel, ("leaf", "grp"), axis=0, tiled=True)
        panel_group = lax.all_gather(group_panel[0], "grp", axis=0, tiled=True)

    sums, leaf_solved, dense = leaf_forward(
        rhs_leaf[0],
        inv_leaf[0],
        leaf_tiles[0],
        tile_column[0],
        tile_target[0],
        tile_count[0],
        n_grp,
        group_cols,
        upper_cols,
    )
    with jax.named_scope("reduce_group"):
        pieces = lax.all_to_all(sums, "grp", 0, 0, tiled=True)
        section = jnp.sum(pieces.astype(F32), axis=0)
    with jax.named_scope("gather_group"):
        rhs_mine = lax.dynamic_slice_in_dim(rhs_group[0], mine * group_rows, group_rows, 0)
        residual = (rhs_mine - section[:group_rows]).astype(BF)
        spread = jnp.broadcast_to(residual[None], (n_grp,) + residual.shape)
        residual = lax.all_to_all(spread, "grp", 0, 0, tiled=True).reshape(group_cols, width)
    group_solved, partial = group_forward(
        residual, inv_group[0], group_panel[0], section[group_rows:]
    )
    with jax.named_scope("sum_leaf"):
        members = [partial]
        for other in range(1, n_leaf):
            pairs = [(i, i ^ other) for i in range(n_leaf)]
            members.append(lax.ppermute(partial, "leaf", pairs))
        members = [m.astype(F32) for m in members]
        while len(members) > 1:
            members = [members[i] + members[i + 1] for i in range(0, len(members), 2)]
        rhs_upper = jnp.concatenate([rhs_middle, rhs_top], axis=0)
        rhs_mine = lax.dynamic_slice_in_dim(rhs_upper, mine * upper_rows, upper_rows, 0)
        upper = (rhs_mine - members[0]).astype(BF)
    with jax.named_scope("gather_upper"):
        upper = lax.all_gather(upper, "grp", axis=0, tiled=True)
    leaf_out, group_out, mid_out, top_out = backward(
        upper,
        group_solved,
        leaf_solved,
        inv_leaf[0],
        inv_middle,
        panel_mid,
        inv_top,
        panel_group,
        inv_group[0],
        dense,
    )
    return leaf_out[None], group_out[None], mid_out, top_out


def solution(mesh):
    n_leaf = mesh.shape["leaf"]
    n_grp = mesh.shape["grp"]
    placed = (
        P("leaf", "grp", None),
        P("leaf", None, None),
        P(),
        P(),
        P("leaf", "grp", None, None),
        P("leaf", None, None),
        P(),
        P(),
        P("leaf", "grp", None, None),
        P("leaf", "grp"),
        P("leaf", "grp"),
        P("leaf", "grp"),
        P("leaf", "grp", None),
        P(("leaf", "grp"), None),
    )
    return jax.shard_map(
        functools.partial(body, n_leaf, n_grp),
        mesh=mesh,
        in_specs=placed,
        out_specs=(P("leaf", "grp", None), P("leaf", None, None), P(), P()),
        check_vma=False,
    )
```

time: 886 us -> 154 us (0.17)
  the two profiles are of different devices: /device:TPU:14 before, /device:TPU:0 now
where the time goes in v1:
time: 154 us; the launch traced here: 153 us
  waiting for transfers between devices  85.8 us (56%)
  Pallas kernels  24.8 us (16%)
  between operations  14.5 us (9%)
  starting transfers between devices  13.5 us (9%)
  local copies, waits for them, and re-layouts  11.9 us (8%)
  other arithmetic  2.94 us (2%)
    all_to_all x1, waiting for transfers between devices, body(): pieces = lax.all_to_all(sums, 'grp', 0, 0, tiled=True)  35.8 us
    all_gather x1, waiting for transfers between devices, body(): upper = lax.all_gather(upper, 'grp', axis=0, tiled=True)  22.8 us
    pallas_call x1, Pallas kernels, backward(): pl.pallas_call(backward_kernel, out_shape=outs, in_specs=[vmem] * 4 + [an...  12.6 us
    pallas_call x1, Pallas kernels, leaf_forward(): pl.pallas_call(functools.partial(forward_kernel, group_cols), out_shape=(...  11.6 us
    all_to_all x1, waiting for transfers between devices, body(): lax.all_to_all(spread, 'grp', 0, 0, tiled=True).reshape(group_cols, width)  10.8 us
    unnamed x30, local copies, waits for them, and re-layouts  10.5 us
    ppermute x3, waiting for transfers between devices, body(): members.append(lax.ppermute(partial, 'leaf', pairs))  9.22 us
    all_to_all x1, starting transfers between devices, body(): pieces = lax.all_to_all(sums, 'grp', 0, 0, tiled=True)  6.33 us
  transfers between devices with their start and end apart: 8, of which 7 were waited for; matrix products, arithmetic and copies ran while one was open for 3% of the time, Pallas kernels for 8%

profile of v1, /device:TPU:0, one launch (start us, length us, event | category | flops | bytes accessed | tf_op | source)
XLA Modules:
  0.0 153.5 jit_solution(7034558913982868226)
XLA Ops:
  7.9 0.7 all-gather.7.cloned.1.call-update
  9.3 0.9 copy-done.3
  10.2 1.2 copy-done.8
  12.8 11.6 %leaf_forward.1 = (bf16[8,320,256]{2,1,0:T(8,128)(2,1)}, bf16[1024,256]{1,0:T(8,128)(2,1)S(1)}, bf16[2560,1024]{1,0:T(8,128)(2,1)S(1)}) custom-call(s32[256]{0:T(256)S(1)} %bitcast.22, s32[256]{0:T(256)S(1)} %bitcast.23, s32[1]{0:T(128)} %bitcast.14.count, f32[1024,256]{1,0:T(8,128)S(1)} %bitcast.21, bf16[8,128,128]{2,1,0:T(8,128)(2,1)S(1)} %bitcast.17, ...), custom_call_target="tpu_custom_call" | custom-call | tf_op jit(solution)/shard_map/leaf_forward/pallas_call | solution.py:102
  24.5 2.3 %copy-done = bf16[2560,1024]{1,0:T(8,128)(2,1)} copy-done((bf16[2560,1024]{1,0:T(8,128)(2,1)}, bf16[2560,1024]{1,0:T(8,128)(2,1)S(1)}, u32[]{:S(2)}) %copy-start) | copy-done | bytes 5242904
  26.8 0.8 copy-done.9
  27.6 6.3 %all-to-all-start = ((bf16[8,320,256]{2,1,0:T(8,128)(2,1)}), bf16[8,320,256]{2,1,0:T(8,128)(2,1)S(1)}, u32[]{:S(2)}, u32[]{:S(2)}) async-start(bf16[8,320,256]{2,1,0:T(8,128)(2,1)} %get-tuple-element.13), calls=%async_computation | async-start | bytes 2621440 | tf_op jit(solution)/shard_map/reduce_group/all_to_all | solution.py:299
  33.9 35.8 %all-to-all-done = bf16[8,320,256]{2,1,0:T(8,128)(2,1)S(1)} async-done(((bf16[8,320,256]{2,1,0:T(8,128)(2,1)}), bf16[8,320,256]{2,1,0:T(8,128)(2,1)S(1)}, u32[]{:S(2)}, u32[]{:S(2)}) %all-to-all-start) | async-done | bytes 1310752 | tf_op jit(solution)/shard_map/reduce_group/all_to_all | solution.py:299
  69.9 0.9 fusion.3
  70.8 0.7 broadcast_in_dim.12
  71.5 3.4 %all-to-all-start.1 = ((bf16[8,64,256]{2,1,0:T(8,128)(2,1)}), bf16[8,64,256]{2,1,0:T(8,128)(2,1)S(1)}, u32[]{:S(2)}, u32[]{:S(2)}) async-start(bf16[8,64,256]{2,1,0:T(8,128)(2,1)} %broadcast_in_dim.12), calls=%async_computation.1 | async-start | bytes 524288 | tf_op jit(solution)/shard_map/gather_group/all_to_all | solution.py:305
  75.1 0.7 slice.9.section_ref
  75.9 10.8 %all-to-all-done.1 = bf16[8,64,256]{2,1,0:T(8,128)(2,1)S(1)} async-done(((bf16[8,64,256]{2,1,0:T(8,128)(2,1)}), bf16[8,64,256]{2,1,0:T(8,128)(2,1)S(1)}, u32[]{:S(2)}, u32[]{:S(2)}) %all-to-all-start.1) | async-done | bytes 262176 | tf_op jit(solution)/shard_map/gather_group/all_to_all | solution.py:305
  86.6 0.9 copy-done.7
  88.8 2.6 %collective-permute-start.2 = (bf16[256,256]{1,0:T(8,128)(2,1)S(1)}, bf16[256,256]{1,0:T(8,128)(2,1)}, u32[]{:S(2)}, u32[]{:S(2)}) collective-permute-start(bf16[256,256]{1,0:T(8,128)(2,1)S(1)} %get-tuple-element.14), channel_id=1, source_target_pairs={{0,24},{8,16},{16,8},{24,0},{1,25},{9,17},{17,9},{25,1},{2,26},{10... | collective-permute-start | bytes 393224 | tf_op jit(solution)/shard_map/sum_leaf/ppermute | solution.py:313
  92.3 5.8 %collective-permute-done.2 = bf16[256,256]{1,0:T(8,128)(2,1)} collective-permute-done((bf16[256,256]{1,0:T(8,128)(2,1)S(1)}, bf16[256,256]{1,0:T(8,128)(2,1)}, u32[]{:S(2)}, u32[]{:S(2)}) %collective-permute-start.2) | collective-permute-done | bytes 131104 | tf_op jit(solution)/shard_map/sum_leaf/ppermute | solution.py:313
  98.1 2.5 %collective-permute-done.1 = bf16[256,256]{1,0:T(8,128)(2,1)} collective-permute-done((bf16[256,256]{1,0:T(8,128)(2,1)S(1)}, bf16[256,256]{1,0:T(8,128)(2,1)}, u32[]{:S(2)}, u32[]{:S(2)}) %collective-permute-start.1) | collective-permute-done | bytes 131104 | tf_op jit(solution)/shard_map/sum_leaf/ppermute | solution.py:313
  100.7 0.9 collective-permute-done
  101.6 1.9 %fusion.2 = bf16[256,256]{1,0:T(8,128)(2,1)} fusion(s32[]{:T(128)S(6)} %select_n.6, f32[1024,256]{1,0:T(8,128)} %param.16, f32[1024,256]{1,0:T(8,128)} %param.17, bf16[256,256]{1,0:T(8,128)(2,1)} %collective-permute-done.2, bf16[256,256]{1,0:T(8,128)(2,1)} %collective-permute-done.1, bf16[256,256]{1,0:T(8,128)(2,1)} %collective-permute-done, ...), kind=kLoop, calls=%fused_computation.5 | loop fusion | flops 655360 | bytes 2752516 | tf_op jit(solution)/shard_map/sum_leaf/convert_element_type | solution.py:319
  103.5 5.8 %all-gather.7.cloned.1.call-done.panel_mid_hbm = bf16[1024,1024]{1,0:T(8,128)(2,1)} async-done(((bf16[32,1024]{1,0:T(8,128)(2,1)}), bf16[1024,1024]{1,0:T(8,128)(2,1)}) %all-gather.7.cloned.1.call-update) | async-done | bytes 2097168 | tf_op jit(solution)/shard_map/gather_panels/all_gather | solution.py:284
  109.3 22.8 %all-gather.5.cloned.1.call-done.upper_ref = bf16[2048,256]{1,0:T(8,128)(2,1)} async-done(((bf16[256,256]{1,0:T(8,128)(2,1)}), bf16[2048,256]{1,0:T(8,128)(2,1)}) %all-gather.5.cloned.1.call-update) | async-done | bytes 1048592 | tf_op jit(solution)/shard_map/gather_upper/all_gather | solution.py:321
  132.1 1.2 copy-done.5
  133.3 0.9 copy-done.12
  134.3 12.6 %backward.1 = (f32[1024,256]{1,0:T(8,128)}, f32[512,256]{1,0:T(8,128)}, f32[1024,256]{1,0:T(8,128)}, f32[1024,256]{1,0:T(8,128)}) custom-call(bf16[2048,256]{1,0:T(8,128)(2,1)S(1)} %copy-done.5, bf16[512,256]{1,0:T(8,128)(2,1)S(1)} %copy-done.12, bf16[1024,256]{1,0:T(8,128)(2,1)S(1)} %copy-done.10, bf16[8,128,128]{2,1,0:T(8,128)(2,1)S(1)} %bitcast.18, ...), custom_call_target="tpu_custom_call" | custom-call | tf_op jit(solution)/shard_map/backward/pallas_call | solution.py:241
  (33 shorter events, 4.7 us)
Async XLA Ops:
  7.2 96.3 %all-gather.9.cloned.1.call-start = ((), (), s32[]{:S(2)}) async-start(), calls=%async_computation.4 | async-start | bytes 2359296 | tf_op jit(solution)/shard_map/gather_panels/all_gather | solution.py:285
  7.9 101.4 %all-gather.7.cloned.1.call-start = ((), (), s32[]{:S(2)}) async-start(), calls=%async_computation.3 | async-start | bytes 2162688 | tf_op jit(solution)/shard_map/gather_panels/all_gather | solution.py:284
  9.3 1.0 copy-start.3
  10.2 1.2 copy-start.8
  11.5 0.7 copy-start.13
  12.2 0.7 copy-start.14
  24.5 2.3 %copy-start = (bf16[2560,1024]{1,0:T(8,128)(2,1)}, bf16[2560,1024]{1,0:T(8,128)(2,1)S(1)}, u32[]{:S(2)}) copy-start(bf16[2560,1024]{1,0:T(8,128)(2,1)S(1)} %get-tuple-element.17.dense_hbm) | copy-start | bytes 15728644
  26.8 0.8 copy-start.9
  27.6 42.1 %all-to-all-start = ((bf16[8,320,256]{2,1,0:T(8,128)(2,1)}), bf16[8,320,256]{2,1,0:T(8,128)(2,1)S(1)}, u32[]{:S(2)}, u32[]{:S(2)}) async-start(bf16[8,320,256]{2,1,0:T(8,128)(2,1)} %get-tuple-element.13), calls=%async_computation | async-start | bytes 2621440 | tf_op jit(solution)/shard_map/reduce_group/all_to_all | solution.py:299
  33.9 52.7 %copy-start.1 = (bf16[1,512,512]{2,1,0:T(8,128)(2,1)S(1)}, bf16[1,512,512]{2,1,0:T(8,128)(2,1)}, u32[]{:S(2)}) copy-start(bf16[1,512,512]{2,1,0:T(8,128)(2,1)} %param.19) | copy-start | bytes 1572868
  33.9 52.7 %copy-start.6 = (bf16[1,256,512]{2,1,0:T(8,128)(2,1)S(1)}, bf16[1,256,512]{2,1,0:T(8,128)(2,1)}, u32[]{:S(2)}) copy-start(bf16[1,256,512]{2,1,0:T(8,128)(2,1)} %param.26) | copy-start | bytes 786436
  71.5 15.1 %all-to-all-start.1 = ((bf16[8,64,256]{2,1,0:T(8,128)(2,1)}), bf16[8,64,256]{2,1,0:T(8,128)(2,1)S(1)}, u32[]{:S(2)}, u32[]{:S(2)}) async-start(bf16[8,64,256]{2,1,0:T(8,128)(2,1)} %broadcast_in_dim.12), calls=%async_computation.1 | async-start | bytes 524288 | tf_op jit(solution)/shard_map/gather_group/all_to_all | solution.py:305
  74.9 57.2 %all-gather.5.cloned.1.call-start = ((), (), s32[]{:S(2)}) async-start(), calls=%async_computation.2 | async-start | bytes 1179648 | tf_op jit(solution)/shard_map/gather_upper/all_gather | solution.py:321
  86.6 1.0 copy-start.7
  87.6 44.5 %copy-start.2 = (bf16[1024,1024]{1,0:T(8,128)(2,1)S(1)}, bf16[1024,1024]{1,0:T(8,128)(2,1)}, u32[]{:S(2)}) copy-start(bf16[1024,1024]{1,0:T(8,128)(2,1)} %inv_mid_hbm.1) | copy-start | bytes 6291460
  87.6 44.5 %copy-start.4 = (bf16[1,8,128,128]{3,2,1,0:T(8,128)(2,1)S(1)}, bf16[1,8,128,128]{3,2,1,0:T(8,128)(2,1)}, u32[]{:S(2)}) copy-start(bf16[1,8,128,128]{3,2,1,0:T(8,128)(2,1)} %param.18) | copy-start | bytes 786436
  88.1 0.7 copy-start.11
  88.8 43.3 %copy-start.10 = (bf16[1024,256]{1,0:T(8,128)(2,1)S(1)}, bf16[1024,256]{1,0:T(8,128)(2,1)}, u32[]{:S(2)}) copy-start(bf16[1024,256]{1,0:T(8,128)(2,1)} %copy-done.9) | copy-start | bytes 1572868
  88.8 9.3 %collective-permute-start.2 = (bf16[256,256]{1,0:T(8,128)(2,1)S(1)}, bf16[256,256]{1,0:T(8,128)(2,1)}, u32[]{:S(2)}, u32[]{:S(2)}) collective-permute-start(bf16[256,256]{1,0:T(8,128)(2,1)S(1)} %get-tuple-element.14), channel_id=1, source_target_pairs={{0,24},{8,16},{16,8},{24,0},{1,25},{9,17},{17,9},{25,1},{2,26},{10... | collective-permute-start | bytes 393224 | tf_op jit(solution)/shard_map/sum_leaf/ppermute | solution.py:313
  91.5 9.2 %collective-permute-start.1 = (bf16[256,256]{1,0:T(8,128)(2,1)S(1)}, bf16[256,256]{1,0:T(8,128)(2,1)}, u32[]{:S(2)}, u32[]{:S(2)}) collective-permute-start(bf16[256,256]{1,0:T(8,128)(2,1)S(1)} %get-tuple-element.14), channel_id=1, source_target_pairs={{0,16},{8,24},{16,0},{24,8},{1,17},{9,25},{17,1},{25,9},{2,18},{10... | collective-permute-start | bytes 393224 | tf_op jit(solution)/shard_map/sum_leaf/ppermute | solution.py:313
  91.9 9.6 %collective-permute-start = (bf16[256,256]{1,0:T(8,128)(2,1)S(1)}, bf16[256,256]{1,0:T(8,128)(2,1)}, u32[]{:S(2)}, u32[]{:S(2)}) collective-permute-start(bf16[256,256]{1,0:T(8,128)(2,1)S(1)} %get-tuple-element.14), channel_id=1, source_target_pairs={{0,8},{8,0},{16,24},{24,16},{1,9},{9,1},{17,25},{25,17},{2,10},{10... | collective-permute-start | bytes 393224 | tf_op jit(solution)/shard_map/sum_leaf/ppermute | solution.py:313
  132.1 1.2 copy-start.5
  133.3 0.9 copy-start.12
Sparse Core Ops, SparseCore 0:
  9.6 34.4 all-gather.8
  47.1 62.1 all-gather.6
  111.4 20.6 all-gather.4

commit v2 on v1

v2 whole, which is shorter than its diff:
```python
import functools

import jax
import jax.numpy as jnp
from jax import lax
from jax.experimental import pallas as pl
from jax.experimental.pallas import tpu as pltpu
from jax.sharding import PartitionSpec as P

BF = jnp.bfloat16
F32 = jnp.float32
MIB = 1024 * 1024
CHUNKS = 16
UNROLL = 4
HBM = pl.BlockSpec(memory_space=pltpu.HBM)
VMEM = pl.BlockSpec(memory_space=pltpu.VMEM)
SMEM = pl.BlockSpec(memory_space=pltpu.SMEM)


def dot(a, b):
    return jnp.dot(a, b, preferred_element_type=F32)


def place():
    g = lax.axis_index("grp")
    return lax.axis_index("leaf"), g >> 1, g & 1


def forward_kernel(
    sec,
    count,
    cols_hbm,
    tgts_hbm,
    rhs_hbm,
    inv_hbm,
    tiles_hbm,
    keep_hbm,
    send_hbm,
    solved_hbm,
    dense_hbm,
    cols,
    tgts,
    rhs,
    inv,
    tiles,
    acc,
    dense,
    solved,
    stage,
    in_sems,
    tile_sems,
    out_sems,
):
    slots, block, _ = tiles.shape
    supernodes = inv.shape[0]
    targets = acc.shape[0]
    chunks = tile_sems.shape[0]
    step = slots // chunks
    group_cols = stage.shape[1] - (targets * block - stage.shape[1])
    _, _, core = place()

    def tile_copy(k):
        span = pl.ds(k * step, step)
        return pltpu.make_async_copy(tiles_hbm.at[span], tiles.at[span], tile_sems.at[k])

    pairs = ((cols_hbm, cols), (tgts_hbm, tgts), (rhs_hbm, rhs), (inv_hbm, inv))
    loads = [pltpu.make_async_copy(a, b, in_sems.at[i]) for i, (a, b) in enumerate(pairs)]
    for load in loads:
        load.start()
    for k in range(chunks):
        tile_copy(k).start()

    acc[...] = jnp.zeros_like(acc)
    for load in loads:
        load.wait()
    for s in range(supernodes):
        rows = pl.ds(s * block, block)
        solved[rows, :] = dot(inv[s], rhs[rows, :].astype(BF)).astype(BF)
    stores = [pltpu.make_async_copy(solved, solved_hbm, out_sems.at[0])]
    stores[0].start()

    live = count[0]

    def add(p):
        t = tgts[0, p]
        c = cols[0, p]
        acc[t, c] = acc[t, c] + tiles[p].astype(F32)

    def add_some(i, carry):
        for u in range(UNROLL):
            add(i * UNROLL + u)
        return carry

    def add_one(p, carry):
        add(p)
        return carry

    whole = live // UNROLL
    per = step // UNROLL
    for k in range(chunks):
        tile_copy(k).wait()
        lax.fori_loop(k * per, jnp.clip(whole, k * per, (k + 1) * per), add_some, 0)
    lax.fori_loop(whole * UNROLL, live, add_one, 0)

    span = group_cols
    blocks = span // block
    for i in range(targets // blocks):
        for t in range(i * blocks, (i + 1) * blocks):
            for c in range(supernodes):
                dense[t * block : (t + 1) * block, c * block : (c + 1) * block] = acc[t, c].astype(BF)
        rows = pl.ds(i * span, span)
        stores.append(pltpu.make_async_copy(dense.at[rows], dense_hbm.at[rows], out_sems.at[3 + i]))
        stores[-1].start()
        total = dot(dense[rows, :], solved[...]).astype(BF)
        if i == 0:
            stage[0, 0:span, :] = total
            stage[1, 0:span, :] = total
        else:
            for q in range(0, span, sec):
                section = ((i - 1) * span + q) // sec
                begin = group_cols + (section // 2) * sec
                stage[(section % 2) ^ core, begin : begin + sec, :] = total[q : q + sec, :]
    for k, target in enumerate((keep_hbm, send_hbm)):
        stores.append(pltpu.make_async_copy(stage.at[k], target, out_sems.at[1 + k]))
        stores[-1].start()
    for store in stores:
        store.wait()


def leaf_forward(rhs, inverse, tiles, cols, tgts, count, sec, group_cols, upper_cols):
    slots, block, _ = tiles.shape
    supernodes = inverse.shape[0]
    targets = (group_cols + upper_cols) // block
    width = rhs.shape[-1]
    half = group_cols + upper_cols // 2
    return pl.pallas_call(
        functools.partial(forward_kernel, sec),
        out_shape=(
            jax.ShapeDtypeStruct((half, width), BF),
            jax.ShapeDtypeStruct((half, width), BF),
            jax.ShapeDtypeStruct((supernodes * block, width), BF),
            jax.ShapeDtypeStruct((targets * block, supernodes * block), BF),
        ),
        in_specs=[SMEM] + [HBM] * 5,
        out_specs=(HBM,) * 4,
        scratch_shapes=[
            pltpu.SMEM(cols.shape, cols.dtype),
            pltpu.SMEM(tgts.shape, tgts.dtype),
            pltpu.VMEM(rhs.shape, rhs.dtype),
            pltpu.VMEM(inverse.shape, inverse.dtype),
            pltpu.VMEM((slots, block, block), BF),
            pltpu.VMEM((targets, supernodes, block, block), F32),
            pltpu.VMEM((targets * block, supernodes * block), BF),
            pltpu.VMEM((supernodes * block, width), BF),
            pltpu.VMEM((2, half, width), BF),
            pltpu.SemaphoreType.DMA((4,)),
            pltpu.SemaphoreType.DMA((CHUNKS,)),
            pltpu.SemaphoreType.DMA((3 + targets * block // group_cols,)),
        ],
        compiler_params=pltpu.CompilerParams(vmem_limit_bytes=40 * MIB),
        name="leaf_forward",
    )(count, cols, tgts, rhs, inverse, tiles)


def fold_kernel(n_leaf, n_pos, keep, recv, inv, rhs, panel, *refs):
    outs, (gsum, stage) = refs[: n_leaf + 1], refs[n_leaf + 1 :]
    leaf, pos, core = place()
    group_cols = inv.shape[0]
    sec = panel.shape[0] // n_pos
    q = sec // n_leaf
    gq = group_cols // (2 * n_pos)
    gsum[...] = keep[0:group_cols, :].astype(F32) + recv[0:group_cols, :].astype(F32)
    residual = rhs[...] * (1.0 / n_pos) - gsum[...]
    solved = dot(inv[...], residual.astype(BF)).astype(BF)
    for p in range(n_pos):
        rows = pl.ds(group_cols + p * sec, sec)
        terms = dot(panel[p * sec : (p + 1) * sec, :], solved)
        terms = (terms + (keep[rows, :].astype(F32) + recv[rows, :].astype(F32))).astype(BF)
        for j in range(n_leaf):
            stage[j ^ leaf, p * q : (p + 1) * q, :] = terms[j * q : (j + 1) * q, :]
        begin = pl.multiple_of(core * (group_cols // 2) + p * gq, gq)
        outs[n_leaf][p ^ pos] = gsum[pl.ds(begin, gq), :].astype(BF)
    for k in range(n_leaf):
        outs[k][...] = stage[k]


def fold(keep, recv, inverse, rhs, panel, n_leaf, n_pos):
    width = rhs.shape[-1]
    part = (panel.shape[0] // n_leaf, width)
    gq = inverse.shape[0] // (2 * n_pos)
    return pl.pallas_call(
        functools.partial(fold_kernel, n_leaf, n_pos),
        out_shape=[jax.ShapeDtypeStruct(part, BF)] * n_leaf
        + [jax.ShapeDtypeStruct((n_pos, gq, width), BF)],
        in_specs=[VMEM] * 5,
        out_specs=[VMEM] * (n_leaf + 1),
        scratch_shapes=[pltpu.VMEM(rhs.shape, F32), pltpu.VMEM((n_leaf,) + part, BF)],
        compiler_params=pltpu.CompilerParams(vmem_limit_bytes=24 * MIB),
        name="fold_group",
    )(keep, recv, inverse, rhs, panel)


def sum_leaf_kernel(n_leaf, n_pos, *refs):
    parts, group, outs, stage = refs[:n_leaf], refs[n_leaf], refs[n_leaf + 1 : -1], refs[-1]
    _, pos, _ = place()
    q = stage.shape[1]
    total = parts[0][...].astype(F32)
    for part in parts[1:]:
        total = total + part[...].astype(F32)
    total = total.astype(BF)
    for p in range(n_pos):
        stage[p ^ pos] = total[p * q : (p + 1) * q, :]
    for k in range(n_pos):
        outs[k][0:q, :] = stage[k]
        outs[k][q:, :] = group[k]


def sum_leaf(parts, group):
    n_pos, gq, width = group.shape
    q = parts[0].shape[0] // n_pos
    return pl.pallas_call(
        functools.partial(sum_leaf_kernel, len(parts), n_pos),
        out_shape=[jax.ShapeDtypeStruct((q + gq, width), BF)] * n_pos,
        in_specs=[VMEM] * (len(parts) + 1),
        out_specs=[VMEM] * n_pos,
        scratch_shapes=[pltpu.VMEM((n_pos, q, width), BF)],
        name="sum_leaf",
    )(*parts, group)


def sum_pos_kernel(rhs, *refs):
    total = refs[0][...].astype(F32)
    for part in refs[1:-1]:
        total = total + part[...].astype(F32)
    refs[-1][...] = (rhs[...] - total).astype(BF)


def sum_pos(rhs, parts):
    return pl.pallas_call(
        sum_pos_kernel,
        out_shape=jax.ShapeDtypeStruct(rhs.shape, BF),
        in_specs=[VMEM] * (len(parts) + 1),
        out_specs=VMEM,
        name="sum_pos",
    )(rhs, *parts)


def backward_kernel(
    n_leaf,
    n_pos,
    mine,
    theirs,
    leaf_solved_hbm,
    inv_leaf_hbm,
    inv_mid_hbm,
    panel_mid_hbm,
    inv_top_hbm,
    inv_group_hbm,
    panel_group_hbm,
    dense_hbm,
    leaf_hbm,
    group_hbm,
    mid_hbm,
    top_hbm,
    leaf_solved,
    inv_leaf,
    inv_mid,
    panel_mid,
    inv_top,
    inv_group,
    panel_group,
    dense,
    leaf_out,
    group_out,
    mid_out,
    top_out,
    upper,
    residual,
    above,
    sems,
    out_sems,
):
    pairs = (
        (inv_mid_hbm, inv_mid),
        (panel_mid_hbm, panel_mid),
        (inv_top_hbm, inv_top),
        (inv_group_hbm, inv_group),
        (panel_group_hbm, panel_group),
        (dense_hbm, dense),
        (leaf_solved_hbm, leaf_solved),
        (inv_leaf_hbm, inv_leaf),
    )
    loads = [pltpu.make_async_copy(a, b, sems.at[i]) for i, (a, b) in enumerate(pairs)]
    for load in loads:
        load.start()
    mid_rows = inv_mid.shape[0]
    top_rows = inv_top.shape[0]
    group_rows = inv_group.shape[0]
    supernodes, block, _ = inv_leaf.shape
    upper_cols = pl.ds(group_rows, mid_rows + top_rows)
    mid_cols = pl.ds(group_rows, mid_rows)
    top_cols = pl.ds(group_rows + mid_rows, top_rows)
    leaf, pos, core = place()
    sec = (mid_rows + top_rows) // (2 * n_pos)
    q = sec // n_leaf
    gq = group_rows // (2 * n_pos)
    for kc, got in enumerate((mine, theirs)):
        for kz in range(n_pos):
            for kl in range(n_leaf):
                row = sec * (2 * (pos ^ kz) + (core ^ kc)) + q * (leaf ^ kl)
                begin = (kl * n_pos + kz) * q
                upper[pl.ds(pl.multiple_of(row, q), q), :] = got[begin : begin + q, :]
            row = (group_rows // 2) * (core ^ kc) + gq * (pos ^ kz)
            begin = n_leaf * n_pos * q + kz * gq
            residual[pl.ds(pl.multiple_of(row, gq), gq), :] = got[begin : begin + gq, :]

    loads[0].wait()
    mid_solved = dot(inv_mid[...], upper[0:mid_rows, :]).astype(BF)
    loads[1].wait()
    top_residual = upper[mid_rows:, :].astype(F32) - dot(panel_mid[...], mid_solved)
    loads[2].wait()
    top_solved = dot(inv_top[...], top_residual.astype(BF))
    top_t = dot(top_solved.T.astype(BF), inv_top[...])
    above[:, top_cols] = top_t.astype(BF)
    top_out[...] = top_t.T
    stores = [pltpu.make_async_copy(top_out, top_hbm, out_sems.at[0])]
    stores[0].start()
    mid_back = mid_solved.astype(F32).T - dot(above[:, top_cols], panel_mid[...])
    mid_t = dot(mid_back.astype(BF), inv_mid[...])
    above[:, mid_cols] = mid_t.astype(BF)
    mid_out[...] = mid_t.T
    stores.append(pltpu.make_async_copy(mid_out, mid_hbm, out_sems.at[1]))
    stores[1].start()
    loads[3].wait()
    group_solved = dot(inv_group[...], residual[...]).astype(BF).astype(F32).T
    loads[4].wait()
    group_back = group_solved - dot(above[:, upper_cols], panel_group[...])
    group_t = dot(group_back.astype(BF), inv_group[...])
    above[:, 0:group_rows] = group_t.astype(BF)
    group_out[...] = group_t.T
    stores.append(pltpu.make_async_copy(group_out, group_hbm, out_sems.at[2]))
    stores[2].start()
    for load in loads[5:]:
        load.wait()
    for s in range(supernodes):
        cols = pl.ds(s * block, block)
        terms = dot(above[...], dense[:, cols])
        back = (leaf_solved[cols, :].astype(F32).T - terms).astype(BF)
        leaf_out[cols, :] = dot(back, inv_leaf[s]).T
    stores.append(pltpu.make_async_copy(leaf_out, leaf_hbm, out_sems.at[3]))
    stores[3].start()
    for store in stores:
        store.wait()


def backward(
    mine,
    theirs,
    leaf_solved,
    inv_leaf,
    inv_mid,
    panel_mid,
    inv_top,
    inv_group,
    panel_group,
    dense,
    n_leaf,
    n_pos,
):
    width = mine.shape[-1]
    upper_rows = inv_mid.shape[0] + inv_top.shape[0]
    group_rows = inv_group.shape[0]
    heavy = (leaf_solved, inv_leaf, inv_mid, panel_mid, inv_top, inv_group, panel_group, dense)
    outs = (
        jax.ShapeDtypeStruct(leaf_solved.shape, F32),
        jax.ShapeDtypeStruct((group_rows, width), F32),
        jax.ShapeDtypeStruct((inv_mid.shape[0], width), F32),
        jax.ShapeDtypeStruct((inv_top.shape[0], width), F32),
    )
    return pl.pallas_call(
        functools.partial(backward_kernel, n_leaf, n_pos),
        out_shape=outs,
        in_specs=[VMEM] * 2 + [HBM] * len(heavy),
        out_specs=(HBM,) * 4,
        scratch_shapes=[pltpu.VMEM(a.shape, a.dtype) for a in heavy]
        + [pltpu.VMEM(a.shape, a.dtype) for a in outs]
        + [
            pltpu.VMEM((upper_rows, width), BF),
            pltpu.VMEM((group_rows, width), BF),
            pltpu.VMEM((width, dense.shape[0]), BF),
            pltpu.SemaphoreType.DMA((len(heavy),)),
            pltpu.SemaphoreType.DMA((len(outs),)),
        ],
        compiler_params=pltpu.CompilerParams(vmem_limit_bytes=48 * MIB),
        name="backward",
    )(mine, theirs, *heavy)


def swap(x, axis, size, bits):
    return lax.ppermute(x, axis, [(i, i ^ bits) for i in range(size)])


def weave(own, other, core):
    first = jnp.where(core == 0, own, other)
    second = jnp.where(core == 0, other, own)
    both = jnp.stack([first, second], axis=1)
    return both.reshape(-1, both.shape[-1])


def body(
    n_leaf,
    n_grp,
    rhs_leaf,
    rhs_group,
    rhs_middle,
    rhs_top,
    inv_leaf,
    inv_group,
    inv_middle,
    inv_top,
    leaf_tiles,
    tile_column,
    tile_target,
    tile_count,
    group_panel,
    middle_panel,
):
    n_pos = n_grp // 2
    group_cols = rhs_group.shape[1]
    mid_cols = rhs_middle.shape[0]
    upper_cols = mid_cols + rhs_top.shape[0]
    sec = upper_cols // n_grp
    q = sec // n_leaf
    gq = group_cols // n_grp
    leaf, pos, core = place()
    pos_groups = [[2 * p + c for p in range(n_pos)] for c in range(2)]
    chip_groups = [
        [a * n_grp + 2 * p + c for a in range(n_leaf) for p in range(n_pos)] for c in range(2)
    ]

    with jax.named_scope("gather_panels"):
        panel_half = lax.all_gather(group_panel[0], "grp", axis_index_groups=pos_groups)
        middle_half = lax.all_gather(
            middle_panel, ("leaf", "grp"), axis_index_groups=chip_groups
        )

    keep, send, leaf_solved, dense = leaf_forward(
        rhs_leaf[0],
        inv_leaf[0],
        leaf_tiles[0],
        tile_column,
        tile_target,
        tile_count[0],
        sec,
        group_cols,
        upper_cols,
    )
    with jax.named_scope("swap_cores"):
        recv = swap(send, "grp", n_grp, 1)
    *parts, group = fold(
        keep,
        recv,
        inv_group[0],
        rhs_group[0],
        panel_half.reshape(-1, group_cols),
        n_leaf,
        n_pos,
    )
    with jax.named_scope("sum_over_leaf"):
        parts = parts[:1] + [swap(parts[k], "leaf", n_leaf, k) for k in range(1, n_leaf)]
    sends = list(sum_leaf(parts, group))
    with jax.named_scope("sum_over_pos"):
        got = sends[:1] + [swap(sends[k], "grp", n_grp, 2 * k) for k in range(1, n_pos)]
    begin = sec * lax.axis_index("grp") + q * leaf
    low = lax.dynamic_slice_in_dim(rhs_middle, jnp.minimum(begin, mid_cols - q), q, 0)
    high = lax.dynamic_slice_in_dim(rhs_top, jnp.maximum(begin - mid_cols, 0), q, 0)
    group_begin = (group_cols // 2) * core + gq * pos
    group_rhs = lax.dynamic_slice_in_dim(rhs_group[0], group_begin, gq, 0)
    rhs_mine = jnp.concatenate([jnp.where(begin < mid_cols, low, high), group_rhs], axis=0)
    residual = sum_pos(rhs_mine, got)
    with jax.named_scope("gather_pos"):
        got = [residual] + [swap(residual, "grp", n_grp, 2 * k) for k in range(1, n_pos)]
        uppers = jnp.concatenate([x[:q] for x in got], axis=0)
        groups = [x[q:] for x in got]
    with jax.named_scope("gather_leaf"):
        stacks = [uppers] + [swap(uppers, "leaf", n_leaf, k) for k in range(1, n_leaf)]
        mine = jnp.concatenate(stacks + groups, axis=0)
    with jax.named_scope("gather_cores"):
        theirs = swap(mine, "grp", n_grp, 1)
    with jax.named_scope("swap_panels"):
        panel_group = weave(panel_half, swap(panel_half, "grp", n_grp, 1), core)
        panel_mid = weave(middle_half, swap(middle_half, "grp", n_grp, 1), core)
    leaf_out, group_out, mid_out, top_out = backward(
        mine,
        theirs,
        leaf_solved,
        inv_leaf[0],
        inv_middle,
        panel_mid,
        inv_top,
        inv_group[0],
        panel_group,
        dense,
        n_leaf,
        n_pos,
    )
    return leaf_out[None], group_out[None], mid_out, top_out


def solution(mesh):
    n_leaf = mesh.shape["leaf"]
    n_grp = mesh.shape["grp"]
    placed = (
        P("leaf", "grp", None),
        P("leaf", None, None),
        P(),
        P(),
        P("leaf", "grp", None, None),
        P("leaf", None, None),
        P(),
        P(),
        P("leaf", "grp", None, None),
        P("leaf", "grp"),
        P("leaf", "grp"),
        P("leaf", "grp"),
        P("leaf", "grp", None),
        P(("leaf", "grp"), None),
    )
    return jax.shard_map(
        functools.partial(body, n_leaf, n_grp),
        mesh=mesh,
        in_specs=placed,
        out_specs=(P("leaf", "grp", None), P("leaf", None, None), P(), P()),
        check_vma=False,
    )
```

time: 154 us -> 126 us (0.82)
  waiting for transfers between devices: 85.8 us -> 47.9 us
  starting transfers between devices: 13.5 us -> 16.8 us
  Pallas kernels: 24.8 us -> 27.6 us
  other arithmetic: 2.94 us -> 4.9 us
  local copies, waits for them, and re-layouts: 11.9 us -> 13.7 us
    all_to_all x2 -> x0, waiting for transfers between devices: 46.5 us -> none  [the longest x1 35.8 us: body(): pieces = lax.all_to_all(sums, 'grp', 0, 0, tiled=True)]
    ppermute x3 -> x16, starting transfers between devices: 3.49 us -> 16.8 us  [swap(): return lax.ppermute(x, axis, [(i, i ^ bits) for i in range(size)])]
    all_to_all x2 -> x0, starting transfers between devices: 9.74 us -> none  [the longest x1 6.33 us: body(): pieces = lax.all_to_all(sums, 'grp', 0, 0, tiled=True)]
    ppermute x3 -> x16, waiting for transfers between devices: 9.22 us -> 14.9 us  [swap(): return lax.ppermute(x, axis, [(i, i ^ bits) for i in range(size)])]
    all_gather x3 -> x2, waiting for transfers between devices: 28.6 us -> 32.3 us  [the longest x1 18.3 us: body(): lax.all_gather(middle_panel, ('leaf', 'grp'), axis_index_groups=chip_groups)]
    another operation x0 -> x4, other arithmetic: none -> 3.29 us  [weave(): both = jnp.stack([first, second], axis=1)]
    pallas_call x3 -> x5, Pallas kernels: 24.8 us -> 27.6 us  [the longest x1 13.1 us: backward(): pl.pallas_call(functools.partial(backward_kernel, n_leaf, n_pos), out_sha...]
    convert_element_type x2 -> x0, other arithmetic: 2.76 us -> none  [the longest x1 1.9 us: body(): upper = (rhs_mine - members[0]).astype(BF)]
  transfers between devices with their start and end apart: 8 -> 18, of which waited for: 7 -> 9; matrix products, arithmetic and copies ran while one was open for 3% -> 6% of each run, Pallas kernels for 8% -> 11%
where the time goes in v2:
time: 126 us
  waiting for transfers between devices  47.9 us (38%)
  Pallas kernels  27.6 us (22%)
  starting transfers between devices  16.8 us (13%)
  between operations  14.9 us (12%)
  local copies, waits for them, and re-layouts  13.7 us (11%)
  other arithmetic  4.9 us (4%)
    all_gather x1, waiting for transfers between devices, body(): lax.all_gather(middle_panel, ('leaf', 'grp'), axis_index_groups=chip_groups)  18.3 us
    ppermute x16, starting transfers between devices, swap(): return lax.ppermute(x, axis, [(i, i ^ bits) for i in range(size)])  16.8 us
    ppermute x16, waiting for transfers between devices, swap(): return lax.ppermute(x, axis, [(i, i ^ bits) for i in range(size)])  14.9 us
    all_gather x1, waiting for transfers between devices, body(): lax.all_gather(group_panel[0], 'grp', axis_index_groups=pos_groups)  14.1 us
    pallas_call x1, Pallas kernels, backward(): pl.pallas_call(functools.partial(backward_kernel, n_leaf, n_pos), out_sha...  13.1 us
    unnamed x46, local copies, waits for them, and re-layouts  11.4 us
    pallas_call x1, Pallas kernels, leaf_forward(): pl.pallas_call(functools.partial(forward_kernel, sec), out_shape=(jax.Sha...  9.18 us
    another operation x4, other arithmetic, weave(): both = jnp.stack([first, second], axis=1)  3.29 us
  transfers between devices with their start and end apart: 18, of which 9 were waited for; matrix products, arithmetic and copies ran while one was open for 6% of the time, Pallas kernels for 11%

profile of v2, /device:TPU:0, one launch (start us, length us, event | category | flops | bytes accessed | tf_op | source)
XLA Modules:
  0.0 125.8 jit_solution(8563329657875971824)
XLA Ops:
  12.1 9.2 %leaf_forward.1 = (bf16[1536,256]{1,0:T(8,128)(2,1)S(1)}, bf16[1536,256]{1,0:T(8,128)(2,1)}, bf16[1024,256]{1,0:T(8,128)(2,1)S(1)}, bf16[2560,1024]{1,0:T(8,128)(2,1)S(1)}) custom-call(s32[1]{0:T(128)} %bitcast.24.count, s32[1,256]{1,0:T(1,128)S(1)} %copy-done.11, s32[1,256]{1,0:T(1,128)S(1)} %copy-done.12, f32[1024,256]{1,0:T(8,128)S(1)} %bitcast.30, ...), custom_call_target="tpu_custom_call" | custom-call | tf_op jit(solution)/shard_map/leaf_forward/pallas_call | solution.py:136
  21.3 2.3 %copy-done = bf16[2560,1024]{1,0:T(8,128)(2,1)} copy-done((bf16[2560,1024]{1,0:T(8,128)(2,1)}, bf16[2560,1024]{1,0:T(8,128)(2,1)S(1)}, u32[]{:S(2)}) %copy-start) | copy-done | bytes 5242904
  24.1 2.1 %collective-permute-done.recv = bf16[1536,256]{1,0:T(8,128)(2,1)S(1)} collective-permute-done((bf16[1536,256]{1,0:T(8,128)(2,1)}, bf16[1536,256]{1,0:T(8,128)(2,1)S(1)}, u32[]{:S(2)}, u32[]{:S(2)}) %collective-permute-start) | collective-permute-done | bytes 786464 | tf_op jit(solution)/shard_map/swap_cores/ppermute | solution.py:400
  26.2 14.1 %all-gather.4.cloned.1.call-done = bf16[4,256,512]{2,1,0:T(8,128)(2,1)} async-done(((bf16[1,256,512]{2,1,0:T(8,128)(2,1)}), bf16[4,256,512]{2,1,0:T(8,128)(2,1)}) %all-gather.4.cloned.1.call-update) | async-done | bytes 1048592 | tf_op jit(solution)/shard_map/gather_panels/all_gather | solution.py:442
  41.5 1.6 %fold_group.1 = (bf16[256,256]{1,0:T(8,128)(2,1)S(1)}, bf16[256,256]{1,0:T(8,128)(2,1)}, bf16[256,256]{1,0:T(8,128)(2,1)}, bf16[256,256]{1,0:T(8,128)(2,1)S(1)}, bf16[4,64,256]{2,1,0:T(8,128)(2,1)S(1)}) custom-call(bf16[1536,256]{1,0:T(8,128)(2,1)S(1)} %get-tuple-element.21.keep, bf16[1536,256]{1,0:T(8,128)(2,1)S(1)} %collective-permute-done.recv, ...), custom_call_target="tpu_custom_call" | custom-call | tf_op jit(solution)/shard_map/fold_group/pallas_call | solution.py:191
  44.4 1.5 %collective-permute-start.1 = (bf16[256,256]{1,0:T(8,128)(2,1)}, bf16[256,256]{1,0:T(8,128)(2,1)S(1)}, u32[]{:S(2)}, u32[]{:S(2)}) collective-permute-start(bf16[256,256]{1,0:T(8,128)(2,1)} %get-tuple-element.24), channel_id=1, source_target_pairs={{0,8},{8,0},{16,24},{24,16},{1,9},{9,1},{17,25},{25,17},{2,10},{10... | collective-permute-start | bytes 393224 | tf_op jit(solution)/shard_map/sum_over_leaf/ppermute | solution.py:400
  45.9 1.5 %collective-permute-start.2 = (bf16[256,256]{1,0:T(8,128)(2,1)}, bf16[256,256]{1,0:T(8,128)(2,1)S(1)}, u32[]{:S(2)}, u32[]{:S(2)}) collective-permute-start(bf16[256,256]{1,0:T(8,128)(2,1)} %get-tuple-element.25), channel_id=1, source_target_pairs={{0,16},{8,24},{16,0},{24,8},{1,17},{9,25},{17,1},{25,9},{2,18},{10... | collective-permute-start | bytes 393224 | tf_op jit(solution)/shard_map/sum_over_leaf/ppermute | solution.py:400
  48.9 1.5 %collective-permute-done.1.refs_1_ = bf16[256,256]{1,0:T(8,128)(2,1)S(1)} collective-permute-done((bf16[256,256]{1,0:T(8,128)(2,1)}, bf16[256,256]{1,0:T(8,128)(2,1)S(1)}, u32[]{:S(2)}, u32[]{:S(2)}) %collective-permute-start.1) | collective-permute-done | bytes 131104 | tf_op jit(solution)/shard_map/sum_over_leaf/ppermute | solution.py:400
  50.4 3.5 %collective-permute-done.2.refs_2_ = bf16[256,256]{1,0:T(8,128)(2,1)S(1)} collective-permute-done((bf16[256,256]{1,0:T(8,128)(2,1)}, bf16[256,256]{1,0:T(8,128)(2,1)S(1)}, u32[]{:S(2)}, u32[]{:S(2)}) %collective-permute-start.2) | collective-permute-done | bytes 131104 | tf_op jit(solution)/shard_map/sum_over_leaf/ppermute | solution.py:400
  54.6 2.0 %sum_leaf.1 = (bf16[128,256]{1,0:T(8,128)(2,1)}, bf16[128,256]{1,0:T(8,128)(2,1)}, bf16[128,256]{1,0:T(8,128)(2,1)}, bf16[128,256]{1,0:T(8,128)(2,1)}) custom-call(bf16[256,256]{1,0:T(8,128)(2,1)} %copy-done.9, bf16[256,256]{1,0:T(8,128)(2,1)} %copy-done.14, bf16[256,256]{1,0:T(8,128)(2,1)} %copy-done.15, bf16[256,256]{1,0:T(8,128)(2,1)} %copy-done.16, ...), custom_call_target="tpu_custom_call" | custom-call | tf_op jit(solution)/shard_map/sum_leaf/pallas_call | solution.py:221
  56.6 1.5 %collective-permute-start.4 = (bf16[128,256]{1,0:T(8,128)(2,1)}, bf16[128,256]{1,0:T(8,128)(2,1)S(1)}, u32[]{:S(2)}, u32[]{:S(2)}) collective-permute-start(bf16[128,256]{1,0:T(8,128)(2,1)} %get-tuple-element.29), channel_id=1, source_target_pairs={{0,2},{1,3},{2,0},{3,1},{4,6},{5,7},{6,4},{7,5},{8,10},{9,11},{10,... | collective-permute-start | bytes 196616 | tf_op jit(solution)/shard_map/sum_over_pos/ppermute | solution.py:400
  59.2 1.8 %collective-permute-start.6 = (bf16[128,256]{1,0:T(8,128)(2,1)}, bf16[128,256]{1,0:T(8,128)(2,1)S(1)}, u32[]{:S(2)}, u32[]{:S(2)}) collective-permute-start(bf16[128,256]{1,0:T(8,128)(2,1)} %get-tuple-element.31), channel_id=1, source_target_pairs={{0,6},{1,7},{2,4},{3,5},{4,2},{5,3},{6,0},{7,1},{8,14},{9,15},{10,... | collective-permute-start | bytes 196616 | tf_op jit(solution)/shard_map/sum_over_pos/ppermute | solution.py:400
  61.7 2.9 %collective-permute-done.5.refs_2_ = bf16[128,256]{1,0:T(8,128)(2,1)S(1)} collective-permute-done((bf16[128,256]{1,0:T(8,128)(2,1)}, bf16[128,256]{1,0:T(8,128)(2,1)S(1)}, u32[]{:S(2)}, u32[]{:S(2)}) %collective-permute-start.5) | collective-permute-done | bytes 65568 | tf_op jit(solution)/shard_map/sum_over_pos/ppermute | solution.py:400
  66.2 1.7 %sum_pos.1 = bf16[128,256]{1,0:T(8,128)(2,1)} custom-call(f32[128,256]{1,0:T(8,128)} %pad_maximum_fusion.2.rhs, bf16[128,256]{1,0:T(8,128)(2,1)} %get-tuple-element.28.refs_0_, bf16[128,256]{1,0:T(8,128)(2,1)} %copy-done.17, bf16[128,256]{1,0:T(8,128)(2,1)} %copy-done.18, bf16[128,256]{1,0:T(8,128)(2,1)} %copy-done.19), custom_call_target="tpu_custom_call" | custom-call | tf_op jit(solution)/shard_map/sum_pos/pallas_call | solution.py:239
  67.8 1.9 %collective-permute-start.9 = (bf16[128,256]{1,0:T(8,128)(2,1)}, bf16[128,256]{1,0:T(8,128)(2,1)S(1)}, u32[]{:S(2)}, u32[]{:S(2)}) collective-permute-start(bf16[128,256]{1,0:T(8,128)(2,1)} %sum_pos.1), channel_id=1, source_target_pairs={{0,6},{1,7},{2,4},{3,5},{4,2},{5,3},{6,0},{7,1},{8,14},{9,15},{10,... | collective-permute-start | bytes 196616 | tf_op jit(solution)/shard_map/gather_pos/ppermute | solution.py:400
  70.3 1.9 %collective-permute-start.7 = (bf16[128,256]{1,0:T(8,128)(2,1)}, bf16[128,256]{1,0:T(8,128)(2,1)S(1)}, u32[]{:S(2)}, u32[]{:S(2)}) collective-permute-start(bf16[128,256]{1,0:T(8,128)(2,1)} %sum_pos.1), channel_id=1, source_target_pairs={{0,2},{1,3},{2,0},{3,1},{4,6},{5,7},{6,4},{7,5},{8,10},{9,11},{10,... | collective-permute-start | bytes 196616 | tf_op jit(solution)/shard_map/gather_pos/ppermute | solution.py:400
  73.0 2.2 %collective-permute-done.7 = bf16[128,256]{1,0:T(8,128)(2,1)S(1)} collective-permute-done((bf16[128,256]{1,0:T(8,128)(2,1)}, bf16[128,256]{1,0:T(8,128)(2,1)S(1)}, u32[]{:S(2)}, u32[]{:S(2)}) %collective-permute-start.7) | collective-permute-done | bytes 65568 | tf_op jit(solution)/shard_map/gather_pos/ppermute | solution.py:400
  75.2 1.6 %collective-permute-done.8 = bf16[128,256]{1,0:T(8,128)(2,1)S(1)} collective-permute-done((bf16[128,256]{1,0:T(8,128)(2,1)}, bf16[128,256]{1,0:T(8,128)(2,1)S(1)}, u32[]{:S(2)}, u32[]{:S(2)}) %collective-permute-start.8) | collective-permute-done | bytes 65568 | tf_op jit(solution)/shard_map/gather_pos/ppermute | solution.py:400
  76.9 1.8 %collective-permute-start.10 = (bf16[256,256]{1,0:T(8,128)(2,1)S(1)}, bf16[256,256]{1,0:T(8,128)(2,1)S(1)}, u32[]{:S(2)}, u32[]{:S(2)}) collective-permute-start(bf16[256,256]{1,0:T(8,128)(2,1)S(1)} %pad_maximum_fusion.3), channel_id=1, source_target_pairs={{0,8},{8,0},{16,24},{24,16},{1,9},{9,1},{17,25},{25,17},{2,10},{10... | collective-permute-start | bytes 393224 | tf_op jit(solution)/shard_map/gather_leaf/ppermute | solution.py:400
  80.5 18.3 %all-gather.6.cloned.1.call-done = bf16[512,1024]{1,0:T(8,128)(2,1)} async-done(((bf16[32,1024]{1,0:T(8,128)(2,1)}), bf16[512,1024]{1,0:T(8,128)(2,1)}) %all-gather.6.cloned.1.call-update) | async-done | bytes 1048592 | tf_op jit(solution)/shard_map/gather_panels/all_gather | solution.py:443
  100.2 1.4 %select_bitcast_fusion.1 = (bf16[4,1,256,512]{3,2,0,1:T(8,128)(2,1)S(1)}, bf16[4,1,256,512]{3,2,0,1:T(8,128)(2,1)S(1)}) fusion(bf16[4,256,512]{2,1,0:T(8,128)(2,1)S(1)} %copy-done.2, bf16[4,256,512]{2,1,0:T(8,128)(2,1)} %collective-permute-done.15, pred[]{:T(512)S(6)} %eq.2), kind=kLoop, calls=%fused_computation.3 | loop fusion | flops 1048576 | bytes 4194305 | tf_op jit(solution)/shard_map/swap_panels/stack | solution.py:406
  101.7 1.4 %copy.21 = bf16[4,2,256,512]{3,2,1,0:T(8,128)(2,1)} copy(bf16[4,2,256,512]{3,2,0,1:T(8,128)(2,1)S(1)} %pad_maximum_fusion.1) | data formatting | bytes 4194304 | tf_op jit(solution)/shard_map/swap_panels/stack | solution.py:406
  103.5 1.6 %pad_maximum_fusion = bf16[16,2,32,1024]{3,2,1,0:T(8,128)(2,1)} fusion(bf16[16,1,32,1024]{3,2,1,0:T(8,128)(2,1)S(1)} %get-tuple-element.41, bf16[16,1,32,1024]{3,2,1,0:T(8,128)(2,1)S(1)} %get-tuple-element.40), kind=kLoop, calls=%fused_computation | loop fusion | flops 1048576 | bytes 4194304 | tf_op jit(solution)/shard_map/swap_panels/stack | solution.py:406
  105.8 13.1 %backward.1 = (f32[1024,256]{1,0:T(8,128)}, f32[512,256]{1,0:T(8,128)}, f32[1024,256]{1,0:T(8,128)}, f32[1024,256]{1,0:T(8,128)}) custom-call(bf16[1280,256]{1,0:T(8,128)(2,1)S(1)} %slice_dynamic-update-slice_fusion.mine, bf16[1280,256]{1,0:T(8,128)(2,1)S(1)} %collective-permute-done.13.theirs, bf16[1024,256]{1,0:T(8,128)(2,1)S(1)} %get-tuple-element.32.leaf_solved_hbm, ...), custom_call_target="tpu_custom_call" | custom-call | tf_op jit(solution)/shard_map/backward/pallas_call | solution.py:380
  (79 shorter events, 18.5 us)
Async XLA Ops:
  7.2 33.1 %all-gather.4.cloned.1.call-start = ((), (), s32[]{:S(2)}) async-start(), calls=%async_computation | async-start | bytes 1310720 | tf_op jit(solution)/shard_map/gather_panels/all_gather | solution.py:442
  7.9 90.8 %all-gather.6.cloned.1.call-start = ((), (), s32[]{:S(2)}) async-start(), calls=%async_computation.1 | async-start | bytes 1114112 | tf_op jit(solution)/shard_map/gather_panels/all_gather | solution.py:443
  12.1 28.1 %copy-start.3 = (bf16[1,512,512]{2,1,0:T(8,128)(2,1)S(1)}, bf16[1,512,512]{2,1,0:T(8,128)(2,1)}, u32[]{:S(2)}) copy-start(bf16[1,512,512]{2,1,0:T(8,128)(2,1)} %param.19) | copy-start | bytes 1572868
  12.1 28.1 %copy-start.8 = (f32[1,512,256]{2,1,0:T(8,128)S(1)}, f32[1,512,256]{2,1,0:T(8,128)}, u32[]{:S(2)}) copy-start(f32[1,512,256]{2,1,0:T(8,128)} %param.15) | copy-start | bytes 1572868
  21.3 2.4 %copy-start = (bf16[2560,1024]{1,0:T(8,128)(2,1)}, bf16[2560,1024]{1,0:T(8,128)(2,1)S(1)}, u32[]{:S(2)}) copy-start(bf16[2560,1024]{1,0:T(8,128)(2,1)S(1)} %get-tuple-element.33.dense_hbm) | copy-start | bytes 15728644
  23.7 2.5 %collective-permute-start = (bf16[1536,256]{1,0:T(8,128)(2,1)}, bf16[1536,256]{1,0:T(8,128)(2,1)S(1)}, u32[]{:S(2)}, u32[]{:S(2)}) collective-permute-start(bf16[1536,256]{1,0:T(8,128)(2,1)} %get-tuple-element.22), channel_id=1, source_target_pairs={{0,1},{1,0},{2,3},{3,2},{4,5},{5,4},{6,7},{7,6},{8,9},{9,8},{10,11... | collective-permute-start | bytes 2359304 | tf_op jit(solution)/shard_map/swap_cores/ppermute | solution.py:400
  44.4 34.8 %copy-start.2 = (bf16[4,256,512]{2,1,0:T(8,128)(2,1)S(1)}, bf16[4,256,512]{2,1,0:T(8,128)(2,1)}, u32[]{:S(2)}) copy-start(bf16[4,256,512]{2,1,0:T(8,128)(2,1)} %all-gather.4.cloned.1.call-done) | copy-start | bytes 3145732
  44.4 6.0 %collective-permute-start.1 = (bf16[256,256]{1,0:T(8,128)(2,1)}, bf16[256,256]{1,0:T(8,128)(2,1)S(1)}, u32[]{:S(2)}, u32[]{:S(2)}) collective-permute-start(bf16[256,256]{1,0:T(8,128)(2,1)} %get-tuple-element.24), channel_id=1, source_target_pairs={{0,8},{8,0},{16,24},{24,16},{1,9},{9,1},{17,25},{25,17},{2,10},{10... | collective-permute-start | bytes 393224 | tf_op jit(solution)/shard_map/sum_over_leaf/ppermute | solution.py:400
  45.9 8.1 %collective-permute-start.2 = (bf16[256,256]{1,0:T(8,128)(2,1)}, bf16[256,256]{1,0:T(8,128)(2,1)S(1)}, u32[]{:S(2)}, u32[]{:S(2)}) collective-permute-start(bf16[256,256]{1,0:T(8,128)(2,1)} %get-tuple-element.25), channel_id=1, source_target_pairs={{0,16},{8,24},{16,0},{24,8},{1,17},{9,25},{17,1},{25,9},{2,18},{10... | collective-permute-start | bytes 393224 | tf_op jit(solution)/shard_map/sum_over_leaf/ppermute | solution.py:400
  47.4 6.6 %collective-permute-start.3 = (bf16[256,256]{1,0:T(8,128)(2,1)S(1)}, bf16[256,256]{1,0:T(8,128)(2,1)S(1)}, u32[]{:S(2)}, u32[]{:S(2)}) collective-permute-start(bf16[256,256]{1,0:T(8,128)(2,1)S(1)} %get-tuple-element.26), channel_id=1, source_target_pairs={{0,24},{8,16},{16,8},{24,0},{1,25},{9,17},{17,9},{25,1},{2,26},{10... | collective-permute-start | bytes 393224 | tf_op jit(solution)/shard_map/sum_over_leaf/ppermute | solution.py:400
  50.4 3.5 %copy-start.14 = (bf16[256,256]{1,0:T(8,128)(2,1)}, bf16[256,256]{1,0:T(8,128)(2,1)S(1)}, u32[]{:S(2)}) copy-start(bf16[256,256]{1,0:T(8,128)(2,1)S(1)} %collective-permute-done.1.refs_1_) | copy-start | bytes 393220
  56.6 5.1 %collective-permute-start.4 = (bf16[128,256]{1,0:T(8,128)(2,1)}, bf16[128,256]{1,0:T(8,128)(2,1)S(1)}, u32[]{:S(2)}, u32[]{:S(2)}) collective-permute-start(bf16[128,256]{1,0:T(8,128)(2,1)} %get-tuple-element.29), channel_id=1, source_target_pairs={{0,2},{1,3},{2,0},{3,1},{4,6},{5,7},{6,4},{7,5},{8,10},{9,11},{10,... | collective-permute-start | bytes 196616 | tf_op jit(solution)/shard_map/sum_over_pos/ppermute | solution.py:400
  58.1 6.5 %collective-permute-start.5 = (bf16[128,256]{1,0:T(8,128)(2,1)}, bf16[128,256]{1,0:T(8,128)(2,1)S(1)}, u32[]{:S(2)}, u32[]{:S(2)}) collective-permute-start(bf16[128,256]{1,0:T(8,128)(2,1)} %get-tuple-element.30), channel_id=1, source_target_pairs={{0,4},{1,5},{2,6},{3,7},{4,0},{5,1},{6,2},{7,3},{8,12},{9,13},{10,... | collective-permute-start | bytes 196616 | tf_op jit(solution)/shard_map/sum_over_pos/ppermute | solution.py:400
  59.2 6.4 %collective-permute-start.6 = (bf16[128,256]{1,0:T(8,128)(2,1)}, bf16[128,256]{1,0:T(8,128)(2,1)S(1)}, u32[]{:S(2)}, u32[]{:S(2)}) collective-permute-start(bf16[128,256]{1,0:T(8,128)(2,1)} %get-tuple-element.31), channel_id=1, source_target_pairs={{0,6},{1,7},{2,4},{3,5},{4,2},{5,3},{6,0},{7,1},{8,14},{9,15},{10,... | collective-permute-start | bytes 196616 | tf_op jit(solution)/shard_map/sum_over_pos/ppermute | solution.py:400
  61.7 3.9 %copy-start.17 = (bf16[128,256]{1,0:T(8,128)(2,1)}, bf16[128,256]{1,0:T(8,128)(2,1)S(1)}, u32[]{:S(2)}) copy-start(bf16[128,256]{1,0:T(8,128)(2,1)S(1)} %collective-permute-done.4.refs_1_) | copy-start | bytes 196612
  67.8 9.0 %collective-permute-start.9 = (bf16[128,256]{1,0:T(8,128)(2,1)}, bf16[128,256]{1,0:T(8,128)(2,1)S(1)}, u32[]{:S(2)}, u32[]{:S(2)}) collective-permute-start(bf16[128,256]{1,0:T(8,128)(2,1)} %sum_pos.1), channel_id=1, source_target_pairs={{0,6},{1,7},{2,4},{3,5},{4,2},{5,3},{6,0},{7,1},{8,14},{9,15},{10,... | collective-permute-start | bytes 196616 | tf_op jit(solution)/shard_map/gather_pos/ppermute | solution.py:400
  69.7 7.1 %collective-permute-start.8 = (bf16[128,256]{1,0:T(8,128)(2,1)}, bf16[128,256]{1,0:T(8,128)(2,1)S(1)}, u32[]{:S(2)}, u32[]{:S(2)}) collective-permute-start(bf16[128,256]{1,0:T(8,128)(2,1)} %sum_pos.1), channel_id=1, source_target_pairs={{0,4},{1,5},{2,6},{3,7},{4,0},{5,1},{6,2},{7,3},{8,12},{9,13},{10,... | collective-permute-start | bytes 196616 | tf_op jit(solution)/shard_map/gather_pos/ppermute | solution.py:400
  70.3 4.9 %collective-permute-start.7 = (bf16[128,256]{1,0:T(8,128)(2,1)}, bf16[128,256]{1,0:T(8,128)(2,1)S(1)}, u32[]{:S(2)}, u32[]{:S(2)}) collective-permute-start(bf16[128,256]{1,0:T(8,128)(2,1)} %sum_pos.1), channel_id=1, source_target_pairs={{0,2},{1,3},{2,0},{3,1},{4,6},{5,7},{6,4},{7,5},{8,10},{9,11},{10,... | collective-permute-start | bytes 196616 | tf_op jit(solution)/shard_map/gather_pos/ppermute | solution.py:400
  76.9 21.8 %collective-permute-start.10 = (bf16[256,256]{1,0:T(8,128)(2,1)S(1)}, bf16[256,256]{1,0:T(8,128)(2,1)S(1)}, u32[]{:S(2)}, u32[]{:S(2)}) collective-permute-start(bf16[256,256]{1,0:T(8,128)(2,1)S(1)} %pad_maximum_fusion.3), channel_id=1, source_target_pairs={{0,8},{8,0},{16,24},{24,16},{1,9},{9,1},{17,25},{25,17},{2,10},{10... | collective-permute-start | bytes 393224 | tf_op jit(solution)/shard_map/gather_leaf/ppermute | solution.py:400
  78.7 20.0 %collective-permute-start.11 = (bf16[256,256]{1,0:T(8,128)(2,1)S(1)}, bf16[256,256]{1,0:T(8,128)(2,1)S(1)}, u32[]{:S(2)}, u32[]{:S(2)}) collective-permute-start(bf16[256,256]{1,0:T(8,128)(2,1)S(1)} %pad_maximum_fusion.3), channel_id=1, source_target_pairs={{0,16},{8,24},{16,0},{24,8},{1,17},{9,25},{17,1},{25,9},{2,18},{10... | collective-permute-start | bytes 393224 | tf_op jit(solution)/shard_map/gather_leaf/ppermute | solution.py:400
  79.2 20.9 %collective-permute-start.15 = (bf16[4,256,512]{2,1,0:T(8,128)(2,1)S(1)}, bf16[4,256,512]{2,1,0:T(8,128)(2,1)}, u32[]{:S(2)}, u32[]{:S(2)}) collective-permute-start(bf16[4,256,512]{2,1,0:T(8,128)(2,1)S(1)} %copy-done.2), channel_id=1, source_target_pairs={{0,1},{1,0},{2,3},{3,2},{4,5},{5,4},{6,7},{7,6},{8,9},{9,8},{10,11... | collective-permute-start | bytes 3145736 | tf_op jit(solution)/shard_map/swap_panels/ppermute | solution.py:400
  79.2 19.5 %collective-permute-start.12 = (bf16[256,256]{1,0:T(8,128)(2,1)S(1)}, bf16[256,256]{1,0:T(8,128)(2,1)S(1)}, u32[]{:S(2)}, u32[]{:S(2)}) collective-permute-start(bf16[256,256]{1,0:T(8,128)(2,1)S(1)} %pad_maximum_fusion.3), channel_id=1, source_target_pairs={{0,24},{8,16},{16,8},{24,0},{1,25},{9,17},{17,9},{25,1},{2,26},{10... | collective-permute-start | bytes 393224 | tf_op jit(solution)/shard_map/gather_leaf/ppermute | solution.py:400
  98.7 4.5 %collective-permute-start.14 = (bf16[16,32,1024]{2,1,0:T(8,128)(2,1)}, bf16[16,32,1024]{2,1,0:T(8,128)(2,1)S(1)}, u32[]{:S(2)}, u32[]{:S(2)}) collective-permute-start(bf16[16,32,1024]{2,1,0:T(8,128)(2,1)} %bitcast.35), channel_id=1, source_target_pairs={{0,1},{1,0},{2,3},{3,2},{4,5},{5,4},{6,7},{7,6},{8,9},{9,8},{10,11... | collective-permute-start | bytes 3145736 | tf_op jit(solution)/shard_map/swap_panels/ppermute | solution.py:400
  99.6 5.5 %collective-permute-start.13 = (bf16[1280,256]{1,0:T(8,128)(2,1)S(1)}, bf16[1280,256]{1,0:T(8,128)(2,1)S(1)}, u32[]{:S(2)}, u32[]{:S(2)}) collective-permute-start(bf16[1280,256]{1,0:T(8,128)(2,1)S(1)} %slice_dynamic-update-slice_fusion.mine), channel_id=1, source_target_pairs={{0,1},{1,0},{2,3},{3,2},{4,5},{5,4},{6,7},{7,6},{8,9},{9,8},{10,11... | collective-permute-start | bytes 1966088 | tf_op jit(solution)/shard_map/gather_cores/ppermute | solution.py:400
  (14 other events, 15.3 us)
Sparse Core Ops, SparseCore 0:
  9.6 30.6 all-gather.3
  43.0 55.6 all-gather.5

commit v3 on v2

v3 whole, which is shorter than its diff:
```python
import functools

import jax
import jax.numpy as jnp
from jax import lax
from jax.experimental import pallas as pl
from jax.experimental.pallas import tpu as pltpu
from jax.sharding import PartitionSpec as P

BF = jnp.bfloat16
F32 = jnp.float32
MIB = 1024 * 1024
CHUNKS = 16
UNROLL = 4
HBM = pl.BlockSpec(memory_space=pltpu.HBM)
VMEM = pl.BlockSpec(memory_space=pltpu.VMEM)
BIG = 58 * MIB
SMALL = 4 * MIB


def dot(a, b):
    return jnp.dot(a, b, preferred_element_type=F32)


def place():
    g = lax.axis_index("grp")
    return lax.axis_index("leaf"), g >> 1, g & 1


def forward_kernel(
    sec,
    inv_rows,
    count_hbm,
    cols_hbm,
    tgts_hbm,
    rhs_hbm,
    inv_hbm,
    tiles_hbm,
    keep_hbm,
    send_hbm,
    solved_hbm,
    dense_hbm,
    count,
    cols,
    tgts,
    rhs,
    inv,
    tiles,
    acc,
    dense,
    solved,
    stage,
    in_sems,
    tile_sems,
    out_sems,
):
    slots, block, _ = tiles.shape
    supernodes = inv.shape[0]
    targets = acc.shape[0]
    chunks = tile_sems.shape[0]
    step = slots // chunks
    group_cols = inv_rows
    _, _, core = place()

    def tile_copy(k):
        span = pl.ds(k * step, step)
        return pltpu.make_async_copy(tiles_hbm.at[span], tiles.at[span], tile_sems.at[k])

    pairs = (
        (count_hbm, count),
        (cols_hbm, cols),
        (tgts_hbm, tgts),
        (rhs_hbm, rhs),
        (inv_hbm, inv),
    )
    loads = [pltpu.make_async_copy(a, b, in_sems.at[i]) for i, (a, b) in enumerate(pairs)]
    for load in loads:
        load.start()
    for k in range(chunks):
        tile_copy(k).start()

    acc[...] = jnp.zeros_like(acc)
    for load in loads:
        load.wait()
    for s in range(supernodes):
        rows = pl.ds(s * block, block)
        solved[rows, :] = dot(inv[s], rhs[rows, :].astype(BF)).astype(BF)
    stores = [pltpu.make_async_copy(solved, solved_hbm, out_sems.at[0])]
    stores[0].start()

    live = count[0, 0]

    def add(p):
        t = tgts[0, p]
        c = cols[0, p]
        acc[t, c] = acc[t, c] + tiles[p].astype(F32)

    def add_some(i, carry):
        for u in range(UNROLL):
            add(i * UNROLL + u)
        return carry

    def add_one(p, carry):
        add(p)
        return carry

    whole = live // UNROLL
    per = step // UNROLL
    for k in range(chunks):
        tile_copy(k).wait()
        lax.fori_loop(k * per, jnp.clip(whole, k * per, (k + 1) * per), add_some, 0)
    lax.fori_loop(whole * UNROLL, live, add_one, 0)

    span = group_cols
    blocks = span // block
    for i in range(targets // blocks):
        for t in range(i * blocks, (i + 1) * blocks):
            for c in range(supernodes):
                dense[t * block : (t + 1) * block, c * block : (c + 1) * block] = acc[t, c].astype(BF)
        rows = pl.ds(i * span, span)
        stores.append(pltpu.make_async_copy(dense.at[rows], dense_hbm.at[rows], out_sems.at[3 + i]))
        stores[-1].start()
        total = dot(dense[rows, :], solved[...]).astype(BF)
        if i == 0:
            for c in range(2):
                stage[c ^ core, 0 : span // 2, :] = total[c * span // 2 : (c + 1) * span // 2, :]
        else:
            for q in range(0, span, sec):
                section = ((i - 1) * span + q) // sec
                begin = group_cols // 2 + (section // 2) * sec
                stage[(section % 2) ^ core, begin : begin + sec, :] = total[q : q + sec, :]
    for k, target in enumerate((keep_hbm, send_hbm)):
        stores.append(pltpu.make_async_copy(stage.at[k], target, out_sems.at[1 + k]))
        stores[-1].start()
    for store in stores:
        store.wait()


def leaf_forward(rhs, inverse, tiles, cols, tgts, count, sec, group_cols, upper_cols):
    slots, block, _ = tiles.shape
    supernodes = inverse.shape[0]
    targets = (group_cols + upper_cols) // block
    width = rhs.shape[-1]
    half = (group_cols + upper_cols) // 2
    return pl.pallas_call(
        functools.partial(forward_kernel, sec, group_cols),
        out_shape=(
            jax.ShapeDtypeStruct((half, width), BF),
            jax.ShapeDtypeStruct((half, width), BF),
            jax.ShapeDtypeStruct((supernodes * block, width), BF),
            jax.ShapeDtypeStruct((targets * block, supernodes * block), BF),
        ),
        in_specs=[HBM] * 6,
        out_specs=(HBM,) * 4,
        scratch_shapes=[
            pltpu.SMEM(count.shape, count.dtype),
            pltpu.SMEM(cols.shape, cols.dtype),
            pltpu.SMEM(tgts.shape, tgts.dtype),
            pltpu.VMEM(rhs.shape, rhs.dtype),
            pltpu.VMEM(inverse.shape, inverse.dtype),
            pltpu.VMEM((slots, block, block), BF),
            pltpu.VMEM((targets, supernodes, block, block), F32),
            pltpu.VMEM((targets * block, supernodes * block), BF),
            pltpu.VMEM((supernodes * block, width), BF),
            pltpu.VMEM((2, half, width), BF),
            pltpu.SemaphoreType.DMA((5,)),
            pltpu.SemaphoreType.DMA((CHUNKS,)),
            pltpu.SemaphoreType.DMA((3 + targets * block // group_cols,)),
        ],
        compiler_params=pltpu.CompilerParams(vmem_limit_bytes=BIG),
        cost_estimate=pl.CostEstimate(
            flops=2 * targets * block * supernodes * block * width,
            bytes_accessed=2 * tiles.size + 4 * rhs.size,
            transcendentals=0,
        ),
        name="leaf_forward",
    )(count, cols, tgts, rhs, inverse, tiles)


def small(kernel, name, shapes, *args):
    return pl.pallas_call(
        kernel,
        out_shape=[jax.ShapeDtypeStruct(shape, BF) for shape in shapes],
        in_specs=[VMEM] * len(args),
        out_specs=[VMEM] * len(shapes),
        compiler_params=pltpu.CompilerParams(vmem_limit_bytes=SMALL),
        name=name,
    )(*args)


def total_of(refs):
    total = refs[0][...].astype(F32)
    for ref in refs[1:]:
        total = total + ref[...].astype(F32)
    return total


def pair_sum_kernel(n_leaf, n_pos, keep, recv, *refs):
    groups, parts = refs[:n_pos], refs[n_pos:]
    leaf, pos, _ = place()
    gq = groups[0].shape[0]
    q = parts[0].shape[0] // n_pos

    def both(begin, rows):
        span = pl.ds(pl.multiple_of(begin, rows), rows)
        return (keep[span, :].astype(F32) + recv[span, :].astype(F32)).astype(BF)

    for k in range(n_pos):
        p = pos ^ k
        groups[k][...] = both(p * gq, gq)
        for j in range(n_leaf):
            begin = n_pos * gq + (p * n_leaf + (leaf ^ j)) * q
            parts[j][k * q : (k + 1) * q, :] = both(begin, q)


def pair_sum(keep, recv, n_leaf, n_pos, gq, q):
    width = keep.shape[-1]
    shapes = [(gq, width)] * n_pos + [(n_pos * q, width)] * n_leaf
    kernel = functools.partial(pair_sum_kernel, n_leaf, n_pos)
    outs = small(kernel, "pair_sum", shapes, keep, recv)
    return list(outs[:n_pos]), list(outs[n_pos:])


def residual_kernel(rhs, *refs):
    refs[-1][...] = (rhs[...] - total_of(refs[:-1])).astype(BF)


def residual_of(rhs, parts):
    return small(residual_kernel, "residual", [rhs.shape], rhs, *parts)[0]


def group_kernel(n_leaf, n_pos, mine, theirs, inv, panel, *refs):
    solved, outs, residual = refs[0], refs[1:-1], refs[-1]
    leaf, pos, core = place()
    rows = inv.shape[0] // (2 * n_pos)
    for kc, got in enumerate((mine, theirs)):
        for k in range(n_pos):
            begin = ((core ^ kc) * n_pos + (pos ^ k)) * rows
            span = pl.ds(pl.multiple_of(begin, rows), rows)
            residual[span, :] = got[k * rows : (k + 1) * rows, :]
    solved[...] = dot(inv[...], residual[...]).astype(BF)
    q = panel.shape[0] // n_leaf
    for j in range(n_leaf):
        span = pl.ds(pl.multiple_of((leaf ^ j) * q, q), q)
        outs[j][...] = dot(panel[span, :], solved[...]).astype(BF)


def group_forward(mine, theirs, inverse, panel, n_leaf, n_pos):
    group_cols, width = inverse.shape[0], mine.shape[-1]
    part = (panel.shape[0] // n_leaf, width)
    outs = pl.pallas_call(
        functools.partial(group_kernel, n_leaf, n_pos),
        out_shape=[jax.ShapeDtypeStruct((group_cols, width), BF)]
        + [jax.ShapeDtypeStruct(part, BF)] * n_leaf,
        in_specs=[VMEM] * 4,
        out_specs=[VMEM] * (1 + n_leaf),
        scratch_shapes=[pltpu.VMEM((group_cols, width), BF)],
        compiler_params=pltpu.CompilerParams(vmem_limit_bytes=SMALL),
        name="group_forward",
    )(mine, theirs, inverse, panel)
    return outs[0], list(outs[1:])


def sum_leaf_kernel(n_leaf, *refs):
    total = total_of(refs[:n_leaf]).astype(BF)
    for k, out in enumerate(refs[n_leaf:]):
        q = out.shape[0]
        out[...] = total[k * q : (k + 1) * q, :]


def sum_leaf(parts, n_pos):
    rows, width = parts[0].shape
    kernel = functools.partial(sum_leaf_kernel, len(parts))
    return list(small(kernel, "sum_leaf", [(rows // n_pos, width)] * n_pos, *parts))


def stack_kernel(*refs):
    begin = 0
    for part in refs[:-1]:
        rows = part.shape[0]
        refs[-1][begin : begin + rows, :] = part[...]
        begin += rows


def stack(parts):
    rows = sum(part.shape[0] for part in parts)
    return small(stack_kernel, "stack", [(rows, parts[0].shape[1])], *parts)[0]


def backward_kernel(
    n_leaf,
    n_pos,
    n_mid,
    mine,
    theirs,
    group_solved_ref,
    leaf_solved_hbm,
    inv_leaf_hbm,
    inv_mid_hbm,
    inv_top_hbm,
    inv_group_hbm,
    dense_hbm,
    *refs,
):
    backward_steps(
        n_leaf,
        n_pos,
        refs[:n_mid],
        refs[n_mid : n_mid + 2],
        mine,
        theirs,
        group_solved_ref,
        leaf_solved_hbm,
        inv_leaf_hbm,
        inv_mid_hbm,
        inv_top_hbm,
        inv_group_hbm,
        dense_hbm,
        *refs[n_mid + 2 :],
    )


def backward_steps(
    n_leaf,
    n_pos,
    mid_parts,
    group_parts,
    mine,
    theirs,
    group_solved_ref,
    leaf_solved_hbm,
    inv_leaf_hbm,
    inv_mid_hbm,
    inv_top_hbm,
    inv_group_hbm,
    dense_hbm,
    leaf_hbm,
    group_hbm,
    mid_hbm,
    top_hbm,
    leaf_solved,
    inv_leaf,
    inv_mid,
    inv_top,
    inv_group,
    dense,
    panel_mid,
    panel_group,
    leaf_out,
    group_out,
    mid_out,
    top_out,
    upper,
    above,
    sems,
    mid_sems,
    group_sems,
    out_sems,
):
    leaf, pos, core = place()
    pairs = (
        (inv_mid_hbm, inv_mid),
        (inv_top_hbm, inv_top),
        (inv_group_hbm, inv_group),
        (dense_hbm, dense),
        (leaf_solved_hbm, leaf_solved),
        (inv_leaf_hbm, inv_leaf),
    )
    loads = [pltpu.make_async_copy(a, b, sems.at[i]) for i, (a, b) in enumerate(pairs)]
    mid_loads = []
    if len(mid_parts) == 1:
        mid_loads.append(pltpu.make_async_copy(mid_parts[0], panel_mid, mid_sems.at[0]))
    else:
        rows = mid_parts[0].shape[0] // n_pos
        for i, part in enumerate(mid_parts):
            kc, kl = divmod(i, n_leaf)
            for kz in range(n_pos):
                block = (leaf ^ kl) * (2 * n_pos) + 2 * (pos ^ kz) + (core ^ kc)
                span = pl.ds(pl.multiple_of(block * rows, rows), rows)
                got = part.at[pl.ds(kz * rows, rows)]
                sem = mid_sems.at[i * n_pos + kz]
                mid_loads.append(pltpu.make_async_copy(got, panel_mid.at[span], sem))
    group_loads = []
    for kc, part in enumerate(group_parts):
        rows = part.shape[1]
        for p in range(n_pos):
            span = pl.ds(pl.multiple_of((2 * p + (core ^ kc)) * rows, rows), rows)
            sem = group_sems.at[kc * n_pos + p]
            group_loads.append(pltpu.make_async_copy(part.at[p], panel_group.at[span], sem))
    for load in loads[:1] + mid_loads + loads[1:3] + group_loads + loads[3:]:
        load.start()
    mid_rows = inv_mid.shape[0]
    top_rows = inv_top.shape[0]
    group_rows = inv_group.shape[0]
    supernodes, block, _ = inv_leaf.shape
    upper_cols = pl.ds(group_rows, mid_rows + top_rows)
    mid_cols = pl.ds(group_rows, mid_rows)
    top_cols = pl.ds(group_rows + mid_rows, top_rows)
    sec = (mid_rows + top_rows) // (2 * n_pos)
    q = sec // n_leaf
    for kc, got in enumerate((mine, theirs)):
        for kz in range(n_pos):
            for kl in range(n_leaf):
                row = sec * (2 * (pos ^ kz) + (core ^ kc)) + q * (leaf ^ kl)
                begin = (kl * n_pos + kz) * q
                upper[pl.ds(pl.multiple_of(row, q), q), :] = got[begin : begin + q, :]

    loads[0].wait()
    mid_solved = dot(inv_mid[...], upper[0:mid_rows, :]).astype(BF)
    for load in mid_loads:
        load.wait()
    top_residual = upper[mid_rows:, :].astype(F32) - dot(panel_mid[...], mid_solved)
    loads[1].wait()
    top_solved = dot(inv_top[...], top_residual.astype(BF))
    top_t = dot(top_solved.T.astype(BF), inv_top[...])
    above[:, top_cols] = top_t.astype(BF)
    top_out[...] = top_t.T
    stores = [pltpu.make_async_copy(top_out, top_hbm, out_sems.at[0])]
    stores[0].start()
    mid_back = mid_solved.astype(F32).T - dot(above[:, top_cols], panel_mid[...])
    mid_t = dot(mid_back.astype(BF), inv_mid[...])
    above[:, mid_cols] = mid_t.astype(BF)
    mid_out[...] = mid_t.T
    stores.append(pltpu.make_async_copy(mid_out, mid_hbm, out_sems.at[1]))
    stores[1].start()
    loads[2].wait()
    group_solved = group_solved_ref[...].astype(F32).T
    for load in group_loads:
        load.wait()
    group_back = group_solved - dot(above[:, upper_cols], panel_group[...])
    group_t = dot(group_back.astype(BF), inv_group[...])
    above[:, 0:group_rows] = group_t.astype(BF)
    group_out[...] = group_t.T
    stores.append(pltpu.make_async_copy(group_out, group_hbm, out_sems.at[2]))
    stores[2].start()
    for load in loads[3:]:
        load.wait()
    for s in range(supernodes):
        cols = pl.ds(s * block, block)
        terms = dot(above[...], dense[:, cols])
        back = (leaf_solved[cols, :].astype(F32).T - terms).astype(BF)
        leaf_out[cols, :] = dot(back, inv_leaf[s]).T
    stores.append(pltpu.make_async_copy(leaf_out, leaf_hbm, out_sems.at[3]))
    stores[3].start()
    for store in stores:
        store.wait()


def backward(
    mine,
    theirs,
    group_solved,
    leaf_solved,
    inv_leaf,
    inv_mid,
    inv_top,
    inv_group,
    dense,
    mid_parts,
    group_parts,
    n_leaf,
    n_pos,
):
    width = mine.shape[-1]
    upper_rows = inv_mid.shape[0] + inv_top.shape[0]
    group_rows = inv_group.shape[0]
    heavy = (leaf_solved, inv_leaf, inv_mid, inv_top, inv_group, dense)
    outs = (
        jax.ShapeDtypeStruct(leaf_solved.shape, F32),
        jax.ShapeDtypeStruct((group_rows, width), F32),
        jax.ShapeDtypeStruct((inv_mid.shape[0], width), F32),
        jax.ShapeDtypeStruct((inv_top.shape[0], width), F32),
    )
    return pl.pallas_call(
        functools.partial(backward_kernel, n_leaf, n_pos, len(mid_parts)),
        out_shape=outs,
        in_specs=[VMEM] * 3 + [HBM] * (len(heavy) + len(mid_parts) + len(group_parts)),
        out_specs=(HBM,) * 4,
        scratch_shapes=[pltpu.VMEM(a.shape, a.dtype) for a in heavy]
        + [
            pltpu.VMEM((inv_top.shape[0], inv_mid.shape[0]), BF),
            pltpu.VMEM((upper_rows, group_rows), BF),
        ]
        + [pltpu.VMEM(a.shape, a.dtype) for a in outs]
        + [
            pltpu.VMEM((upper_rows, width), BF),
            pltpu.VMEM((width, dense.shape[0]), BF),
            pltpu.SemaphoreType.DMA((len(heavy),)),
            pltpu.SemaphoreType.DMA((len(mid_parts) * n_pos,)),
            pltpu.SemaphoreType.DMA((2 * n_pos,)),
            pltpu.SemaphoreType.DMA((len(outs),)),
        ],
        compiler_params=pltpu.CompilerParams(vmem_limit_bytes=36 * MIB),
        name="backward",
    )(mine, theirs, group_solved, *heavy, *mid_parts, *group_parts)


def swap(x, axis, size, bits):
    return lax.ppermute(x, axis, [(i, i ^ bits) for i in range(size)])


def swaps(x, axis, size, unit=1):
    return [x] + [swap(x, axis, size, unit * k) for k in range(1, size // unit)]


def after(x, *others):
    return lax.optimization_barrier((x, others))[0]


def body(
    n_leaf,
    n_grp,
    rhs_leaf,
    rhs_group,
    rhs_middle,
    rhs_top,
    inv_leaf,
    inv_group,
    inv_middle,
    inv_top,
    leaf_tiles,
    tile_column,
    tile_target,
    tile_count,
    group_panel,
    middle_panel,
):
    n_pos = n_grp // 2
    group_cols = rhs_group.shape[1]
    mid_cols = rhs_middle.shape[0]
    upper_cols = mid_cols + rhs_top.shape[0]
    sec = upper_cols // n_grp
    q = sec // n_leaf
    gq = group_cols // n_grp
    leaf, pos, core = place()
    by_parts = middle_panel.shape[0] % 16 == 0
    pos_groups = [[2 * p + c for p in range(n_pos)] for c in range(2)]
    with jax.named_scope("gather_group_panel"):
        panel_half = lax.all_gather(group_panel[0], "grp", axis_index_groups=pos_groups)
    with jax.named_scope("gather_middle_panel"):
        if by_parts:
            middles = swaps(middle_panel, "grp", n_grp, 2)
        else:
            middles = [lax.all_gather(middle_panel, ("leaf", "grp"), axis=0, tiled=True)]
    keep, send, leaf_solved, dense = leaf_forward(
        rhs_leaf[0],
        inv_leaf[0],
        leaf_tiles[0],
        tile_column,
        tile_target,
        tile_count,
        sec,
        group_cols,
        upper_cols,
    )
    with jax.named_scope("swap_cores"):
        if by_parts:
            send = after(send, middles)
        recv = swap(send, "grp", n_grp, 1)
    groups, parts = pair_sum(keep, recv, n_leaf, n_pos, gq, q)
    with jax.named_scope("sum_group_over_pos"):
        groups = groups[:1] + [swap(groups[k], "grp", n_grp, 2 * k) for k in range(1, n_pos)]
    with jax.named_scope("sum_upper_over_leaf"):
        parts = parts[:1] + [swap(parts[k], "leaf", n_leaf, k) for k in range(1, n_leaf)]
    with jax.named_scope("gather_middle_panel"):
        if by_parts:
            middle = stack(middles)
            groups = after(groups, middle)
            middles = swaps(middle, "leaf", n_leaf)
    group_begin = (group_cols // 2) * core + gq * pos
    group_rhs = lax.dynamic_slice_in_dim(rhs_group[0], group_begin, gq, 0)
    residual = residual_of(group_rhs, groups)
    with jax.named_scope("gather_group"):
        mine = stack(after(swaps(residual, "grp", n_grp, 2), parts))
        theirs = swap(mine, "grp", n_grp, 1)
    with jax.named_scope("sum_upper_over_pos"):
        uppers = sum_leaf(parts, n_pos)
        uppers = uppers[:1] + [swap(uppers[k], "grp", n_grp, 2 * k) for k in range(1, n_pos)]
    if by_parts:
        theirs = after(theirs, middles)
    group_solved, terms = group_forward(mine, theirs, inv_group[0], group_panel[0], n_leaf, n_pos)
    with jax.named_scope("sum_panel_over_leaf"):
        terms = terms[:1] + [swap(terms[k], "leaf", n_leaf, k) for k in range(1, n_leaf)]
    begin = sec * lax.axis_index("grp") + q * leaf
    low = lax.dynamic_slice_in_dim(rhs_middle, jnp.minimum(begin, mid_cols - q), q, 0)
    high = lax.dynamic_slice_in_dim(rhs_top, jnp.maximum(begin - mid_cols, 0), q, 0)
    with jax.named_scope("gather_middle_panel"):
        if by_parts:
            middles = middles + [swap(x, "grp", n_grp, 1) for x in middles]
    residual = residual_of(jnp.where(begin < mid_cols, low, high), uppers + terms)
    with jax.named_scope("gather_pos"):
        uppers = stack(swaps(residual, "grp", n_grp, 2))
    with jax.named_scope("swap_group_panel"):
        uppers = after(uppers, panel_half)
        panels = [panel_half, swap(panel_half, "grp", n_grp, 1)]
    with jax.named_scope("gather_leaf"):
        stacks = swaps(uppers, "leaf", n_leaf)
    with jax.named_scope("gather_cores"):
        mine = stack(after(stacks, middles, panels))
        theirs = swap(mine, "grp", n_grp, 1)
    leaf_out, group_out, mid_out, top_out = backward(
        mine,
        theirs,
        group_solved,
        leaf_solved,
        inv_leaf[0],
        inv_middle,
        inv_top,
        inv_group[0],
        dense,
        middles,
        panels,
        n_leaf,
        n_pos,
    )
    return leaf_out[None], group_out[None], mid_out, top_out


def solution(mesh):
    n_leaf = mesh.shape["leaf"]
    n_grp = mesh.shape["grp"]
    placed = (
        P("leaf", "grp", None),
        P("leaf", None, None),
        P(),
        P(),
        P("leaf", "grp", None, None),
        P("leaf", None, None),
        P(),
        P(),
        P("leaf", "grp", None, None),
        P("leaf", "grp"),
        P("leaf", "grp"),
        P("leaf", "grp"),
        P("leaf", "grp", None),
        P(("leaf", "grp"), None),
    )
    return jax.shard_map(
        functools.partial(body, n_leaf, n_grp),
        mesh=mesh,
        in_specs=placed,
        out_specs=(P("leaf", "grp", None), P("leaf", None, None), P(), P()),
        check_vma=False,
    )
```

time: 126 us -> 162 us (1.29)
  starting transfers between devices: 16.8 us -> 31.9 us
  local copies, waits for them, and re-layouts: 13.7 us -> 25.6 us
  waiting for transfers between devices: 47.9 us -> 56.5 us
  other arithmetic: 4.9 us -> 0.94 us
  Pallas kernels: 27.6 us -> 30.8 us
    ppermute x16 -> x35, waiting for transfers between devices: 14.9 us -> 40.4 us  [swap(): return lax.ppermute(x, axis, [(i, i ^ bits) for i in range(size)])]
    all_gather x1 -> x0, waiting for transfers between devices: 18.3 us -> none  [body(): lax.all_gather(middle_panel, ('leaf', 'grp'), axis_index_groups=chip_groups)]
    ppermute x16 -> x35, starting transfers between devices: 16.8 us -> 31.8 us  [swap(): return lax.ppermute(x, axis, [(i, i ^ bits) for i in range(size)])]
    unnamed x46 -> x74, local copies, waits for them, and re-layouts: 11.4 us -> 25.6 us
    another operation x4 -> x0, other arithmetic: 3.29 us -> none  [weave(): both = jnp.stack([first, second], axis=1)]
    pallas_call x5 -> x11, Pallas kernels: 27.6 us -> 30.8 us  [the longest x1 16.8 us: backward(): pl.pallas_call(functools.partial(backward_kernel, n_leaf, n_pos, len(mid_...]
  transfers between devices with their start and end apart: 18 -> 36, of which waited for: 9 -> 15; matrix products, arithmetic and copies ran while one was open for 6% -> 1% of each run, Pallas kernels for 11% -> 9%
where the time goes in v3:
time: 162 us; the launch traced here: 161 us
  waiting for transfers between devices  56.5 us (35%)
  starting transfers between devices  31.9 us (20%)
  Pallas kernels  30.8 us (19%)
  local copies, waits for them, and re-layouts  25.6 us (16%)
  between operations  14.9 us (9%)
    ppermute x35, waiting for transfers between devices, swap(): return lax.ppermute(x, axis, [(i, i ^ bits) for i in range(size)])  40.4 us
    ppermute x35, starting transfers between devices, swap(): return lax.ppermute(x, axis, [(i, i ^ bits) for i in range(size)])  31.8 us
    unnamed x74, local copies, waits for them, and re-layouts  25.6 us
    pallas_call x1, Pallas kernels, backward(): pl.pallas_call(functools.partial(backward_kernel, n_leaf, n_pos, len(mid_...  16.8 us
    all_gather x1, waiting for transfers between devices, body(): lax.all_gather(group_panel[0], 'grp', axis_index_groups=pos_groups)  15.4 us
    pallas_call x1, Pallas kernels, leaf_forward(): pl.pallas_call(functools.partial(forward_kernel, sec, group_cols), out_sh...  8.64 us
    pallas_call x8, Pallas kernels, small(): pl.pallas_call(kernel, out_shape=[jax.ShapeDtypeStruct(shape, BF) for sha...  4.09 us
  transfers between devices with their start and end apart: 36, of which 15 were waited for; matrix products, arithmetic and copies ran while one was open for 1% of the time, Pallas kernels for 9%

profile of v3, /device:TPU:0, one launch (start us, length us, event | category | flops | bytes accessed | tf_op | source)
XLA Modules:
  0.0 160.6 jit_solution(6267876586396295519)
XLA Ops:
  7.9 5.1 %collective-permute-start.2 = (bf16[32,1024]{1,0:T(8,128)(2,1)}, bf16[32,1024]{1,0:T(8,128)(2,1)S(1)}, u32[]{:S(2)}, u32[]{:S(2)}) collective-permute-start(bf16[32,1024]{1,0:T(8,128)(2,1)} %refs_0_.1), channel_id=1, source_target_pairs={{0,6},{1,7},{2,4},{3,5},{4,2},{5,3},{6,0},{7,1},{8,14},{9,15},{10,... | collective-permute-start | bytes 196616 | tf_op jit(solution)/shard_map/gather_middle_panel/ppermute | solution.py:499
  14.3 8.6 %leaf_forward.1 = (bf16[1280,256]{1,0:T(8,128)(2,1)}, bf16[1280,256]{1,0:T(8,128)(2,1)}, bf16[1024,256]{1,0:T(8,128)(2,1)}, bf16[2560,1024]{1,0:T(8,128)(2,1)}) custom-call(s32[1,1]{1,0:T(1,128)S(6)} %copy.18.count_hbm, s32[1,256]{1,0:T(1,128)} %cols_hbm.1, s32[1,256]{1,0:T(1,128)} %tgts_hbm.1, f32[1024,256]{1,0:T(8,128)} %bitcast.15, ...), custom_call_target="tpu_custom_call" | custom-call | flops 1342177280 | bytes 9437184 | tf_op jit(solution)/shard_map/leaf_forward/pallas_call | solution.py:145
  24.9 15.4 %all-gather.2.cloned.1.call-done.refs_8_ = bf16[4,256,512]{2,1,0:T(8,128)(2,1)} async-done(((bf16[1,256,512]{2,1,0:T(8,128)(2,1)}), bf16[4,256,512]{2,1,0:T(8,128)(2,1)}) %all-gather.2.cloned.1.call-update) | async-done | bytes 1048592 | tf_op jit(solution)/shard_map/gather_group_panel/all_gather | solution.py:539
  41.3 1.8 %pair_sum.1 = (bf16[64,256]{1,0:T(8,128)(2,1)S(1)}, bf16[64,256]{1,0:T(8,128)(2,1)}, bf16[64,256]{1,0:T(8,128)(2,1)S(1)}, bf16[64,256]{1,0:T(8,128)(2,1)S(1)}, b...) custom-call(bf16[1280,256]{1,0:T(8,128)(2,1)S(1)} %copy-done.10, ...), custom_call_target="tpu_custom_call" | custom-call | tf_op jit(solution)/shard_map/pair_sum/pallas_call | solution.py:181
  49.4 1.9 %collective-permute-start.12 = (bf16[64,256]{1,0:T(8,128)(2,1)}, bf16[64,256]{1,0:T(8,128)(2,1)S(1)}, u32[]{:S(2)}, u32[]{:S(2)}) collective-permute-start(bf16[64,256]{1,0:T(8,128)(2,1)} %copy-done.35), channel_id=1, source_target_pairs={{0,6},{1,7},{2,4},{3,5},{4,2},{5,3},{6,0},{7,1},{8,14},{9,15},{10,... | collective-permute-start | bytes 98312 | tf_op jit(solution)/shard_map/sum_group_over_pos/ppermute | solution.py:499
  59.2 2.0 %collective-permute-start.15 = (bf16[64,256]{1,0:T(8,128)(2,1)S(1)}, bf16[64,256]{1,0:T(8,128)(2,1)S(1)}, u32[]{:S(2)}, u32[]{:S(2)}) collective-permute-start(bf16[64,256]{1,0:T(8,128)(2,1)S(1)} %residual.2.refs_0_), channel_id=1, source_target_pairs={{0,6},{1,7},{2,4},{3,5},{4,2},{5,3},{6,0},{7,1},{8,14},{9,15},{10,... | collective-permute-start | bytes 98312 | tf_op jit(solution)/shard_map/gather_group/ppermute | solution.py:499
  61.3 3.7 %collective-permute-done.15.refs_3_ = bf16[64,256]{1,0:T(8,128)(2,1)S(1)} collective-permute-done((bf16[64,256]{1,0:T(8,128)(2,1)S(1)}, bf16[64,256]{1,0:T(8,128)(2,1)S(1)}, u32[]{:S(2)}, u32[]{:S(2)}) %collective-permute-start.15) | collective-permute-done | bytes 32800 | tf_op jit(solution)/shard_map/gather_group/ppermute | solution.py:499
  66.7 2.3 %collective-permute-done.13.refs_1_ = bf16[64,256]{1,0:T(8,128)(2,1)S(1)} collective-permute-done((bf16[64,256]{1,0:T(8,128)(2,1)S(1)}, bf16[64,256]{1,0:T(8,128)(2,1)S(1)}, u32[]{:S(2)}, u32[]{:S(2)}) %collective-permute-start.13) | collective-permute-done | bytes 32800 | tf_op jit(solution)/shard_map/gather_group/ppermute | solution.py:499
  72.4 6.4 %collective-permute-done.6.refs_3_ = bf16[256,256]{1,0:T(8,128)(2,1)S(1)} collective-permute-done((bf16[256,256]{1,0:T(8,128)(2,1)}, bf16[256,256]{1,0:T(8,128)(2,1)S(1)}, u32[]{:S(2)}, u32[]{:S(2)}) %collective-permute-start.6) | collective-permute-done | bytes 131104 | tf_op jit(solution)/shard_map/sum_upper_over_leaf/ppermute | solution.py:499
  82.7 1.9 %collective-permute-start.9 = (bf16[64,256]{1,0:T(8,128)(2,1)}, bf16[64,256]{1,0:T(8,128)(2,1)S(1)}, u32[]{:S(2)}, u32[]{:S(2)}) collective-permute-start(bf16[64,256]{1,0:T(8,128)(2,1)} %get-tuple-element.54), channel_id=1, source_target_pairs={{0,6},{1,7},{2,4},{3,5},{4,2},{5,3},{6,0},{7,1},{8,14},{9,15},{10,... | collective-permute-start | bytes 98312 | tf_op jit(solution)/shard_map/sum_upper_over_pos/ppermute | solution.py:499
  89.8 2.6 %collective-permute-done.20.refs_5_ = bf16[64,256]{1,0:T(8,128)(2,1)} collective-permute-done((bf16[64,256]{1,0:T(8,128)(2,1)}, bf16[64,256]{1,0:T(8,128)(2,1)}, u32[]{:S(2)}, u32[]{:S(2)}) %collective-permute-start.20) | collective-permute-done | bytes 32800 | tf_op jit(solution)/shard_map/sum_panel_over_leaf/ppermute | solution.py:499
  93.0 1.5 collective-permute-start.22
  95.4 2.6 %collective-permute-done.22.refs_7_ = bf16[64,256]{1,0:T(8,128)(2,1)S(1)} collective-permute-done((bf16[64,256]{1,0:T(8,128)(2,1)}, bf16[64,256]{1,0:T(8,128)(2,1)S(1)}, u32[]{:S(2)}, u32[]{:S(2)}) %collective-permute-start.22) | collective-permute-done | bytes 32800 | tf_op jit(solution)/shard_map/sum_panel_over_leaf/ppermute | solution.py:499
  99.6 2.0 %collective-permute-start.25 = (bf16[64,256]{1,0:T(8,128)(2,1)S(1)}, bf16[64,256]{1,0:T(8,128)(2,1)S(1)}, u32[]{:S(2)}, u32[]{:S(2)}) collective-permute-start(bf16[64,256]{1,0:T(8,128)(2,1)S(1)} %residual.3.refs_0_), channel_id=1, source_target_pairs={{0,6},{1,7},{2,4},{3,5},{4,2},{5,3},{6,0},{7,1},{8,14},{9,15},{10,... | collective-permute-start | bytes 98312 | tf_op jit(solution)/shard_map/gather_pos/ppermute | solution.py:499
  101.6 3.8 %collective-permute-done.25.refs_3_ = bf16[64,256]{1,0:T(8,128)(2,1)S(1)} collective-permute-done((bf16[64,256]{1,0:T(8,128)(2,1)S(1)}, bf16[64,256]{1,0:T(8,128)(2,1)S(1)}, u32[]{:S(2)}, u32[]{:S(2)}) %collective-permute-start.25) | collective-permute-done | bytes 32800 | tf_op jit(solution)/shard_map/gather_pos/ppermute | solution.py:499
  105.4 4.8 %collective-permute-done.24.refs_2_ = bf16[64,256]{1,0:T(8,128)(2,1)S(1)} collective-permute-done((bf16[64,256]{1,0:T(8,128)(2,1)S(1)}, bf16[64,256]{1,0:T(8,128)(2,1)S(1)}, u32[]{:S(2)}, u32[]{:S(2)}) %collective-permute-start.24) | collective-permute-done | bytes 32800 | tf_op jit(solution)/shard_map/gather_pos/ppermute | solution.py:499
  110.2 3.9 %collective-permute-done.23.refs_1_ = bf16[64,256]{1,0:T(8,128)(2,1)S(1)} collective-permute-done((bf16[64,256]{1,0:T(8,128)(2,1)S(1)}, bf16[64,256]{1,0:T(8,128)(2,1)S(1)}, u32[]{:S(2)}, u32[]{:S(2)}) %collective-permute-start.23) | collective-permute-done | bytes 32800 | tf_op jit(solution)/shard_map/gather_pos/ppermute | solution.py:499
  114.1 1.7 %collective-permute-start.28 = (bf16[256,256]{1,0:T(8,128)(2,1)S(1)}, bf16[256,256]{1,0:T(8,128)(2,1)S(1)}, u32[]{:S(2)}, u32[]{:S(2)}) collective-permute-start(bf16[256,256]{1,0:T(8,128)(2,1)S(1)} %stack.6.refs_0_), channel_id=1, source_target_pairs={{0,24},{8,16},{16,8},{24,0},{1,25},{9,17},{17,9},{25,1},{2,26},{10... | collective-permute-start | bytes 393224 | tf_op jit(solution)/shard_map/gather_leaf/ppermute | solution.py:499
  117.7 3.7 %collective-permute-done.28.refs_3_ = bf16[256,256]{1,0:T(8,128)(2,1)S(1)} collective-permute-done((bf16[256,256]{1,0:T(8,128)(2,1)S(1)}, bf16[256,256]{1,0:T(8,128)(2,1)S(1)}, u32[]{:S(2)}, u32[]{:S(2)}) %collective-permute-start.28) | collective-permute-done | bytes 131104 | tf_op jit(solution)/shard_map/gather_leaf/ppermute | solution.py:499
  121.4 2.4 %collective-permute-done.27.refs_2_ = bf16[256,256]{1,0:T(8,128)(2,1)S(1)} collective-permute-done((bf16[256,256]{1,0:T(8,128)(2,1)S(1)}, bf16[256,256]{1,0:T(8,128)(2,1)S(1)}, u32[]{:S(2)}, u32[]{:S(2)}) %collective-permute-start.27) | collective-permute-done | bytes 131104 | tf_op jit(solution)/shard_map/gather_leaf/ppermute | solution.py:499
  124.0 1.9 %collective-permute-done.34.theirs = bf16[1024,256]{1,0:T(8,128)(2,1)S(1)} collective-permute-done((bf16[1024,256]{1,0:T(8,128)(2,1)S(1)}, bf16[1024,256]{1,0:T(8,128)(2,1)S(1)}, u32[]{:S(2)}, u32[]{:S(2)}) %collective-permute-start.34) | collective-permute-done | bytes 524320 | tf_op jit(solution)/shard_map/gather_cores/ppermute | solution.py:499
  125.9 2.5 %copy-done.1 = bf16[2560,1024]{1,0:T(8,128)(2,1)S(1)} copy-done((bf16[2560,1024]{1,0:T(8,128)(2,1)S(1)}, bf16[2560,1024]{1,0:T(8,128)(2,1)}, u32[]{:S(2)}) %copy-start.1) | copy-done | bytes 5242904
  128.3 1.6 copy-done.4
  137.0 16.8 %backward.1 = (f32[1024,256]{1,0:T(8,128)}, f32[512,256]{1,0:T(8,128)}, f32[1024,256]{1,0:T(8,128)}, f32[1024,256]{1,0:T(8,128)}) custom-call(bf16[1024,256]{1,0:T(8,128)(2,1)S(1)} %stack.7.mine, bf16[1024,256]{1,0:T(8,128)(2,1)S(1)} %collective-permute-done.34.theirs, bf16[512,256]{1,0:T(8,128)(2,1)S(1)} %copy-done.19, bf16[1024,256]{1,0:T(8,128)(2,1)S(1)} %copy-done.11, ...), custom_call_target="tpu_custom_call" | custom-call | tf_op jit(solution)/shard_map/backward/pallas_call | solution.py:474
  (136 shorter events, 44.9 us)
Async XLA Ops:
  7.2 33.1 %all-gather.2.cloned.1.call-start = ((), (), s32[]{:S(2)}) async-start(), calls=%async_computation | async-start | bytes 1310720 | tf_op jit(solution)/shard_map/gather_group_panel/all_gather | solution.py:539
  7.9 15.1 %collective-permute-start.2 = (bf16[32,1024]{1,0:T(8,128)(2,1)}, bf16[32,1024]{1,0:T(8,128)(2,1)S(1)}, u32[]{:S(2)}, u32[]{:S(2)}) collective-permute-start(bf16[32,1024]{1,0:T(8,128)(2,1)} %refs_0_.1), channel_id=1, source_target_pairs={{0,6},{1,7},{2,4},{3,5},{4,2},{5,3},{6,0},{7,1},{8,14},{9,15},{10,... | collective-permute-start | bytes 196616 | tf_op jit(solution)/shard_map/gather_middle_panel/ppermute | solution.py:499
  13.0 10.6 %collective-permute-start.1 = (bf16[32,1024]{1,0:T(8,128)(2,1)}, bf16[32,1024]{1,0:T(8,128)(2,1)S(1)}, u32[]{:S(2)}, u32[]{:S(2)}) collective-permute-start(bf16[32,1024]{1,0:T(8,128)(2,1)} %refs_0_.1), channel_id=1, source_target_pairs={{0,4},{1,5},{2,6},{3,7},{4,0},{5,1},{6,2},{7,3},{8,12},{9,13},{10,... | collective-permute-start | bytes 196616 | tf_op jit(solution)/shard_map/gather_middle_panel/ppermute | solution.py:499
  13.0 11.2 %collective-permute-start = (bf16[32,1024]{1,0:T(8,128)(2,1)}, bf16[32,1024]{1,0:T(8,128)(2,1)S(1)}, u32[]{:S(2)}, u32[]{:S(2)}) collective-permute-start(bf16[32,1024]{1,0:T(8,128)(2,1)} %refs_0_.1), channel_id=1, source_target_pairs={{0,2},{1,3},{2,0},{3,1},{4,6},{5,7},{6,4},{7,5},{8,10},{9,11},{10,... | collective-permute-start | bytes 196616 | tf_op jit(solution)/shard_map/gather_middle_panel/ppermute | solution.py:499
  24.9 15.4 %collective-permute-start.3 = (bf16[1280,256]{1,0:T(8,128)(2,1)}, bf16[1280,256]{1,0:T(8,128)(2,1)}, u32[]{:S(2)}, u32[]{:S(2)}) collective-permute-start(bf16[1280,256]{1,0:T(8,128)(2,1)} %get-tuple-element.46), channel_id=1, source_target_pairs={{0,1},{1,0},{2,3},{3,2},{4,5},{5,4},{6,7},{7,6},{8,9},{9,8},{10,11... | collective-permute-start | bytes 1966088 | tf_op jit(solution)/shard_map/swap_cores/ppermute | solution.py:499
  40.2 83.6 %collective-permute-start.33 = (bf16[4,256,512]{2,1,0:T(8,128)(2,1)}, bf16[4,256,512]{2,1,0:T(8,128)(2,1)}, u32[]{:S(2)}, u32[]{:S(2)}) collective-permute-start(bf16[4,256,512]{2,1,0:T(8,128)(2,1)} %all-gather.2.cloned.1.call-done.refs_8_), channel_id=1, source_target_pairs={{0,1},{1,0},{2,3},{3,2},{4,5},{5,4},{6,7},{7,6},{8,9},{9,8},{10,11... | collective-permute-start | bytes 3145736 | tf_op jit(solution)/shard_map/swap_group_panel/ppermute | solution.py:499
  46.9 5.9 %collective-permute-start.10 = (bf16[64,256]{1,0:T(8,128)(2,1)}, bf16[64,256]{1,0:T(8,128)(2,1)}, u32[]{:S(2)}, u32[]{:S(2)}) collective-permute-start(bf16[64,256]{1,0:T(8,128)(2,1)} %get-tuple-element.56), channel_id=1, source_target_pairs={{0,2},{1,3},{2,0},{3,1},{4,6},{5,7},{6,4},{7,5},{8,10},{9,11},{10,... | collective-permute-start | bytes 98312 | tf_op jit(solution)/shard_map/sum_group_over_pos/ppermute | solution.py:499
  48.3 9.3 %collective-permute-start.11 = (bf16[64,256]{1,0:T(8,128)(2,1)}, bf16[64,256]{1,0:T(8,128)(2,1)S(1)}, u32[]{:S(2)}, u32[]{:S(2)}) collective-permute-start(bf16[64,256]{1,0:T(8,128)(2,1)} %copy-done.36), channel_id=1, source_target_pairs={{0,4},{1,5},{2,6},{3,7},{4,0},{5,1},{6,2},{7,3},{8,12},{9,13},{10,... | collective-permute-start | bytes 98312 | tf_op jit(solution)/shard_map/sum_group_over_pos/ppermute | solution.py:499
  49.4 8.3 %collective-permute-start.12 = (bf16[64,256]{1,0:T(8,128)(2,1)}, bf16[64,256]{1,0:T(8,128)(2,1)S(1)}, u32[]{:S(2)}, u32[]{:S(2)}) collective-permute-start(bf16[64,256]{1,0:T(8,128)(2,1)} %copy-done.35), channel_id=1, source_target_pairs={{0,6},{1,7},{2,4},{3,5},{4,2},{5,3},{6,0},{7,1},{8,14},{9,15},{10,... | collective-permute-start | bytes 98312 | tf_op jit(solution)/shard_map/sum_group_over_pos/ppermute | solution.py:499
  51.3 18.2 %collective-permute-start.4 = (bf16[256,256]{1,0:T(8,128)(2,1)}, bf16[256,256]{1,0:T(8,128)(2,1)S(1)}, u32[]{:S(2)}, u32[]{:S(2)}) collective-permute-start(bf16[256,256]{1,0:T(8,128)(2,1)} %copy-done.33), channel_id=1, source_target_pairs={{0,8},{8,0},{16,24},{24,16},{1,9},{9,1},{17,25},{25,17},{2,10},{10... | collective-permute-start | bytes 393224 | tf_op jit(solution)/shard_map/sum_upper_over_leaf/ppermute | solution.py:499
  52.7 18.2 %collective-permute-start.5 = (bf16[256,256]{1,0:T(8,128)(2,1)}, bf16[256,256]{1,0:T(8,128)(2,1)S(1)}, u32[]{:S(2)}, u32[]{:S(2)}) collective-permute-start(bf16[256,256]{1,0:T(8,128)(2,1)} %copy-done.32), channel_id=1, source_target_pairs={{0,16},{8,24},{16,0},{24,8},{1,17},{9,25},{17,1},{25,9},{2,18},{10... | collective-permute-start | bytes 393224 | tf_op jit(solution)/shard_map/sum_upper_over_leaf/ppermute | solution.py:499
  66.1 14.0 %collective-permute-start.19 = (bf16[128,1024]{1,0:T(8,128)(2,1)S(1)}, bf16[128,1024]{1,0:T(8,128)(2,1)S(1)}, u32[]{:S(2)}, u32[]{:S(2)}) collective-permute-start(bf16[128,1024]{1,0:T(8,128)(2,1)S(1)} %stack.4.refs_0_), channel_id=1, source_target_pairs={{0,24},{8,16},{16,8},{24,0},{1,25},{9,17},{17,9},{25,1},{2,26},{10... | collective-permute-start | bytes 786440 | tf_op jit(solution)/shard_map/gather_middle_panel/ppermute | solution.py:499
  68.9 9.9 %collective-permute-start.6 = (bf16[256,256]{1,0:T(8,128)(2,1)}, bf16[256,256]{1,0:T(8,128)(2,1)S(1)}, u32[]{:S(2)}, u32[]{:S(2)}) collective-permute-start(bf16[256,256]{1,0:T(8,128)(2,1)} %copy-done.31), channel_id=1, source_target_pairs={{0,24},{8,16},{16,8},{24,0},{1,25},{9,17},{17,9},{25,1},{2,26},{10... | collective-permute-start | bytes 393224 | tf_op jit(solution)/shard_map/sum_upper_over_leaf/ppermute | solution.py:499
  69.5 12.1 %collective-permute-start.18 = (bf16[128,1024]{1,0:T(8,128)(2,1)S(1)}, bf16[128,1024]{1,0:T(8,128)(2,1)S(1)}, u32[]{:S(2)}, u32[]{:S(2)}) collective-permute-start(bf16[128,1024]{1,0:T(8,128)(2,1)S(1)} %stack.4.refs_0_), channel_id=1, source_target_pairs={{0,16},{8,24},{16,0},{24,8},{1,17},{9,25},{17,1},{25,9},{2,18},{10... | collective-permute-start | bytes 786440 | tf_op jit(solution)/shard_map/gather_middle_panel/ppermute | solution.py:499
  70.9 11.8 %collective-permute-start.17 = (bf16[128,1024]{1,0:T(8,128)(2,1)S(1)}, bf16[128,1024]{1,0:T(8,128)(2,1)S(1)}, u32[]{:S(2)}, u32[]{:S(2)}) collective-permute-start(bf16[128,1024]{1,0:T(8,128)(2,1)S(1)} %stack.4.refs_0_), channel_id=1, source_target_pairs={{0,8},{8,0},{16,24},{24,16},{1,9},{9,1},{17,25},{25,17},{2,10},{10... | collective-permute-start | bytes 786440 | tf_op jit(solution)/shard_map/gather_middle_panel/ppermute | solution.py:499
  80.2 8.6 %collective-permute-start.7 = (bf16[64,256]{1,0:T(8,128)(2,1)S(1)}, bf16[64,256]{1,0:T(8,128)(2,1)S(1)}, u32[]{:S(2)}, u32[]{:S(2)}) collective-permute-start(bf16[64,256]{1,0:T(8,128)(2,1)S(1)} %get-tuple-element.52), channel_id=1, source_target_pairs={{0,2},{1,3},{2,0},{3,1},{4,6},{5,7},{6,4},{7,5},{8,10},{9,11},{10,... | collective-permute-start | bytes 98312 | tf_op jit(solution)/shard_map/sum_upper_over_pos/ppermute | solution.py:499
  81.6 7.8 %collective-permute-start.8 = (bf16[64,256]{1,0:T(8,128)(2,1)}, bf16[64,256]{1,0:T(8,128)(2,1)S(1)}, u32[]{:S(2)}, u32[]{:S(2)}) collective-permute-start(bf16[64,256]{1,0:T(8,128)(2,1)} %get-tuple-element.53), channel_id=1, source_target_pairs={{0,4},{1,5},{2,6},{3,7},{4,0},{5,1},{6,2},{7,3},{8,12},{9,13},{10,... | collective-permute-start | bytes 98312 | tf_op jit(solution)/shard_map/sum_upper_over_pos/ppermute | solution.py:499
  82.7 6.6 %collective-permute-start.9 = (bf16[64,256]{1,0:T(8,128)(2,1)}, bf16[64,256]{1,0:T(8,128)(2,1)S(1)}, u32[]{:S(2)}, u32[]{:S(2)}) collective-permute-start(bf16[64,256]{1,0:T(8,128)(2,1)} %get-tuple-element.54), channel_id=1, source_target_pairs={{0,6},{1,7},{2,4},{3,5},{4,2},{5,3},{6,0},{7,1},{8,14},{9,15},{10,... | collective-permute-start | bytes 98312 | tf_op jit(solution)/shard_map/sum_upper_over_pos/ppermute | solution.py:499
  89.3 24.8 %collective-permute-start.29 = (bf16[128,1024]{1,0:T(8,128)(2,1)}, bf16[128,1024]{1,0:T(8,128)(2,1)S(1)}, u32[]{:S(2)}, u32[]{:S(2)}) collective-permute-start(bf16[128,1024]{1,0:T(8,128)(2,1)} %copy-done.6), channel_id=1, source_target_pairs={{0,1},{1,0},{2,3},{3,2},{4,5},{5,4},{6,7},{7,6},{8,9},{9,8},{10,11... | collective-permute-start | bytes 786440 | tf_op jit(solution)/shard_map/gather_middle_panel/ppermute | solution.py:499
  89.3 26.5 %collective-permute-start.32 = (bf16[128,1024]{1,0:T(8,128)(2,1)}, bf16[128,1024]{1,0:T(8,128)(2,1)S(1)}, u32[]{:S(2)}, u32[]{:S(2)}) collective-permute-start(bf16[128,1024]{1,0:T(8,128)(2,1)} %copy-done.12), channel_id=1, source_target_pairs={{0,1},{1,0},{2,3},{3,2},{4,5},{5,4},{6,7},{7,6},{8,9},{9,8},{10,11... | collective-permute-start | bytes 786440 | tf_op jit(solution)/shard_map/gather_middle_panel/ppermute | solution.py:499
  92.5 24.9 %collective-permute-start.31 = (bf16[128,1024]{1,0:T(8,128)(2,1)}, bf16[128,1024]{1,0:T(8,128)(2,1)S(1)}, u32[]{:S(2)}, u32[]{:S(2)}) collective-permute-start(bf16[128,1024]{1,0:T(8,128)(2,1)} %copy-done.14), channel_id=1, source_target_pairs={{0,1},{1,0},{2,3},{3,2},{4,5},{5,4},{6,7},{7,6},{8,9},{9,8},{10,11... | collective-permute-start | bytes 786440 | tf_op jit(solution)/shard_map/gather_middle_panel/ppermute | solution.py:499
  114.1 7.3 %collective-permute-start.28 = (bf16[256,256]{1,0:T(8,128)(2,1)S(1)}, bf16[256,256]{1,0:T(8,128)(2,1)S(1)}, u32[]{:S(2)}, u32[]{:S(2)}) collective-permute-start(bf16[256,256]{1,0:T(8,128)(2,1)S(1)} %stack.6.refs_0_), channel_id=1, source_target_pairs={{0,24},{8,16},{16,8},{24,0},{1,25},{9,17},{17,9},{25,1},{2,26},{10... | collective-permute-start | bytes 393224 | tf_op jit(solution)/shard_map/gather_leaf/ppermute | solution.py:499
  115.9 8.0 %collective-permute-start.27 = (bf16[256,256]{1,0:T(8,128)(2,1)S(1)}, bf16[256,256]{1,0:T(8,128)(2,1)S(1)}, u32[]{:S(2)}, u32[]{:S(2)}) collective-permute-start(bf16[256,256]{1,0:T(8,128)(2,1)S(1)} %stack.6.refs_0_), channel_id=1, source_target_pairs={{0,16},{8,24},{16,0},{24,8},{1,17},{9,25},{17,1},{25,9},{2,18},{10... | collective-permute-start | bytes 393224 | tf_op jit(solution)/shard_map/gather_leaf/ppermute | solution.py:499
  117.3 6.5 %collective-permute-start.26 = (bf16[256,256]{1,0:T(8,128)(2,1)S(1)}, bf16[256,256]{1,0:T(8,128)(2,1)S(1)}, u32[]{:S(2)}, u32[]{:S(2)}) collective-permute-start(bf16[256,256]{1,0:T(8,128)(2,1)S(1)} %stack.6.refs_0_), channel_id=1, source_target_pairs={{0,8},{8,0},{16,24},{24,16},{1,9},{9,1},{17,25},{25,17},{2,10},{10... | collective-permute-start | bytes 393224 | tf_op jit(solution)/shard_map/gather_leaf/ppermute | solution.py:499
  (49 other events, 435.5 us)
Sparse Core Ops, SparseCore 0:
  9.6 30.6 all-gather.1

commit v4 on v3

v4 whole, which is shorter than its diff:
```python
import functools

import jax
import jax.numpy as jnp
from jax import lax
from jax.experimental import pallas as pl
from jax.experimental.pallas import tpu as pltpu
from jax.sharding import PartitionSpec as P

BF = jnp.bfloat16
F32 = jnp.float32
MIB = 1024 * 1024
CHUNKS = 16
UNROLL = 4
HBM = pl.BlockSpec(memory_space=pltpu.HBM)
VMEM = pl.BlockSpec(memory_space=pltpu.VMEM)
BIG = 40 * MIB
SMALL = 12 * MIB


def in_hbm(*arrays):
    return [pltpu.with_memory_space_constraint(x, pltpu.HBM) for x in arrays]


def in_vmem(*arrays):
    return [pltpu.with_memory_space_constraint(x, pltpu.VMEM) for x in arrays]


def small(kernel, name, shapes, scratch, *args):
    return pl.pallas_call(
        kernel,
        out_shape=[pltpu.VMEM(shape, BF) for shape in shapes],
        in_specs=[VMEM] * len(args),
        out_specs=[VMEM] * len(shapes),
        scratch_shapes=scratch,
        compiler_params=pltpu.CompilerParams(vmem_limit_bytes=SMALL),
        name=name,
    )(*in_vmem(*args))


def dot(a, b):
    return jnp.dot(a, b, preferred_element_type=F32)


def place():
    g = lax.axis_index("grp")
    return lax.axis_index("leaf"), g >> 1, g & 1


def forward_kernel(
    sec,
    count_hbm,
    cols_hbm,
    tgts_hbm,
    rhs_hbm,
    inv_hbm,
    tiles_hbm,
    keep,
    send,
    solved_hbm,
    dense_hbm,
    count,
    cols,
    tgts,
    rhs,
    inv,
    tiles,
    acc,
    dense,
    solved,
    stage,
    in_sems,
    tile_sems,
    out_sems,
):
    slots, block, _ = tiles.shape
    supernodes = inv.shape[0]
    targets = acc.shape[0]
    chunks = tile_sems.shape[0]
    step = slots // chunks
    group_cols = stage.shape[1] - (targets * block - stage.shape[1])
    _, _, core = place()

    def tile_copy(k):
        span = pl.ds(k * step, step)
        return pltpu.make_async_copy(tiles_hbm.at[span], tiles.at[span], tile_sems.at[k])

    pairs = (
        (count_hbm, count),
        (cols_hbm, cols),
        (tgts_hbm, tgts),
        (rhs_hbm, rhs),
        (inv_hbm, inv),
    )
    loads = [pltpu.make_async_copy(a, b, in_sems.at[i]) for i, (a, b) in enumerate(pairs)]
    for load in loads:
        load.start()
    for k in range(chunks):
        tile_copy(k).start()

    acc[...] = jnp.zeros_like(acc)
    for load in loads:
        load.wait()
    for s in range(supernodes):
        rows = pl.ds(s * block, block)
        solved[rows, :] = dot(inv[s], rhs[rows, :].astype(BF)).astype(BF)
    stores = [pltpu.make_async_copy(solved, solved_hbm, out_sems.at[0])]
    stores[0].start()

    live = count[0, 0]

    def add(p):
        t = tgts[0, p]
        c = cols[0, p]
        acc[t, c] = acc[t, c] + tiles[p].astype(F32)

    def add_some(i, carry):
        for u in range(UNROLL):
            add(i * UNROLL + u)
        return carry

    def add_one(p, carry):
        add(p)
        return carry

    whole = live // UNROLL
    per = step // UNROLL
    for k in range(chunks):
        tile_copy(k).wait()
        lax.fori_loop(k * per, jnp.clip(whole, k * per, (k + 1) * per), add_some, 0)
    lax.fori_loop(whole * UNROLL, live, add_one, 0)

    span = group_cols
    blocks = span // block
    for i in range(targets // blocks):
        for t in range(i * blocks, (i + 1) * blocks):
            for c in range(supernodes):
                dense[t * block : (t + 1) * block, c * block : (c + 1) * block] = acc[t, c].astype(BF)
        rows = pl.ds(i * span, span)
        stores.append(pltpu.make_async_copy(dense.at[rows], dense_hbm.at[rows], out_sems.at[1 + i]))
        stores[-1].start()
        total = dot(dense[rows, :], solved[...]).astype(BF)
        if i == 0:
            stage[0, 0:span, :] = total
            stage[1, 0:span, :] = total
        else:
            for q in range(0, span, sec):
                section = ((i - 1) * span + q) // sec
                begin = group_cols + (section // 2) * sec
                stage[(section % 2) ^ core, begin : begin + sec, :] = total[q : q + sec, :]
    keep[...] = stage[0]
    send[...] = stage[1]
    for store in stores:
        store.wait()


def leaf_forward(rhs, inverse, tiles, cols, tgts, count, sec, group_cols, upper_cols):
    slots, block, _ = tiles.shape
    supernodes = inverse.shape[0]
    targets = (group_cols + upper_cols) // block
    width = rhs.shape[-1]
    half = group_cols + upper_cols // 2
    return pl.pallas_call(
        functools.partial(forward_kernel, sec),
        out_shape=(
            pltpu.VMEM((half, width), BF),
            pltpu.VMEM((half, width), BF),
            pltpu.HBM((supernodes * block, width), BF),
            pltpu.HBM((targets * block, supernodes * block), BF),
        ),
        in_specs=[HBM] * 6,
        out_specs=(VMEM, VMEM, HBM, HBM),
        scratch_shapes=[
            pltpu.SMEM(count.shape, count.dtype),
            pltpu.SMEM(cols.shape, cols.dtype),
            pltpu.SMEM(tgts.shape, tgts.dtype),
            pltpu.VMEM(rhs.shape, rhs.dtype),
            pltpu.VMEM(inverse.shape, inverse.dtype),
            pltpu.VMEM((slots, block, block), BF),
            pltpu.VMEM((targets, supernodes, block, block), F32),
            pltpu.VMEM((targets * block, supernodes * block), BF),
            pltpu.VMEM((supernodes * block, width), BF),
            pltpu.VMEM((2, half, width), BF),
            pltpu.SemaphoreType.DMA((5,)),
            pltpu.SemaphoreType.DMA((CHUNKS,)),
            pltpu.SemaphoreType.DMA((1 + targets * block // group_cols,)),
        ],
        compiler_params=pltpu.CompilerParams(vmem_limit_bytes=BIG),
        cost_estimate=pl.CostEstimate(
            flops=2 * targets * block * supernodes * block * width,
            bytes_accessed=2 * tiles.size + 4 * rhs.size,
            transcendentals=0,
        ),
        name="leaf_forward",
    )(count, *in_hbm(cols, tgts, rhs, inverse, tiles))


def fold_kernel(n_leaf, n_pos, keep, recv, inv, rhs, late, *refs):
    early, outs = refs[:n_pos], refs[n_pos : n_pos + n_leaf + 1]
    gsum, stage = refs[n_pos + n_leaf + 1 :]
    leaf, pos, core = place()
    group_cols = inv.shape[0]
    cut = early[0].shape[0]
    sec = cut + late.shape[1]
    q = sec // n_leaf
    gq = group_cols // (2 * n_pos)
    gsum[...] = keep[0:group_cols, :].astype(F32) + recv[0:group_cols, :].astype(F32)
    residual = rhs[...] * (1.0 / n_pos) - gsum[...]
    solved = dot(inv[...], residual.astype(BF)).astype(BF)
    for k in range(n_pos):
        p = pos ^ k
        for begin, panel in ((0, early[k]), (cut, late.at[p])):
            span = panel.shape[0]
            rows = pl.ds(pl.multiple_of(group_cols + p * sec + begin, cut), span)
            terms = dot(panel[...], solved)
            terms = (terms + (keep[rows, :].astype(F32) + recv[rows, :].astype(F32))).astype(BF)
            for j in range(begin // q, (begin + span) // q):
                stage[j ^ leaf, k * q : (k + 1) * q, :] = terms[j * q - begin : (j + 1) * q - begin, :]
        begin = pl.multiple_of(core * (group_cols // 2) + p * gq, gq)
        outs[n_leaf][k * gq : (k + 1) * gq, :] = gsum[pl.ds(begin, gq), :].astype(BF)
    for k in range(n_leaf):
        outs[k][...] = stage[k]


def fold(keep, recv, inverse, rhs, early, late, n_leaf):
    width = rhs.shape[-1]
    n_pos = len(early)
    part = (n_pos * (early[0].shape[0] + late.shape[1]) // n_leaf, width)
    outs = small(
        functools.partial(fold_kernel, n_leaf, n_pos),
        "fold_group",
        [part] * n_leaf + [(inverse.shape[0] // 2, width)],
        [pltpu.VMEM(rhs.shape, F32), pltpu.VMEM((n_leaf,) + part, BF)],
        keep,
        recv,
        inverse,
        rhs,
        late,
        *early,
    )
    return list(outs[:n_leaf]), outs[n_leaf]


def total_of(refs):
    total = refs[0][...].astype(F32)
    for ref in refs[1:]:
        total = total + ref[...].astype(F32)
    return total


def sum_leaf_kernel(n_leaf, *refs):
    group, outs = refs[n_leaf], refs[n_leaf + 1 :]
    n_pos = len(outs)
    q = refs[0].shape[0] // n_pos
    gq = group.shape[0] // n_pos
    total = total_of(refs[:n_leaf]).astype(BF)
    for k, out in enumerate(outs):
        out[0:q, :] = total[k * q : (k + 1) * q, :]
        out[q:, :] = group[k * gq : (k + 1) * gq, :]


def sum_leaf(parts, group, n_pos):
    rows = (parts[0].shape[0] + group.shape[0]) // n_pos
    kernel = functools.partial(sum_leaf_kernel, len(parts))
    shapes = [(rows, group.shape[1])] * n_pos
    return list(small(kernel, "sum_leaf", shapes, [], *parts, group))


def sum_pos_kernel(high, group, *refs):
    parts, out = refs[:-1], refs[-1]
    q = high.shape[0]
    total = total_of(parts)
    out[0:q, :] = (high[...] - total[0:q, :]).astype(BF)
    out[q:, :] = (group[...] - total[q:, :]).astype(BF)


def sum_pos(high, group, parts):
    return small(sum_pos_kernel, "sum_pos", [parts[0].shape], [], high, group, *parts)[0]


def stack_pos_kernel(q, *refs):
    parts, (uppers, groups) = refs[:-2], refs[-2:]
    gq = parts[0].shape[0] - q
    for k, part in enumerate(parts):
        uppers[k * q : (k + 1) * q, :] = part[0:q, :]
        groups[k * gq : (k + 1) * gq, :] = part[q:, :]


def stack_pos(parts, q):
    n_pos, (rows, width) = len(parts), parts[0].shape
    shapes = [(n_pos * q, width), (n_pos * (rows - q), width)]
    return small(functools.partial(stack_pos_kernel, q), "stack_pos", shapes, [], *parts)


def stack_kernel(*refs):
    begin = 0
    for part in refs[:-1]:
        rows = part.shape[0]
        refs[-1][begin : begin + rows, :] = part[...]
        begin += rows


def stack(parts):
    rows = sum(part.shape[0] for part in parts)
    return small(stack_kernel, "stack", [(rows, parts[0].shape[1])], [], *parts)[0]


def backward_kernel(
    n_leaf,
    n_pos,
    mine,
    theirs,
    leaf_solved_hbm,
    inv_leaf_hbm,
    inv_mid_hbm,
    inv_top_hbm,
    inv_group_hbm,
    dense_hbm,
    mid_hbm_parts,
    *refs,
):
    backward_steps(
        n_leaf,
        n_pos,
        mid_hbm_parts,
        refs[:4],
        mine,
        theirs,
        leaf_solved_hbm,
        inv_leaf_hbm,
        inv_mid_hbm,
        inv_top_hbm,
        inv_group_hbm,
        dense_hbm,
        *refs[4:],
    )


def backward_steps(
    n_leaf,
    n_pos,
    mid_parts,
    group_parts,
    mine,
    theirs,
    leaf_solved_hbm,
    inv_leaf_hbm,
    inv_mid_hbm,
    inv_top_hbm,
    inv_group_hbm,
    dense_hbm,
    leaf_hbm,
    group_hbm,
    mid_hbm,
    top_hbm,
    leaf_solved,
    inv_leaf,
    inv_mid,
    inv_top,
    inv_group,
    dense,
    panel_mid,
    panel_group,
    leaf_out,
    group_out,
    mid_out,
    top_out,
    upper,
    residual,
    above,
    sems,
    mid_sems,
    group_sems,
    out_sems,
):
    leaf, pos, core = place()
    pairs = (
        (inv_mid_hbm, inv_mid),
        (inv_top_hbm, inv_top),
        (inv_group_hbm, inv_group),
        (dense_hbm, dense),
        (leaf_solved_hbm, leaf_solved),
        (inv_leaf_hbm, inv_leaf),
    )
    loads = [pltpu.make_async_copy(a, b, sems.at[i]) for i, (a, b) in enumerate(pairs)]
    mid_loads = []
    if mid_parts.ndim == 2:
        mid_loads.append(pltpu.make_async_copy(mid_parts, panel_mid, mid_sems.at[0]))
    else:
        rows = mid_parts.shape[1] // n_leaf
        for i in range(2 * n_pos * n_leaf):
            g, k = divmod(i, n_leaf)
            begin = ((leaf ^ k) * (2 * n_pos) + g) * rows
            span = pl.ds(pl.multiple_of(begin, rows), rows)
            got = mid_parts.at[g, pl.ds(k * rows, rows)]
            mid_loads.append(pltpu.make_async_copy(got, panel_mid.at[span], mid_sems.at[i]))
    group_loads = []
    early, late = group_parts[:2], group_parts[2:]
    cut = early[0].shape[0] // n_pos
    sec = cut + late[0].shape[1]
    for kc in range(2):
        for k in range(n_pos):
            for j, (got, p, shift, rows) in enumerate((
                (early[kc].at[pl.ds(k * cut, cut)], pos ^ k, 0, cut),
                (late[kc].at[k], k, cut, sec - cut),
            )):
                begin = (2 * p + (core ^ kc)) * sec + shift
                span = pl.ds(pl.multiple_of(begin, cut), rows)
                sem = group_sems.at[(kc * n_pos + k) * 2 + j]
                group_loads.append(pltpu.make_async_copy(got, panel_group.at[span], sem))
    for load in loads[:1] + mid_loads + loads[1:3] + group_loads + loads[3:]:
        load.start()
    mid_rows = inv_mid.shape[0]
    top_rows = inv_top.shape[0]
    group_rows = inv_group.shape[0]
    supernodes, block, _ = inv_leaf.shape
    upper_cols = pl.ds(group_rows, mid_rows + top_rows)
    mid_cols = pl.ds(group_rows, mid_rows)
    top_cols = pl.ds(group_rows + mid_rows, top_rows)
    sec = (mid_rows + top_rows) // (2 * n_pos)
    q = sec // n_leaf
    gq = group_rows // (2 * n_pos)
    for kc, got in enumerate((mine, theirs)):
        for kz in range(n_pos):
            for kl in range(n_leaf):
                row = sec * (2 * (pos ^ kz) + (core ^ kc)) + q * (leaf ^ kl)
                begin = (kl * n_pos + kz) * q
                upper[pl.ds(pl.multiple_of(row, q), q), :] = got[begin : begin + q, :]
            row = (group_rows // 2) * (core ^ kc) + gq * (pos ^ kz)
            begin = n_leaf * n_pos * q + kz * gq
            residual[pl.ds(pl.multiple_of(row, gq), gq), :] = got[begin : begin + gq, :]

    loads[0].wait()
    mid_solved = dot(inv_mid[...], upper[0:mid_rows, :]).astype(BF)
    for load in mid_loads:
        load.wait()
    top_residual = upper[mid_rows:, :].astype(F32) - dot(panel_mid[...], mid_solved)
    loads[1].wait()
    top_solved = dot(inv_top[...], top_residual.astype(BF))
    top_t = dot(top_solved.T.astype(BF), inv_top[...])
    above[:, top_cols] = top_t.astype(BF)
    top_out[...] = top_t.T
    stores = [pltpu.make_async_copy(top_out, top_hbm, out_sems.at[0])]
    stores[0].start()
    mid_back = mid_solved.astype(F32).T - dot(above[:, top_cols], panel_mid[...])
    mid_t = dot(mid_back.astype(BF), inv_mid[...])
    above[:, mid_cols] = mid_t.astype(BF)
    mid_out[...] = mid_t.T
    stores.append(pltpu.make_async_copy(mid_out, mid_hbm, out_sems.at[1]))
    stores[1].start()
    loads[2].wait()
    group_solved = dot(inv_group[...], residual[...]).astype(BF).astype(F32).T
    for load in group_loads:
        load.wait()
    group_back = group_solved - dot(above[:, upper_cols], panel_group[...])
    group_t = dot(group_back.astype(BF), inv_group[...])
    above[:, 0:group_rows] = group_t.astype(BF)
    group_out[...] = group_t.T
    stores.append(pltpu.make_async_copy(group_out, group_hbm, out_sems.at[2]))
    stores[2].start()
    for load in loads[3:]:
        load.wait()
    for s in range(supernodes):
        cols = pl.ds(s * block, block)
        terms = dot(above[...], dense[:, cols])
        back = (leaf_solved[cols, :].astype(F32).T - terms).astype(BF)
        leaf_out[cols, :] = dot(back, inv_leaf[s]).T
    stores.append(pltpu.make_async_copy(leaf_out, leaf_hbm, out_sems.at[3]))
    stores[3].start()
    for store in stores:
        store.wait()


def backward(
    mine,
    theirs,
    leaf_solved,
    inv_leaf,
    inv_mid,
    inv_top,
    inv_group,
    dense,
    mid_parts,
    group_parts,
    n_leaf,
    n_pos,
):
    width = mine.shape[-1]
    upper_rows = inv_mid.shape[0] + inv_top.shape[0]
    group_rows = inv_group.shape[0]
    heavy = (leaf_solved, inv_leaf, inv_mid, inv_top, inv_group, dense)
    outs = (
        pltpu.HBM(leaf_solved.shape, F32),
        pltpu.HBM((group_rows, width), F32),
        pltpu.HBM((inv_mid.shape[0], width), F32),
        pltpu.HBM((inv_top.shape[0], width), F32),
    )
    return pl.pallas_call(
        functools.partial(backward_kernel, n_leaf, n_pos),
        out_shape=outs,
        in_specs=[VMEM] * 2 + [HBM] * (len(heavy) + 1 + len(group_parts)),
        out_specs=(HBM,) * 4,
        scratch_shapes=[pltpu.VMEM(a.shape, a.dtype) for a in heavy]
        + [
            pltpu.VMEM((inv_top.shape[0], inv_mid.shape[0]), BF),
            pltpu.VMEM((upper_rows, group_rows), BF),
        ]
        + [pltpu.VMEM(a.shape, a.dtype) for a in outs]
        + [
            pltpu.VMEM((upper_rows, width), BF),
            pltpu.VMEM((group_rows, width), BF),
            pltpu.VMEM((width, dense.shape[0]), BF),
            pltpu.SemaphoreType.DMA((len(heavy),)),
            pltpu.SemaphoreType.DMA((2 * n_pos * n_leaf,)),
            pltpu.SemaphoreType.DMA((4 * n_pos,)),
            pltpu.SemaphoreType.DMA((len(outs),)),
        ],
        compiler_params=pltpu.CompilerParams(vmem_limit_bytes=BIG),
        name="backward",
    )(*in_vmem(mine, theirs), *in_hbm(*heavy, mid_parts, *group_parts))


def swap(x, axis, size, bits):
    return lax.ppermute(x, axis, [(i, i ^ bits) for i in range(size)])


def swaps(x, axis, size, unit=1):
    return [x] + [swap(x, axis, size, unit * k) for k in range(1, size // unit)]


def after(x, *others):
    return lax.optimization_barrier((x, others))[0]


def body(
    n_leaf,
    n_grp,
    rhs_leaf,
    rhs_group,
    rhs_middle,
    rhs_top,
    inv_leaf,
    inv_group,
    inv_middle,
    inv_top,
    leaf_tiles,
    tile_column,
    tile_target,
    tile_count,
    group_panel,
    middle_panel,
):
    n_pos = n_grp // 2
    group_cols = rhs_group.shape[1]
    mid_cols = rhs_middle.shape[0]
    upper_cols = mid_cols + rhs_top.shape[0]
    sec = upper_cols // n_grp
    q = sec // n_leaf
    gq = group_cols // n_grp
    leaf, pos, core = place()
    by_parts = middle_panel.shape[0] % 16 == 0
    pos_groups = [[2 * p + c for p in range(n_pos)] for c in range(2)]
    cut = sec // 2
    with jax.named_scope("gather_group_panel"):
        late = lax.all_gather(group_panel[0, cut:], "grp", axis_index_groups=pos_groups)
        early = swaps(group_panel[0, :cut], "grp", n_grp, 2)
    if by_parts:
        with jax.named_scope("gather_middle_panel"):
            middle = swaps(middle_panel, "leaf", n_leaf)
    keep, send, leaf_solved, dense = leaf_forward(
        rhs_leaf[0],
        inv_leaf[0],
        leaf_tiles[0],
        tile_column,
        tile_target,
        tile_count,
        sec,
        group_cols,
        upper_cols,
    )
    with jax.named_scope("gather_middle_panel"):
        if by_parts:
            middle = stack(middle)
            send, early = after((send, early), middle)
            middle = lax.all_gather(middle, "grp")
        else:
            middle = lax.all_gather(middle_panel, ("leaf", "grp"), axis=0, tiled=True)
    with jax.named_scope("swap_cores"):
        recv = swap(send, "grp", n_grp, 1)
    parts, group = fold(keep, recv, inv_group[0], rhs_group[0], early, late, n_leaf)
    with jax.named_scope("sum_over_leaf"):
        parts = parts[:1] + [swap(parts[k], "leaf", n_leaf, k) for k in range(1, n_leaf)]
    sends = sum_leaf(parts, group, n_pos)
    with jax.named_scope("sum_over_pos"):
        got = sends[:1] + [swap(sends[k], "grp", n_grp, 2 * k) for k in range(1, n_pos)]
    begin = sec * lax.axis_index("grp") + q * leaf
    low = lax.dynamic_slice_in_dim(rhs_middle, jnp.minimum(begin, mid_cols - q), q, 0)
    high = lax.dynamic_slice_in_dim(rhs_top, jnp.maximum(begin - mid_cols, 0), q, 0)
    rhs_mine = jnp.where(begin < mid_cols, low, high)
    group_begin = (group_cols // 2) * core + gq * pos
    group_mine = lax.dynamic_slice_in_dim(rhs_group[0], group_begin, gq, 0)
    residual = sum_pos(rhs_mine, group_mine, got)
    with jax.named_scope("gather_pos"):
        uppers, groups = stack_pos(swaps(residual, "grp", n_grp, 2), q)
    with jax.named_scope("gather_leaf"):
        stacks = swaps(uppers, "leaf", n_leaf)
    with jax.named_scope("swap_group_panel"):
        early = stack(early)
        panels = [early, swap(early, "grp", n_grp, 1), late, swap(late, "grp", n_grp, 1)]
    with jax.named_scope("gather_cores"):
        mine = stack(after(stacks, panels) + [groups])
        theirs = swap(mine, "grp", n_grp, 1)
    leaf_out, group_out, mid_out, top_out = backward(
        mine,
        theirs,
        leaf_solved,
        inv_leaf[0],
        inv_middle,
        inv_top,
        inv_group[0],
        dense,
        middle,
        panels,
        n_leaf,
        n_pos,
    )
    return leaf_out[None], group_out[None], mid_out, top_out


def solution(mesh):
    n_leaf = mesh.shape["leaf"]
    n_grp = mesh.shape["grp"]
    placed = (
        P("leaf", "grp", None),
        P("leaf", None, None),
        P(),
        P(),
        P("leaf", "grp", None, None),
        P("leaf", None, None),
        P(),
        P(),
        P("leaf", "grp", None, None),
        P("leaf", "grp"),
        P("leaf", "grp"),
        P("leaf", "grp"),
        P("leaf", "grp", None),
        P(("leaf", "grp"), None),
    )
    return jax.shard_map(
        functools.partial(body, n_leaf, n_grp),
        mesh=mesh,
        in_specs=placed,
        out_specs=(P("leaf", "grp", None), P("leaf", None, None), P(), P()),
        check_vma=False,
    )
```

time: 162 us -> 121 us (0.75)
  waiting for transfers between devices: 56.5 us -> 32.5 us
  local copies, waits for them, and re-layouts: 25.6 us -> 1.86 us
  blocking collectives: 0 us -> 17.7 us
  starting transfers between devices: 31.9 us -> 25.7 us
  Pallas kernels: 30.8 us -> 27.5 us
    unnamed x74 -> x12, local copies, waits for them, and re-layouts: 25.6 us -> 0.86 us
    all_gather x0 -> x1, blocking collectives: none -> 17.7 us  [body(): lax.all_gather(group_panel[0, cut:], 'grp', axis_index_groups=pos_groups)]
    all_gather x1, waiting for transfers between devices: 15.4 us -> 0.01 us  [body(): middle = lax.all_gather(middle, 'grp')]
    ppermute x35 -> x22, waiting for transfers between devices: 40.4 us -> 32.5 us  [swap(): return lax.ppermute(x, axis, [(i, i ^ bits) for i in range(size)])]
    ppermute x35 -> x22, starting transfers between devices: 31.8 us -> 25.7 us  [swap(): return lax.ppermute(x, axis, [(i, i ^ bits) for i in range(size)])]
    pallas_call x11 -> x9, Pallas kernels: 30.8 us -> 27.5 us  [the longest x1 16.8 us: backward(): pl.pallas_call(functools.partial(backward_kernel, n_leaf, n_pos), out_sha...]
  transfers between devices with their start and end apart: 36 -> 23, of which waited for: 15 -> 13; matrix products, arithmetic and copies ran while one was open for 1% -> 2% of each run, Pallas kernels for 9% -> 8%
where the time goes in v4:
time: 121 us
  waiting for transfers between devices  32.5 us (27%)
  Pallas kernels  27.5 us (23%)
  starting transfers between devices  25.7 us (21%)
  blocking collectives  17.7 us (15%)
  between operations  14.8 us (12%)
  local copies, waits for them, and re-layouts  1.86 us (2%)
    ppermute x22, waiting for transfers between devices, swap(): return lax.ppermute(x, axis, [(i, i ^ bits) for i in range(size)])  32.5 us
    ppermute x22, starting transfers between devices, swap(): return lax.ppermute(x, axis, [(i, i ^ bits) for i in range(size)])  25.7 us
    all_gather x1, blocking collectives, body(): lax.all_gather(group_panel[0, cut:], 'grp', axis_index_groups=pos_groups)  17.7 us
    pallas_call x1, Pallas kernels, backward(): pl.pallas_call(functools.partial(backward_kernel, n_leaf, n_pos), out_sha...  16.8 us
    pallas_call x1, Pallas kernels, leaf_forward(): pl.pallas_call(functools.partial(forward_kernel, sec), out_shape=(pltpu.V...  8.71 us
  transfers between devices with their start and end apart: 23, of which 13 were waited for; matrix products, arithmetic and copies ran while one was open for 2% of the time, Pallas kernels for 8%

profile of v4, /device:TPU:0, one launch (start us, length us, event | category | flops | bytes accessed | tf_op | source)
XLA Modules:
  0.0 121.0 jit_solution(11216723809987933074)
XLA Ops:
  7.2 3.0 %collective-permute-start.4 = (bf16[32,1024]{1,0:T(8,128)(2,1)}, bf16[32,1024]{1,0:T(8,128)(2,1)S(1)}, u32[]{:S(2)}, u32[]{:S(2)}) collective-permute-start(bf16[32,1024]{1,0:T(8,128)(2,1)} %refs_0_.1), channel_id=1, source_target_pairs={{0,16},{8,24},{16,0},{24,8},{1,17},{9,25},{17,1},{25,9},{2,18},{10... | collective-permute-start | bytes 196616 | tf_op jit(solution)/shard_map/gather_middle_panel/ppermute | solution.py:524
  10.2 1.5 %collective-permute-start.3 = (bf16[32,1024]{1,0:T(8,128)(2,1)}, bf16[32,1024]{1,0:T(8,128)(2,1)S(1)}, u32[]{:S(2)}, u32[]{:S(2)}) collective-permute-start(bf16[32,1024]{1,0:T(8,128)(2,1)} %refs_0_.1), channel_id=1, source_target_pairs={{0,8},{8,0},{16,24},{24,16},{1,9},{9,1},{17,25},{25,17},{2,10},{10... | collective-permute-start | bytes 196616 | tf_op jit(solution)/shard_map/gather_middle_panel/ppermute | solution.py:524
  12.7 2.5 %collective-permute-done.3.refs_1_ = bf16[32,1024]{1,0:T(8,128)(2,1)S(1)} collective-permute-done((bf16[32,1024]{1,0:T(8,128)(2,1)}, bf16[32,1024]{1,0:T(8,128)(2,1)S(1)}, u32[]{:S(2)}, u32[]{:S(2)}) %collective-permute-start.3) | collective-permute-done | bytes 65568 | tf_op jit(solution)/shard_map/gather_middle_panel/ppermute | solution.py:524
  15.2 1.9 %collective-permute-done.5.refs_3_ = bf16[32,1024]{1,0:T(8,128)(2,1)S(1)} collective-permute-done((bf16[32,1024]{1,0:T(8,128)(2,1)}, bf16[32,1024]{1,0:T(8,128)(2,1)S(1)}, u32[]{:S(2)}, u32[]{:S(2)}) %collective-permute-start.5) | collective-permute-done | bytes 65568 | tf_op jit(solution)/shard_map/gather_middle_panel/ppermute | solution.py:524
  19.7 3.7 %collective-permute-start.2 = (bf16[128,512]{1,0:T(8,128)(2,1)S(1)}, bf16[128,512]{1,0:T(8,128)(2,1)S(1)}, u32[]{:S(2)}, u32[]{:S(2)}) collective-permute-start(bf16[128,512]{1,0:T(8,128)(2,1)S(1)} %get-tuple-element.35.refs_0_), channel_id=1, source_target_pairs={{0,6},{1,7},{2,4},{3,5},{4,2},{5,3},{6,0},{7,1},{8,14},{9,15},{10,... | collective-permute-start | bytes 393224 | tf_op jit(solution)/shard_map/gather_group_panel/ppermute | solution.py:524
  24.8 8.7 %leaf_forward.1 = (bf16[1536,256]{1,0:T(8,128)(2,1)S(1)}, bf16[1536,256]{1,0:T(8,128)(2,1)S(1)}, bf16[1024,256]{1,0:T(8,128)(2,1)}, bf16[2560,1024]{1,0:T(8,128)(2,1)}) custom-call(s32[1,1]{1,0:T(1,128)S(6)} %copy.18.count_hbm, s32[1,256]{1,0:T(1,128)} %cols_hbm.1, s32[1,256]{1,0:T(1,128)} %tgts_hbm.1, f32[1024,256]{1,0:T(8,128)} %bitcast.19, ...), custom_call_target="tpu_custom_call" | custom-call | flops 1342177280 | bytes 9437184 | tf_op jit(solution)/shard_map/leaf_forward/pallas_call | solution.py:163
  33.5 8.8 %collective-permute-done.1.refs_2_ = bf16[128,512]{1,0:T(8,128)(2,1)S(1)} collective-permute-done((bf16[128,512]{1,0:T(8,128)(2,1)S(1)}, bf16[128,512]{1,0:T(8,128)(2,1)S(1)}, u32[]{:S(2)}, u32[]{:S(2)}) %collective-permute-start.1) | collective-permute-done | bytes 131104 | tf_op jit(solution)/shard_map/gather_group_panel/ppermute | solution.py:524
  42.4 17.7 %all_gather.9.late.refs_2_ = bf16[4,128,512]{2,1,0:T(8,128)(2,1)S(1)} all-gather(bf16[1,128,512]{2,1,0:T(8,128)(2,1)S(1)} %get-tuple-element.60), channel_id=1, replica_groups={{0,2,4,6},{1,3,5,7},{8,10,12,14},{9,11,13,15},{16,18,20,22},{17,19,21,2..., dimensions={0}, use_global_device_ids=true | all-gather | bytes 655360 | tf_op jit(solution)/shard_map/gather_group_panel/all_gather | solution.py:565
  62.7 2.6 %collective-permute-start.9 = (bf16[256,256]{1,0:T(8,128)(2,1)S(1)}, bf16[256,256]{1,0:T(8,128)(2,1)S(1)}, u32[]{:S(2)}, u32[]{:S(2)}) collective-permute-start(bf16[256,256]{1,0:T(8,128)(2,1)S(1)} %get-tuple-element.42), channel_id=1, source_target_pairs={{0,24},{8,16},{16,8},{24,0},{1,25},{9,17},{17,9},{25,1},{2,26},{10... | collective-permute-start | bytes 393224 | tf_op jit(solution)/shard_map/sum_over_leaf/ppermute | solution.py:524
  65.3 2.9 %collective-permute-done.7.refs_1_ = bf16[256,256]{1,0:T(8,128)(2,1)S(1)} collective-permute-done((bf16[256,256]{1,0:T(8,128)(2,1)S(1)}, bf16[256,256]{1,0:T(8,128)(2,1)S(1)}, u32[]{:S(2)}, u32[]{:S(2)}) %collective-permute-start.7) | collective-permute-done | bytes 131104 | tf_op jit(solution)/shard_map/sum_over_leaf/ppermute | solution.py:524
  68.2 2.0 %collective-permute-done.8.refs_2_ = bf16[256,256]{1,0:T(8,128)(2,1)S(1)} collective-permute-done((bf16[256,256]{1,0:T(8,128)(2,1)S(1)}, bf16[256,256]{1,0:T(8,128)(2,1)S(1)}, u32[]{:S(2)}, u32[]{:S(2)}) %collective-permute-start.8) | collective-permute-done | bytes 131104 | tf_op jit(solution)/shard_map/sum_over_leaf/ppermute | solution.py:524
  70.3 1.3 %collective-permute-start.10 = (bf16[128,256]{1,0:T(8,128)(2,1)S(1)}, bf16[128,256]{1,0:T(8,128)(2,1)S(1)}, u32[]{:S(2)}, u32[]{:S(2)}) collective-permute-start(bf16[128,256]{1,0:T(8,128)(2,1)S(1)} %get-tuple-element.45), channel_id=1, source_target_pairs={{0,2},{1,3},{2,0},{3,1},{4,6},{5,7},{6,4},{7,5},{8,10},{9,11},{10,... | collective-permute-start | bytes 196616 | tf_op jit(solution)/shard_map/sum_over_pos/ppermute | solution.py:524
  71.6 2.5 %collective-permute-start.11 = (bf16[128,256]{1,0:T(8,128)(2,1)S(1)}, bf16[128,256]{1,0:T(8,128)(2,1)S(1)}, u32[]{:S(2)}, u32[]{:S(2)}) collective-permute-start(bf16[128,256]{1,0:T(8,128)(2,1)S(1)} %get-tuple-element.46), channel_id=1, source_target_pairs={{0,4},{1,5},{2,6},{3,7},{4,0},{5,1},{6,2},{7,3},{8,12},{9,13},{10,... | collective-permute-start | bytes 196616 | tf_op jit(solution)/shard_map/sum_over_pos/ppermute | solution.py:524
  75.7 2.5 %collective-permute-done.11.refs_2_ = bf16[128,256]{1,0:T(8,128)(2,1)S(1)} collective-permute-done((bf16[128,256]{1,0:T(8,128)(2,1)S(1)}, bf16[128,256]{1,0:T(8,128)(2,1)S(1)}, u32[]{:S(2)}, u32[]{:S(2)}) %collective-permute-start.11) | collective-permute-done | bytes 65568 | tf_op jit(solution)/shard_map/sum_over_pos/ppermute | solution.py:524
  78.1 2.1 %collective-permute-done.12.refs_3_ = bf16[128,256]{1,0:T(8,128)(2,1)S(1)} collective-permute-done((bf16[128,256]{1,0:T(8,128)(2,1)S(1)}, bf16[128,256]{1,0:T(8,128)(2,1)S(1)}, u32[]{:S(2)}, u32[]{:S(2)}) %collective-permute-start.12) | collective-permute-done | bytes 65568 | tf_op jit(solution)/shard_map/sum_over_pos/ppermute | solution.py:524
  81.7 3.0 %collective-permute-start.13 = (bf16[128,256]{1,0:T(8,128)(2,1)S(1)}, bf16[128,256]{1,0:T(8,128)(2,1)S(1)}, u32[]{:S(2)}, u32[]{:S(2)}) collective-permute-start(bf16[128,256]{1,0:T(8,128)(2,1)S(1)} %sum_pos.1.refs_0_), channel_id=1, source_target_pairs={{0,2},{1,3},{2,0},{3,1},{4,6},{5,7},{6,4},{7,5},{8,10},{9,11},{10,... | collective-permute-start | bytes 196616 | tf_op jit(solution)/shard_map/gather_pos/ppermute | solution.py:524
  84.7 1.8 %collective-permute-done.15.refs_3_ = bf16[128,256]{1,0:T(8,128)(2,1)S(1)} collective-permute-done((bf16[128,256]{1,0:T(8,128)(2,1)S(1)}, bf16[128,256]{1,0:T(8,128)(2,1)S(1)}, u32[]{:S(2)}, u32[]{:S(2)}) %collective-permute-start.15) | collective-permute-done | bytes 65568 | tf_op jit(solution)/shard_map/gather_pos/ppermute | solution.py:524
  86.5 1.2 %collective-permute-done.14.refs_2_ = bf16[128,256]{1,0:T(8,128)(2,1)S(1)} collective-permute-done((bf16[128,256]{1,0:T(8,128)(2,1)S(1)}, bf16[128,256]{1,0:T(8,128)(2,1)S(1)}, u32[]{:S(2)}, u32[]{:S(2)}) %collective-permute-start.14) | collective-permute-done | bytes 65568 | tf_op jit(solution)/shard_map/gather_pos/ppermute | solution.py:524
  87.8 1.5 %collective-permute-start.18 = (bf16[256,256]{1,0:T(8,128)(2,1)S(1)}, bf16[256,256]{1,0:T(8,128)(2,1)S(1)}, u32[]{:S(2)}, u32[]{:S(2)}) collective-permute-start(bf16[256,256]{1,0:T(8,128)(2,1)S(1)} %get-tuple-element.49.refs_0_), channel_id=1, source_target_pairs={{0,24},{8,16},{16,8},{24,0},{1,25},{9,17},{17,9},{25,1},{2,26},{10... | collective-permute-start | bytes 393224 | tf_op jit(solution)/shard_map/gather_leaf/ppermute | solution.py:524
  89.7 1.6 %collective-permute-start.16 = (bf16[256,256]{1,0:T(8,128)(2,1)S(1)}, bf16[256,256]{1,0:T(8,128)(2,1)S(1)}, u32[]{:S(2)}, u32[]{:S(2)}) collective-permute-start(bf16[256,256]{1,0:T(8,128)(2,1)S(1)} %get-tuple-element.49.refs_0_), channel_id=1, source_target_pairs={{0,8},{8,0},{16,24},{24,16},{1,9},{9,1},{17,25},{25,17},{2,10},{10... | collective-permute-start | bytes 393224 | tf_op jit(solution)/shard_map/gather_leaf/ppermute | solution.py:524
  91.3 2.5 %collective-permute-done.18.refs_3_ = bf16[256,256]{1,0:T(8,128)(2,1)S(1)} collective-permute-done((bf16[256,256]{1,0:T(8,128)(2,1)S(1)}, bf16[256,256]{1,0:T(8,128)(2,1)S(1)}, u32[]{:S(2)}, u32[]{:S(2)}) %collective-permute-start.18) | collective-permute-done | bytes 131104 | tf_op jit(solution)/shard_map/gather_leaf/ppermute | solution.py:524
  93.8 1.3 %collective-permute-done.17.refs_2_ = bf16[256,256]{1,0:T(8,128)(2,1)S(1)} collective-permute-done((bf16[256,256]{1,0:T(8,128)(2,1)S(1)}, bf16[256,256]{1,0:T(8,128)(2,1)S(1)}, u32[]{:S(2)}, u32[]{:S(2)}) %collective-permute-start.17) | collective-permute-done | bytes 131104 | tf_op jit(solution)/shard_map/gather_leaf/ppermute | solution.py:524
  95.2 2.1 %collective-permute-done.21.theirs = bf16[1280,256]{1,0:T(8,128)(2,1)S(1)} collective-permute-done((bf16[1280,256]{1,0:T(8,128)(2,1)S(1)}, bf16[1280,256]{1,0:T(8,128)(2,1)S(1)}, u32[]{:S(2)}, u32[]{:S(2)}) %collective-permute-start.21) | collective-permute-done | bytes 655392 | tf_op jit(solution)/shard_map/gather_cores/ppermute | solution.py:524
  97.3 16.8 %backward.1 = (f32[1024,256]{1,0:T(8,128)}, f32[512,256]{1,0:T(8,128)}, f32[1024,256]{1,0:T(8,128)}, f32[1024,256]{1,0:T(8,128)}) custom-call(bf16[1280,256]{1,0:T(8,128)(2,1)S(1)} %stack.5.mine, bf16[1280,256]{1,0:T(8,128)(2,1)S(1)} %collective-permute-done.21.theirs, bf16[1024,256]{1,0:T(8,128)(2,1)} %get-tuple-element.54.leaf_solved_hbm, ...), custom_call_target="tpu_custom_call" | custom-call | tf_op jit(solution)/shard_map/backward/pallas_call | solution.py:498
  (48 shorter events, 10.8 us)
Async XLA Ops:
  7.2 90.2 %all-gather.3.cloned.1.call-start = ((), (), s32[]{:S(2)}) async-start(), calls=%async_computation | async-start | bytes 2359296 | tf_op jit(solution)/shard_map/gather_middle_panel/all_gather | solution.py:585
  7.2 5.5 %collective-permute-start.4 = (bf16[32,1024]{1,0:T(8,128)(2,1)}, bf16[32,1024]{1,0:T(8,128)(2,1)S(1)}, u32[]{:S(2)}, u32[]{:S(2)}) collective-permute-start(bf16[32,1024]{1,0:T(8,128)(2,1)} %refs_0_.1), channel_id=1, source_target_pairs={{0,16},{8,24},{16,0},{24,8},{1,17},{9,25},{17,1},{25,9},{2,18},{10... | collective-permute-start | bytes 196616 | tf_op jit(solution)/shard_map/gather_middle_panel/ppermute | solution.py:524
  10.2 4.9 %collective-permute-start.3 = (bf16[32,1024]{1,0:T(8,128)(2,1)}, bf16[32,1024]{1,0:T(8,128)(2,1)S(1)}, u32[]{:S(2)}, u32[]{:S(2)}) collective-permute-start(bf16[32,1024]{1,0:T(8,128)(2,1)} %refs_0_.1), channel_id=1, source_target_pairs={{0,8},{8,0},{16,24},{24,16},{1,9},{9,1},{17,25},{25,17},{2,10},{10... | collective-permute-start | bytes 196616 | tf_op jit(solution)/shard_map/gather_middle_panel/ppermute | solution.py:524
  11.7 5.4 %collective-permute-start.5 = (bf16[32,1024]{1,0:T(8,128)(2,1)}, bf16[32,1024]{1,0:T(8,128)(2,1)S(1)}, u32[]{:S(2)}, u32[]{:S(2)}) collective-permute-start(bf16[32,1024]{1,0:T(8,128)(2,1)} %refs_0_.1), channel_id=1, source_target_pairs={{0,24},{8,16},{16,8},{24,0},{1,25},{9,17},{17,9},{25,1},{2,26},{10... | collective-permute-start | bytes 196616 | tf_op jit(solution)/shard_map/gather_middle_panel/ppermute | solution.py:524
  19.7 13.9 %collective-permute-start.2 = (bf16[128,512]{1,0:T(8,128)(2,1)S(1)}, bf16[128,512]{1,0:T(8,128)(2,1)S(1)}, u32[]{:S(2)}, u32[]{:S(2)}) collective-permute-start(bf16[128,512]{1,0:T(8,128)(2,1)S(1)} %get-tuple-element.35.refs_0_), channel_id=1, source_target_pairs={{0,6},{1,7},{2,4},{3,5},{4,2},{5,3},{6,0},{7,1},{8,14},{9,15},{10,... | collective-permute-start | bytes 393224 | tf_op jit(solution)/shard_map/gather_group_panel/ppermute | solution.py:524
  23.4 19.0 %collective-permute-start.1 = (bf16[128,512]{1,0:T(8,128)(2,1)S(1)}, bf16[128,512]{1,0:T(8,128)(2,1)S(1)}, u32[]{:S(2)}, u32[]{:S(2)}) collective-permute-start(bf16[128,512]{1,0:T(8,128)(2,1)S(1)} %get-tuple-element.35.refs_0_), channel_id=1, source_target_pairs={{0,4},{1,5},{2,6},{3,7},{4,0},{5,1},{6,2},{7,3},{8,12},{9,13},{10,... | collective-permute-start | bytes 393224 | tf_op jit(solution)/shard_map/gather_group_panel/ppermute | solution.py:524
  23.4 19.0 %collective-permute-start = (bf16[128,512]{1,0:T(8,128)(2,1)S(1)}, bf16[128,512]{1,0:T(8,128)(2,1)S(1)}, u32[]{:S(2)}, u32[]{:S(2)}) collective-permute-start(bf16[128,512]{1,0:T(8,128)(2,1)S(1)} %get-tuple-element.35.refs_0_), channel_id=1, source_target_pairs={{0,2},{1,3},{2,0},{3,1},{4,6},{5,7},{6,4},{7,5},{8,10},{9,11},{10,... | collective-permute-start | bytes 393224 | tf_op jit(solution)/shard_map/gather_group_panel/ppermute | solution.py:524
  24.8 35.9 %copy-start.1 = (bf16[1,512,512]{2,1,0:T(8,128)(2,1)S(1)}, bf16[1,512,512]{2,1,0:T(8,128)(2,1)}, u32[]{:S(2)}) copy-start(bf16[1,512,512]{2,1,0:T(8,128)(2,1)} %param.19) | copy-start | bytes 1572868
  42.4 18.3 %collective-permute-start.6 = (bf16[1536,256]{1,0:T(8,128)(2,1)S(1)}, bf16[1536,256]{1,0:T(8,128)(2,1)S(1)}, u32[]{:S(2)}, u32[]{:S(2)}) collective-permute-start(bf16[1536,256]{1,0:T(8,128)(2,1)S(1)} %get-tuple-element.34), channel_id=1, source_target_pairs={{0,1},{1,0},{2,3},{3,2},{4,5},{5,4},{6,7},{7,6},{8,9},{9,8},{10,11... | collective-permute-start | bytes 2359304 | tf_op jit(solution)/shard_map/swap_cores/ppermute | solution.py:524
  60.1 31.3 %collective-permute-start.20 = (bf16[4,128,512]{2,1,0:T(8,128)(2,1)S(1)}, bf16[4,128,512]{2,1,0:T(8,128)(2,1)S(1)}, u32[]{:S(2)}, u32[]{:S(2)}) collective-permute-start(bf16[4,128,512]{2,1,0:T(8,128)(2,1)S(1)} %all_gather.9.late.refs_2_), channel_id=1, source_target_pairs={{0,1},{1,0},{2,3},{3,2},{4,5},{5,4},{6,7},{7,6},{8,9},{9,8},{10,11... | collective-permute-start | bytes 1572872 | tf_op jit(solution)/shard_map/swap_group_panel/ppermute | solution.py:524
  60.1 31.2 %collective-permute-start.19 = (bf16[512,512]{1,0:T(8,128)(2,1)S(1)}, bf16[512,512]{1,0:T(8,128)(2,1)}, u32[]{:S(2)}, u32[]{:S(2)}) collective-permute-start(bf16[512,512]{1,0:T(8,128)(2,1)S(1)} %stack.4.refs_0_), channel_id=1, source_target_pairs={{0,1},{1,0},{2,3},{3,2},{4,5},{5,4},{6,7},{7,6},{8,9},{9,8},{10,11... | collective-permute-start | bytes 1572872 | tf_op jit(solution)/shard_map/swap_group_panel/ppermute | solution.py:524
  61.7 6.4 %collective-permute-start.7 = (bf16[256,256]{1,0:T(8,128)(2,1)S(1)}, bf16[256,256]{1,0:T(8,128)(2,1)S(1)}, u32[]{:S(2)}, u32[]{:S(2)}) collective-permute-start(bf16[256,256]{1,0:T(8,128)(2,1)S(1)} %get-tuple-element.40), channel_id=1, source_target_pairs={{0,8},{8,0},{16,24},{24,16},{1,9},{9,1},{17,25},{25,17},{2,10},{10... | collective-permute-start | bytes 393224 | tf_op jit(solution)/shard_map/sum_over_leaf/ppermute | solution.py:524
  62.2 8.0 %collective-permute-start.8 = (bf16[256,256]{1,0:T(8,128)(2,1)S(1)}, bf16[256,256]{1,0:T(8,128)(2,1)S(1)}, u32[]{:S(2)}, u32[]{:S(2)}) collective-permute-start(bf16[256,256]{1,0:T(8,128)(2,1)S(1)} %get-tuple-element.41), channel_id=1, source_target_pairs={{0,16},{8,24},{16,0},{24,8},{1,17},{9,25},{17,1},{25,9},{2,18},{10... | collective-permute-start | bytes 393224 | tf_op jit(solution)/shard_map/sum_over_leaf/ppermute | solution.py:524
  62.7 7.5 %collective-permute-start.9 = (bf16[256,256]{1,0:T(8,128)(2,1)S(1)}, bf16[256,256]{1,0:T(8,128)(2,1)S(1)}, u32[]{:S(2)}, u32[]{:S(2)}) collective-permute-start(bf16[256,256]{1,0:T(8,128)(2,1)S(1)} %get-tuple-element.42), channel_id=1, source_target_pairs={{0,24},{8,16},{16,8},{24,0},{1,25},{9,17},{17,9},{25,1},{2,26},{10... | collective-permute-start | bytes 393224 | tf_op jit(solution)/shard_map/sum_over_leaf/ppermute | solution.py:524
  70.3 5.4 %collective-permute-start.10 = (bf16[128,256]{1,0:T(8,128)(2,1)S(1)}, bf16[128,256]{1,0:T(8,128)(2,1)S(1)}, u32[]{:S(2)}, u32[]{:S(2)}) collective-permute-start(bf16[128,256]{1,0:T(8,128)(2,1)S(1)} %get-tuple-element.45), channel_id=1, source_target_pairs={{0,2},{1,3},{2,0},{3,1},{4,6},{5,7},{6,4},{7,5},{8,10},{9,11},{10,... | collective-permute-start | bytes 196616 | tf_op jit(solution)/shard_map/sum_over_pos/ppermute | solution.py:524
  71.6 6.6 %collective-permute-start.11 = (bf16[128,256]{1,0:T(8,128)(2,1)S(1)}, bf16[128,256]{1,0:T(8,128)(2,1)S(1)}, u32[]{:S(2)}, u32[]{:S(2)}) collective-permute-start(bf16[128,256]{1,0:T(8,128)(2,1)S(1)} %get-tuple-element.46), channel_id=1, source_target_pairs={{0,4},{1,5},{2,6},{3,7},{4,0},{5,1},{6,2},{7,3},{8,12},{9,13},{10,... | collective-permute-start | bytes 196616 | tf_op jit(solution)/shard_map/sum_over_pos/ppermute | solution.py:524
  74.1 6.1 %collective-permute-start.12 = (bf16[128,256]{1,0:T(8,128)(2,1)S(1)}, bf16[128,256]{1,0:T(8,128)(2,1)S(1)}, u32[]{:S(2)}, u32[]{:S(2)}) collective-permute-start(bf16[128,256]{1,0:T(8,128)(2,1)S(1)} %get-tuple-element.47), channel_id=1, source_target_pairs={{0,6},{1,7},{2,4},{3,5},{4,2},{5,3},{6,0},{7,1},{8,14},{9,15},{10,... | collective-permute-start | bytes 196616 | tf_op jit(solution)/shard_map/sum_over_pos/ppermute | solution.py:524
  80.3 6.3 %collective-permute-start.15 = (bf16[128,256]{1,0:T(8,128)(2,1)S(1)}, bf16[128,256]{1,0:T(8,128)(2,1)S(1)}, u32[]{:S(2)}, u32[]{:S(2)}) collective-permute-start(bf16[128,256]{1,0:T(8,128)(2,1)S(1)} %sum_pos.1.refs_0_), channel_id=1, source_target_pairs={{0,6},{1,7},{2,4},{3,5},{4,2},{5,3},{6,0},{7,1},{8,14},{9,15},{10,... | collective-permute-start | bytes 196616 | tf_op jit(solution)/shard_map/gather_pos/ppermute | solution.py:524
  81.2 6.6 %collective-permute-start.14 = (bf16[128,256]{1,0:T(8,128)(2,1)S(1)}, bf16[128,256]{1,0:T(8,128)(2,1)S(1)}, u32[]{:S(2)}, u32[]{:S(2)}) collective-permute-start(bf16[128,256]{1,0:T(8,128)(2,1)S(1)} %sum_pos.1.refs_0_), channel_id=1, source_target_pairs={{0,4},{1,5},{2,6},{3,7},{4,0},{5,1},{6,2},{7,3},{8,12},{9,13},{10,... | collective-permute-start | bytes 196616 | tf_op jit(solution)/shard_map/gather_pos/ppermute | solution.py:524
  81.7 6.0 %collective-permute-start.13 = (bf16[128,256]{1,0:T(8,128)(2,1)S(1)}, bf16[128,256]{1,0:T(8,128)(2,1)S(1)}, u32[]{:S(2)}, u32[]{:S(2)}) collective-permute-start(bf16[128,256]{1,0:T(8,128)(2,1)S(1)} %sum_pos.1.refs_0_), channel_id=1, source_target_pairs={{0,2},{1,3},{2,0},{3,1},{4,6},{5,7},{6,4},{7,5},{8,10},{9,11},{10,... | collective-permute-start | bytes 196616 | tf_op jit(solution)/shard_map/gather_pos/ppermute | solution.py:524
  87.8 6.0 %collective-permute-start.18 = (bf16[256,256]{1,0:T(8,128)(2,1)S(1)}, bf16[256,256]{1,0:T(8,128)(2,1)S(1)}, u32[]{:S(2)}, u32[]{:S(2)}) collective-permute-start(bf16[256,256]{1,0:T(8,128)(2,1)S(1)} %get-tuple-element.49.refs_0_), channel_id=1, source_target_pairs={{0,24},{8,16},{16,8},{24,0},{1,25},{9,17},{17,9},{25,1},{2,26},{10... | collective-permute-start | bytes 393224 | tf_op jit(solution)/shard_map/gather_leaf/ppermute | solution.py:524
  89.3 5.9 %collective-permute-start.17 = (bf16[256,256]{1,0:T(8,128)(2,1)S(1)}, bf16[256,256]{1,0:T(8,128)(2,1)S(1)}, u32[]{:S(2)}, u32[]{:S(2)}) collective-permute-start(bf16[256,256]{1,0:T(8,128)(2,1)S(1)} %get-tuple-element.49.refs_0_), channel_id=1, source_target_pairs={{0,16},{8,24},{16,0},{24,8},{1,17},{9,25},{17,1},{25,9},{2,18},{10... | collective-permute-start | bytes 393224 | tf_op jit(solution)/shard_map/gather_leaf/ppermute | solution.py:524
  89.7 5.4 %collective-permute-start.16 = (bf16[256,256]{1,0:T(8,128)(2,1)S(1)}, bf16[256,256]{1,0:T(8,128)(2,1)S(1)}, u32[]{:S(2)}, u32[]{:S(2)}) collective-permute-start(bf16[256,256]{1,0:T(8,128)(2,1)S(1)} %get-tuple-element.49.refs_0_), channel_id=1, source_target_pairs={{0,8},{8,0},{16,24},{24,16},{1,9},{9,1},{17,25},{25,17},{2,10},{10... | collective-permute-start | bytes 393224 | tf_op jit(solution)/shard_map/gather_leaf/ppermute | solution.py:524
  95.2 2.2 %collective-permute-start.21 = (bf16[1280,256]{1,0:T(8,128)(2,1)S(1)}, bf16[1280,256]{1,0:T(8,128)(2,1)S(1)}, u32[]{:S(2)}, u32[]{:S(2)}) collective-permute-start(bf16[1280,256]{1,0:T(8,128)(2,1)S(1)} %stack.5.mine), channel_id=1, source_target_pairs={{0,1},{1,0},{2,3},{3,2},{4,5},{5,4},{6,7},{7,6},{8,9},{9,8},{10,11... | collective-permute-start | bytes 1966088 | tf_op jit(solution)/shard_map/gather_cores/ppermute | solution.py:524
  (5 other events, 54.5 us)
Sparse Core Ops, SparseCore 0:
  18.8 34.2 all-gather.2

commit v5 on v3

v5 whole, which is shorter than its diff:
```python
import functools

import jax
import jax.numpy as jnp
from jax import lax
from jax.experimental import pallas as pl
from jax.experimental.pallas import tpu as pltpu
from jax.sharding import PartitionSpec as P

BF = jnp.bfloat16
F32 = jnp.float32
MIB = 1024 * 1024
CHUNKS = 16
UNROLL = 4
HBM = pl.BlockSpec(memory_space=pltpu.HBM)
VMEM = pl.BlockSpec(memory_space=pltpu.VMEM)
BIG = 32 * MIB
SMALL = 4 * MIB


def in_hbm(*arrays):
    return [pltpu.with_memory_space_constraint(x, pltpu.HBM) for x in arrays]


def in_vmem(*arrays):
    return [pltpu.with_memory_space_constraint(x, pltpu.VMEM) for x in arrays]


def small(kernel, name, shapes, scratch, *args):
    return pl.pallas_call(
        kernel,
        out_shape=[pltpu.VMEM(shape, BF) for shape in shapes],
        in_specs=[VMEM] * len(args),
        out_specs=[VMEM] * len(shapes),
        scratch_shapes=scratch,
        compiler_params=pltpu.CompilerParams(vmem_limit_bytes=SMALL),
        name=name,
    )(*in_vmem(*args))


def dot(a, b):
    return jnp.dot(a, b, preferred_element_type=F32)


def place():
    g = lax.axis_index("grp")
    return lax.axis_index("leaf"), g >> 1, g & 1


def forward_kernel(
    sec,
    group_cols,
    count_hbm,
    cols_hbm,
    tgts_hbm,
    rhs_hbm,
    inv_hbm,
    tiles_hbm,
    keep,
    send,
    solved,
    dense,
    count,
    cols,
    tgts,
    rhs,
    inv,
    tiles,
    acc,
    stage,
    in_sems,
    tile_sems,
):
    slots, block, _ = tiles.shape
    supernodes = inv.shape[0]
    targets = acc.shape[0]
    chunks = tile_sems.shape[0]
    step = slots // chunks
    _, _, core = place()

    def tile_copy(k):
        span = pl.ds(k * step, step)
        return pltpu.make_async_copy(tiles_hbm.at[span], tiles.at[span], tile_sems.at[k])

    pairs = (
        (count_hbm, count),
        (cols_hbm, cols),
        (tgts_hbm, tgts),
        (rhs_hbm, rhs),
        (inv_hbm, inv),
    )
    loads = [pltpu.make_async_copy(a, b, in_sems.at[i]) for i, (a, b) in enumerate(pairs)]
    for load in loads:
        load.start()
    for k in range(chunks):
        tile_copy(k).start()

    acc[...] = jnp.zeros_like(acc)
    for load in loads:
        load.wait()
    for s in range(supernodes):
        rows = pl.ds(s * block, block)
        solved[rows, :] = dot(inv[s], rhs[rows, :].astype(BF)).astype(BF)

    live = count[0, 0]

    def add(p):
        t = tgts[0, p]
        c = cols[0, p]
        acc[t, c] = acc[t, c] + tiles[p].astype(F32)

    def add_some(i, carry):
        for u in range(UNROLL):
            add(i * UNROLL + u)
        return carry

    def add_one(p, carry):
        add(p)
        return carry

    whole = live // UNROLL
    per = step // UNROLL
    for k in range(chunks):
        tile_copy(k).wait()
        lax.fori_loop(k * per, jnp.clip(whole, k * per, (k + 1) * per), add_some, 0)
    lax.fori_loop(whole * UNROLL, live, add_one, 0)

    span = group_cols
    blocks = span // block
    for i in range(targets // blocks):
        for t in range(i * blocks, (i + 1) * blocks):
            for c in range(supernodes):
                dense[t * block : (t + 1) * block, c * block : (c + 1) * block] = acc[t, c].astype(BF)
        total = dot(dense[i * span : (i + 1) * span, :], solved[...]).astype(BF)
        if i == 0:
            for c in range(2):
                stage[c ^ core, 0 : span // 2, :] = total[c * span // 2 : (c + 1) * span // 2, :]
        else:
            for q in range(0, span, sec):
                section = ((i - 1) * span + q) // sec
                begin = group_cols // 2 + (section // 2) * sec
                stage[(section % 2) ^ core, begin : begin + sec, :] = total[q : q + sec, :]
    keep[...] = stage[0]
    send[...] = stage[1]


def leaf_forward(rhs, inverse, tiles, cols, tgts, count, sec, group_cols, upper_cols):
    slots, block, _ = tiles.shape
    supernodes = inverse.shape[0]
    targets = (group_cols + upper_cols) // block
    width = rhs.shape[-1]
    half = (group_cols + upper_cols) // 2
    return pl.pallas_call(
        functools.partial(forward_kernel, sec, group_cols),
        out_shape=(
            pltpu.VMEM((half, width), BF),
            pltpu.VMEM((half, width), BF),
            pltpu.VMEM((supernodes * block, width), BF),
            pltpu.VMEM((targets * block, supernodes * block), BF),
        ),
        in_specs=[HBM] * 6,
        out_specs=(VMEM,) * 4,
        scratch_shapes=[
            pltpu.SMEM(count.shape, count.dtype),
            pltpu.SMEM(cols.shape, cols.dtype),
            pltpu.SMEM(tgts.shape, tgts.dtype),
            pltpu.VMEM(rhs.shape, rhs.dtype),
            pltpu.VMEM(inverse.shape, inverse.dtype),
            pltpu.VMEM((slots, block, block), BF),
            pltpu.VMEM((targets, supernodes, block, block), F32),
            pltpu.VMEM((2, half, width), BF),
            pltpu.SemaphoreType.DMA((5,)),
            pltpu.SemaphoreType.DMA((CHUNKS,)),
        ],
        compiler_params=pltpu.CompilerParams(vmem_limit_bytes=BIG),
        cost_estimate=pl.CostEstimate(
            flops=2 * targets * block * supernodes * block * width,
            bytes_accessed=2 * tiles.size + 4 * rhs.size,
            transcendentals=0,
        ),
        name="leaf_forward",
    )(count, *in_hbm(cols, tgts, rhs, inverse, tiles))


def total_of(refs):
    total = refs[0][...].astype(F32)
    for ref in refs[1:]:
        total = total + ref[...].astype(F32)
    return total


def pair_sum_kernel(n_leaf, n_pos, keep, recv, *refs):
    groups, parts = refs[:n_pos], refs[n_pos:]
    leaf, pos, _ = place()
    gq = groups[0].shape[0]
    q = parts[0].shape[0] // n_pos

    def both(begin, rows):
        span = pl.ds(pl.multiple_of(begin, rows), rows)
        return (keep[span, :].astype(F32) + recv[span, :].astype(F32)).astype(BF)

    for k in range(n_pos):
        p = pos ^ k
        groups[k][...] = both(p * gq, gq)
        for j in range(n_leaf):
            begin = n_pos * gq + (p * n_leaf + (leaf ^ j)) * q
            parts[j][k * q : (k + 1) * q, :] = both(begin, q)


def pair_sum(keep, recv, n_leaf, n_pos, gq, q):
    width = keep.shape[-1]
    shapes = [(gq, width)] * n_pos + [(n_pos * q, width)] * n_leaf
    kernel = functools.partial(pair_sum_kernel, n_leaf, n_pos)
    outs = small(kernel, "pair_sum", shapes, [], keep, recv)
    return list(outs[:n_pos]), list(outs[n_pos:])


def residual_kernel(rhs, *refs):
    refs[-1][...] = (rhs[...] - total_of(refs[:-1])).astype(BF)


def residual_of(rhs, parts):
    return small(residual_kernel, "residual", [rhs.shape], [], rhs, *parts)[0]


def group_kernel(n_leaf, n_pos, mine, theirs, inv, panel, *refs):
    solved, outs, residual = refs[0], refs[1:-1], refs[-1]
    leaf, pos, core = place()
    rows = inv.shape[0] // (2 * n_pos)
    for kc, got in enumerate((mine, theirs)):
        for k in range(n_pos):
            begin = ((core ^ kc) * n_pos + (pos ^ k)) * rows
            span = pl.ds(pl.multiple_of(begin, rows), rows)
            residual[span, :] = got[k * rows : (k + 1) * rows, :]
    solved[...] = dot(inv[...], residual[...]).astype(BF)
    q = panel.shape[0] // n_leaf
    for j in range(n_leaf):
        span = pl.ds(pl.multiple_of((leaf ^ j) * q, q), q)
        outs[j][...] = dot(panel[span, :], solved[...]).astype(BF)


def group_forward(mine, theirs, inverse, panel, n_leaf, n_pos):
    width = mine.shape[-1]
    shape = (inverse.shape[0], width)
    outs = small(
        functools.partial(group_kernel, n_leaf, n_pos),
        "group_forward",
        [shape] + [(panel.shape[0] // n_leaf, width)] * n_leaf,
        [pltpu.VMEM(shape, BF)],
        mine,
        theirs,
        inverse,
        panel,
    )
    return outs[0], list(outs[1:])


def sum_leaf_kernel(n_leaf, *refs):
    total = total_of(refs[:n_leaf]).astype(BF)
    for k, out in enumerate(refs[n_leaf:]):
        q = out.shape[0]
        out[...] = total[k * q : (k + 1) * q, :]


def sum_leaf(parts, n_pos):
    rows, width = parts[0].shape
    kernel = functools.partial(sum_leaf_kernel, len(parts))
    return list(small(kernel, "sum_leaf", [(rows // n_pos, width)] * n_pos, [], *parts))


def stack_kernel(*refs):
    begin = 0
    for part in refs[:-1]:
        rows = part.shape[0]
        refs[-1][begin : begin + rows, :] = part[...]
        begin += rows


def stack(parts):
    rows = sum(part.shape[0] for part in parts)
    return small(stack_kernel, "stack", [(rows, parts[0].shape[1])], [], *parts)[0]


def weave_kernel(n_leaf, n_pos, own, other, out):
    leaf, pos, core = place()
    rows = own.shape[0] // (n_leaf * n_pos)
    for kc, part in enumerate((own, other)):
        for kl in range(n_leaf):
            for k in range(n_pos):
                block = (leaf ^ kl) * (2 * n_pos) + 2 * (pos ^ k) + (core ^ kc)
                span = pl.ds(pl.multiple_of(block * rows, rows), rows)
                begin = (kl * n_pos + k) * rows
                out[span, :] = part[begin : begin + rows, :]


def weave(own, other, n_leaf, n_pos):
    shape = (2 * own.shape[0], own.shape[1])
    kernel = functools.partial(weave_kernel, n_leaf, n_pos)
    return small(kernel, "weave", [shape], [], own, other)[0]


def backward_kernel(
    n_leaf,
    n_pos,
    mine,
    theirs,
    group_solved_ref,
    leaf_solved,
    dense,
    inv_mid,
    panel_mid,
    inv_top_hbm,
    inv_group_hbm,
    panel_group_hbm,
    inv_leaf_hbm,
    leaf_hbm,
    group_hbm,
    mid_hbm,
    top_hbm,
    inv_top,
    inv_group,
    panel_group,
    inv_leaf,
    leaf_out,
    group_out,
    mid_out,
    top_out,
    upper,
    above,
    sems,
    out_sems,
):
    leaf, pos, core = place()
    pairs = (
        (inv_top_hbm, inv_top),
        (inv_group_hbm, inv_group),
        (panel_group_hbm, panel_group),
        (inv_leaf_hbm, inv_leaf),
    )
    loads = [pltpu.make_async_copy(a, b, sems.at[i]) for i, (a, b) in enumerate(pairs)]
    for load in loads:
        load.start()
    mid_rows = inv_mid.shape[0]
    top_rows = inv_top.shape[0]
    group_rows = inv_group.shape[0]
    supernodes, block, _ = inv_leaf.shape
    upper_cols = pl.ds(group_rows, mid_rows + top_rows)
    mid_cols = pl.ds(group_rows, mid_rows)
    top_cols = pl.ds(group_rows + mid_rows, top_rows)
    sec = (mid_rows + top_rows) // (2 * n_pos)
    q = sec // n_leaf
    for kc, got in enumerate((mine, theirs)):
        for kz in range(n_pos):
            for kl in range(n_leaf):
                row = sec * (2 * (pos ^ kz) + (core ^ kc)) + q * (leaf ^ kl)
                begin = (kl * n_pos + kz) * q
                upper[pl.ds(pl.multiple_of(row, q), q), :] = got[begin : begin + q, :]

    mid_solved = dot(inv_mid[...], upper[0:mid_rows, :]).astype(BF)
    top_residual = upper[mid_rows:, :].astype(F32) - dot(panel_mid[...], mid_solved)
    loads[0].wait()
    top_solved = dot(inv_top[...], top_residual.astype(BF))
    top_t = dot(top_solved.T.astype(BF), inv_top[...])
    above[:, top_cols] = top_t.astype(BF)
    top_out[...] = top_t.T
    stores = [pltpu.make_async_copy(top_out, top_hbm, out_sems.at[0])]
    stores[0].start()
    mid_back = mid_solved.astype(F32).T - dot(above[:, top_cols], panel_mid[...])
    mid_t = dot(mid_back.astype(BF), inv_mid[...])
    above[:, mid_cols] = mid_t.astype(BF)
    mid_out[...] = mid_t.T
    stores.append(pltpu.make_async_copy(mid_out, mid_hbm, out_sems.at[1]))
    stores[1].start()
    for load in loads[1:]:
        load.wait()
    group_solved = group_solved_ref[...].astype(F32).T
    group_back = group_solved - dot(above[:, upper_cols], panel_group[...])
    group_t = dot(group_back.astype(BF), inv_group[...])
    above[:, 0:group_rows] = group_t.astype(BF)
    group_out[...] = group_t.T
    stores.append(pltpu.make_async_copy(group_out, group_hbm, out_sems.at[2]))
    stores[2].start()
    for s in range(supernodes):
        cols = pl.ds(s * block, block)
        terms = dot(above[...], dense[:, cols])
        back = (leaf_solved[cols, :].astype(F32).T - terms).astype(BF)
        leaf_out[cols, :] = dot(back, inv_leaf[s]).T
    stores.append(pltpu.make_async_copy(leaf_out, leaf_hbm, out_sems.at[3]))
    stores[3].start()
    for store in stores:
        store.wait()


def backward(close, far, n_leaf, n_pos):
    mine, _, group_solved, leaf_solved, dense, inv_mid, panel_mid = close
    inv_top, inv_group, _, _ = far
    width = mine.shape[-1]
    outs = (
        leaf_solved.shape,
        group_solved.shape,
        (inv_mid.shape[0], width),
        (inv_top.shape[0], width),
    )
    return pl.pallas_call(
        functools.partial(backward_kernel, n_leaf, n_pos),
        out_shape=[pltpu.HBM(shape, F32) for shape in outs],
        in_specs=[VMEM] * len(close) + [HBM] * len(far),
        out_specs=[HBM] * 4,
        scratch_shapes=[pltpu.VMEM(x.shape, x.dtype) for x in far]
        + [pltpu.VMEM(shape, F32) for shape in outs]
        + [
            pltpu.VMEM((inv_mid.shape[0] + inv_top.shape[0], width), BF),
            pltpu.VMEM((width, dense.shape[0]), BF),
            pltpu.SemaphoreType.DMA((len(far),)),
            pltpu.SemaphoreType.DMA((len(outs),)),
        ],
        compiler_params=pltpu.CompilerParams(vmem_limit_bytes=BIG),
        name="backward",
    )(*in_vmem(*close), *in_hbm(*far))


def swap(x, axis, size, bits):
    return lax.ppermute(x, axis, [(i, i ^ bits) for i in range(size)])


def swaps(x, axis, size, unit=1):
    return [x] + [swap(x, axis, size, unit * k) for k in range(1, size // unit)]


def after(x, *others):
    return lax.optimization_barrier((x, others))[0]


def body(
    n_leaf,
    n_grp,
    rhs_leaf,
    rhs_group,
    rhs_middle,
    rhs_top,
    inv_leaf,
    inv_group,
    inv_middle,
    inv_top,
    leaf_tiles,
    tile_column,
    tile_target,
    tile_count,
    group_panel,
    middle_panel,
):
    n_pos = n_grp // 2
    group_cols = rhs_group.shape[1]
    mid_cols = rhs_middle.shape[0]
    upper_cols = mid_cols + rhs_top.shape[0]
    sec = upper_cols // n_grp
    q = sec // n_leaf
    gq = group_cols // n_grp
    leaf, pos, core = place()
    by_parts = middle_panel.shape[0] % 16 == 0
    with jax.named_scope("gather_group_panel"):
        panel = lax.all_gather(group_panel[0], "grp", axis=0, tiled=True)
    with jax.named_scope("gather_middle_panel"):
        if by_parts:
            middles = swaps(middle_panel, "grp", n_grp, 2)
        else:
            middle = lax.all_gather(middle_panel, ("leaf", "grp"), axis=0, tiled=True)
    keep, send, leaf_solved, dense = leaf_forward(
        rhs_leaf[0],
        inv_leaf[0],
        leaf_tiles[0],
        tile_column,
        tile_target,
        tile_count,
        sec,
        group_cols,
        upper_cols,
    )
    with jax.named_scope("swap_cores"):
        if by_parts:
            send = after(send, middles)
        recv = swap(send, "grp", n_grp, 1)
    groups, parts = pair_sum(keep, recv, n_leaf, n_pos, gq, q)
    with jax.named_scope("sum_group_over_pos"):
        groups = groups[:1] + [swap(groups[k], "grp", n_grp, 2 * k) for k in range(1, n_pos)]
    with jax.named_scope("sum_upper_over_leaf"):
        parts = parts[:1] + [swap(parts[k], "leaf", n_leaf, k) for k in range(1, n_leaf)]
    group_begin = (group_cols // 2) * core + gq * pos
    group_rhs = lax.dynamic_slice_in_dim(rhs_group[0], group_begin, gq, 0)
    residual = residual_of(group_rhs, after(groups, parts))
    with jax.named_scope("sum_upper_over_pos"):
        uppers = sum_leaf(parts, n_pos)
        uppers = uppers[:1] + [swap(uppers[k], "grp", n_grp, 2 * k) for k in range(1, n_pos)]
    with jax.named_scope("gather_group"):
        mine = stack(after(swaps(residual, "grp", n_grp, 2), uppers))
        theirs = swap(mine, "grp", n_grp, 1)
    group_solved, terms = group_forward(mine, theirs, inv_group[0], group_panel[0], n_leaf, n_pos)
    with jax.named_scope("sum_panel_over_leaf"):
        terms = terms[:1] + [swap(terms[k], "leaf", n_leaf, k) for k in range(1, n_leaf)]
    begin = sec * lax.axis_index("grp") + q * leaf
    low = lax.dynamic_slice_in_dim(rhs_middle, jnp.minimum(begin, mid_cols - q), q, 0)
    high = lax.dynamic_slice_in_dim(rhs_top, jnp.maximum(begin - mid_cols, 0), q, 0)
    rhs_mine = jnp.where(begin < mid_cols, low, high)
    residual = residual_of(rhs_mine, uppers + terms)
    with jax.named_scope("gather_middle_panel"):
        if by_parts:
            middles = swaps(stack(after(middles, terms)), "leaf", n_leaf)
    with jax.named_scope("gather_pos"):
        uppers = stack(swaps(residual, "grp", n_grp, 2))
    with jax.named_scope("gather_middle_panel"):
        if by_parts:
            middle, uppers = after((stack(middles), uppers), (middles, panel))
            middle = weave(middle, swap(middle, "grp", n_grp, 1), n_leaf, n_pos)
    with jax.named_scope("gather_leaf"):
        stacks = swaps(uppers, "leaf", n_leaf)
    with jax.named_scope("gather_cores"):
        mine = stack(after(stacks, middle))
        theirs = swap(mine, "grp", n_grp, 1)
    leaf_out, group_out, mid_out, top_out = backward(
        (mine, theirs, group_solved, leaf_solved, dense, inv_middle, middle),
        (inv_top, inv_group[0], panel, inv_leaf[0]),
        n_leaf,
        n_pos,
    )
    return leaf_out[None], group_out[None], mid_out, top_out


def solution(mesh):
    n_leaf = mesh.shape["leaf"]
    n_grp = mesh.shape["grp"]
    placed = (
        P("leaf", "grp", None),
        P("leaf", None, None),
        P(),
        P(),
        P("leaf", "grp", None, None),
        P("leaf", None, None),
        P(),
        P(),
        P("leaf", "grp", None, None),
        P("leaf", "grp"),
        P("leaf", "grp"),
        P("leaf", "grp"),
        P("leaf", "grp", None),
        P(("leaf", "grp"), None),
    )
    return jax.shard_map(
        functools.partial(body, n_leaf, n_grp),
        mesh=mesh,
        in_specs=placed,
        out_specs=(P("leaf", "grp", None), P("leaf", None, None), P(), P()),
        check_vma=False,
    )
```

time: 162 us -> 112 us (0.69)
  waiting for transfers between devices: 56.5 us -> 31.4 us
  local copies, waits for them, and re-layouts: 25.6 us -> 5.6 us
  Pallas kernels: 30.8 us -> 20.6 us
  starting transfers between devices: 31.9 us -> 37.8 us
    unnamed x74 -> x18, local copies, waits for them, and re-layouts: 25.6 us -> 5.59 us
    all_gather x1, waiting for transfers between devices: 15.4 us -> 0.02 us  [body(): panel = lax.all_gather(group_panel[0], 'grp', axis=0, tiled=True)]
    ppermute x35 -> x31, waiting for transfers between devices: 40.4 us -> 30.7 us  [swap(): return lax.ppermute(x, axis, [(i, i ^ bits) for i in range(size)])]
    pallas_call x10 -> x12, Pallas kernels: 22.2 us -> 13 us  [the longest x1 11.7 us: backward(): pl.pallas_call(functools.partial(backward_kernel, n_leaf, n_pos), out_sha...]
    ppermute x35 -> x31, starting transfers between devices: 31.8 us -> 37.7 us  [swap(): return lax.ppermute(x, axis, [(i, i ^ bits) for i in range(size)])]
  transfers between devices with their start and end apart: 36 -> 32, of which waited for: 15 -> 15; matrix products, arithmetic and copies ran while one was open for 1% -> 1% of each run, Pallas kernels for 9% -> 8%
where the time goes in v5:
time: 112 us; the launch traced here: 111 us
  starting transfers between devices  37.8 us (34%)
  waiting for transfers between devices  31.4 us (28%)
  Pallas kernels  20.6 us (18%)
  between operations  14.9 us (13%)
  local copies, waits for them, and re-layouts  5.6 us (5%)
    ppermute x31, starting transfers between devices, swap(): return lax.ppermute(x, axis, [(i, i ^ bits) for i in range(size)])  37.7 us
    ppermute x31, waiting for transfers between devices, swap(): return lax.ppermute(x, axis, [(i, i ^ bits) for i in range(size)])  30.7 us
    pallas_call x1, Pallas kernels, backward(): pl.pallas_call(functools.partial(backward_kernel, n_leaf, n_pos), out_sha...  11.7 us
    pallas_call x1, Pallas kernels, leaf_forward(): pl.pallas_call(functools.partial(forward_kernel, sec, group_cols), out_sh...  7.58 us
    unnamed x18, local copies, waits for them, and re-layouts  5.59 us
  transfers between devices with their start and end apart: 32, of which 15 were waited for; matrix products, arithmetic and copies ran while one was open for 1% of the time, Pallas kernels for 8%

profile of v5, /device:TPU:0, one launch (start us, length us, event | category | flops | bytes accessed | tf_op | source)
XLA Modules:
  0.0 111.2 jit_solution(15741822915213971101)
XLA Ops:
  7.9 5.1 %collective-permute-start.2 = (bf16[32,1024]{1,0:T(8,128)(2,1)}, bf16[32,1024]{1,0:T(8,128)(2,1)S(1)}, u32[]{:S(2)}, u32[]{:S(2)}) collective-permute-start(bf16[32,1024]{1,0:T(8,128)(2,1)} %refs_0_), channel_id=1, source_target_pairs={{0,6},{1,7},{2,4},{3,5},{4,2},{5,3},{6,0},{7,1},{8,14},{9,15},{10,... | collective-permute-start | bytes 196616 | tf_op jit(solution)/shard_map/gather_middle_panel/ppermute | solution.py:423
  14.3 7.6 %leaf_forward.1 = (bf16[1280,256]{1,0:T(8,128)(2,1)S(1)}, bf16[1280,256]{1,0:T(8,128)(2,1)S(1)}, bf16[1024,256]{1,0:T(8,128)(2,1)S(1)}, bf16[2560,1024]{1,0:T(8,128)(2,1)S(1)}) custom-call(s32[1,1]{1,0:T(1,128)S(6)} %copy.18.count_hbm, s32[1,256]{1,0:T(1,128)} %cols_hbm.1, s32[1,256]{1,0:T(1,128)} %tgts_hbm.1, f32[1024,256]{1,0:T(8,128)} %bitcast.17, ...), custom_call_target="tpu_custom_call" | custom-call | flops 1342177280 | bytes 9437184 | tf_op jit(solution)/shard_map/leaf_forward/pallas_call | solution.py:153
  21.9 2.3 %copy-done.1 = bf16[2560,1024]{1,0:T(8,128)(2,1)} copy-done((bf16[2560,1024]{1,0:T(8,128)(2,1)}, bf16[2560,1024]{1,0:T(8,128)(2,1)S(1)}, u32[]{:S(2)}) %copy-start.1) | copy-done | bytes 5242904
  24.4 2.1 %collective-permute-done.3.recv = bf16[1280,256]{1,0:T(8,128)(2,1)S(1)} collective-permute-done((bf16[1280,256]{1,0:T(8,128)(2,1)S(1)}, bf16[1280,256]{1,0:T(8,128)(2,1)S(1)}, u32[]{:S(2)}, u32[]{:S(2)}) %collective-permute-start.3) | collective-permute-done | bytes 655392 | tf_op jit(solution)/shard_map/swap_cores/ppermute | solution.py:423
  26.6 1.5 %collective-permute-start.4 = (bf16[64,256]{1,0:T(8,128)(2,1)S(1)}, bf16[64,256]{1,0:T(8,128)(2,1)S(1)}, u32[]{:S(2)}, u32[]{:S(2)}) collective-permute-start(bf16[64,256]{1,0:T(8,128)(2,1)S(1)} %get-tuple-element.52), channel_id=1, source_target_pairs={{0,2},{1,3},{2,0},{3,1},{4,6},{5,7},{6,4},{7,5},{8,10},{9,11},{10,... | collective-permute-start | bytes 98312 | tf_op jit(solution)/shard_map/sum_group_over_pos/ppermute | solution.py:423
  30.1 1.5 %collective-permute-start.9 = (bf16[256,256]{1,0:T(8,128)(2,1)S(1)}, bf16[256,256]{1,0:T(8,128)(2,1)S(1)}, u32[]{:S(2)}, u32[]{:S(2)}) collective-permute-start(bf16[256,256]{1,0:T(8,128)(2,1)S(1)} %get-tuple-element.58), channel_id=1, source_target_pairs={{0,24},{8,16},{16,8},{24,0},{1,25},{9,17},{17,9},{25,1},{2,26},{10... | collective-permute-start | bytes 393224 | tf_op jit(solution)/shard_map/sum_upper_over_leaf/ppermute | solution.py:423
  31.6 2.7 %collective-permute-start.5 = (bf16[64,256]{1,0:T(8,128)(2,1)S(1)}, bf16[64,256]{1,0:T(8,128)(2,1)S(1)}, u32[]{:S(2)}, u32[]{:S(2)}) collective-permute-start(bf16[64,256]{1,0:T(8,128)(2,1)S(1)} %get-tuple-element.53), channel_id=1, source_target_pairs={{0,4},{1,5},{2,6},{3,7},{4,0},{5,1},{6,2},{7,3},{8,12},{9,13},{10,... | collective-permute-start | bytes 98312 | tf_op jit(solution)/shard_map/sum_group_over_pos/ppermute | solution.py:423
  34.3 2.6 %collective-permute-start.6 = (bf16[64,256]{1,0:T(8,128)(2,1)S(1)}, bf16[64,256]{1,0:T(8,128)(2,1)S(1)}, u32[]{:S(2)}, u32[]{:S(2)}) collective-permute-start(bf16[64,256]{1,0:T(8,128)(2,1)S(1)} %get-tuple-element.54), channel_id=1, source_target_pairs={{0,6},{1,7},{2,4},{3,5},{4,2},{5,3},{6,0},{7,1},{8,14},{9,15},{10,... | collective-permute-start | bytes 98312 | tf_op jit(solution)/shard_map/sum_group_over_pos/ppermute | solution.py:423
  36.9 1.8 %collective-permute-done.5.refs_2_ = bf16[64,256]{1,0:T(8,128)(2,1)S(1)} collective-permute-done((bf16[64,256]{1,0:T(8,128)(2,1)S(1)}, bf16[64,256]{1,0:T(8,128)(2,1)S(1)}, u32[]{:S(2)}, u32[]{:S(2)}) %collective-permute-start.5) | collective-permute-done | bytes 32800 | tf_op jit(solution)/shard_map/sum_group_over_pos/ppermute | solution.py:423
  38.7 2.0 %collective-permute-done.6.refs_3_ = bf16[64,256]{1,0:T(8,128)(2,1)S(1)} collective-permute-done((bf16[64,256]{1,0:T(8,128)(2,1)S(1)}, bf16[64,256]{1,0:T(8,128)(2,1)S(1)}, u32[]{:S(2)}, u32[]{:S(2)}) %collective-permute-start.6) | collective-permute-done | bytes 32800 | tf_op jit(solution)/shard_map/sum_group_over_pos/ppermute | solution.py:423
  40.8 2.6 %collective-permute-start.12 = (bf16[64,256]{1,0:T(8,128)(2,1)S(1)}, bf16[64,256]{1,0:T(8,128)(2,1)S(1)}, u32[]{:S(2)}, u32[]{:S(2)}) collective-permute-start(bf16[64,256]{1,0:T(8,128)(2,1)S(1)} %residual.2.refs_0_), channel_id=1, source_target_pairs={{0,6},{1,7},{2,4},{3,5},{4,2},{5,3},{6,0},{7,1},{8,14},{9,15},{10,... | collective-permute-start | bytes 98312 | tf_op jit(solution)/shard_map/gather_group/ppermute | solution.py:423
  45.9 2.5 %collective-permute-start.14 = (bf16[64,256]{1,0:T(8,128)(2,1)S(1)}, bf16[64,256]{1,0:T(8,128)(2,1)S(1)}, u32[]{:S(2)}, u32[]{:S(2)}) collective-permute-start(bf16[64,256]{1,0:T(8,128)(2,1)S(1)} %get-tuple-element.65), channel_id=1, source_target_pairs={{0,4},{1,5},{2,6},{3,7},{4,0},{5,1},{6,2},{7,3},{8,12},{9,13},{10,... | collective-permute-start | bytes 98312 | tf_op jit(solution)/shard_map/sum_upper_over_pos/ppermute | solution.py:423
  50.8 3.4 %collective-permute-done.15.refs_3_ = bf16[64,256]{1,0:T(8,128)(2,1)S(1)} collective-permute-done((bf16[64,256]{1,0:T(8,128)(2,1)S(1)}, bf16[64,256]{1,0:T(8,128)(2,1)S(1)}, u32[]{:S(2)}, u32[]{:S(2)}) %collective-permute-start.15) | collective-permute-done | bytes 32800 | tf_op jit(solution)/shard_map/sum_upper_over_pos/ppermute | solution.py:423
  61.4 1.9 %collective-permute-done.19.refs_7_ = bf16[64,256]{1,0:T(8,128)(2,1)S(1)} collective-permute-done((bf16[64,256]{1,0:T(8,128)(2,1)S(1)}, bf16[64,256]{1,0:T(8,128)(2,1)S(1)}, u32[]{:S(2)}, u32[]{:S(2)}) %collective-permute-start.19) | collective-permute-done | bytes 32800 | tf_op jit(solution)/shard_map/sum_panel_over_leaf/ppermute | solution.py:423
  63.3 1.6 %collective-permute-start.22 = (bf16[128,1024]{1,0:T(8,128)(2,1)S(1)}, bf16[128,1024]{1,0:T(8,128)(2,1)S(1)}, u32[]{:S(2)}, u32[]{:S(2)}) collective-permute-start(bf16[128,1024]{1,0:T(8,128)(2,1)S(1)} %stack.6.refs_0_), channel_id=1, source_target_pairs={{0,24},{8,16},{16,8},{24,0},{1,25},{9,17},{17,9},{25,1},{2,26},{10... | collective-permute-start | bytes 786440 | tf_op jit(solution)/shard_map/gather_middle_panel/ppermute | solution.py:423
  67.9 1.8 %collective-permute-start.25 = (bf16[64,256]{1,0:T(8,128)(2,1)S(1)}, bf16[64,256]{1,0:T(8,128)(2,1)S(1)}, u32[]{:S(2)}, u32[]{:S(2)}) collective-permute-start(bf16[64,256]{1,0:T(8,128)(2,1)S(1)} %residual.3.refs_0_), channel_id=1, source_target_pairs={{0,6},{1,7},{2,4},{3,5},{4,2},{5,3},{6,0},{7,1},{8,14},{9,15},{10,... | collective-permute-start | bytes 98312 | tf_op jit(solution)/shard_map/gather_pos/ppermute | solution.py:423
  69.7 4.0 %collective-permute-done.25.refs_3_ = bf16[64,256]{1,0:T(8,128)(2,1)S(1)} collective-permute-done((bf16[64,256]{1,0:T(8,128)(2,1)S(1)}, bf16[64,256]{1,0:T(8,128)(2,1)S(1)}, u32[]{:S(2)}, u32[]{:S(2)}) %collective-permute-start.25) | collective-permute-done | bytes 32800 | tf_op jit(solution)/shard_map/gather_pos/ppermute | solution.py:423
  74.5 3.1 %collective-permute-done.23.refs_1_ = bf16[64,256]{1,0:T(8,128)(2,1)S(1)} collective-permute-done((bf16[64,256]{1,0:T(8,128)(2,1)S(1)}, bf16[64,256]{1,0:T(8,128)(2,1)S(1)}, u32[]{:S(2)}, u32[]{:S(2)}) %collective-permute-start.23) | collective-permute-done | bytes 32800 | tf_op jit(solution)/shard_map/gather_pos/ppermute | solution.py:423
  79.5 1.6 %collective-permute-start.28 = (bf16[256,256]{1,0:T(8,128)(2,1)S(1)}, bf16[256,256]{1,0:T(8,128)(2,1)S(1)}, u32[]{:S(2)}, u32[]{:S(2)}) collective-permute-start(bf16[256,256]{1,0:T(8,128)(2,1)S(1)} %stack.8.refs_0_), channel_id=1, source_target_pairs={{0,24},{8,16},{16,8},{24,0},{1,25},{9,17},{17,9},{25,1},{2,26},{10... | collective-permute-start | bytes 393224 | tf_op jit(solution)/shard_map/gather_leaf/ppermute | solution.py:423
  83.2 3.6 %collective-permute-done.28.refs_3_ = bf16[256,256]{1,0:T(8,128)(2,1)S(1)} collective-permute-done((bf16[256,256]{1,0:T(8,128)(2,1)S(1)}, bf16[256,256]{1,0:T(8,128)(2,1)S(1)}, u32[]{:S(2)}, u32[]{:S(2)}) %collective-permute-start.28) | collective-permute-done | bytes 131104 | tf_op jit(solution)/shard_map/gather_leaf/ppermute | solution.py:423
  86.8 2.3 %collective-permute-done.27.refs_2_ = bf16[256,256]{1,0:T(8,128)(2,1)S(1)} collective-permute-done((bf16[256,256]{1,0:T(8,128)(2,1)S(1)}, bf16[256,256]{1,0:T(8,128)(2,1)S(1)}, u32[]{:S(2)}, u32[]{:S(2)}) %collective-permute-start.27) | collective-permute-done | bytes 131104 | tf_op jit(solution)/shard_map/gather_leaf/ppermute | solution.py:423
  89.2 1.9 %collective-permute-done.30.theirs = bf16[1024,256]{1,0:T(8,128)(2,1)S(1)} collective-permute-done((bf16[1024,256]{1,0:T(8,128)(2,1)S(1)}, bf16[1024,256]{1,0:T(8,128)(2,1)S(1)}, u32[]{:S(2)}, u32[]{:S(2)}) %collective-permute-start.30) | collective-permute-done | bytes 524320 | tf_op jit(solution)/shard_map/gather_cores/ppermute | solution.py:423
  91.1 1.6 %copy-done.4 = bf16[1024,1024]{1,0:T(8,128)(2,1)S(1)} copy-done((bf16[1024,1024]{1,0:T(8,128)(2,1)S(1)}, bf16[1024,1024]{1,0:T(8,128)(2,1)}, u32[]{:S(2)}) %copy-start.4) | copy-done | bytes 2097176
  92.7 11.7 %backward.1 = (f32[1024,256]{1,0:T(8,128)}, f32[512,256]{1,0:T(8,128)}, f32[1024,256]{1,0:T(8,128)}, f32[1024,256]{1,0:T(8,128)}) custom-call(bf16[1024,256]{1,0:T(8,128)(2,1)S(1)} %stack.9.mine, bf16[1024,256]{1,0:T(8,128)(2,1)S(1)} %collective-permute-done.30.theirs, bf16[512,256]{1,0:T(8,128)(2,1)S(1)} %get-tuple-element.85.group_solved_ref, ...), custom_call_target="tpu_custom_call" | custom-call | tf_op jit(solution)/shard_map/backward/pallas_call | solution.py:404
  (74 shorter events, 23.5 us)
Async XLA Ops:
  7.2 72.2 %all-gather.3.cloned.1.call-start = ((), (), s32[]{:S(2)}) async-start(), calls=%async_computation | async-start | bytes 2359296 | tf_op jit(solution)/shard_map/gather_group_panel/all_gather | solution.py:462
  7.9 16.3 %collective-permute-start.2 = (bf16[32,1024]{1,0:T(8,128)(2,1)}, bf16[32,1024]{1,0:T(8,128)(2,1)S(1)}, u32[]{:S(2)}, u32[]{:S(2)}) collective-permute-start(bf16[32,1024]{1,0:T(8,128)(2,1)} %refs_0_), channel_id=1, source_target_pairs={{0,6},{1,7},{2,4},{3,5},{4,2},{5,3},{6,0},{7,1},{8,14},{9,15},{10,... | collective-permute-start | bytes 196616 | tf_op jit(solution)/shard_map/gather_middle_panel/ppermute | solution.py:423
  13.0 11.2 %collective-permute-start.1 = (bf16[32,1024]{1,0:T(8,128)(2,1)}, bf16[32,1024]{1,0:T(8,128)(2,1)S(1)}, u32[]{:S(2)}, u32[]{:S(2)}) collective-permute-start(bf16[32,1024]{1,0:T(8,128)(2,1)} %refs_0_), channel_id=1, source_target_pairs={{0,4},{1,5},{2,6},{3,7},{4,0},{5,1},{6,2},{7,3},{8,12},{9,13},{10,... | collective-permute-start | bytes 196616 | tf_op jit(solution)/shard_map/gather_middle_panel/ppermute | solution.py:423
  13.0 11.2 %collective-permute-start = (bf16[32,1024]{1,0:T(8,128)(2,1)}, bf16[32,1024]{1,0:T(8,128)(2,1)S(1)}, u32[]{:S(2)}, u32[]{:S(2)}) collective-permute-start(bf16[32,1024]{1,0:T(8,128)(2,1)} %refs_0_), channel_id=1, source_target_pairs={{0,2},{1,3},{2,0},{3,1},{4,6},{5,7},{6,4},{7,5},{8,10},{9,11},{10,... | collective-permute-start | bytes 196616 | tf_op jit(solution)/shard_map/gather_middle_panel/ppermute | solution.py:423
  26.6 7.7 %collective-permute-start.4 = (bf16[64,256]{1,0:T(8,128)(2,1)S(1)}, bf16[64,256]{1,0:T(8,128)(2,1)S(1)}, u32[]{:S(2)}, u32[]{:S(2)}) collective-permute-start(bf16[64,256]{1,0:T(8,128)(2,1)S(1)} %get-tuple-element.52), channel_id=1, source_target_pairs={{0,2},{1,3},{2,0},{3,1},{4,6},{5,7},{6,4},{7,5},{8,10},{9,11},{10,... | collective-permute-start | bytes 98312 | tf_op jit(solution)/shard_map/sum_group_over_pos/ppermute | solution.py:423
  28.1 12.6 %collective-permute-start.7 = (bf16[256,256]{1,0:T(8,128)(2,1)S(1)}, bf16[256,256]{1,0:T(8,128)(2,1)S(1)}, u32[]{:S(2)}, u32[]{:S(2)}) collective-permute-start(bf16[256,256]{1,0:T(8,128)(2,1)S(1)} %get-tuple-element.56), channel_id=1, source_target_pairs={{0,8},{8,0},{16,24},{24,16},{1,9},{9,1},{17,25},{25,17},{2,10},{10... | collective-permute-start | bytes 393224 | tf_op jit(solution)/shard_map/sum_upper_over_leaf/ppermute | solution.py:423
  29.0 11.7 %collective-permute-start.8 = (bf16[256,256]{1,0:T(8,128)(2,1)S(1)}, bf16[256,256]{1,0:T(8,128)(2,1)S(1)}, u32[]{:S(2)}, u32[]{:S(2)}) collective-permute-start(bf16[256,256]{1,0:T(8,128)(2,1)S(1)} %get-tuple-element.57), channel_id=1, source_target_pairs={{0,16},{8,24},{16,0},{24,8},{1,17},{9,25},{17,1},{25,9},{2,18},{10... | collective-permute-start | bytes 393224 | tf_op jit(solution)/shard_map/sum_upper_over_leaf/ppermute | solution.py:423
  30.1 10.6 %collective-permute-start.9 = (bf16[256,256]{1,0:T(8,128)(2,1)S(1)}, bf16[256,256]{1,0:T(8,128)(2,1)S(1)}, u32[]{:S(2)}, u32[]{:S(2)}) collective-permute-start(bf16[256,256]{1,0:T(8,128)(2,1)S(1)} %get-tuple-element.58), channel_id=1, source_target_pairs={{0,24},{8,16},{16,8},{24,0},{1,25},{9,17},{17,9},{25,1},{2,26},{10... | collective-permute-start | bytes 393224 | tf_op jit(solution)/shard_map/sum_upper_over_leaf/ppermute | solution.py:423
  31.6 7.1 %collective-permute-start.5 = (bf16[64,256]{1,0:T(8,128)(2,1)S(1)}, bf16[64,256]{1,0:T(8,128)(2,1)S(1)}, u32[]{:S(2)}, u32[]{:S(2)}) collective-permute-start(bf16[64,256]{1,0:T(8,128)(2,1)S(1)} %get-tuple-element.53), channel_id=1, source_target_pairs={{0,4},{1,5},{2,6},{3,7},{4,0},{5,1},{6,2},{7,3},{8,12},{9,13},{10,... | collective-permute-start | bytes 98312 | tf_op jit(solution)/shard_map/sum_group_over_pos/ppermute | solution.py:423
  34.3 6.4 %collective-permute-start.6 = (bf16[64,256]{1,0:T(8,128)(2,1)S(1)}, bf16[64,256]{1,0:T(8,128)(2,1)S(1)}, u32[]{:S(2)}, u32[]{:S(2)}) collective-permute-start(bf16[64,256]{1,0:T(8,128)(2,1)S(1)} %get-tuple-element.54), channel_id=1, source_target_pairs={{0,6},{1,7},{2,4},{3,5},{4,2},{5,3},{6,0},{7,1},{8,14},{9,15},{10,... | collective-permute-start | bytes 98312 | tf_op jit(solution)/shard_map/sum_group_over_pos/ppermute | solution.py:423
  40.8 7.7 %collective-permute-start.12 = (bf16[64,256]{1,0:T(8,128)(2,1)S(1)}, bf16[64,256]{1,0:T(8,128)(2,1)S(1)}, u32[]{:S(2)}, u32[]{:S(2)}) collective-permute-start(bf16[64,256]{1,0:T(8,128)(2,1)S(1)} %residual.2.refs_0_), channel_id=1, source_target_pairs={{0,6},{1,7},{2,4},{3,5},{4,2},{5,3},{6,0},{7,1},{8,14},{9,15},{10,... | collective-permute-start | bytes 98312 | tf_op jit(solution)/shard_map/gather_group/ppermute | solution.py:423
  43.4 6.4 %collective-permute-start.11 = (bf16[64,256]{1,0:T(8,128)(2,1)S(1)}, bf16[64,256]{1,0:T(8,128)(2,1)S(1)}, u32[]{:S(2)}, u32[]{:S(2)}) collective-permute-start(bf16[64,256]{1,0:T(8,128)(2,1)S(1)} %residual.2.refs_0_), channel_id=1, source_target_pairs={{0,4},{1,5},{2,6},{3,7},{4,0},{5,1},{6,2},{7,3},{8,12},{9,13},{10,... | collective-permute-start | bytes 98312 | tf_op jit(solution)/shard_map/gather_group/ppermute | solution.py:423
  43.8 6.0 %collective-permute-start.10 = (bf16[64,256]{1,0:T(8,128)(2,1)S(1)}, bf16[64,256]{1,0:T(8,128)(2,1)S(1)}, u32[]{:S(2)}, u32[]{:S(2)}) collective-permute-start(bf16[64,256]{1,0:T(8,128)(2,1)S(1)} %residual.2.refs_0_), channel_id=1, source_target_pairs={{0,2},{1,3},{2,0},{3,1},{4,6},{5,7},{6,4},{7,5},{8,10},{9,11},{10,... | collective-permute-start | bytes 98312 | tf_op jit(solution)/shard_map/gather_group/ppermute | solution.py:423
  45.9 4.8 %collective-permute-start.14 = (bf16[64,256]{1,0:T(8,128)(2,1)S(1)}, bf16[64,256]{1,0:T(8,128)(2,1)S(1)}, u32[]{:S(2)}, u32[]{:S(2)}) collective-permute-start(bf16[64,256]{1,0:T(8,128)(2,1)S(1)} %get-tuple-element.65), channel_id=1, source_target_pairs={{0,4},{1,5},{2,6},{3,7},{4,0},{5,1},{6,2},{7,3},{8,12},{9,13},{10,... | collective-permute-start | bytes 98312 | tf_op jit(solution)/shard_map/sum_upper_over_pos/ppermute | solution.py:423
  48.5 5.7 %collective-permute-start.15 = (bf16[64,256]{1,0:T(8,128)(2,1)S(1)}, bf16[64,256]{1,0:T(8,128)(2,1)S(1)}, u32[]{:S(2)}, u32[]{:S(2)}) collective-permute-start(bf16[64,256]{1,0:T(8,128)(2,1)S(1)} %get-tuple-element.66), channel_id=1, source_target_pairs={{0,6},{1,7},{2,4},{3,5},{4,2},{5,3},{6,0},{7,1},{8,14},{9,15},{10,... | collective-permute-start | bytes 98312 | tf_op jit(solution)/shard_map/sum_upper_over_pos/ppermute | solution.py:423
  58.5 4.8 %collective-permute-start.19 = (bf16[64,256]{1,0:T(8,128)(2,1)S(1)}, bf16[64,256]{1,0:T(8,128)(2,1)S(1)}, u32[]{:S(2)}, u32[]{:S(2)}) collective-permute-start(bf16[64,256]{1,0:T(8,128)(2,1)S(1)} %get-tuple-element.74), channel_id=1, source_target_pairs={{0,24},{8,16},{16,8},{24,0},{1,25},{9,17},{17,9},{25,1},{2,26},{10... | collective-permute-start | bytes 98312 | tf_op jit(solution)/shard_map/sum_panel_over_leaf/ppermute | solution.py:423
  63.3 14.3 %collective-permute-start.22 = (bf16[128,1024]{1,0:T(8,128)(2,1)S(1)}, bf16[128,1024]{1,0:T(8,128)(2,1)S(1)}, u32[]{:S(2)}, u32[]{:S(2)}) collective-permute-start(bf16[128,1024]{1,0:T(8,128)(2,1)S(1)} %stack.6.refs_0_), channel_id=1, source_target_pairs={{0,24},{8,16},{16,8},{24,0},{1,25},{9,17},{17,9},{25,1},{2,26},{10... | collective-permute-start | bytes 786440 | tf_op jit(solution)/shard_map/gather_middle_panel/ppermute | solution.py:423
  64.9 12.7 %collective-permute-start.21 = (bf16[128,1024]{1,0:T(8,128)(2,1)S(1)}, bf16[128,1024]{1,0:T(8,128)(2,1)S(1)}, u32[]{:S(2)}, u32[]{:S(2)}) collective-permute-start(bf16[128,1024]{1,0:T(8,128)(2,1)S(1)} %stack.6.refs_0_), channel_id=1, source_target_pairs={{0,16},{8,24},{16,0},{24,8},{1,17},{9,25},{17,1},{25,9},{2,18},{10... | collective-permute-start | bytes 786440 | tf_op jit(solution)/shard_map/gather_middle_panel/ppermute | solution.py:423
  65.6 12.0 %collective-permute-start.20 = (bf16[128,1024]{1,0:T(8,128)(2,1)S(1)}, bf16[128,1024]{1,0:T(8,128)(2,1)S(1)}, u32[]{:S(2)}, u32[]{:S(2)}) collective-permute-start(bf16[128,1024]{1,0:T(8,128)(2,1)S(1)} %stack.6.refs_0_), channel_id=1, source_target_pairs={{0,8},{8,0},{16,24},{24,16},{1,9},{9,1},{17,25},{25,17},{2,10},{10... | collective-permute-start | bytes 786440 | tf_op jit(solution)/shard_map/gather_middle_panel/ppermute | solution.py:423
  67.9 5.8 %collective-permute-start.25 = (bf16[64,256]{1,0:T(8,128)(2,1)S(1)}, bf16[64,256]{1,0:T(8,128)(2,1)S(1)}, u32[]{:S(2)}, u32[]{:S(2)}) collective-permute-start(bf16[64,256]{1,0:T(8,128)(2,1)S(1)} %residual.3.refs_0_), channel_id=1, source_target_pairs={{0,6},{1,7},{2,4},{3,5},{4,2},{5,3},{6,0},{7,1},{8,14},{9,15},{10,... | collective-permute-start | bytes 98312 | tf_op jit(solution)/shard_map/gather_pos/ppermute | solution.py:423
  69.7 4.8 %collective-permute-start.24 = (bf16[64,256]{1,0:T(8,128)(2,1)S(1)}, bf16[64,256]{1,0:T(8,128)(2,1)S(1)}, u32[]{:S(2)}, u32[]{:S(2)}) collective-permute-start(bf16[64,256]{1,0:T(8,128)(2,1)S(1)} %residual.3.refs_0_), channel_id=1, source_target_pairs={{0,4},{1,5},{2,6},{3,7},{4,0},{5,1},{6,2},{7,3},{8,12},{9,13},{10,... | collective-permute-start | bytes 98312 | tf_op jit(solution)/shard_map/gather_pos/ppermute | solution.py:423
  79.5 7.3 %collective-permute-start.28 = (bf16[256,256]{1,0:T(8,128)(2,1)S(1)}, bf16[256,256]{1,0:T(8,128)(2,1)S(1)}, u32[]{:S(2)}, u32[]{:S(2)}) collective-permute-start(bf16[256,256]{1,0:T(8,128)(2,1)S(1)} %stack.8.refs_0_), channel_id=1, source_target_pairs={{0,24},{8,16},{16,8},{24,0},{1,25},{9,17},{17,9},{25,1},{2,26},{10... | collective-permute-start | bytes 393224 | tf_op jit(solution)/shard_map/gather_leaf/ppermute | solution.py:423
  81.0 8.1 %collective-permute-start.27 = (bf16[256,256]{1,0:T(8,128)(2,1)S(1)}, bf16[256,256]{1,0:T(8,128)(2,1)S(1)}, u32[]{:S(2)}, u32[]{:S(2)}) collective-permute-start(bf16[256,256]{1,0:T(8,128)(2,1)S(1)} %stack.8.refs_0_), channel_id=1, source_target_pairs={{0,16},{8,24},{16,0},{24,8},{1,17},{9,25},{17,1},{25,9},{2,18},{10... | collective-permute-start | bytes 393224 | tf_op jit(solution)/shard_map/gather_leaf/ppermute | solution.py:423
  81.7 7.4 %collective-permute-start.26 = (bf16[256,256]{1,0:T(8,128)(2,1)S(1)}, bf16[256,256]{1,0:T(8,128)(2,1)S(1)}, u32[]{:S(2)}, u32[]{:S(2)}) collective-permute-start(bf16[256,256]{1,0:T(8,128)(2,1)S(1)} %stack.8.refs_0_), channel_id=1, source_target_pairs={{0,8},{8,0},{16,24},{24,16},{1,9},{9,1},{17,25},{25,17},{2,10},{10... | collective-permute-start | bytes 393224 | tf_op jit(solution)/shard_map/gather_leaf/ppermute | solution.py:423
  (17 other events, 174.3 us)
Sparse Core Ops, SparseCore 0:
  9.6 35.5 all-gather.2

commit v6 on v5

--- a/solution.py
+++ b/solution.py
@@ -14,8 +14,8 @@
 UNROLL = 4
 HBM = pl.BlockSpec(memory_space=pltpu.HBM)
 VMEM = pl.BlockSpec(memory_space=pltpu.VMEM)
-BIG = 32 * MIB
-SMALL = 4 * MIB
+BIG = 40 * MIB
+SMALL = 6 * MIB
 
 
 def in_hbm(*arrays):
@@ -58,8 +58,8 @@
     tiles_hbm,
     keep,
     send,
-    solved,
-    dense,
+    solved_hbm,
+    dense_hbm,
     count,
     cols,
     tgts,
@@ -68,8 +68,11 @@
     tiles,
     acc,
     stage,
+    solved,
+    dense,
     in_sems,
     tile_sems,
+    out_sems,
 ):
     slots, block, _ = tiles.shape
     supernodes = inv.shape[0]
@@ -101,6 +104,8 @@
     for s in range(supernodes):
         rows = pl.ds(s * block, block)
         solved[rows, :] = dot(inv[s], rhs[rows, :].astype(BF)).astype(BF)
+    stores = [pltpu.make_async_copy(solved, solved_hbm, out_sems.at[0])]
+    stores[0].start()
 
     live = count[0, 0]
 
@@ -131,17 +136,22 @@
         for t in range(i * blocks, (i + 1) * blocks):
             for c in range(supernodes):
                 dense[t * block : (t + 1) * block, c * block : (c + 1) * block] = acc[t, c].astype(BF)
-        total = dot(dense[i * span : (i + 1) * span, :], solved[...]).astype(BF)
+        rows = pl.ds(i * span, span)
+        stores.append(pltpu.make_async_copy(dense.at[rows], dense_hbm.at[rows], out_sems.at[1 + i]))
+        stores[-1].start()
+        total = dot(dense[rows, :], solved[...]).astype(BF)
         if i == 0:
-            for c in range(2):
-                stage[c ^ core, 0 : span // 2, :] = total[c * span // 2 : (c + 1) * span // 2, :]
+            stage[0, 0:span, :] = total
+            stage[1, 0:span, :] = total
         else:
             for q in range(0, span, sec):
                 section = ((i - 1) * span + q) // sec
-                begin = group_cols // 2 + (section // 2) * sec
+                begin = group_cols + (section // 2) * sec
                 stage[(section % 2) ^ core, begin : begin + sec, :] = total[q : q + sec, :]
     keep[...] = stage[0]
     send[...] = stage[1]
+    for store in stores:
+        store.wait()
 
 
 def leaf_forward(rhs, inverse, tiles, cols, tgts, count, sec, group_cols, upper_cols):
@@ -149,17 +159,17 @@
     supernodes = inverse.shape[0]
     targets = (group_cols + upper_cols) // block
     width = rhs.shape[-1]
-    half = (group_cols + upper_cols) // 2
+    half = group_cols + upper_cols // 2
     return pl.pallas_call(
         functools.partial(forward_kernel, sec, group_cols),
         out_shape=(
             pltpu.VMEM((half, width), BF),
             pltpu.VMEM((half, width), BF),
-            pltpu.VMEM((supernodes * block, width), BF),
-            pltpu.VMEM((targets * block, supernodes * block), BF),
+            pltpu.HBM((supernodes * block, width), BF),
+            pltpu.HBM((targets * block, supernodes * block), BF),
         ),
         in_specs=[HBM] * 6,
-        out_specs=(VMEM,) * 4,
+        out_specs=(VMEM, VMEM, HBM, HBM),
         scratch_shapes=[
             pltpu.SMEM(count.shape, count.dtype),
             pltpu.SMEM(cols.shape, cols.dtype),
@@ -169,8 +179,11 @@
             pltpu.VMEM((slots, block, block), BF),
             pltpu.VMEM((targets, supernodes, block, block), F32),
             pltpu.VMEM((2, half, width), BF),
+            pltpu.VMEM((supernodes * block, width), BF),
+            pltpu.VMEM((targets * block, supernodes * block), BF),
             pltpu.SemaphoreType.DMA((5,)),
             pltpu.SemaphoreType.DMA((CHUNKS,)),
+            pltpu.SemaphoreType.DMA((1 + targets * block // group_cols,)),
         ],
         compiler_params=pltpu.CompilerParams(vmem_limit_bytes=BIG),
         cost_estimate=pl.CostEstimate(
@@ -189,83 +202,100 @@
     return total
 
 
-def pair_sum_kernel(n_leaf, n_pos, keep, recv, *refs):
-    groups, parts = refs[:n_pos], refs[n_pos:]
-    leaf, pos, _ = place()
-    gq = groups[0].shape[0]
-    q = parts[0].shape[0] // n_pos
-
-    def both(begin, rows):
-        span = pl.ds(pl.multiple_of(begin, rows), rows)
-        return (keep[span, :].astype(F32) + recv[span, :].astype(F32)).astype(BF)
-
+def fold_kernel(n_leaf, n_pos, keep, recv, inv, rhs, panel_hbm, *refs):
+    parts, group, (gsum, stage, panel, sems) = refs[:n_leaf], refs[n_leaf], refs[n_leaf + 1 :]
+    loads = [
+        pltpu.make_async_copy(panel_hbm.at[p], panel.at[p], sems.at[p]) for p in range(n_pos)
+    ]
+    for load in loads:
+        load.start()
+    leaf, pos, core = place()
+    group_cols = inv.shape[0]
+    sec = panel.shape[1]
+    q = sec // n_leaf
+    gq = group_cols // (2 * n_pos)
+    gsum[...] = keep[0:group_cols, :].astype(F32) + recv[0:group_cols, :].astype(F32)
+    residual = rhs[...] * (1.0 / n_pos) - gsum[...]
+    solved = dot(inv[...], residual.astype(BF)).astype(BF)
+    for load in loads:
+        load.wait()
     for k in range(n_pos):
         p = pos ^ k
-        groups[k][...] = both(p * gq, gq)
+        rows = pl.ds(pl.multiple_of(group_cols + p * sec, sec), sec)
+        terms = dot(panel[p], solved)
+        terms = (terms + (keep[rows, :].astype(F32) + recv[rows, :].astype(F32))).astype(BF)
         for j in range(n_leaf):
-            begin = n_pos * gq + (p * n_leaf + (leaf ^ j)) * q
-            parts[j][k * q : (k + 1) * q, :] = both(begin, q)
-
-
-def pair_sum(keep, recv, n_leaf, n_pos, gq, q):
-    width = keep.shape[-1]
-    shapes = [(gq, width)] * n_pos + [(n_pos * q, width)] * n_leaf
-    kernel = functools.partial(pair_sum_kernel, n_leaf, n_pos)
-    outs = small(kernel, "pair_sum", shapes, [], keep, recv)
-    return list(outs[:n_pos]), list(outs[n_pos:])
-
-
-def residual_kernel(rhs, *refs):
-    refs[-1][...] = (rhs[...] - total_of(refs[:-1])).astype(BF)
-
-
-def residual_of(rhs, parts):
-    return small(residual_kernel, "residual", [rhs.shape], [], rhs, *parts)[0]
-
-
-def group_kernel(n_leaf, n_pos, mine, theirs, inv, panel, *refs):
-    solved, outs, residual = refs[0], refs[1:-1], refs[-1]
-    leaf, pos, core = place()
-    rows = inv.shape[0] // (2 * n_pos)
-    for kc, got in enumerate((mine, theirs)):
-        for k in range(n_pos):
-            begin = ((core ^ kc) * n_pos + (pos ^ k)) * rows
-            span = pl.ds(pl.multiple_of(begin, rows), rows)
-            residual[span, :] = got[k * rows : (k + 1) * rows, :]
-    solved[...] = dot(inv[...], residual[...]).astype(BF)
-    q = panel.shape[0] // n_leaf
-    for j in range(n_leaf):
-        span = pl.ds(pl.multiple_of((leaf ^ j) * q, q), q)
-        outs[j][...] = dot(panel[span, :], solved[...]).astype(BF)
-
-
-def group_forward(mine, theirs, inverse, panel, n_leaf, n_pos):
-    width = mine.shape[-1]
-    shape = (inverse.shape[0], width)
-    outs = small(
-        functools.partial(group_kernel, n_leaf, n_pos),
-        "group_forward",
-        [shape] + [(panel.shape[0] // n_leaf, width)] * n_leaf,
-        [pltpu.VMEM(shape, BF)],
-        mine,
-        theirs,
-        inverse,
-        panel,
-    )
-    return outs[0], list(outs[1:])
+            stage[j ^ leaf, k * q : (k + 1) * q, :] = terms[j * q : (j + 1) * q, :]
+        begin = pl.multiple_of(core * (group_cols // 2) + p * gq, gq)
+        group[k * gq : (k + 1) * gq, :] = gsum[pl.ds(begin, gq), :].astype(BF)
+    for k in range(n_leaf):
+        parts[k][...] = stage[k]
+
+
+def fold(keep, recv, inverse, rhs, panel, n_leaf):
+    width = rhs.shape[-1]
+    n_pos, sec, _ = panel.shape
+    part = (n_pos * sec // n_leaf, width)
+    outs = pl.pallas_call(
+        functools.partial(fold_kernel, n_leaf, n_pos),
+        out_shape=[pltpu.VMEM(part, BF)] * n_leaf
+        + [pltpu.VMEM((inverse.shape[0] // 2, width), BF)],
+        in_specs=[VMEM] * 4 + [HBM],
+        out_specs=[VMEM] * (n_leaf + 1),
+        scratch_shapes=[
+            pltpu.VMEM(rhs.shape, F32),
+            pltpu.VMEM((n_leaf,) + part, BF),
+            pltpu.VMEM(panel.shape, BF),
+            pltpu.SemaphoreType.DMA((n_pos,)),
+        ],
+        compiler_params=pltpu.CompilerParams(vmem_limit_bytes=SMALL),
+        name="fold_group",
+    )(*in_vmem(keep, recv, inverse, rhs), *in_hbm(panel))
+    return list(outs[:n_leaf]), outs[n_leaf]
 
 
 def sum_leaf_kernel(n_leaf, *refs):
+    group, outs = refs[n_leaf], refs[n_leaf + 1 :]
+    n_pos = len(outs)
+    q = refs[0].shape[0] // n_pos
+    gq = group.shape[0] // n_pos
     total = total_of(refs[:n_leaf]).astype(BF)
-    for k, out in enumerate(refs[n_leaf:]):
-        q = out.shape[0]
-        out[...] = total[k * q : (k + 1) * q, :]
-
-
-def sum_leaf(parts, n_pos):
-    rows, width = parts[0].shape
+    for k, out in enumerate(outs):
+        out[0:q, :] = total[k * q : (k + 1) * q, :]
+        out[q:, :] = group[k * gq : (k + 1) * gq, :]
+
+
+def sum_leaf(parts, group, n_pos):
+    rows = (parts[0].shape[0] + group.shape[0]) // n_pos
     kernel = functools.partial(sum_leaf_kernel, len(parts))
-    return list(small(kernel, "sum_leaf", [(rows // n_pos, width)] * n_pos, [], *parts))
+    shapes = [(rows, group.shape[1])] * n_pos
+    return list(small(kernel, "sum_leaf", shapes, [], *parts, group))
+
+
+def sum_pos_kernel(high, group, *refs):
+    parts, out = refs[:-1], refs[-1]
+    q = high.shape[0]
+    total = total_of(parts)
+    out[0:q, :] = (high[...] - total[0:q, :]).astype(BF)
+    out[q:, :] = (group[...] - total[q:, :]).astype(BF)
+
+
+def sum_pos(high, group, parts):
+    return small(sum_pos_kernel, "sum_pos", [parts[0].shape], [], high, group, *parts)[0]
+
+
+def stack_pos_kernel(q, *refs):
+    parts, (uppers, groups) = refs[:-2], refs[-2:]
+    gq = parts[0].shape[0] - q
+    for k, part in enumerate(parts):
+        uppers[k * q : (k + 1) * q, :] = part[0:q, :]
+        groups[k * gq : (k + 1) * gq, :] = part[q:, :]
+
+
+def stack_pos(parts, q):
+    n_pos, (rows, width) = len(parts), parts[0].shape
+    shapes = [(n_pos * q, width), (n_pos * (rows - q), width)]
+    return small(functools.partial(stack_pos_kernel, q), "stack_pos", shapes, [], *parts)
 
 
 def stack_kernel(*refs):
@@ -304,15 +334,15 @@
     n_pos,
     mine,
     theirs,
-    group_solved_ref,
-    leaf_solved,
-    dense,
     inv_mid,
     panel_mid,
     inv_top_hbm,
     inv_group_hbm,
-    panel_group_hbm,
+    panel_own_hbm,
+    panel_other_hbm,
+    leaf_solved_hbm,
     inv_leaf_hbm,
+    dense_hbm,
     leaf_hbm,
     group_hbm,
     mid_hbm,
@@ -320,26 +350,34 @@
     inv_top,
     inv_group,
     panel_group,
+    leaf_solved,
     inv_leaf,
+    dense,
     leaf_out,
     group_out,
     mid_out,
     top_out,
     upper,
+    residual,
     above,
     sems,
+    panel_sems,
     out_sems,
 ):
     leaf, pos, core = place()
     pairs = (
         (inv_top_hbm, inv_top),
         (inv_group_hbm, inv_group),
-        (panel_group_hbm, panel_group),
+        (leaf_solved_hbm, leaf_solved),
         (inv_leaf_hbm, inv_leaf),
+        (dense_hbm, dense),
     )
     loads = [pltpu.make_async_copy(a, b, sems.at[i]) for i, (a, b) in enumerate(pairs)]
-    for load in loads:
-        load.start()
+    for kc, got in enumerate((panel_own_hbm, panel_other_hbm)):
+        target = panel_group.at[:, core ^ kc]
+        loads.append(pltpu.make_async_copy(got, target, panel_sems.at[kc]))
+    for i in (0, 1, 5, 6, 2, 3, 4):
+        loads[i].start()
     mid_rows = inv_mid.shape[0]
     top_rows = inv_top.shape[0]
     group_rows = inv_group.shape[0]
@@ -349,12 +387,16 @@
     top_cols = pl.ds(group_rows + mid_rows, top_rows)
     sec = (mid_rows + top_rows) // (2 * n_pos)
     q = sec // n_leaf
+    gq = group_rows // (2 * n_pos)
     for kc, got in enumerate((mine, theirs)):
         for kz in range(n_pos):
             for kl in range(n_leaf):
                 row = sec * (2 * (pos ^ kz) + (core ^ kc)) + q * (leaf ^ kl)
                 begin = (kl * n_pos + kz) * q
                 upper[pl.ds(pl.multiple_of(row, q), q), :] = got[begin : begin + q, :]
+            row = (group_rows // 2) * (core ^ kc) + gq * (pos ^ kz)
+            begin = n_leaf * n_pos * q + kz * gq
+            residual[pl.ds(pl.multiple_of(row, gq), gq), :] = got[begin : begin + gq, :]
 
     mid_solved = dot(inv_mid[...], upper[0:mid_rows, :]).astype(BF)
     top_residual = upper[mid_rows:, :].astype(F32) - dot(panel_mid[...], mid_solved)
@@ -373,8 +415,9 @@
     stores[1].start()
     for load in loads[1:]:
         load.wait()
-    group_solved = group_solved_ref[...].astype(F32).T
-    group_back = group_solved - dot(above[:, upper_cols], panel_group[...])
+    group_solved = dot(inv_group[...], residual[...]).astype(BF).astype(F32).T
+    panel = panel_group[...].reshape(mid_rows + top_rows, group_rows)
+    group_back = group_solved - dot(above[:, upper_cols], panel)
     group_t = dot(group_back.astype(BF), inv_group[...])
     above[:, 0:group_rows] = group_t.astype(BF)
     group_out[...] = group_t.T
@@ -392,12 +435,14 @@
 
 
 def backward(close, far, n_leaf, n_pos):
-    mine, _, group_solved, leaf_solved, dense, inv_mid, panel_mid = close
-    inv_top, inv_group, _, _ = far
+    mine, _, inv_mid, _ = close
+    inv_top, inv_group, panel, _, leaf_solved, inv_leaf, dense = far
     width = mine.shape[-1]
+    held = (inv_top.shape, inv_group.shape, (n_pos, 2) + panel.shape[1:])
+    held += (leaf_solved.shape, inv_leaf.shape, dense.shape)
     outs = (
         leaf_solved.shape,
-        group_solved.shape,
+        (inv_group.shape[0], width),
         (inv_mid.shape[0], width),
         (inv_top.shape[0], width),
     )
@@ -406,12 +451,14 @@
         out_shape=[pltpu.HBM(shape, F32) for shape in outs],
         in_specs=[VMEM] * len(close) + [HBM] * len(far),
         out_specs=[HBM] * 4,
-        scratch_shapes=[pltpu.VMEM(x.shape, x.dtype) for x in far]
+        scratch_shapes=[pltpu.VMEM(shape, BF) for shape in held]
         + [pltpu.VMEM(shape, F32) for shape in outs]
         + [
             pltpu.VMEM((inv_mid.shape[0] + inv_top.shape[0], width), BF),
+            pltpu.VMEM((inv_group.shape[0], width), BF),
             pltpu.VMEM((width, dense.shape[0]), BF),
-            pltpu.SemaphoreType.DMA((len(far),)),
+            pltpu.SemaphoreType.DMA((5,)),
+            pltpu.SemaphoreType.DMA((2,)),
             pltpu.SemaphoreType.DMA((len(outs),)),
         ],
         compiler_params=pltpu.CompilerParams(vmem_limit_bytes=BIG),
@@ -458,13 +505,20 @@
     gq = group_cols // n_grp
     leaf, pos, core = place()
     by_parts = middle_panel.shape[0] % 16 == 0
+    pos_groups = [[2 * p + c for p in range(n_pos)] for c in range(2)]
     with jax.named_scope("gather_group_panel"):
-        panel = lax.all_gather(group_panel[0], "grp", axis=0, tiled=True)
+        panel = lax.all_gather(group_panel[0], "grp", axis_index_groups=pos_groups)
     with jax.named_scope("gather_middle_panel"):
         if by_parts:
             middles = swaps(middle_panel, "grp", n_grp, 2)
         else:
             middle = lax.all_gather(middle_panel, ("leaf", "grp"), axis=0, tiled=True)
+    begin = sec * lax.axis_index("grp") + q * leaf
+    low = lax.dynamic_slice_in_dim(rhs_middle, jnp.minimum(begin, mid_cols - q), q, 0)
+    high = lax.dynamic_slice_in_dim(rhs_top, jnp.maximum(begin - mid_cols, 0), q, 0)
+    rhs_mine = jnp.where(begin < mid_cols, low, high)
+    group_begin = (group_cols // 2) * core + gq * pos
+    group_mine = lax.dynamic_slice_in_dim(rhs_group[0], group_begin, gq, 0)
     keep, send, leaf_solved, dense = leaf_forward(
         rhs_leaf[0],
         inv_leaf[0],
@@ -480,45 +534,33 @@
         if by_parts:
             send = after(send, middles)
         recv = swap(send, "grp", n_grp, 1)
-    groups, parts = pair_sum(keep, recv, n_leaf, n_pos, gq, q)
-    with jax.named_scope("sum_group_over_pos"):
-        groups = groups[:1] + [swap(groups[k], "grp", n_grp, 2 * k) for k in range(1, n_pos)]
-    with jax.named_scope("sum_upper_over_leaf"):
-        parts = parts[:1] + [swap(parts[k], "leaf", n_leaf, k) for k in range(1, n_leaf)]
-    group_begin = (group_cols // 2) * core + gq * pos
-    group_rhs = lax.dynamic_slice_in_dim(rhs_group[0], group_begin, gq, 0)
-    residual = residual_of(group_rhs, after(groups, parts))
-    with jax.named_scope("sum_upper_over_pos"):
-        uppers = sum_leaf(parts, n_pos)
-        uppers = uppers[:1] + [swap(uppers[k], "grp", n_grp, 2 * k) for k in range(1, n_pos)]
-    with jax.named_scope("gather_group"):
-        mine = stack(after(swaps(residual, "grp", n_grp, 2), uppers))
-        theirs = swap(mine, "grp", n_grp, 1)
-    group_solved, terms = group_forward(mine, theirs, inv_group[0], group_panel[0], n_leaf, n_pos)
-    with jax.named_scope("sum_panel_over_leaf"):
-        terms = terms[:1] + [swap(terms[k], "leaf", n_leaf, k) for k in range(1, n_leaf)]
-    begin = sec * lax.axis_index("grp") + q * leaf
-    low = lax.dynamic_slice_in_dim(rhs_middle, jnp.minimum(begin, mid_cols - q), q, 0)
-    high = lax.dynamic_slice_in_dim(rhs_top, jnp.maximum(begin - mid_cols, 0), q, 0)
-    rhs_mine = jnp.where(begin < mid_cols, low, high)
-    residual = residual_of(rhs_mine, uppers + terms)
     with jax.named_scope("gather_middle_panel"):
         if by_parts:
-            middles = swaps(stack(after(middles, terms)), "leaf", n_leaf)
-    with jax.named_scope("gather_pos"):
-        uppers = stack(swaps(residual, "grp", n_grp, 2))
+            middles = swaps(stack(after(middles, send)), "leaf", n_leaf)
+            recv = after(recv, (middles, rhs_mine, group_mine))
+            middle = stack(middles)
+    parts, group = fold(keep, recv, inv_group[0], rhs_group[0], panel, n_leaf)
+    with jax.named_scope("sum_over_leaf"):
+        parts = parts[:1] + [swap(parts[k], "leaf", n_leaf, k) for k in range(1, n_leaf)]
     with jax.named_scope("gather_middle_panel"):
         if by_parts:
-            middle, uppers = after((stack(middles), uppers), (middles, panel))
             middle = weave(middle, swap(middle, "grp", n_grp, 1), n_leaf, n_pos)
+    sends = sum_leaf(after(parts, middle), group, n_pos)
+    with jax.named_scope("sum_over_pos"):
+        got = sends[:1] + [swap(sends[k], "grp", n_grp, 2 * k) for k in range(1, n_pos)]
+    with jax.named_scope("swap_group_panel"):
+        panel_other = swap(panel, "grp", n_grp, 1)
+    residual = sum_pos(rhs_mine, group_mine, got)
+    with jax.named_scope("gather_pos"):
+        uppers, groups = stack_pos(swaps(residual, "grp", n_grp, 2), q)
     with jax.named_scope("gather_leaf"):
         stacks = swaps(uppers, "leaf", n_leaf)
     with jax.named_scope("gather_cores"):
-        mine = stack(after(stacks, middle))
+        mine = stack(after(stacks, panel_other) + [groups])
         theirs = swap(mine, "grp", n_grp, 1)
     leaf_out, group_out, mid_out, top_out = backward(
-        (mine, theirs, group_solved, leaf_solved, dense, inv_middle, middle),
-        (inv_top, inv_group[0], panel, inv_leaf[0]),
+        (mine, theirs, inv_middle, middle),
+        (inv_top, inv_group[0], panel, panel_other, leaf_solved, inv_leaf[0], dense),
         n_leaf,
         n_pos,
     )

time: 112 us -> 103 us (0.920)
  starting transfers between devices: 37.8 us -> 26 us
  Pallas kernels: 20.6 us -> 25 us
  local copies, waits for them, and re-layouts: 5.6 us -> 1.9 us
  waiting for transfers between devices: 31.4 us -> 33.7 us
    ppermute x31 -> x22, starting transfers between devices: 37.7 us -> 26 us  [swap(): return lax.ppermute(x, axis, [(i, i ^ bits) for i in range(size)])]
    unnamed x18 -> x8, local copies, waits for them, and re-layouts: 5.59 us -> 1.06 us
    pallas_call x0 -> x1, Pallas kernels: none -> 3.19 us  [fold(): pl.pallas_call(functools.partial(fold_kernel, n_leaf, n_pos), out_shape=[...]
    pallas_call x1, Pallas kernels: 7.58 us -> 9.41 us  [leaf_forward(): pl.pallas_call(functools.partial(forward_kernel, sec, group_cols), out_sh...]
    all_gather x1, waiting for transfers between devices: 0.02 us -> 1.78 us  [body(): panel = lax.all_gather(group_panel[0], 'grp', axis_index_groups=pos_groups)]
    ppermute x31 -> x22, waiting for transfers between devices: 30.7 us -> 31.2 us  [swap(): return lax.ppermute(x, axis, [(i, i ^ bits) for i in range(size)])]
  transfers between devices with their start and end apart: 32 -> 23, of which waited for: 15 -> 14; matrix products, arithmetic and copies ran while one was open for 1% -> 2% of each run, Pallas kernels for 8% -> 13%
where the time goes in v6:
time: 103 us; the launch traced here: 102 us
  waiting for transfers between devices  33.7 us (33%)
  starting transfers between devices  26 us (25%)
  Pallas kernels  25 us (24%)
  between operations  14.8 us (14%)
  local copies, waits for them, and re-layouts  1.9 us (2%)
    ppermute x22, waiting for transfers between devices, swap(): return lax.ppermute(x, axis, [(i, i ^ bits) for i in range(size)])  31.2 us
    ppermute x22, starting transfers between devices, swap(): return lax.ppermute(x, axis, [(i, i ^ bits) for i in range(size)])  26 us
    pallas_call x1, Pallas kernels, backward(): pl.pallas_call(functools.partial(backward_kernel, n_leaf, n_pos), out_sha...  12 us
    pallas_call x1, Pallas kernels, leaf_forward(): pl.pallas_call(functools.partial(forward_kernel, sec, group_cols), out_sh...  9.41 us
    pallas_call x1, Pallas kernels, fold(): pl.pallas_call(functools.partial(fold_kernel, n_leaf, n_pos), out_shape=[...  3.19 us
  transfers between devices with their start and end apart: 23, of which 14 were waited for; matrix products, arithmetic and copies ran while one was open for 2% of the time, Pallas kernels for 13%

profile of v6, /device:TPU:0, one launch (start us, length us, event | category | flops | bytes accessed | tf_op | source)
XLA Modules:
  0.0 102.3 jit_solution(18305096210876121460)
XLA Ops:
  7.9 5.1 %collective-permute-start.2 = (bf16[32,1024]{1,0:T(8,128)(2,1)}, bf16[32,1024]{1,0:T(8,128)(2,1)S(1)}, u32[]{:S(2)}, u32[]{:S(2)}) collective-permute-start(bf16[32,1024]{1,0:T(8,128)(2,1)} %refs_0_), channel_id=1, source_target_pairs={{0,6},{1,7},{2,4},{3,5},{4,2},{5,3},{6,0},{7,1},{8,14},{9,15},{10,... | collective-permute-start | bytes 196616 | tf_op jit(solution)/shard_map/gather_middle_panel/ppermute | solution.py:470
  14.3 9.4 %leaf_forward.1 = (bf16[1536,256]{1,0:T(8,128)(2,1)S(1)}, bf16[1536,256]{1,0:T(8,128)(2,1)}, bf16[1024,256]{1,0:T(8,128)(2,1)}, bf16[2560,1024]{1,0:T(8,128)(2,1)}) custom-call(s32[1,1]{1,0:T(1,128)S(6)} %copy.18.count_hbm, s32[1,256]{1,0:T(1,128)} %cols_hbm.1, s32[1,256]{1,0:T(1,128)} %tgts_hbm.1, f32[1024,256]{1,0:T(8,128)} %bitcast.15, ...), custom_call_target="tpu_custom_call" | custom-call | flops 1342177280 | bytes 9437184 | tf_op jit(solution)/shard_map/leaf_forward/pallas_call | solution.py:163
  23.8 2.7 %collective-permute-start.6 = (bf16[128,1024]{1,0:T(8,128)(2,1)S(1)}, bf16[128,1024]{1,0:T(8,128)(2,1)S(1)}, u32[]{:S(2)}, u32[]{:S(2)}) collective-permute-start(bf16[128,1024]{1,0:T(8,128)(2,1)S(1)} %stack.3.refs_0_), channel_id=1, source_target_pairs={{0,24},{8,16},{16,8},{24,0},{1,25},{9,17},{17,9},{25,1},{2,26},{10... | collective-permute-start | bytes 786440 | tf_op jit(solution)/shard_map/gather_middle_panel/ppermute | solution.py:470
  27.4 6.7 %collective-permute-done.6.refs_3_ = bf16[128,1024]{1,0:T(8,128)(2,1)S(1)} collective-permute-done((bf16[128,1024]{1,0:T(8,128)(2,1)S(1)}, bf16[128,1024]{1,0:T(8,128)(2,1)S(1)}, u32[]{:S(2)}, u32[]{:S(2)}) %collective-permute-start.6) | collective-permute-done | bytes 262176 | tf_op jit(solution)/shard_map/gather_middle_panel/ppermute | solution.py:470
  34.1 3.1 %collective-permute-done.5.refs_2_ = bf16[128,1024]{1,0:T(8,128)(2,1)S(1)} collective-permute-done((bf16[128,1024]{1,0:T(8,128)(2,1)S(1)}, bf16[128,1024]{1,0:T(8,128)(2,1)S(1)}, u32[]{:S(2)}, u32[]{:S(2)}) %collective-permute-start.5) | collective-permute-done | bytes 262176 | tf_op jit(solution)/shard_map/gather_middle_panel/ppermute | solution.py:470
  38.5 1.8 %all-gather.2.cloned.1.call-done.panel_hbm.panel_own_hbm = bf16[4,256,512]{2,1,0:T(8,128)(2,1)} async-done(((bf16[1,256,512]{2,1,0:T(8,128)(2,1)}), bf16[4,256,512]{2,1,0:T(8,128)(2,1)}) %all-gather.2.cloned.1.call-update) | async-done | bytes 1048592 | tf_op jit(solution)/shard_map/gather_group_panel/all_gather | solution.py:510
  43.1 3.2 %fold_group.1 = (bf16[256,256]{1,0:T(8,128)(2,1)S(1)}, bf16[256,256]{1,0:T(8,128)(2,1)S(1)}, bf16[256,256]{1,0:T(8,128)(2,1)S(1)}, bf16[256,256]{1,0:T(8,128)(2,1)S(1)}, bf16[256,256]{1,0:T(8,128)(2,1)S(1)}) custom-call(bf16[1536,256]{1,0:T(8,128)(2,1)S(1)} %get-tuple-element.37.keep, bf16[1536,256]{1,0:T(8,128)(2,1)} %collective-permute-done.3.recv, ...), custom_call_target="tpu_custom_call" | custom-call | tf_op jit(solution)/shard_map/fold_group/pallas_call | solution.py:239
  46.3 1.5 %collective-permute-start.7 = (bf16[256,256]{1,0:T(8,128)(2,1)S(1)}, bf16[256,256]{1,0:T(8,128)(2,1)S(1)}, u32[]{:S(2)}, u32[]{:S(2)}) collective-permute-start(bf16[256,256]{1,0:T(8,128)(2,1)S(1)} %get-tuple-element.46), channel_id=1, source_target_pairs={{0,8},{8,0},{16,24},{24,16},{1,9},{9,1},{17,25},{25,17},{2,10},{10... | collective-permute-start | bytes 393224 | tf_op jit(solution)/shard_map/sum_over_leaf/ppermute | solution.py:470
  47.8 1.5 %collective-permute-start.8 = (bf16[256,256]{1,0:T(8,128)(2,1)S(1)}, bf16[256,256]{1,0:T(8,128)(2,1)S(1)}, u32[]{:S(2)}, u32[]{:S(2)}) collective-permute-start(bf16[256,256]{1,0:T(8,128)(2,1)S(1)} %get-tuple-element.47), channel_id=1, source_target_pairs={{0,16},{8,24},{16,0},{24,8},{1,17},{9,25},{17,1},{25,9},{2,18},{10... | collective-permute-start | bytes 393224 | tf_op jit(solution)/shard_map/sum_over_leaf/ppermute | solution.py:470
  50.0 2.6 %collective-permute-done.7.refs_1_ = bf16[256,256]{1,0:T(8,128)(2,1)S(1)} collective-permute-done((bf16[256,256]{1,0:T(8,128)(2,1)S(1)}, bf16[256,256]{1,0:T(8,128)(2,1)S(1)}, u32[]{:S(2)}, u32[]{:S(2)}) %collective-permute-start.7) | collective-permute-done | bytes 131104 | tf_op jit(solution)/shard_map/sum_over_leaf/ppermute | solution.py:470
  52.7 3.6 %collective-permute-done.8.refs_2_ = bf16[256,256]{1,0:T(8,128)(2,1)S(1)} collective-permute-done((bf16[256,256]{1,0:T(8,128)(2,1)S(1)}, bf16[256,256]{1,0:T(8,128)(2,1)S(1)}, u32[]{:S(2)}, u32[]{:S(2)}) %collective-permute-start.8) | collective-permute-done | bytes 131104 | tf_op jit(solution)/shard_map/sum_over_leaf/ppermute | solution.py:470
  56.3 1.7 %collective-permute-start.11 = (bf16[128,256]{1,0:T(8,128)(2,1)S(1)}, bf16[128,256]{1,0:T(8,128)(2,1)S(1)}, u32[]{:S(2)}, u32[]{:S(2)}) collective-permute-start(bf16[128,256]{1,0:T(8,128)(2,1)S(1)} %get-tuple-element.55), channel_id=1, source_target_pairs={{0,2},{1,3},{2,0},{3,1},{4,6},{5,7},{6,4},{7,5},{8,10},{9,11},{10,... | collective-permute-start | bytes 196616 | tf_op jit(solution)/shard_map/sum_over_pos/ppermute | solution.py:470
  58.0 1.9 %collective-permute-start.12 = (bf16[128,256]{1,0:T(8,128)(2,1)S(1)}, bf16[128,256]{1,0:T(8,128)(2,1)S(1)}, u32[]{:S(2)}, u32[]{:S(2)}) collective-permute-start(bf16[128,256]{1,0:T(8,128)(2,1)S(1)} %get-tuple-element.56), channel_id=1, source_target_pairs={{0,4},{1,5},{2,6},{3,7},{4,0},{5,1},{6,2},{7,3},{8,12},{9,13},{10,... | collective-permute-start | bytes 196616 | tf_op jit(solution)/shard_map/sum_over_pos/ppermute | solution.py:470
  60.8 3.8 %collective-permute-done.12.refs_2_ = bf16[128,256]{1,0:T(8,128)(2,1)S(1)} collective-permute-done((bf16[128,256]{1,0:T(8,128)(2,1)S(1)}, bf16[128,256]{1,0:T(8,128)(2,1)S(1)}, u32[]{:S(2)}, u32[]{:S(2)}) %collective-permute-start.12) | collective-permute-done | bytes 65568 | tf_op jit(solution)/shard_map/sum_over_pos/ppermute | solution.py:470
  64.6 1.5 %collective-permute-done.13.refs_3_ = bf16[128,256]{1,0:T(8,128)(2,1)S(1)} collective-permute-done((bf16[128,256]{1,0:T(8,128)(2,1)S(1)}, bf16[128,256]{1,0:T(8,128)(2,1)S(1)}, u32[]{:S(2)}, u32[]{:S(2)}) %collective-permute-start.13) | collective-permute-done | bytes 65568 | tf_op jit(solution)/shard_map/sum_over_pos/ppermute | solution.py:470
  67.8 2.8 %collective-permute-start.14 = (bf16[128,256]{1,0:T(8,128)(2,1)S(1)}, bf16[128,256]{1,0:T(8,128)(2,1)S(1)}, u32[]{:S(2)}, u32[]{:S(2)}) collective-permute-start(bf16[128,256]{1,0:T(8,128)(2,1)S(1)} %sum_pos.1.refs_0_), channel_id=1, source_target_pairs={{0,2},{1,3},{2,0},{3,1},{4,6},{5,7},{6,4},{7,5},{8,10},{9,11},{10,... | collective-permute-start | bytes 196616 | tf_op jit(solution)/shard_map/gather_pos/ppermute | solution.py:470
  70.6 1.7 %collective-permute-done.16.refs_3_ = bf16[128,256]{1,0:T(8,128)(2,1)S(1)} collective-permute-done((bf16[128,256]{1,0:T(8,128)(2,1)S(1)}, bf16[128,256]{1,0:T(8,128)(2,1)S(1)}, u32[]{:S(2)}, u32[]{:S(2)}) %collective-permute-start.16) | collective-permute-done | bytes 65568 | tf_op jit(solution)/shard_map/gather_pos/ppermute | solution.py:470
  72.4 1.3 %collective-permute-done.15.refs_2_ = bf16[128,256]{1,0:T(8,128)(2,1)S(1)} collective-permute-done((bf16[128,256]{1,0:T(8,128)(2,1)S(1)}, bf16[128,256]{1,0:T(8,128)(2,1)S(1)}, u32[]{:S(2)}, u32[]{:S(2)}) %collective-permute-start.15) | collective-permute-done | bytes 65568 | tf_op jit(solution)/shard_map/gather_pos/ppermute | solution.py:470
  73.7 1.4 %collective-permute-start.19 = (bf16[256,256]{1,0:T(8,128)(2,1)S(1)}, bf16[256,256]{1,0:T(8,128)(2,1)S(1)}, u32[]{:S(2)}, u32[]{:S(2)}) collective-permute-start(bf16[256,256]{1,0:T(8,128)(2,1)S(1)} %get-tuple-element.59.refs_0_), channel_id=1, source_target_pairs={{0,24},{8,16},{16,8},{24,0},{1,25},{9,17},{17,9},{25,1},{2,26},{10... | collective-permute-start | bytes 393224 | tf_op jit(solution)/shard_map/gather_leaf/ppermute | solution.py:470
  75.1 1.2 %collective-permute-start.18 = (bf16[256,256]{1,0:T(8,128)(2,1)S(1)}, bf16[256,256]{1,0:T(8,128)(2,1)S(1)}, u32[]{:S(2)}, u32[]{:S(2)}) collective-permute-start(bf16[256,256]{1,0:T(8,128)(2,1)S(1)} %get-tuple-element.59.refs_0_), channel_id=1, source_target_pairs={{0,16},{8,24},{16,0},{24,8},{1,17},{9,25},{17,1},{25,9},{2,18},{10... | collective-permute-start | bytes 393224 | tf_op jit(solution)/shard_map/gather_leaf/ppermute | solution.py:470
  77.3 2.5 %collective-permute-done.19.refs_3_ = bf16[256,256]{1,0:T(8,128)(2,1)S(1)} collective-permute-done((bf16[256,256]{1,0:T(8,128)(2,1)S(1)}, bf16[256,256]{1,0:T(8,128)(2,1)S(1)}, u32[]{:S(2)}, u32[]{:S(2)}) %collective-permute-start.19) | collective-permute-done | bytes 131104 | tf_op jit(solution)/shard_map/gather_leaf/ppermute | solution.py:470
  79.8 1.3 %collective-permute-done.18.refs_2_ = bf16[256,256]{1,0:T(8,128)(2,1)S(1)} collective-permute-done((bf16[256,256]{1,0:T(8,128)(2,1)S(1)}, bf16[256,256]{1,0:T(8,128)(2,1)S(1)}, u32[]{:S(2)}, u32[]{:S(2)}) %collective-permute-start.18) | collective-permute-done | bytes 131104 | tf_op jit(solution)/shard_map/gather_leaf/ppermute | solution.py:470
  81.4 2.1 %collective-permute-done.21.theirs = bf16[1280,256]{1,0:T(8,128)(2,1)S(1)} collective-permute-done((bf16[1280,256]{1,0:T(8,128)(2,1)S(1)}, bf16[1280,256]{1,0:T(8,128)(2,1)S(1)}, u32[]{:S(2)}, u32[]{:S(2)}) %collective-permute-start.21) | collective-permute-done | bytes 655392 | tf_op jit(solution)/shard_map/gather_cores/ppermute | solution.py:470
  83.5 12.0 %backward.1 = (f32[1024,256]{1,0:T(8,128)}, f32[512,256]{1,0:T(8,128)}, f32[1024,256]{1,0:T(8,128)}, f32[1024,256]{1,0:T(8,128)}) custom-call(bf16[1280,256]{1,0:T(8,128)(2,1)S(1)} %stack.5.mine, bf16[1280,256]{1,0:T(8,128)(2,1)S(1)} %collective-permute-done.21.theirs, bf16[1024,1024]{1,0:T(8,128)(2,1)S(1)} %copy-done.1, ...), custom_call_target="tpu_custom_call" | custom-call | tf_op jit(solution)/shard_map/backward/pallas_call | solution.py:449
  (43 shorter events, 10.9 us)
Async XLA Ops:
  7.2 33.1 %all-gather.2.cloned.1.call-start = ((), (), s32[]{:S(2)}) async-start(), calls=%async_computation | async-start | bytes 1310720 | tf_op jit(solution)/shard_map/gather_group_panel/all_gather | solution.py:510
  7.9 15.9 %collective-permute-start.2 = (bf16[32,1024]{1,0:T(8,128)(2,1)}, bf16[32,1024]{1,0:T(8,128)(2,1)S(1)}, u32[]{:S(2)}, u32[]{:S(2)}) collective-permute-start(bf16[32,1024]{1,0:T(8,128)(2,1)} %refs_0_), channel_id=1, source_target_pairs={{0,6},{1,7},{2,4},{3,5},{4,2},{5,3},{6,0},{7,1},{8,14},{9,15},{10,... | collective-permute-start | bytes 196616 | tf_op jit(solution)/shard_map/gather_middle_panel/ppermute | solution.py:470
  13.0 10.7 %collective-permute-start.1 = (bf16[32,1024]{1,0:T(8,128)(2,1)}, bf16[32,1024]{1,0:T(8,128)(2,1)S(1)}, u32[]{:S(2)}, u32[]{:S(2)}) collective-permute-start(bf16[32,1024]{1,0:T(8,128)(2,1)} %refs_0_), channel_id=1, source_target_pairs={{0,4},{1,5},{2,6},{3,7},{4,0},{5,1},{6,2},{7,3},{8,12},{9,13},{10,... | collective-permute-start | bytes 196616 | tf_op jit(solution)/shard_map/gather_middle_panel/ppermute | solution.py:470
  13.0 10.8 %collective-permute-start = (bf16[32,1024]{1,0:T(8,128)(2,1)}, bf16[32,1024]{1,0:T(8,128)(2,1)S(1)}, u32[]{:S(2)}, u32[]{:S(2)}) collective-permute-start(bf16[32,1024]{1,0:T(8,128)(2,1)} %refs_0_), channel_id=1, source_target_pairs={{0,2},{1,3},{2,0},{3,1},{4,6},{5,7},{6,4},{7,5},{8,10},{9,11},{10,... | collective-permute-start | bytes 196616 | tf_op jit(solution)/shard_map/gather_middle_panel/ppermute | solution.py:470
  23.8 10.3 %collective-permute-start.6 = (bf16[128,1024]{1,0:T(8,128)(2,1)S(1)}, bf16[128,1024]{1,0:T(8,128)(2,1)S(1)}, u32[]{:S(2)}, u32[]{:S(2)}) collective-permute-start(bf16[128,1024]{1,0:T(8,128)(2,1)S(1)} %stack.3.refs_0_), channel_id=1, source_target_pairs={{0,24},{8,16},{16,8},{24,0},{1,25},{9,17},{17,9},{25,1},{2,26},{10... | collective-permute-start | bytes 786440 | tf_op jit(solution)/shard_map/gather_middle_panel/ppermute | solution.py:470
  26.6 10.6 %collective-permute-start.5 = (bf16[128,1024]{1,0:T(8,128)(2,1)S(1)}, bf16[128,1024]{1,0:T(8,128)(2,1)S(1)}, u32[]{:S(2)}, u32[]{:S(2)}) collective-permute-start(bf16[128,1024]{1,0:T(8,128)(2,1)S(1)} %stack.3.refs_0_), channel_id=1, source_target_pairs={{0,16},{8,24},{16,0},{24,8},{1,17},{9,25},{17,1},{25,9},{2,18},{10... | collective-permute-start | bytes 786440 | tf_op jit(solution)/shard_map/gather_middle_panel/ppermute | solution.py:470
  26.6 11.2 %collective-permute-start.4 = (bf16[128,1024]{1,0:T(8,128)(2,1)S(1)}, bf16[128,1024]{1,0:T(8,128)(2,1)S(1)}, u32[]{:S(2)}, u32[]{:S(2)}) collective-permute-start(bf16[128,1024]{1,0:T(8,128)(2,1)S(1)} %stack.3.refs_0_), channel_id=1, source_target_pairs={{0,8},{8,0},{16,24},{24,16},{1,9},{9,1},{17,25},{25,17},{2,10},{10... | collective-permute-start | bytes 786440 | tf_op jit(solution)/shard_map/gather_middle_panel/ppermute | solution.py:470
  37.9 12.0 %collective-permute-start.10 = (bf16[512,1024]{1,0:T(8,128)(2,1)S(1)}, bf16[512,1024]{1,0:T(8,128)(2,1)S(1)}, u32[]{:S(2)}, u32[]{:S(2)}) collective-permute-start(bf16[512,1024]{1,0:T(8,128)(2,1)S(1)} %stack.4.own), channel_id=1, source_target_pairs={{0,1},{1,0},{2,3},{3,2},{4,5},{5,4},{6,7},{7,6},{8,9},{9,8},{10,11... | collective-permute-start | bytes 3145736 | tf_op jit(solution)/shard_map/gather_middle_panel/ppermute | solution.py:470
  38.0 4.1 %collective-permute-start.3 = (bf16[1536,256]{1,0:T(8,128)(2,1)}, bf16[1536,256]{1,0:T(8,128)(2,1)}, u32[]{:S(2)}, u32[]{:S(2)}) collective-permute-start(bf16[1536,256]{1,0:T(8,128)(2,1)} %get-tuple-element.39), channel_id=1, source_target_pairs={{0,1},{1,0},{2,3},{3,2},{4,5},{5,4},{6,7},{7,6},{8,9},{9,8},{10,11... | collective-permute-start | bytes 2359304 | tf_op jit(solution)/shard_map/swap_cores/ppermute | solution.py:470
  40.2 41.0 %collective-permute-start.20 = (bf16[4,256,512]{2,1,0:T(8,128)(2,1)}, bf16[4,256,512]{2,1,0:T(8,128)(2,1)}, u32[]{:S(2)}, u32[]{:S(2)}) collective-permute-start(bf16[4,256,512]{2,1,0:T(8,128)(2,1)} %all-gather.2.cloned.1.call-done.panel_hbm.panel_own_hbm), channel_id=1, source_target_pairs={{0,1},{1,0},{2,3},{3,2},{4,5},{5,4},{6,7},{7,6},{8,9},{9,8},{10,11... | collective-permute-start | bytes 3145736 | tf_op jit(solution)/shard_map/swap_group_panel/ppermute | solution.py:470
  46.3 6.4 %collective-permute-start.7 = (bf16[256,256]{1,0:T(8,128)(2,1)S(1)}, bf16[256,256]{1,0:T(8,128)(2,1)S(1)}, u32[]{:S(2)}, u32[]{:S(2)}) collective-permute-start(bf16[256,256]{1,0:T(8,128)(2,1)S(1)} %get-tuple-element.46), channel_id=1, source_target_pairs={{0,8},{8,0},{16,24},{24,16},{1,9},{9,1},{17,25},{25,17},{2,10},{10... | collective-permute-start | bytes 393224 | tf_op jit(solution)/shard_map/sum_over_leaf/ppermute | solution.py:470
  47.8 8.4 %collective-permute-start.8 = (bf16[256,256]{1,0:T(8,128)(2,1)S(1)}, bf16[256,256]{1,0:T(8,128)(2,1)S(1)}, u32[]{:S(2)}, u32[]{:S(2)}) collective-permute-start(bf16[256,256]{1,0:T(8,128)(2,1)S(1)} %get-tuple-element.47), channel_id=1, source_target_pairs={{0,16},{8,24},{16,0},{24,8},{1,17},{9,25},{17,1},{25,9},{2,18},{10... | collective-permute-start | bytes 393224 | tf_op jit(solution)/shard_map/sum_over_leaf/ppermute | solution.py:470
  49.3 7.0 %collective-permute-start.9 = (bf16[256,256]{1,0:T(8,128)(2,1)S(1)}, bf16[256,256]{1,0:T(8,128)(2,1)S(1)}, u32[]{:S(2)}, u32[]{:S(2)}) collective-permute-start(bf16[256,256]{1,0:T(8,128)(2,1)S(1)} %get-tuple-element.48), channel_id=1, source_target_pairs={{0,24},{8,16},{16,8},{24,0},{1,25},{9,17},{17,9},{25,1},{2,26},{10... | collective-permute-start | bytes 393224 | tf_op jit(solution)/shard_map/sum_over_leaf/ppermute | solution.py:470
  50.0 33.5 %copy-start.1 = (bf16[1024,1024]{1,0:T(8,128)(2,1)S(1)}, bf16[1024,1024]{1,0:T(8,128)(2,1)}, u32[]{:S(2)}) copy-start(bf16[1024,1024]{1,0:T(8,128)(2,1)} %inv_mid.1) | copy-start | bytes 6291460
  56.3 4.5 %collective-permute-start.11 = (bf16[128,256]{1,0:T(8,128)(2,1)S(1)}, bf16[128,256]{1,0:T(8,128)(2,1)S(1)}, u32[]{:S(2)}, u32[]{:S(2)}) collective-permute-start(bf16[128,256]{1,0:T(8,128)(2,1)S(1)} %get-tuple-element.55), channel_id=1, source_target_pairs={{0,2},{1,3},{2,0},{3,1},{4,6},{5,7},{6,4},{7,5},{8,10},{9,11},{10,... | collective-permute-start | bytes 196616 | tf_op jit(solution)/shard_map/sum_over_pos/ppermute | solution.py:470
  58.0 6.6 %collective-permute-start.12 = (bf16[128,256]{1,0:T(8,128)(2,1)S(1)}, bf16[128,256]{1,0:T(8,128)(2,1)S(1)}, u32[]{:S(2)}, u32[]{:S(2)}) collective-permute-start(bf16[128,256]{1,0:T(8,128)(2,1)S(1)} %get-tuple-element.56), channel_id=1, source_target_pairs={{0,4},{1,5},{2,6},{3,7},{4,0},{5,1},{6,2},{7,3},{8,12},{9,13},{10,... | collective-permute-start | bytes 196616 | tf_op jit(solution)/shard_map/sum_over_pos/ppermute | solution.py:470
  59.9 6.2 %collective-permute-start.13 = (bf16[128,256]{1,0:T(8,128)(2,1)S(1)}, bf16[128,256]{1,0:T(8,128)(2,1)S(1)}, u32[]{:S(2)}, u32[]{:S(2)}) collective-permute-start(bf16[128,256]{1,0:T(8,128)(2,1)S(1)} %get-tuple-element.57), channel_id=1, source_target_pairs={{0,6},{1,7},{2,4},{3,5},{4,2},{5,3},{6,0},{7,1},{8,14},{9,15},{10,... | collective-permute-start | bytes 196616 | tf_op jit(solution)/shard_map/sum_over_pos/ppermute | solution.py:470
  66.2 6.2 %collective-permute-start.16 = (bf16[128,256]{1,0:T(8,128)(2,1)S(1)}, bf16[128,256]{1,0:T(8,128)(2,1)S(1)}, u32[]{:S(2)}, u32[]{:S(2)}) collective-permute-start(bf16[128,256]{1,0:T(8,128)(2,1)S(1)} %sum_pos.1.refs_0_), channel_id=1, source_target_pairs={{0,6},{1,7},{2,4},{3,5},{4,2},{5,3},{6,0},{7,1},{8,14},{9,15},{10,... | collective-permute-start | bytes 196616 | tf_op jit(solution)/shard_map/gather_pos/ppermute | solution.py:470
  67.3 6.4 %collective-permute-start.15 = (bf16[128,256]{1,0:T(8,128)(2,1)S(1)}, bf16[128,256]{1,0:T(8,128)(2,1)S(1)}, u32[]{:S(2)}, u32[]{:S(2)}) collective-permute-start(bf16[128,256]{1,0:T(8,128)(2,1)S(1)} %sum_pos.1.refs_0_), channel_id=1, source_target_pairs={{0,4},{1,5},{2,6},{3,7},{4,0},{5,1},{6,2},{7,3},{8,12},{9,13},{10,... | collective-permute-start | bytes 196616 | tf_op jit(solution)/shard_map/gather_pos/ppermute | solution.py:470
  67.8 5.9 %collective-permute-start.14 = (bf16[128,256]{1,0:T(8,128)(2,1)S(1)}, bf16[128,256]{1,0:T(8,128)(2,1)S(1)}, u32[]{:S(2)}, u32[]{:S(2)}) collective-permute-start(bf16[128,256]{1,0:T(8,128)(2,1)S(1)} %sum_pos.1.refs_0_), channel_id=1, source_target_pairs={{0,2},{1,3},{2,0},{3,1},{4,6},{5,7},{6,4},{7,5},{8,10},{9,11},{10,... | collective-permute-start | bytes 196616 | tf_op jit(solution)/shard_map/gather_pos/ppermute | solution.py:470
  73.7 6.0 %collective-permute-start.19 = (bf16[256,256]{1,0:T(8,128)(2,1)S(1)}, bf16[256,256]{1,0:T(8,128)(2,1)S(1)}, u32[]{:S(2)}, u32[]{:S(2)}) collective-permute-start(bf16[256,256]{1,0:T(8,128)(2,1)S(1)} %get-tuple-element.59.refs_0_), channel_id=1, source_target_pairs={{0,24},{8,16},{16,8},{24,0},{1,25},{9,17},{17,9},{25,1},{2,26},{10... | collective-permute-start | bytes 393224 | tf_op jit(solution)/shard_map/gather_leaf/ppermute | solution.py:470
  75.1 6.0 %collective-permute-start.18 = (bf16[256,256]{1,0:T(8,128)(2,1)S(1)}, bf16[256,256]{1,0:T(8,128)(2,1)S(1)}, u32[]{:S(2)}, u32[]{:S(2)}) collective-permute-start(bf16[256,256]{1,0:T(8,128)(2,1)S(1)} %get-tuple-element.59.refs_0_), channel_id=1, source_target_pairs={{0,16},{8,24},{16,0},{24,8},{1,17},{9,25},{17,1},{25,9},{2,18},{10... | collective-permute-start | bytes 393224 | tf_op jit(solution)/shard_map/gather_leaf/ppermute | solution.py:470
  76.3 5.0 %collective-permute-start.17 = (bf16[256,256]{1,0:T(8,128)(2,1)S(1)}, bf16[256,256]{1,0:T(8,128)(2,1)S(1)}, u32[]{:S(2)}, u32[]{:S(2)}) collective-permute-start(bf16[256,256]{1,0:T(8,128)(2,1)S(1)} %get-tuple-element.59.refs_0_), channel_id=1, source_target_pairs={{0,8},{8,0},{16,24},{24,16},{1,9},{9,1},{17,25},{25,17},{2,10},{10... | collective-permute-start | bytes 393224 | tf_op jit(solution)/shard_map/gather_leaf/ppermute | solution.py:470
  81.3 2.2 %collective-permute-start.21 = (bf16[1280,256]{1,0:T(8,128)(2,1)S(1)}, bf16[1280,256]{1,0:T(8,128)(2,1)S(1)}, u32[]{:S(2)}, u32[]{:S(2)}) collective-permute-start(bf16[1280,256]{1,0:T(8,128)(2,1)S(1)} %stack.5.mine), channel_id=1, source_target_pairs={{0,1},{1,0},{2,3},{3,2},{4,5},{5,4},{6,7},{7,6},{8,9},{9,8},{10,11... | collective-permute-start | bytes 1966088 | tf_op jit(solution)/shard_map/gather_cores/ppermute | solution.py:470
  (3 other events, 28.9 us)
Sparse Core Ops, SparseCore 0:
  9.6 30.6 all-gather.1

commit v7 on v6

--- a/solution.py
+++ b/solution.py
@@ -15,7 +15,7 @@
 HBM = pl.BlockSpec(memory_space=pltpu.HBM)
 VMEM = pl.BlockSpec(memory_space=pltpu.VMEM)
 BIG = 40 * MIB
-SMALL = 6 * MIB
+SMALL = 8 * MIB
 
 
 def in_hbm(*arrays):
@@ -186,11 +186,6 @@
             pltpu.SemaphoreType.DMA((1 + targets * block // group_cols,)),
         ],
         compiler_params=pltpu.CompilerParams(vmem_limit_bytes=BIG),
-        cost_estimate=pl.CostEstimate(
-            flops=2 * targets * block * supernodes * block * width,
-            bytes_accessed=2 * tiles.size + 4 * rhs.size,
-            transcendentals=0,
-        ),
         name="leaf_forward",
     )(count, *in_hbm(cols, tgts, rhs, inverse, tiles))
 
@@ -202,13 +197,8 @@
     return total
 
 
-def fold_kernel(n_leaf, n_pos, keep, recv, inv, rhs, panel_hbm, *refs):
-    parts, group, (gsum, stage, panel, sems) = refs[:n_leaf], refs[n_leaf], refs[n_leaf + 1 :]
-    loads = [
-        pltpu.make_async_copy(panel_hbm.at[p], panel.at[p], sems.at[p]) for p in range(n_pos)
-    ]
-    for load in loads:
-        load.start()
+def fold_kernel(n_leaf, n_pos, keep, recv, inv, rhs, panel, *refs):
+    parts, group, (gsum, stage) = refs[:n_leaf], refs[n_leaf], refs[n_leaf + 1 :]
     leaf, pos, core = place()
     group_cols = inv.shape[0]
     sec = panel.shape[1]
@@ -217,8 +207,6 @@
     gsum[...] = keep[0:group_cols, :].astype(F32) + recv[0:group_cols, :].astype(F32)
     residual = rhs[...] * (1.0 / n_pos) - gsum[...]
     solved = dot(inv[...], residual.astype(BF)).astype(BF)
-    for load in loads:
-        load.wait()
     for k in range(n_pos):
         p = pos ^ k
         rows = pl.ds(pl.multiple_of(group_cols + p * sec, sec), sec)
@@ -236,21 +224,17 @@
     width = rhs.shape[-1]
     n_pos, sec, _ = panel.shape
     part = (n_pos * sec // n_leaf, width)
-    outs = pl.pallas_call(
+    outs = small(
         functools.partial(fold_kernel, n_leaf, n_pos),
-        out_shape=[pltpu.VMEM(part, BF)] * n_leaf
-        + [pltpu.VMEM((inverse.shape[0] // 2, width), BF)],
-        in_specs=[VMEM] * 4 + [HBM],
-        out_specs=[VMEM] * (n_leaf + 1),
-        scratch_shapes=[
-            pltpu.VMEM(rhs.shape, F32),
-            pltpu.VMEM((n_leaf,) + part, BF),
-            pltpu.VMEM(panel.shape, BF),
-            pltpu.SemaphoreType.DMA((n_pos,)),
-        ],
-        compiler_params=pltpu.CompilerParams(vmem_limit_bytes=SMALL),
-        name="fold_group",
-    )(*in_vmem(keep, recv, inverse, rhs), *in_hbm(panel))
+        "fold_group",
+        [part] * n_leaf + [(inverse.shape[0] // 2, width)],
+        [pltpu.VMEM(rhs.shape, F32), pltpu.VMEM((n_leaf,) + part, BF)],
+        keep,
+        recv,
+        inverse,
+        rhs,
+        panel,
+    )
     return list(outs[:n_leaf]), outs[n_leaf]
 
 
@@ -311,7 +295,15 @@
     return small(stack_kernel, "stack", [(rows, parts[0].shape[1])], [], *parts)[0]
 
 
-def weave_kernel(n_leaf, n_pos, own, other, out):
+def turn(source, target):
+    rows, cols = source.shape
+    step = min(256, rows)
+    for i in range(0, rows, step):
+        for j in range(0, cols, step):
+            target[j : j + step, i : i + step] = source[i : i + step, j : j + step].T
+
+
+def weave_kernel(n_leaf, n_pos, own, other, out, out_t):
     leaf, pos, core = place()
     rows = own.shape[0] // (n_leaf * n_pos)
     for kc, part in enumerate((own, other)):
@@ -321,12 +313,70 @@
                 span = pl.ds(pl.multiple_of(block * rows, rows), rows)
                 begin = (kl * n_pos + k) * rows
                 out[span, :] = part[begin : begin + rows, :]
+    turn(out, out_t)
 
 
 def weave(own, other, n_leaf, n_pos):
     shape = (2 * own.shape[0], own.shape[1])
     kernel = functools.partial(weave_kernel, n_leaf, n_pos)
-    return small(kernel, "weave", [shape], [], own, other)[0]
+    return small(kernel, "weave", [shape, shape[::-1]], [], own, other)
+
+
+def weave_group_kernel(own, other, out_t, both, sems):
+    _, _, core = place()
+    n_pos, sec, cols = own.shape
+    loads = []
+    for kc, got in enumerate((own, other)):
+        for p in range(n_pos):
+            begin = pl.multiple_of((2 * p + (core ^ kc)) * sec, sec)
+            target = both.at[pl.ds(begin, sec)]
+            sem = sems.at[kc * n_pos + p]
+            loads.append(pltpu.make_async_copy(got.at[p], target, sem))
+    for load in loads:
+        load.start()
+    for load in loads:
+        load.wait()
+    turn(both, out_t)
+
+
+def weave_group(own, other):
+    n_pos, sec, cols = own.shape
+    rows = 2 * n_pos * sec
+    return pl.pallas_call(
+        weave_group_kernel,
+        out_shape=pltpu.VMEM((cols, rows), BF),
+        in_specs=[HBM] * 2,
+        out_specs=VMEM,
+        scratch_shapes=[
+            pltpu.VMEM((rows, cols), BF),
+            pltpu.SemaphoreType.DMA((2 * n_pos,)),
+        ],
+        compiler_params=pltpu.CompilerParams(vmem_limit_bytes=SMALL),
+        cost_estimate=pl.CostEstimate(
+            flops=0, bytes_accessed=6 * rows * cols, transcendentals=0
+        ),
+        name="weave_group",
+    )(*in_hbm(own, other))
+
+
+def turned_kernel(source_hbm, target, source, sem):
+    load = pltpu.make_async_copy(source_hbm, source, sem)
+    load.start()
+    load.wait()
+    turn(source, target)
+
+
+def turned(x, name):
+    return pl.pallas_call(
+        turned_kernel,
+        out_shape=pltpu.VMEM(x.shape[::-1], BF),
+        in_specs=[HBM],
+        out_specs=VMEM,
+        scratch_shapes=[pltpu.VMEM(x.shape, BF), pltpu.SemaphoreType.DMA],
+        compiler_params=pltpu.CompilerParams(vmem_limit_bytes=BIG // 2),
+        cost_estimate=pl.CostEstimate(flops=1, bytes_accessed=1, transcendentals=0),
+        name=name,
+    )(*in_hbm(x))
 
 
 def backward_kernel(
@@ -335,24 +385,25 @@
     mine,
     theirs,
     inv_mid,
+    inv_mid_t,
+    inv_top_t,
+    inv_group_t,
     panel_mid,
+    panel_mid_t,
+    panel_group_t,
+    dense_t,
     inv_top_hbm,
     inv_group_hbm,
-    panel_own_hbm,
-    panel_other_hbm,
     leaf_solved_hbm,
     inv_leaf_hbm,
-    dense_hbm,
     leaf_hbm,
     group_hbm,
     mid_hbm,
     top_hbm,
     inv_top,
     inv_group,
-    panel_group,
     leaf_solved,
     inv_leaf,
-    dense,
     leaf_out,
     group_out,
     mid_out,
@@ -361,7 +412,6 @@
     residual,
     above,
     sems,
-    panel_sems,
     out_sems,
 ):
     leaf, pos, core = place()
@@ -370,21 +420,17 @@
         (inv_group_hbm, inv_group),
         (leaf_solved_hbm, leaf_solved),
         (inv_leaf_hbm, inv_leaf),
-        (dense_hbm, dense),
     )
     loads = [pltpu.make_async_copy(a, b, sems.at[i]) for i, (a, b) in enumerate(pairs)]
-    for kc, got in enumerate((panel_own_hbm, panel_other_hbm)):
-        target = panel_group.at[:, core ^ kc]
-        loads.append(pltpu.make_async_copy(got, target, panel_sems.at[kc]))
-    for i in (0, 1, 5, 6, 2, 3, 4):
-        loads[i].start()
+    for load in loads:
+        load.start()
     mid_rows = inv_mid.shape[0]
     top_rows = inv_top.shape[0]
     group_rows = inv_group.shape[0]
     supernodes, block, _ = inv_leaf.shape
-    upper_cols = pl.ds(group_rows, mid_rows + top_rows)
-    mid_cols = pl.ds(group_rows, mid_rows)
-    top_cols = pl.ds(group_rows + mid_rows, top_rows)
+    upper_span = pl.ds(group_rows, mid_rows + top_rows)
+    mid_span = pl.ds(group_rows, mid_rows)
+    top_span = pl.ds(group_rows + mid_rows, top_rows)
     sec = (mid_rows + top_rows) // (2 * n_pos)
     q = sec // n_leaf
     gq = group_rows // (2 * n_pos)
@@ -401,45 +447,43 @@
     mid_solved = dot(inv_mid[...], upper[0:mid_rows, :]).astype(BF)
     top_residual = upper[mid_rows:, :].astype(F32) - dot(panel_mid[...], mid_solved)
     loads[0].wait()
-    top_solved = dot(inv_top[...], top_residual.astype(BF))
-    top_t = dot(top_solved.T.astype(BF), inv_top[...])
-    above[:, top_cols] = top_t.astype(BF)
-    top_out[...] = top_t.T
+    top_solved = dot(inv_top[...], top_residual.astype(BF)).astype(BF)
+    top_out[...] = dot(inv_top_t[...], top_solved)
+    above[top_span, :] = top_out[...].astype(BF)
     stores = [pltpu.make_async_copy(top_out, top_hbm, out_sems.at[0])]
     stores[0].start()
-    mid_back = mid_solved.astype(F32).T - dot(above[:, top_cols], panel_mid[...])
-    mid_t = dot(mid_back.astype(BF), inv_mid[...])
-    above[:, mid_cols] = mid_t.astype(BF)
-    mid_out[...] = mid_t.T
+    mid_back = mid_solved.astype(F32) - dot(panel_mid_t[...], above[top_span, :])
+    mid_out[...] = dot(inv_mid_t[...], mid_back.astype(BF))
+    above[mid_span, :] = mid_out[...].astype(BF)
     stores.append(pltpu.make_async_copy(mid_out, mid_hbm, out_sems.at[1]))
     stores[1].start()
     for load in loads[1:]:
         load.wait()
-    group_solved = dot(inv_group[...], residual[...]).astype(BF).astype(F32).T
-    panel = panel_group[...].reshape(mid_rows + top_rows, group_rows)
-    group_back = group_solved - dot(above[:, upper_cols], panel)
-    group_t = dot(group_back.astype(BF), inv_group[...])
-    above[:, 0:group_rows] = group_t.astype(BF)
-    group_out[...] = group_t.T
+    group_solved = dot(inv_group[...], residual[...]).astype(BF).astype(F32)
+    group_back = group_solved - dot(panel_group_t[...], above[upper_span, :])
+    group_out[...] = dot(inv_group_t[...], group_back.astype(BF))
+    above[0:group_rows, :] = group_out[...].astype(BF)
     stores.append(pltpu.make_async_copy(group_out, group_hbm, out_sems.at[2]))
     stores[2].start()
-    for s in range(supernodes):
-        cols = pl.ds(s * block, block)
-        terms = dot(above[...], dense[:, cols])
-        back = (leaf_solved[cols, :].astype(F32).T - terms).astype(BF)
-        leaf_out[cols, :] = dot(back, inv_leaf[s]).T
-    stores.append(pltpu.make_async_copy(leaf_out, leaf_hbm, out_sems.at[3]))
-    stores[3].start()
+    half = supernodes // 2
+    for i in range(2):
+        rows = pl.ds(i * half * block, half * block)
+        terms = dot(dense_t[rows, :], above[...])
+        back = (leaf_solved[rows, :].astype(F32) - terms).astype(BF)
+        for s in range(half):
+            span = pl.ds((i * half + s) * block, block)
+            inverse_t = inv_leaf[i * half + s].T
+            leaf_out[span, :] = dot(inverse_t, back[s * block : (s + 1) * block, :])
+        stores.append(pltpu.make_async_copy(leaf_out.at[rows], leaf_hbm.at[rows], out_sems.at[3 + i]))
+        stores[-1].start()
     for store in stores:
         store.wait()
 
 
 def backward(close, far, n_leaf, n_pos):
-    mine, _, inv_mid, _ = close
-    inv_top, inv_group, panel, _, leaf_solved, inv_leaf, dense = far
+    mine, inv_mid, dense_t = close[0], close[2], close[-1]
+    inv_top, inv_group, leaf_solved, _ = far
     width = mine.shape[-1]
-    held = (inv_top.shape, inv_group.shape, (n_pos, 2) + panel.shape[1:])
-    held += (leaf_solved.shape, inv_leaf.shape, dense.shape)
     outs = (
         leaf_solved.shape,
         (inv_group.shape[0], width),
@@ -451,17 +495,16 @@
         out_shape=[pltpu.HBM(shape, F32) for shape in outs],
         in_specs=[VMEM] * len(close) + [HBM] * len(far),
         out_specs=[HBM] * 4,
-        scratch_shapes=[pltpu.VMEM(shape, BF) for shape in held]
+        scratch_shapes=[pltpu.VMEM(x.shape, BF) for x in far]
         + [pltpu.VMEM(shape, F32) for shape in outs]
         + [
             pltpu.VMEM((inv_mid.shape[0] + inv_top.shape[0], width), BF),
             pltpu.VMEM((inv_group.shape[0], width), BF),
-            pltpu.VMEM((width, dense.shape[0]), BF),
+            pltpu.VMEM((dense_t.shape[1], width), BF),
+            pltpu.SemaphoreType.DMA((4,)),
             pltpu.SemaphoreType.DMA((5,)),
-            pltpu.SemaphoreType.DMA((2,)),
-            pltpu.SemaphoreType.DMA((len(outs),)),
         ],
-        compiler_params=pltpu.CompilerParams(vmem_limit_bytes=BIG),
+        compiler_params=pltpu.CompilerParams(vmem_limit_bytes=BIG // 2),
         name="backward",
     )(*in_vmem(*close), *in_hbm(*far))
 
@@ -537,30 +580,42 @@
     with jax.named_scope("gather_middle_panel"):
         if by_parts:
             middles = swaps(stack(after(middles, send)), "leaf", n_leaf)
-            recv = after(recv, (middles, rhs_mine, group_mine))
-            middle = stack(middles)
+            recv = after(recv, middles)
+    turns = (
+        turned(inv_middle, "turn_inv_middle"),
+        turned(inv_top, "turn_inv_top"),
+        turned(inv_group[0], "turn_inv_group"),
+        turned(dense, "turn_dense"),
+    )
+    recv = after(recv, (turns, rhs_mine, group_mine))
+    if by_parts:
+        middle = stack(after(middles, (turns, rhs_mine, group_mine)))
+        middle, panel = lax.optimization_barrier((middle, panel))
     parts, group = fold(keep, recv, inv_group[0], rhs_group[0], panel, n_leaf)
     with jax.named_scope("sum_over_leaf"):
         parts = parts[:1] + [swap(parts[k], "leaf", n_leaf, k) for k in range(1, n_leaf)]
     with jax.named_scope("gather_middle_panel"):
         if by_parts:
-            middle = weave(middle, swap(middle, "grp", n_grp, 1), n_leaf, n_pos)
+            middle, middle_t = weave(middle, swap(middle, "grp", n_grp, 1), n_leaf, n_pos)
+        else:
+            middle_t = turned(middle, "turn_middle")
     sends = sum_leaf(after(parts, middle), group, n_pos)
     with jax.named_scope("sum_over_pos"):
         got = sends[:1] + [swap(sends[k], "grp", n_grp, 2 * k) for k in range(1, n_pos)]
     with jax.named_scope("swap_group_panel"):
-        panel_other = swap(panel, "grp", n_grp, 1)
+        panel_other = swap(after(panel, group), "grp", n_grp, 1)
     residual = sum_pos(rhs_mine, group_mine, got)
     with jax.named_scope("gather_pos"):
         uppers, groups = stack_pos(swaps(residual, "grp", n_grp, 2), q)
     with jax.named_scope("gather_leaf"):
         stacks = swaps(uppers, "leaf", n_leaf)
+    panel_t = weave_group(panel, panel_other)
     with jax.named_scope("gather_cores"):
-        mine = stack(after(stacks, panel_other) + [groups])
+        mine = stack(after(stacks, panel_t) + [groups])
         theirs = swap(mine, "grp", n_grp, 1)
     leaf_out, group_out, mid_out, top_out = backward(
-        (mine, theirs, inv_middle, middle),
-        (inv_top, inv_group[0], panel, panel_other, leaf_solved, inv_leaf[0], dense),
+        (mine, theirs, inv_middle) + turns[:3] + (middle, middle_t, panel_t, turns[3]),
+        (inv_top, inv_group[0], leaf_solved, inv_leaf[0]),
         n_leaf,
         n_pos,
     )

time: 103 us -> 115 us (1.12)
  waiting for transfers between devices: 33.7 us -> 17.4 us
  local copies, waits for them, and re-layouts: 1.9 us -> 16.3 us
  Pallas kernels: 25 us -> 38.5 us
    ppermute x22, waiting for transfers between devices: 31.2 us -> 16.7 us  [swap(): return lax.ppermute(x, axis, [(i, i ^ bits) for i in range(size)])]
    unnamed x8 -> x44, local copies, waits for them, and re-layouts: 1.06 us -> 15.5 us
    pallas_call x1 -> x5, Pallas kernels: 3.19 us -> 11.8 us  [the longest x4 9.62 us: turned(): pl.pallas_call(turned_kernel, out_shape=pltpu.VMEM(x.shape[::-1], BF), in...]
    pallas_call x7 -> x8, Pallas kernels: 0.4 us -> 3.58 us  [small(): pl.pallas_call(kernel, out_shape=[pltpu.VMEM(shape, BF) for shape in shap...]
    all_gather x1, waiting for transfers between devices: 1.78 us -> 0.01 us  [body(): panel = lax.all_gather(group_panel[0], 'grp', axis_index_groups=pos_groups)]
    pallas_call x1, Pallas kernels: 12 us -> 13.4 us  [backward(): pl.pallas_call(functools.partial(backward_kernel, n_leaf, n_pos), out_sha...]
  transfers between devices with their start and end apart: 23 -> 23, of which waited for: 14 -> 10; matrix products, arithmetic and copies ran while one was open for 2% -> 2% of each run, Pallas kernels for 13% -> 22%
where the time goes in v7:
time: 115 us; the launch traced here: 114 us
  Pallas kernels  38.5 us (33%)
  starting transfers between devices  26 us (23%)
  waiting for transfers between devices  17.4 us (15%)
  local copies, waits for them, and re-layouts  16.3 us (14%)
  between operations  15 us (13%)
    ppermute x22, starting transfers between devices, swap(): return lax.ppermute(x, axis, [(i, i ^ bits) for i in range(size)])  26 us
    ppermute x22, waiting for transfers between devices, swap(): return lax.ppermute(x, axis, [(i, i ^ bits) for i in range(size)])  16.7 us
    unnamed x44, local copies, waits for them, and re-layouts  15.5 us
    pallas_call x1, Pallas kernels, backward(): pl.pallas_call(functools.partial(backward_kernel, n_leaf, n_pos), out_sha...  13.4 us
    pallas_call x1, Pallas kernels, leaf_forward(): pl.pallas_call(functools.partial(forward_kernel, sec, group_cols), out_sh...  9.74 us
    pallas_call x4, Pallas kernels, turned(): pl.pallas_call(turned_kernel, out_shape=pltpu.VMEM(x.shape[::-1], BF), in...  9.62 us
    pallas_call x8, Pallas kernels, small(): pl.pallas_call(kernel, out_shape=[pltpu.VMEM(shape, BF) for shape in shap...  3.58 us
  transfers between devices with their start and end apart: 23, of which 10 were waited for; matrix products, arithmetic and copies ran while one was open for 2% of the time, Pallas kernels for 22%

profile of v7, /device:TPU:0, one launch (start us, length us, event | category | flops | bytes accessed | tf_op | source)
XLA Modules:
  0.0 114.1 jit_solution(1843114957679970034)
XLA Ops:
  7.9 5.1 %collective-permute-start.2 = (bf16[32,1024]{1,0:T(8,128)(2,1)}, bf16[32,1024]{1,0:T(8,128)(2,1)S(1)}, u32[]{:S(2)}, u32[]{:S(2)}) collective-permute-start(bf16[32,1024]{1,0:T(8,128)(2,1)} %refs_0_), channel_id=1, source_target_pairs={{0,6},{1,7},{2,4},{3,5},{4,2},{5,3},{6,0},{7,1},{8,14},{9,15},{10,... | collective-permute-start | bytes 196616 | tf_op jit(solution)/shard_map/gather_middle_panel/ppermute | solution.py:513
  14.3 9.7 %leaf_forward.1 = (bf16[1536,256]{1,0:T(8,128)(2,1)S(1)}, bf16[1536,256]{1,0:T(8,128)(2,1)}, bf16[1024,256]{1,0:T(8,128)(2,1)}, bf16[2560,1024]{1,0:T(8,128)(2,1)}) custom-call(s32[1,1]{1,0:T(1,128)S(6)} %copy.18.count_hbm, s32[1,256]{1,0:T(1,128)} %cols_hbm.1, s32[1,256]{1,0:T(1,128)} %tgts_hbm.1, f32[1024,256]{1,0:T(8,128)} %bitcast.18, ...), custom_call_target="tpu_custom_call" | custom-call | tf_op jit(solution)/shard_map/leaf_forward/pallas_call | solution.py:163
  25.1 2.1 %collective-permute-start.6 = (bf16[128,1024]{1,0:T(8,128)(2,1)S(1)}, bf16[128,1024]{1,0:T(8,128)(2,1)S(1)}, u32[]{:S(2)}, u32[]{:S(2)}) collective-permute-start(bf16[128,1024]{1,0:T(8,128)(2,1)S(1)} %stack.3.refs_0_), channel_id=1, source_target_pairs={{0,24},{8,16},{16,8},{24,0},{1,25},{9,17},{17,9},{25,1},{2,26},{10... | collective-permute-start | bytes 786440 | tf_op jit(solution)/shard_map/gather_middle_panel/ppermute | solution.py:513
  30.7 2.2 %turn_inv_middle.1.inv_mid_t = bf16[1024,1024]{1,0:T(8,128)(2,1)S(1)} custom-call(bf16[1024,1024]{1,0:T(8,128)(2,1)} %inv_mid.1), custom_call_target="tpu_custom_call" | custom-call | flops 1 | bytes 1 | tf_op jit(solution)/shard_map/turn_inv_middle/pallas_call | solution.py:370
  32.9 2.2 %turn_inv_top.1.inv_top_t = bf16[1024,1024]{1,0:T(8,128)(2,1)S(1)} custom-call(bf16[1024,1024]{1,0:T(8,128)(2,1)} %inv_top_hbm.1), custom_call_target="tpu_custom_call" | custom-call | flops 1 | bytes 1 | tf_op jit(solution)/shard_map/turn_inv_top/pallas_call | solution.py:370
  35.2 1.3 %copy-done.2 = bf16[1024,1024]{1,0:T(8,128)(2,1)} copy-done((bf16[1024,1024]{1,0:T(8,128)(2,1)}, bf16[1024,1024]{1,0:T(8,128)(2,1)S(1)}, u32[]{:S(2)}) %copy-start.2) | copy-done | bytes 2097176
  36.5 3.9 %turn_dense.1.dense_t = bf16[1024,2560]{1,0:T(8,128)(2,1)S(1)} custom-call(bf16[2560,1024]{1,0:T(8,128)(2,1)} %get-tuple-element.55.source_hbm), custom_call_target="tpu_custom_call" | custom-call | flops 1 | bytes 1 | tf_op jit(solution)/shard_map/turn_dense/pallas_call | solution.py:370
  40.4 2.3 %copy-done = bf16[1024,2560]{1,0:T(8,128)(2,1)} copy-done((bf16[1024,2560]{1,0:T(8,128)(2,1)}, bf16[1024,2560]{1,0:T(8,128)(2,1)S(1)}, u32[]{:S(2)}) %copy-start) | copy-done | bytes 5242904
  53.8 2.5 %fold_group.1 = (bf16[256,256]{1,0:T(8,128)(2,1)S(1)}, bf16[256,256]{1,0:T(8,128)(2,1)S(1)}, bf16[256,256]{1,0:T(8,128)(2,1)S(1)}, bf16[256,256]{1,0:T(8,128)(2,1)S(1)}, bf16[256,256]{1,0:T(8,128)(2,1)S(1)}) custom-call(bf16[1536,256]{1,0:T(8,128)(2,1)S(1)} %copy-done.10, bf16[1536,256]{1,0:T(8,128)(2,1)} %collective-permute-done.3.recv, ...), custom_call_target="tpu_custom_call" | custom-call | tf_op jit(solution)/shard_map/fold_group/pallas_call | solution.py:30
  57.7 1.9 %collective-permute-start.8 = (bf16[256,256]{1,0:T(8,128)(2,1)S(1)}, bf16[256,256]{1,0:T(8,128)(2,1)S(1)}, u32[]{:S(2)}, u32[]{:S(2)}) collective-permute-start(bf16[256,256]{1,0:T(8,128)(2,1)S(1)} %get-tuple-element.64), channel_id=1, source_target_pairs={{0,16},{8,24},{16,0},{24,8},{1,17},{9,25},{17,1},{25,9},{2,18},{10... | collective-permute-start | bytes 393224 | tf_op jit(solution)/shard_map/sum_over_leaf/ppermute | solution.py:513
  61.2 2.1 %collective-permute-done.7.refs_1_ = bf16[256,256]{1,0:T(8,128)(2,1)S(1)} collective-permute-done((bf16[256,256]{1,0:T(8,128)(2,1)S(1)}, bf16[256,256]{1,0:T(8,128)(2,1)S(1)}, u32[]{:S(2)}, u32[]{:S(2)}) %collective-permute-start.7) | collective-permute-done | bytes 131104 | tf_op jit(solution)/shard_map/sum_over_leaf/ppermute | solution.py:513
  63.3 1.8 %collective-permute-done.8.refs_2_ = bf16[256,256]{1,0:T(8,128)(2,1)S(1)} collective-permute-done((bf16[256,256]{1,0:T(8,128)(2,1)S(1)}, bf16[256,256]{1,0:T(8,128)(2,1)S(1)}, u32[]{:S(2)}, u32[]{:S(2)}) %collective-permute-start.8) | collective-permute-done | bytes 131104 | tf_op jit(solution)/shard_map/sum_over_leaf/ppermute | solution.py:513
  66.2 1.4 %collective-permute-start.11 = (bf16[128,256]{1,0:T(8,128)(2,1)S(1)}, bf16[128,256]{1,0:T(8,128)(2,1)S(1)}, u32[]{:S(2)}, u32[]{:S(2)}) collective-permute-start(bf16[128,256]{1,0:T(8,128)(2,1)S(1)} %get-tuple-element.74), channel_id=1, source_target_pairs={{0,2},{1,3},{2,0},{3,1},{4,6},{5,7},{6,4},{7,5},{8,10},{9,11},{10,... | collective-permute-start | bytes 196616 | tf_op jit(solution)/shard_map/sum_over_pos/ppermute | solution.py:513
  67.6 3.0 %collective-permute-start.12 = (bf16[128,256]{1,0:T(8,128)(2,1)S(1)}, bf16[128,256]{1,0:T(8,128)(2,1)S(1)}, u32[]{:S(2)}, u32[]{:S(2)}) collective-permute-start(bf16[128,256]{1,0:T(8,128)(2,1)S(1)} %get-tuple-element.75), channel_id=1, source_target_pairs={{0,4},{1,5},{2,6},{3,7},{4,0},{5,1},{6,2},{7,3},{8,12},{9,13},{10,... | collective-permute-start | bytes 196616 | tf_op jit(solution)/shard_map/sum_over_pos/ppermute | solution.py:513
  71.1 3.5 %collective-permute-done.12.refs_2_ = bf16[128,256]{1,0:T(8,128)(2,1)S(1)} collective-permute-done((bf16[128,256]{1,0:T(8,128)(2,1)S(1)}, bf16[128,256]{1,0:T(8,128)(2,1)S(1)}, u32[]{:S(2)}, u32[]{:S(2)}) %collective-permute-start.12) | collective-permute-done | bytes 65568 | tf_op jit(solution)/shard_map/sum_over_pos/ppermute | solution.py:513
  74.6 2.1 %collective-permute-done.13.refs_3_ = bf16[128,256]{1,0:T(8,128)(2,1)S(1)} collective-permute-done((bf16[128,256]{1,0:T(8,128)(2,1)S(1)}, bf16[128,256]{1,0:T(8,128)(2,1)S(1)}, u32[]{:S(2)}, u32[]{:S(2)}) %collective-permute-start.13) | collective-permute-done | bytes 65568 | tf_op jit(solution)/shard_map/sum_over_pos/ppermute | solution.py:513
  77.8 3.4 %collective-permute-start.14 = (bf16[128,256]{1,0:T(8,128)(2,1)S(1)}, bf16[128,256]{1,0:T(8,128)(2,1)S(1)}, u32[]{:S(2)}, u32[]{:S(2)}) collective-permute-start(bf16[128,256]{1,0:T(8,128)(2,1)S(1)} %sum_pos.1.refs_0_), channel_id=1, source_target_pairs={{0,2},{1,3},{2,0},{3,1},{4,6},{5,7},{6,4},{7,5},{8,10},{9,11},{10,... | collective-permute-start | bytes 196616 | tf_op jit(solution)/shard_map/gather_pos/ppermute | solution.py:513
  81.2 1.8 %collective-permute-done.16.refs_3_ = bf16[128,256]{1,0:T(8,128)(2,1)S(1)} collective-permute-done((bf16[128,256]{1,0:T(8,128)(2,1)S(1)}, bf16[128,256]{1,0:T(8,128)(2,1)S(1)}, u32[]{:S(2)}, u32[]{:S(2)}) %collective-permute-start.16) | collective-permute-done | bytes 65568 | tf_op jit(solution)/shard_map/gather_pos/ppermute | solution.py:513
  82.9 1.3 %collective-permute-done.15.refs_2_ = bf16[128,256]{1,0:T(8,128)(2,1)S(1)} collective-permute-done((bf16[128,256]{1,0:T(8,128)(2,1)S(1)}, bf16[128,256]{1,0:T(8,128)(2,1)S(1)}, u32[]{:S(2)}, u32[]{:S(2)}) %collective-permute-start.15) | collective-permute-done | bytes 65568 | tf_op jit(solution)/shard_map/gather_pos/ppermute | solution.py:513
  84.3 1.7 %collective-permute-start.19 = (bf16[256,256]{1,0:T(8,128)(2,1)S(1)}, bf16[256,256]{1,0:T(8,128)(2,1)S(1)}, u32[]{:S(2)}, u32[]{:S(2)}) collective-permute-start(bf16[256,256]{1,0:T(8,128)(2,1)S(1)} %get-tuple-element.79.refs_0_), channel_id=1, source_target_pairs={{0,24},{8,16},{16,8},{24,0},{1,25},{9,17},{17,9},{25,1},{2,26},{10... | collective-permute-start | bytes 393224 | tf_op jit(solution)/shard_map/gather_leaf/ppermute | solution.py:513
  86.5 1.4 %collective-permute-start.17 = (bf16[256,256]{1,0:T(8,128)(2,1)S(1)}, bf16[256,256]{1,0:T(8,128)(2,1)S(1)}, u32[]{:S(2)}, u32[]{:S(2)}) collective-permute-start(bf16[256,256]{1,0:T(8,128)(2,1)S(1)} %get-tuple-element.79.refs_0_), channel_id=1, source_target_pairs={{0,8},{8,0},{16,24},{24,16},{1,9},{9,1},{17,25},{25,17},{2,10},{10... | collective-permute-start | bytes 393224 | tf_op jit(solution)/shard_map/gather_leaf/ppermute | solution.py:513
  88.9 2.2 %weave_group.1.panel_group_t = bf16[512,2048]{1,0:T(8,128)(2,1)S(1)} custom-call(bf16[4,256,512]{2,1,0:T(8,128)(2,1)} %all-gather.2.cloned.1.call-done.panel.own, bf16[4,256,512]{2,1,0:T(8,128)(2,1)} %copy-done.19), custom_call_target="tpu_custom_call" | custom-call | bytes 6291456 | tf_op jit(solution)/shard_map/weave_group/pallas_call | solution.py:345
  91.8 2.1 %collective-permute-done.21.theirs = bf16[1280,256]{1,0:T(8,128)(2,1)S(1)} collective-permute-done((bf16[1280,256]{1,0:T(8,128)(2,1)S(1)}, bf16[1280,256]{1,0:T(8,128)(2,1)S(1)}, u32[]{:S(2)}, u32[]{:S(2)}) %collective-permute-start.21) | collective-permute-done | bytes 655392 | tf_op jit(solution)/shard_map/gather_cores/ppermute | solution.py:513
  93.9 13.4 %backward.1 = (f32[1024,256]{1,0:T(8,128)}, f32[512,256]{1,0:T(8,128)}, f32[1024,256]{1,0:T(8,128)}, f32[1024,256]{1,0:T(8,128)}) custom-call(bf16[1280,256]{1,0:T(8,128)(2,1)S(1)} %stack.5.mine, bf16[1280,256]{1,0:T(8,128)(2,1)S(1)} %collective-permute-done.21.theirs, bf16[1024,1024]{1,0:T(8,128)(2,1)S(1)} %copy-done.1, ...), custom_call_target="tpu_custom_call" | custom-call | tf_op jit(solution)/shard_map/backward/pallas_call | solution.py:493
  (85 shorter events, 24.7 us)
Async XLA Ops:
  7.2 43.4 %all-gather.2.cloned.1.call-start = ((), (), s32[]{:S(2)}) async-start(), calls=%async_computation | async-start | bytes 1310720 | tf_op jit(solution)/shard_map/gather_group_panel/all_gather | solution.py:553
  7.9 17.0 %collective-permute-start.2 = (bf16[32,1024]{1,0:T(8,128)(2,1)}, bf16[32,1024]{1,0:T(8,128)(2,1)S(1)}, u32[]{:S(2)}, u32[]{:S(2)}) collective-permute-start(bf16[32,1024]{1,0:T(8,128)(2,1)} %refs_0_), channel_id=1, source_target_pairs={{0,6},{1,7},{2,4},{3,5},{4,2},{5,3},{6,0},{7,1},{8,14},{9,15},{10,... | collective-permute-start | bytes 196616 | tf_op jit(solution)/shard_map/gather_middle_panel/ppermute | solution.py:513
  13.0 11.9 %collective-permute-start.1 = (bf16[32,1024]{1,0:T(8,128)(2,1)}, bf16[32,1024]{1,0:T(8,128)(2,1)S(1)}, u32[]{:S(2)}, u32[]{:S(2)}) collective-permute-start(bf16[32,1024]{1,0:T(8,128)(2,1)} %refs_0_), channel_id=1, source_target_pairs={{0,4},{1,5},{2,6},{3,7},{4,0},{5,1},{6,2},{7,3},{8,12},{9,13},{10,... | collective-permute-start | bytes 196616 | tf_op jit(solution)/shard_map/gather_middle_panel/ppermute | solution.py:513
  13.0 11.9 %collective-permute-start = (bf16[32,1024]{1,0:T(8,128)(2,1)}, bf16[32,1024]{1,0:T(8,128)(2,1)S(1)}, u32[]{:S(2)}, u32[]{:S(2)}) collective-permute-start(bf16[32,1024]{1,0:T(8,128)(2,1)} %refs_0_), channel_id=1, source_target_pairs={{0,2},{1,3},{2,0},{3,1},{4,6},{5,7},{6,4},{7,5},{8,10},{9,11},{10,... | collective-permute-start | bytes 196616 | tf_op jit(solution)/shard_map/gather_middle_panel/ppermute | solution.py:513
  25.0 25.6 %collective-permute-start.3 = (bf16[1536,256]{1,0:T(8,128)(2,1)}, bf16[1536,256]{1,0:T(8,128)(2,1)}, u32[]{:S(2)}, u32[]{:S(2)}) collective-permute-start(bf16[1536,256]{1,0:T(8,128)(2,1)} %get-tuple-element.49), channel_id=1, source_target_pairs={{0,1},{1,0},{2,3},{3,2},{4,5},{5,4},{6,7},{7,6},{8,9},{9,8},{10,11... | collective-permute-start | bytes 2359304 | tf_op jit(solution)/shard_map/swap_cores/ppermute | solution.py:513
  25.1 19.5 %collective-permute-start.6 = (bf16[128,1024]{1,0:T(8,128)(2,1)S(1)}, bf16[128,1024]{1,0:T(8,128)(2,1)S(1)}, u32[]{:S(2)}, u32[]{:S(2)}) collective-permute-start(bf16[128,1024]{1,0:T(8,128)(2,1)S(1)} %stack.3.refs_0_), channel_id=1, source_target_pairs={{0,24},{8,16},{16,8},{24,0},{1,25},{9,17},{17,9},{25,1},{2,26},{10... | collective-permute-start | bytes 786440 | tf_op jit(solution)/shard_map/gather_middle_panel/ppermute | solution.py:513
  27.2 18.1 %collective-permute-start.5 = (bf16[128,1024]{1,0:T(8,128)(2,1)S(1)}, bf16[128,1024]{1,0:T(8,128)(2,1)S(1)}, u32[]{:S(2)}, u32[]{:S(2)}) collective-permute-start(bf16[128,1024]{1,0:T(8,128)(2,1)S(1)} %stack.3.refs_0_), channel_id=1, source_target_pairs={{0,16},{8,24},{16,0},{24,8},{1,17},{9,25},{17,1},{25,9},{2,18},{10... | collective-permute-start | bytes 786440 | tf_op jit(solution)/shard_map/gather_middle_panel/ppermute | solution.py:513
  27.4 18.6 %collective-permute-start.4 = (bf16[128,1024]{1,0:T(8,128)(2,1)S(1)}, bf16[128,1024]{1,0:T(8,128)(2,1)S(1)}, u32[]{:S(2)}, u32[]{:S(2)}) collective-permute-start(bf16[128,1024]{1,0:T(8,128)(2,1)S(1)} %stack.3.refs_0_), channel_id=1, source_target_pairs={{0,8},{8,0},{16,24},{24,16},{1,9},{9,1},{17,25},{25,17},{2,10},{10... | collective-permute-start | bytes 786440 | tf_op jit(solution)/shard_map/gather_middle_panel/ppermute | solution.py:513
  49.5 44.4 %slice-start = ((s8[5242880]{0:T(1024)(128)(4,1)}), s8[1048576]{0:T(1024)(128)(4,1)S(1)}, s32[]{:S(2)}) async-start(s8[5242880]{0:T(1024)(128)(4,1)} %bitcast.9), calls=%async_computation.1 | async-start | bytes 2097152
  50.6 9.8 %collective-permute-start.10 = (bf16[512,1024]{1,0:T(8,128)(2,1)}, bf16[512,1024]{1,0:T(8,128)(2,1)S(1)}, u32[]{:S(2)}, u32[]{:S(2)}) collective-permute-start(bf16[512,1024]{1,0:T(8,128)(2,1)} %copy-done.5), channel_id=1, source_target_pairs={{0,1},{1,0},{2,3},{3,2},{4,5},{5,4},{6,7},{7,6},{8,9},{9,8},{10,11... | collective-permute-start | bytes 3145736 | tf_op jit(solution)/shard_map/gather_middle_panel/ppermute | solution.py:513
  56.4 31.5 %collective-permute-start.20 = (bf16[4,256,512]{2,1,0:T(8,128)(2,1)}, bf16[4,256,512]{2,1,0:T(8,128)(2,1)S(1)}, u32[]{:S(2)}, u32[]{:S(2)}) collective-permute-start(bf16[4,256,512]{2,1,0:T(8,128)(2,1)} %all-gather.2.cloned.1.call-done.panel.own), channel_id=1, source_target_pairs={{0,1},{1,0},{2,3},{3,2},{4,5},{5,4},{6,7},{7,6},{8,9},{9,8},{10,11... | collective-permute-start | bytes 3145736 | tf_op jit(solution)/shard_map/swap_group_panel/ppermute | solution.py:513
  56.9 6.4 %collective-permute-start.7 = (bf16[256,256]{1,0:T(8,128)(2,1)S(1)}, bf16[256,256]{1,0:T(8,128)(2,1)S(1)}, u32[]{:S(2)}, u32[]{:S(2)}) collective-permute-start(bf16[256,256]{1,0:T(8,128)(2,1)S(1)} %get-tuple-element.63), channel_id=1, source_target_pairs={{0,8},{8,0},{16,24},{24,16},{1,9},{9,1},{17,25},{25,17},{2,10},{10... | collective-permute-start | bytes 393224 | tf_op jit(solution)/shard_map/sum_over_leaf/ppermute | solution.py:513
  57.7 7.4 %collective-permute-start.8 = (bf16[256,256]{1,0:T(8,128)(2,1)S(1)}, bf16[256,256]{1,0:T(8,128)(2,1)S(1)}, u32[]{:S(2)}, u32[]{:S(2)}) collective-permute-start(bf16[256,256]{1,0:T(8,128)(2,1)S(1)} %get-tuple-element.64), channel_id=1, source_target_pairs={{0,16},{8,24},{16,0},{24,8},{1,17},{9,25},{17,1},{25,9},{2,18},{10... | collective-permute-start | bytes 393224 | tf_op jit(solution)/shard_map/sum_over_leaf/ppermute | solution.py:513
  59.6 6.6 %collective-permute-start.9 = (bf16[256,256]{1,0:T(8,128)(2,1)S(1)}, bf16[256,256]{1,0:T(8,128)(2,1)S(1)}, u32[]{:S(2)}, u32[]{:S(2)}) collective-permute-start(bf16[256,256]{1,0:T(8,128)(2,1)S(1)} %get-tuple-element.65), channel_id=1, source_target_pairs={{0,24},{8,16},{16,8},{24,0},{1,25},{9,17},{17,9},{25,1},{2,26},{10... | collective-permute-start | bytes 393224 | tf_op jit(solution)/shard_map/sum_over_leaf/ppermute | solution.py:513
  66.2 4.9 %collective-permute-start.11 = (bf16[128,256]{1,0:T(8,128)(2,1)S(1)}, bf16[128,256]{1,0:T(8,128)(2,1)S(1)}, u32[]{:S(2)}, u32[]{:S(2)}) collective-permute-start(bf16[128,256]{1,0:T(8,128)(2,1)S(1)} %get-tuple-element.74), channel_id=1, source_target_pairs={{0,2},{1,3},{2,0},{3,1},{4,6},{5,7},{6,4},{7,5},{8,10},{9,11},{10,... | collective-permute-start | bytes 196616 | tf_op jit(solution)/shard_map/sum_over_pos/ppermute | solution.py:513
  67.6 7.0 %collective-permute-start.12 = (bf16[128,256]{1,0:T(8,128)(2,1)S(1)}, bf16[128,256]{1,0:T(8,128)(2,1)S(1)}, u32[]{:S(2)}, u32[]{:S(2)}) collective-permute-start(bf16[128,256]{1,0:T(8,128)(2,1)S(1)} %get-tuple-element.75), channel_id=1, source_target_pairs={{0,4},{1,5},{2,6},{3,7},{4,0},{5,1},{6,2},{7,3},{8,12},{9,13},{10,... | collective-permute-start | bytes 196616 | tf_op jit(solution)/shard_map/sum_over_pos/ppermute | solution.py:513
  70.6 6.1 %collective-permute-start.13 = (bf16[128,256]{1,0:T(8,128)(2,1)S(1)}, bf16[128,256]{1,0:T(8,128)(2,1)S(1)}, u32[]{:S(2)}, u32[]{:S(2)}) collective-permute-start(bf16[128,256]{1,0:T(8,128)(2,1)S(1)} %get-tuple-element.76), channel_id=1, source_target_pairs={{0,6},{1,7},{2,4},{3,5},{4,2},{5,3},{6,0},{7,1},{8,14},{9,15},{10,... | collective-permute-start | bytes 196616 | tf_op jit(solution)/shard_map/sum_over_pos/ppermute | solution.py:513
  76.7 6.2 %collective-permute-start.16 = (bf16[128,256]{1,0:T(8,128)(2,1)S(1)}, bf16[128,256]{1,0:T(8,128)(2,1)S(1)}, u32[]{:S(2)}, u32[]{:S(2)}) collective-permute-start(bf16[128,256]{1,0:T(8,128)(2,1)S(1)} %sum_pos.1.refs_0_), channel_id=1, source_target_pairs={{0,6},{1,7},{2,4},{3,5},{4,2},{5,3},{6,0},{7,1},{8,14},{9,15},{10,... | collective-permute-start | bytes 196616 | tf_op jit(solution)/shard_map/gather_pos/ppermute | solution.py:513
  77.8 6.4 %collective-permute-start.15 = (bf16[128,256]{1,0:T(8,128)(2,1)S(1)}, bf16[128,256]{1,0:T(8,128)(2,1)S(1)}, u32[]{:S(2)}, u32[]{:S(2)}) collective-permute-start(bf16[128,256]{1,0:T(8,128)(2,1)S(1)} %sum_pos.1.refs_0_), channel_id=1, source_target_pairs={{0,4},{1,5},{2,6},{3,7},{4,0},{5,1},{6,2},{7,3},{8,12},{9,13},{10,... | collective-permute-start | bytes 196616 | tf_op jit(solution)/shard_map/gather_pos/ppermute | solution.py:513
  77.8 6.4 %collective-permute-start.14 = (bf16[128,256]{1,0:T(8,128)(2,1)S(1)}, bf16[128,256]{1,0:T(8,128)(2,1)S(1)}, u32[]{:S(2)}, u32[]{:S(2)}) collective-permute-start(bf16[128,256]{1,0:T(8,128)(2,1)S(1)} %sum_pos.1.refs_0_), channel_id=1, source_target_pairs={{0,2},{1,3},{2,0},{3,1},{4,6},{5,7},{6,4},{7,5},{8,10},{9,11},{10,... | collective-permute-start | bytes 196616 | tf_op jit(solution)/shard_map/gather_pos/ppermute | solution.py:513
  84.3 6.7 %collective-permute-start.19 = (bf16[256,256]{1,0:T(8,128)(2,1)S(1)}, bf16[256,256]{1,0:T(8,128)(2,1)S(1)}, u32[]{:S(2)}, u32[]{:S(2)}) collective-permute-start(bf16[256,256]{1,0:T(8,128)(2,1)S(1)} %get-tuple-element.79.refs_0_), channel_id=1, source_target_pairs={{0,24},{8,16},{16,8},{24,0},{1,25},{9,17},{17,9},{25,1},{2,26},{10... | collective-permute-start | bytes 393224 | tf_op jit(solution)/shard_map/gather_leaf/ppermute | solution.py:513
  86.0 5.7 %collective-permute-start.18 = (bf16[256,256]{1,0:T(8,128)(2,1)S(1)}, bf16[256,256]{1,0:T(8,128)(2,1)S(1)}, u32[]{:S(2)}, u32[]{:S(2)}) collective-permute-start(bf16[256,256]{1,0:T(8,128)(2,1)S(1)} %get-tuple-element.79.refs_0_), channel_id=1, source_target_pairs={{0,16},{8,24},{16,0},{24,8},{1,17},{9,25},{17,1},{25,9},{2,18},{10... | collective-permute-start | bytes 393224 | tf_op jit(solution)/shard_map/gather_leaf/ppermute | solution.py:513
  86.5 5.2 %collective-permute-start.17 = (bf16[256,256]{1,0:T(8,128)(2,1)S(1)}, bf16[256,256]{1,0:T(8,128)(2,1)S(1)}, u32[]{:S(2)}, u32[]{:S(2)}) collective-permute-start(bf16[256,256]{1,0:T(8,128)(2,1)S(1)} %get-tuple-element.79.refs_0_), channel_id=1, source_target_pairs={{0,8},{8,0},{16,24},{24,16},{1,9},{9,1},{17,25},{25,17},{2,10},{10... | collective-permute-start | bytes 393224 | tf_op jit(solution)/shard_map/gather_leaf/ppermute | solution.py:513
  91.7 2.2 %collective-permute-start.21 = (bf16[1280,256]{1,0:T(8,128)(2,1)S(1)}, bf16[1280,256]{1,0:T(8,128)(2,1)S(1)}, u32[]{:S(2)}, u32[]{:S(2)}) collective-permute-start(bf16[1280,256]{1,0:T(8,128)(2,1)S(1)} %stack.5.mine), channel_id=1, source_target_pairs={{0,1},{1,0},{2,3},{3,2},{4,5},{5,4},{6,7},{7,6},{8,9},{9,8},{10,11... | collective-permute-start | bytes 1966088 | tf_op jit(solution)/shard_map/gather_cores/ppermute | solution.py:513
  (21 other events, 95.9 us)
Sparse Core Ops, SparseCore 0:
  9.6 30.6 all-gather.1

commit v8 on v6

--- a/solution.py
+++ b/solution.py
@@ -57,7 +57,8 @@
     inv_hbm,
     tiles_hbm,
     keep,
-    send,
+    send_low,
+    send_high,
     solved_hbm,
     dense_hbm,
     count,
@@ -149,7 +150,9 @@
                 begin = group_cols + (section // 2) * sec
                 stage[(section % 2) ^ core, begin : begin + sec, :] = total[q : q + sec, :]
     keep[...] = stage[0]
-    send[...] = stage[1]
+    cut = send_low.shape[0]
+    send_low[...] = stage[1, 0:cut, :]
+    send_high[...] = stage[1, cut:, :]
     for store in stores:
         store.wait()
 
@@ -164,12 +167,13 @@
         functools.partial(forward_kernel, sec, group_cols),
         out_shape=(
             pltpu.VMEM((half, width), BF),
-            pltpu.VMEM((half, width), BF),
+            pltpu.VMEM((half // 2, width), BF),
+            pltpu.VMEM((half // 2, width), BF),
             pltpu.HBM((supernodes * block, width), BF),
             pltpu.HBM((targets * block, supernodes * block), BF),
         ),
         in_specs=[HBM] * 6,
-        out_specs=(VMEM, VMEM, HBM, HBM),
+        out_specs=(VMEM, VMEM, VMEM, HBM, HBM),
         scratch_shapes=[
             pltpu.SMEM(count.shape, count.dtype),
             pltpu.SMEM(cols.shape, cols.dtype),
@@ -202,32 +206,27 @@
     return total
 
 
-def fold_kernel(n_leaf, n_pos, keep, recv, inv, rhs, panel_hbm, *refs):
-    parts, group, (gsum, stage, panel, sems) = refs[:n_leaf], refs[n_leaf], refs[n_leaf + 1 :]
-    loads = [
-        pltpu.make_async_copy(panel_hbm.at[p], panel.at[p], sems.at[p]) for p in range(n_pos)
-    ]
-    for load in loads:
-        load.start()
-    leaf, pos, core = place()
+def fold_kernel(n_leaf, n_pos, keep, low, high, inv, rhs, panel, *refs):
+    parts, group, (gsum, stage) = refs[:n_leaf], refs[n_leaf], refs[n_leaf + 1 :]
+    leaf, _, core = place()
     group_cols = inv.shape[0]
     sec = panel.shape[1]
     q = sec // n_leaf
-    gq = group_cols // (2 * n_pos)
-    gsum[...] = keep[0:group_cols, :].astype(F32) + recv[0:group_cols, :].astype(F32)
+    cut = low.shape[0]
+
+    def both(begin, rows):
+        recv = low[begin : begin + rows, :] if begin < cut else high[begin - cut : begin - cut + rows, :]
+        return keep[begin : begin + rows, :].astype(F32) + recv.astype(F32)
+
+    gsum[...] = both(0, group_cols)
     residual = rhs[...] * (1.0 / n_pos) - gsum[...]
     solved = dot(inv[...], residual.astype(BF)).astype(BF)
-    for load in loads:
-        load.wait()
-    for k in range(n_pos):
-        p = pos ^ k
-        rows = pl.ds(pl.multiple_of(group_cols + p * sec, sec), sec)
-        terms = dot(panel[p], solved)
-        terms = (terms + (keep[rows, :].astype(F32) + recv[rows, :].astype(F32))).astype(BF)
+    for p in range(n_pos):
+        terms = (dot(panel[p], solved) + both(group_cols + p * sec, sec)).astype(BF)
         for j in range(n_leaf):
-            stage[j ^ leaf, k * q : (k + 1) * q, :] = terms[j * q : (j + 1) * q, :]
-        begin = pl.multiple_of(core * (group_cols // 2) + p * gq, gq)
-        group[k * gq : (k + 1) * gq, :] = gsum[pl.ds(begin, gq), :].astype(BF)
+            stage[j ^ leaf, p * q : (p + 1) * q, :] = terms[j * q : (j + 1) * q, :]
+    half = group_cols // 2
+    group[...] = gsum[pl.ds(pl.multiple_of(core * half, half), half), :].astype(BF)
     for k in range(n_leaf):
         parts[k][...] = stage[k]
 
@@ -236,66 +235,34 @@
     width = rhs.shape[-1]
     n_pos, sec, _ = panel.shape
     part = (n_pos * sec // n_leaf, width)
-    outs = pl.pallas_call(
+    outs = small(
         functools.partial(fold_kernel, n_leaf, n_pos),
-        out_shape=[pltpu.VMEM(part, BF)] * n_leaf
-        + [pltpu.VMEM((inverse.shape[0] // 2, width), BF)],
-        in_specs=[VMEM] * 4 + [HBM],
-        out_specs=[VMEM] * (n_leaf + 1),
-        scratch_shapes=[
-            pltpu.VMEM(rhs.shape, F32),
-            pltpu.VMEM((n_leaf,) + part, BF),
-            pltpu.VMEM(panel.shape, BF),
-            pltpu.SemaphoreType.DMA((n_pos,)),
-        ],
-        compiler_params=pltpu.CompilerParams(vmem_limit_bytes=SMALL),
-        name="fold_group",
-    )(*in_vmem(keep, recv, inverse, rhs), *in_hbm(panel))
+        "fold_group",
+        [part] * n_leaf + [(inverse.shape[0] // 2, width)],
+        [pltpu.VMEM(rhs.shape, F32), pltpu.VMEM((n_leaf,) + part, BF)],
+        keep,
+        *recv,
+        inverse,
+        rhs,
+        panel,
+    )
     return list(outs[:n_leaf]), outs[n_leaf]
 
 
-def sum_leaf_kernel(n_leaf, *refs):
-    group, outs = refs[n_leaf], refs[n_leaf + 1 :]
-    n_pos = len(outs)
-    q = refs[0].shape[0] // n_pos
-    gq = group.shape[0] // n_pos
-    total = total_of(refs[:n_leaf]).astype(BF)
-    for k, out in enumerate(outs):
-        out[0:q, :] = total[k * q : (k + 1) * q, :]
-        out[q:, :] = group[k * gq : (k + 1) * gq, :]
-
-
-def sum_leaf(parts, group, n_pos):
-    rows = (parts[0].shape[0] + group.shape[0]) // n_pos
-    kernel = functools.partial(sum_leaf_kernel, len(parts))
-    shapes = [(rows, group.shape[1])] * n_pos
-    return list(small(kernel, "sum_leaf", shapes, [], *parts, group))
-
-
-def sum_pos_kernel(high, group, *refs):
-    parts, out = refs[:-1], refs[-1]
-    q = high.shape[0]
-    total = total_of(parts)
-    out[0:q, :] = (high[...] - total[0:q, :]).astype(BF)
-    out[q:, :] = (group[...] - total[q:, :]).astype(BF)
-
-
-def sum_pos(high, group, parts):
-    return small(sum_pos_kernel, "sum_pos", [parts[0].shape], [], high, group, *parts)[0]
-
-
-def stack_pos_kernel(q, *refs):
-    parts, (uppers, groups) = refs[:-2], refs[-2:]
-    gq = parts[0].shape[0] - q
-    for k, part in enumerate(parts):
-        uppers[k * q : (k + 1) * q, :] = part[0:q, :]
-        groups[k * gq : (k + 1) * gq, :] = part[q:, :]
-
-
-def stack_pos(parts, q):
-    n_pos, (rows, width) = len(parts), parts[0].shape
-    shapes = [(n_pos * q, width), (n_pos * (rows - q), width)]
-    return small(functools.partial(stack_pos_kernel, q), "stack_pos", shapes, [], *parts)
+def sum_kernel(*refs):
+    refs[-1][...] = total_of(refs[:-1]).astype(BF)
+
+
+def sum_of(*parts):
+    return small(sum_kernel, "sum", [parts[0].shape], [], *parts)[0]
+
+
+def residual_kernel(rhs, *refs):
+    refs[-1][...] = (rhs[...] - total_of(refs[:-1])).astype(BF)
+
+
+def residual_of(rhs, *parts):
+    return small(residual_kernel, "residual", [rhs.shape], [], rhs, *parts)[0]
 
 
 def stack_kernel(*refs):
@@ -387,16 +354,15 @@
     top_cols = pl.ds(group_rows + mid_rows, top_rows)
     sec = (mid_rows + top_rows) // (2 * n_pos)
     q = sec // n_leaf
-    gq = group_rows // (2 * n_pos)
+    half = group_rows // 2
     for kc, got in enumerate((mine, theirs)):
-        for kz in range(n_pos):
+        for p in range(n_pos):
             for kl in range(n_leaf):
-                row = sec * (2 * (pos ^ kz) + (core ^ kc)) + q * (leaf ^ kl)
-                begin = (kl * n_pos + kz) * q
+                row = sec * (2 * p + (core ^ kc)) + q * (leaf ^ kl)
+                begin = (kl * n_pos + p) * q
                 upper[pl.ds(pl.multiple_of(row, q), q), :] = got[begin : begin + q, :]
-            row = (group_rows // 2) * (core ^ kc) + gq * (pos ^ kz)
-            begin = n_leaf * n_pos * q + kz * gq
-            residual[pl.ds(pl.multiple_of(row, gq), gq), :] = got[begin : begin + gq, :]
+        span = pl.ds(pl.multiple_of(half * (core ^ kc), half), half)
+        residual[span, :] = got[n_leaf * n_pos * q :, :]
 
     mid_solved = dot(inv_mid[...], upper[0:mid_rows, :]).astype(BF)
     top_residual = upper[mid_rows:, :].astype(F32) - dot(panel_mid[...], mid_solved)
@@ -502,7 +468,6 @@
     upper_cols = mid_cols + rhs_top.shape[0]
     sec = upper_cols // n_grp
     q = sec // n_leaf
-    gq = group_cols // n_grp
     leaf, pos, core = place()
     by_parts = middle_panel.shape[0] % 16 == 0
     pos_groups = [[2 * p + c for p in range(n_pos)] for c in range(2)]
@@ -513,13 +478,16 @@
             middles = swaps(middle_panel, "grp", n_grp, 2)
         else:
             middle = lax.all_gather(middle_panel, ("leaf", "grp"), axis=0, tiled=True)
-    begin = sec * lax.axis_index("grp") + q * leaf
-    low = lax.dynamic_slice_in_dim(rhs_middle, jnp.minimum(begin, mid_cols - q), q, 0)
-    high = lax.dynamic_slice_in_dim(rhs_top, jnp.maximum(begin - mid_cols, 0), q, 0)
-    rhs_mine = jnp.where(begin < mid_cols, low, high)
-    group_begin = (group_cols // 2) * core + gq * pos
-    group_mine = lax.dynamic_slice_in_dim(rhs_group[0], group_begin, gq, 0)
-    keep, send, leaf_solved, dense = leaf_forward(
+    def mine_of(rhs):
+        blocks = rhs.reshape(-1, 2, n_leaf, q, rhs.shape[-1])
+        blocks = lax.dynamic_index_in_dim(blocks, core, 1, keepdims=False)
+        return lax.dynamic_index_in_dim(blocks, leaf, 1, keepdims=False)
+
+    upper_rhs = jnp.concatenate([mine_of(rhs_middle), mine_of(rhs_top)], axis=0)
+    upper_rhs = upper_rhs.reshape(n_pos * q, -1)
+    half = group_cols // 2
+    group_rhs = lax.dynamic_slice_in_dim(rhs_group[0], half * core, half, 0)
+    keep, *send, leaf_solved, dense = leaf_forward(
         rhs_leaf[0],
         inv_leaf[0],
         leaf_tiles[0],
@@ -533,30 +501,37 @@
     with jax.named_scope("swap_cores"):
         if by_parts:
             send = after(send, middles)
-        recv = swap(send, "grp", n_grp, 1)
+        recv = [swap(x, "grp", n_grp, 1) for x in send]
+    recv = after(recv, (upper_rhs, group_rhs))
     with jax.named_scope("gather_middle_panel"):
         if by_parts:
             middles = swaps(stack(after(middles, send)), "leaf", n_leaf)
-            recv = after(recv, (middles, rhs_mine, group_mine))
-            middle = stack(middles)
+            middle = stack(after(middles, (upper_rhs, group_rhs, recv)))
+            middle, panel = lax.optimization_barrier((middle, panel))
     parts, group = fold(keep, recv, inv_group[0], rhs_group[0], panel, n_leaf)
     with jax.named_scope("sum_over_leaf"):
         parts = parts[:1] + [swap(parts[k], "leaf", n_leaf, k) for k in range(1, n_leaf)]
+    steps = [2 << i for i in range((n_pos - 1).bit_length())]
+    with jax.named_scope("sum_group_over_pos"):
+        for bits in steps[:-1]:
+            group = sum_of(group, swap(group, "grp", n_grp, bits))
     with jax.named_scope("gather_middle_panel"):
         if by_parts:
             middle = weave(middle, swap(middle, "grp", n_grp, 1), n_leaf, n_pos)
-    sends = sum_leaf(after(parts, middle), group, n_pos)
+    upper = sum_of(*after(parts, (middle, group)))
+    with jax.named_scope("swap_group_panel"):
+        panel_other = swap(after(panel, upper), "grp", n_grp, 1)
     with jax.named_scope("sum_over_pos"):
-        got = sends[:1] + [swap(sends[k], "grp", n_grp, 2 * k) for k in range(1, n_pos)]
-    with jax.named_scope("swap_group_panel"):
-        panel_other = swap(panel, "grp", n_grp, 1)
-    residual = sum_pos(rhs_mine, group_mine, got)
-    with jax.named_scope("gather_pos"):
-        uppers, groups = stack_pos(swaps(residual, "grp", n_grp, 2), q)
+        for bits in steps[:-1]:
+            upper = sum_of(upper, swap(upper, "grp", n_grp, bits))
+        upper = residual_of(upper_rhs, upper, swap(upper, "grp", n_grp, steps[-1]))
     with jax.named_scope("gather_leaf"):
-        stacks = swaps(uppers, "leaf", n_leaf)
+        stacks = swaps(upper, "leaf", n_leaf)
+    with jax.named_scope("sum_group_over_pos"):
+        group = after(group, upper)
+        group = residual_of(group_rhs, group, swap(group, "grp", n_grp, steps[-1]))
     with jax.named_scope("gather_cores"):
-        mine = stack(after(stacks, panel_other) + [groups])
+        mine = stack(after(stacks, panel_other) + [group])
         theirs = swap(mine, "grp", n_grp, 1)
     leaf_out, group_out, mid_out, top_out = backward(
         (mine, theirs, inv_middle, middle),

time: 103 us -> 105 us (1.019)
  local copies, waits for them, and re-layouts: 1.9 us -> 9.31 us
  starting transfers between devices: 26 us -> 22.7 us
  Pallas kernels: 25 us -> 22.7 us
  waiting for transfers between devices: 33.7 us -> 34.9 us
    unnamed x8 -> x28, local copies, waits for them, and re-layouts: 1.06 us -> 8.29 us
    ppermute x22 -> x21, starting transfers between devices: 26 us -> 22.7 us  [swap(): return lax.ppermute(x, axis, [(i, i ^ bits) for i in range(size)])]
    pallas_call x1 -> x0, Pallas kernels: 3.19 us -> none  [fold(): pl.pallas_call(functools.partial(fold_kernel, n_leaf, n_pos), out_shape=[...]
    ppermute x22 -> x21, waiting for transfers between devices: 31.2 us -> 34.2 us  [swap(): return lax.ppermute(x, axis, [(i, i ^ bits) for i in range(size)])]
    all_gather x1, waiting for transfers between devices: 1.78 us -> 0.02 us  [body(): panel = lax.all_gather(group_panel[0], 'grp', axis_index_groups=pos_groups)]
    pallas_call x7 -> x10, Pallas kernels: 0.4 us -> 1.46 us  [small(): pl.pallas_call(kernel, out_shape=[pltpu.VMEM(shape, BF) for shape in shap...]
  transfers between devices with their start and end apart: 23 -> 22, of which waited for: 14 -> 11; matrix products, arithmetic and copies ran while one was open for 2% -> 1% of each run, Pallas kernels for 13% -> 10%
where the time goes in v8:
time: 105 us
  waiting for transfers between devices  34.9 us (33%)
  starting transfers between devices  22.7 us (22%)
  Pallas kernels  22.7 us (22%)
  between operations  14.9 us (14%)
  local copies, waits for them, and re-layouts  9.31 us (9%)
    ppermute x21, waiting for transfers between devices, swap(): return lax.ppermute(x, axis, [(i, i ^ bits) for i in range(size)])  34.2 us
    ppermute x21, starting transfers between devices, swap(): return lax.ppermute(x, axis, [(i, i ^ bits) for i in range(size)])  22.7 us
    pallas_call x1, Pallas kernels, backward(): pl.pallas_call(functools.partial(backward_kernel, n_leaf, n_pos), out_sha...  12 us
    pallas_call x1, Pallas kernels, leaf_forward(): pl.pallas_call(functools.partial(forward_kernel, sec, group_cols), out_sh...  9.31 us
    unnamed x28, local copies, waits for them, and re-layouts  8.29 us
  transfers between devices with their start and end apart: 22, of which 11 were waited for; matrix products, arithmetic and copies ran while one was open for 1% of the time, Pallas kernels for 10%

profile of v8, /device:TPU:0, one launch (start us, length us, event | category | flops | bytes accessed | tf_op | source)
XLA Modules:
  0.0 104.6 jit_solution(568567207722692340)
XLA Ops:
  7.9 5.1 %collective-permute-start.2 = (bf16[32,1024]{1,0:T(8,128)(2,1)}, bf16[32,1024]{1,0:T(8,128)(2,1)S(1)}, u32[]{:S(2)}, u32[]{:S(2)}) collective-permute-start(bf16[32,1024]{1,0:T(8,128)(2,1)} %refs_0_), channel_id=1, source_target_pairs={{0,6},{1,7},{2,4},{3,5},{4,2},{5,3},{6,0},{7,1},{8,14},{9,15},{10,... | collective-permute-start | bytes 196616 | tf_op jit(solution)/shard_map/gather_middle_panel/ppermute | solution.py:436
  14.3 9.3 %leaf_forward.1 = (bf16[1536,256]{1,0:T(8,128)(2,1)S(1)}, bf16[768,256]{1,0:T(8,128)(2,1)}, bf16[768,256]{1,0:T(8,128)(2,1)}, bf16[1024,256]{1,0:T(8,128)(2,1)}, bf16[2560,1024]{1,0:T(8,128)(2,1)}) custom-call(s32[1,1]{1,0:T(1,128)S(6)} %copy.18.count_hbm, s32[1,256]{1,0:T(1,128)} %cols_hbm.1, s32[1,256]{1,0:T(1,128)} %tgts_hbm.1, f32[1024,256]{1,0:T(8,128)} %bitcast.23, ...), custom_call_target="tpu_custom_call" | custom-call | flops 1342177280 | bytes 9437184 | tf_op jit(solution)/shard_map/leaf_forward/pallas_call | solution.py:166
  25.1 2.8 %collective-permute-start.7 = (bf16[128,1024]{1,0:T(8,128)(2,1)S(1)}, bf16[128,1024]{1,0:T(8,128)(2,1)S(1)}, u32[]{:S(2)}, u32[]{:S(2)}) collective-permute-start(bf16[128,1024]{1,0:T(8,128)(2,1)S(1)} %stack.3.refs_0_), channel_id=1, source_target_pairs={{0,24},{8,16},{16,8},{24,0},{1,25},{9,17},{17,9},{25,1},{2,26},{10... | collective-permute-start | bytes 786440 | tf_op jit(solution)/shard_map/gather_middle_panel/ppermute | solution.py:436
  28.8 1.0 dynamic-slice_bitcast_fusion.1
  30.6 4.7 %collective-permute-done.7.refs_3_ = bf16[128,1024]{1,0:T(8,128)(2,1)S(1)} collective-permute-done((bf16[128,1024]{1,0:T(8,128)(2,1)S(1)}, bf16[128,1024]{1,0:T(8,128)(2,1)S(1)}, u32[]{:S(2)}, u32[]{:S(2)}) %collective-permute-start.7) | collective-permute-done | bytes 262176 | tf_op jit(solution)/shard_map/gather_middle_panel/ppermute | solution.py:436
  35.3 4.8 %collective-permute-done.6.refs_2_ = bf16[128,1024]{1,0:T(8,128)(2,1)S(1)} collective-permute-done((bf16[128,1024]{1,0:T(8,128)(2,1)S(1)}, bf16[128,1024]{1,0:T(8,128)(2,1)S(1)}, u32[]{:S(2)}, u32[]{:S(2)}) %collective-permute-start.6) | collective-permute-done | bytes 262176 | tf_op jit(solution)/shard_map/gather_middle_panel/ppermute | solution.py:436
  41.5 0.9 copy-done.9
  43.7 1.2 %copy-done = bf16[4,256,512]{2,1,0:T(8,128)(2,1)S(1)} copy-done((bf16[4,256,512]{2,1,0:T(8,128)(2,1)S(1)}, bf16[4,256,512]{2,1,0:T(8,128)(2,1)}, u32[]{:S(2)}) %copy-start) | copy-done | bytes 1048600
  44.9 1.1 %copy-done.5 = bf16[1536,256]{1,0:T(8,128)(2,1)S(1)} copy-done((bf16[1536,256]{1,0:T(8,128)(2,1)S(1)}, bf16[1536,256]{1,0:T(8,128)(2,1)}, u32[]{:S(2)}) %copy-start.5) | copy-done | bytes 786456
  46.0 1.0 copy-done.7
  47.0 1.0 fold_group.1
  48.9 1.9 %collective-permute-start.8 = (bf16[256,256]{1,0:T(8,128)(2,1)S(1)}, bf16[256,256]{1,0:T(8,128)(2,1)S(1)}, u32[]{:S(2)}, u32[]{:S(2)}) collective-permute-start(bf16[256,256]{1,0:T(8,128)(2,1)S(1)} %get-tuple-element.59), channel_id=1, source_target_pairs={{0,8},{8,0},{16,24},{24,16},{1,9},{9,1},{17,25},{25,17},{2,10},{10... | collective-permute-start | bytes 393224 | tf_op jit(solution)/shard_map/sum_over_leaf/ppermute | solution.py:436
  52.4 1.5 %collective-permute-done.12.refs_1_ = bf16[256,256]{1,0:T(8,128)(2,1)S(1)} collective-permute-done((bf16[256,256]{1,0:T(8,128)(2,1)S(1)}, bf16[256,256]{1,0:T(8,128)(2,1)S(1)}, u32[]{:S(2)}, u32[]{:S(2)}) %collective-permute-start.12) | collective-permute-done | bytes 131104 | tf_op jit(solution)/shard_map/sum_group_over_pos/ppermute | solution.py:436
  54.6 2.6 %collective-permute-done.9.refs_2_ = bf16[256,256]{1,0:T(8,128)(2,1)S(1)} collective-permute-done((bf16[256,256]{1,0:T(8,128)(2,1)S(1)}, bf16[256,256]{1,0:T(8,128)(2,1)S(1)}, u32[]{:S(2)}, u32[]{:S(2)}) %collective-permute-start.9) | collective-permute-done | bytes 131104 | tf_op jit(solution)/shard_map/sum_over_leaf/ppermute | solution.py:436
  57.2 1.6 %collective-permute-done.10.refs_3_ = bf16[256,256]{1,0:T(8,128)(2,1)S(1)} collective-permute-done((bf16[256,256]{1,0:T(8,128)(2,1)S(1)}, bf16[256,256]{1,0:T(8,128)(2,1)S(1)}, u32[]{:S(2)}, u32[]{:S(2)}) %collective-permute-start.10) | collective-permute-done | bytes 131104 | tf_op jit(solution)/shard_map/sum_over_leaf/ppermute | solution.py:436
  59.8 5.0 %collective-permute-done.13.refs_1_ = bf16[256,256]{1,0:T(8,128)(2,1)S(1)} collective-permute-done((bf16[256,256]{1,0:T(8,128)(2,1)S(1)}, bf16[256,256]{1,0:T(8,128)(2,1)S(1)}, u32[]{:S(2)}, u32[]{:S(2)}) %collective-permute-start.13) | collective-permute-done | bytes 131104 | tf_op jit(solution)/shard_map/sum_over_pos/ppermute | solution.py:436
  64.9 3.4 %collective-permute-start.14 = (bf16[256,256]{1,0:T(8,128)(2,1)S(1)}, bf16[256,256]{1,0:T(8,128)(2,1)S(1)}, u32[]{:S(2)}, u32[]{:S(2)}) collective-permute-start(bf16[256,256]{1,0:T(8,128)(2,1)S(1)} %sum.5.refs_0_), channel_id=1, source_target_pairs={{0,4},{1,5},{2,6},{3,7},{4,0},{5,1},{6,2},{7,3},{8,12},{9,13},{10,... | collective-permute-start | bytes 393224 | tf_op jit(solution)/shard_map/sum_over_pos/ppermute | solution.py:436
  68.3 5.9 %collective-permute-done.14.refs_1_ = bf16[256,256]{1,0:T(8,128)(2,1)S(1)} collective-permute-done((bf16[256,256]{1,0:T(8,128)(2,1)S(1)}, bf16[256,256]{1,0:T(8,128)(2,1)S(1)}, u32[]{:S(2)}, u32[]{:S(2)}) %collective-permute-start.14) | collective-permute-done | bytes 131104 | tf_op jit(solution)/shard_map/sum_over_pos/ppermute | solution.py:436
  74.5 1.5 %collective-permute-start.17 = (bf16[256,256]{1,0:T(8,128)(2,1)S(1)}, bf16[256,256]{1,0:T(8,128)(2,1)S(1)}, u32[]{:S(2)}, u32[]{:S(2)}) collective-permute-start(bf16[256,256]{1,0:T(8,128)(2,1)S(1)} %residual.2.refs_0_), channel_id=1, source_target_pairs={{0,24},{8,16},{16,8},{24,0},{1,25},{9,17},{17,9},{25,1},{2,26},{10... | collective-permute-start | bytes 393224 | tf_op jit(solution)/shard_map/gather_leaf/ppermute | solution.py:436
  76.4 1.6 %collective-permute-start.15 = (bf16[256,256]{1,0:T(8,128)(2,1)S(1)}, bf16[256,256]{1,0:T(8,128)(2,1)S(1)}, u32[]{:S(2)}, u32[]{:S(2)}) collective-permute-start(bf16[256,256]{1,0:T(8,128)(2,1)S(1)} %residual.2.refs_0_), channel_id=1, source_target_pairs={{0,8},{8,0},{16,24},{24,16},{1,9},{9,1},{17,25},{25,17},{2,10},{10... | collective-permute-start | bytes 393224 | tf_op jit(solution)/shard_map/gather_leaf/ppermute | solution.py:436
  78.0 4.4 %collective-permute-done.19.refs_1_ = bf16[256,256]{1,0:T(8,128)(2,1)S(1)} collective-permute-done((bf16[256,256]{1,0:T(8,128)(2,1)S(1)}, bf16[256,256]{1,0:T(8,128)(2,1)S(1)}, u32[]{:S(2)}, u32[]{:S(2)}) %collective-permute-start.19) | collective-permute-done | bytes 131104 | tf_op jit(solution)/shard_map/sum_group_over_pos/ppermute | solution.py:436
  82.4 1.2 %collective-permute-done.16.refs_2_ = bf16[256,256]{1,0:T(8,128)(2,1)S(1)} collective-permute-done((bf16[256,256]{1,0:T(8,128)(2,1)S(1)}, bf16[256,256]{1,0:T(8,128)(2,1)S(1)}, u32[]{:S(2)}, u32[]{:S(2)}) %collective-permute-start.16) | collective-permute-done | bytes 131104 | tf_op jit(solution)/shard_map/gather_leaf/ppermute | solution.py:436
  83.7 2.1 %collective-permute-done.20.theirs = bf16[1280,256]{1,0:T(8,128)(2,1)S(1)} collective-permute-done((bf16[1280,256]{1,0:T(8,128)(2,1)S(1)}, bf16[1280,256]{1,0:T(8,128)(2,1)S(1)}, u32[]{:S(2)}, u32[]{:S(2)}) %collective-permute-start.20) | collective-permute-done | bytes 655392 | tf_op jit(solution)/shard_map/gather_cores/ppermute | solution.py:436
  85.8 12.0 %backward.1 = (f32[1024,256]{1,0:T(8,128)}, f32[512,256]{1,0:T(8,128)}, f32[1024,256]{1,0:T(8,128)}, f32[1024,256]{1,0:T(8,128)}) custom-call(bf16[1280,256]{1,0:T(8,128)(2,1)S(1)} %stack.5.mine, bf16[1280,256]{1,0:T(8,128)(2,1)S(1)} %collective-permute-done.20.theirs, bf16[1024,1024]{1,0:T(8,128)(2,1)S(1)} %copy-done.2, ...), custom_call_target="tpu_custom_call" | custom-call | tf_op jit(solution)/shard_map/backward/pallas_call | solution.py:415
  (64 shorter events, 12.3 us)
Async XLA Ops:
  7.2 36.3 %all-gather.2.cloned.1.call-start = ((), (), s32[]{:S(2)}) async-start(), calls=%async_computation | async-start | bytes 1310720 | tf_op jit(solution)/shard_map/gather_group_panel/all_gather | solution.py:475
  7.9 16.6 %collective-permute-start.2 = (bf16[32,1024]{1,0:T(8,128)(2,1)}, bf16[32,1024]{1,0:T(8,128)(2,1)S(1)}, u32[]{:S(2)}, u32[]{:S(2)}) collective-permute-start(bf16[32,1024]{1,0:T(8,128)(2,1)} %refs_0_), channel_id=1, source_target_pairs={{0,6},{1,7},{2,4},{3,5},{4,2},{5,3},{6,0},{7,1},{8,14},{9,15},{10,... | collective-permute-start | bytes 196616 | tf_op jit(solution)/shard_map/gather_middle_panel/ppermute | solution.py:436
  13.0 11.5 %collective-permute-start.1 = (bf16[32,1024]{1,0:T(8,128)(2,1)}, bf16[32,1024]{1,0:T(8,128)(2,1)S(1)}, u32[]{:S(2)}, u32[]{:S(2)}) collective-permute-start(bf16[32,1024]{1,0:T(8,128)(2,1)} %refs_0_), channel_id=1, source_target_pairs={{0,4},{1,5},{2,6},{3,7},{4,0},{5,1},{6,2},{7,3},{8,12},{9,13},{10,... | collective-permute-start | bytes 196616 | tf_op jit(solution)/shard_map/gather_middle_panel/ppermute | solution.py:436
  13.0 11.5 %collective-permute-start = (bf16[32,1024]{1,0:T(8,128)(2,1)}, bf16[32,1024]{1,0:T(8,128)(2,1)S(1)}, u32[]{:S(2)}, u32[]{:S(2)}) collective-permute-start(bf16[32,1024]{1,0:T(8,128)(2,1)} %refs_0_), channel_id=1, source_target_pairs={{0,2},{1,3},{2,0},{3,1},{4,6},{5,7},{6,4},{7,5},{8,10},{9,11},{10,... | collective-permute-start | bytes 196616 | tf_op jit(solution)/shard_map/gather_middle_panel/ppermute | solution.py:436
  24.5 5.3 %collective-permute-start.3 = (bf16[768,256]{1,0:T(8,128)(2,1)}, bf16[768,256]{1,0:T(8,128)(2,1)S(1)}, u32[]{:S(2)}, u32[]{:S(2)}) collective-permute-start(bf16[768,256]{1,0:T(8,128)(2,1)} %get-tuple-element.45), channel_id=1, source_target_pairs={{0,1},{1,0},{2,3},{3,2},{4,5},{5,4},{6,7},{7,6},{8,9},{9,8},{10,11... | collective-permute-start | bytes 1179656 | tf_op jit(solution)/shard_map/swap_cores/ppermute | solution.py:436
  24.6 5.2 %collective-permute-start.4 = (bf16[768,256]{1,0:T(8,128)(2,1)}, bf16[768,256]{1,0:T(8,128)(2,1)S(1)}, u32[]{:S(2)}, u32[]{:S(2)}) collective-permute-start(bf16[768,256]{1,0:T(8,128)(2,1)} %get-tuple-element.46), channel_id=1, source_target_pairs={{0,1},{1,0},{2,3},{3,2},{4,5},{5,4},{6,7},{7,6},{8,9},{9,8},{10,11... | collective-permute-start | bytes 1179656 | tf_op jit(solution)/shard_map/swap_cores/ppermute | solution.py:436
  25.1 18.5 %copy-start.1 = (bf16[1,512,512]{2,1,0:T(8,128)(2,1)S(1)}, bf16[1,512,512]{2,1,0:T(8,128)(2,1)}, u32[]{:S(2)}) copy-start(bf16[1,512,512]{2,1,0:T(8,128)(2,1)} %param.19) | copy-start | bytes 1572868
  25.1 10.2 %collective-permute-start.7 = (bf16[128,1024]{1,0:T(8,128)(2,1)S(1)}, bf16[128,1024]{1,0:T(8,128)(2,1)S(1)}, u32[]{:S(2)}, u32[]{:S(2)}) collective-permute-start(bf16[128,1024]{1,0:T(8,128)(2,1)S(1)} %stack.3.refs_0_), channel_id=1, source_target_pairs={{0,24},{8,16},{16,8},{24,0},{1,25},{9,17},{17,9},{25,1},{2,26},{10... | collective-permute-start | bytes 786440 | tf_op jit(solution)/shard_map/gather_middle_panel/ppermute | solution.py:436
  27.9 12.2 %collective-permute-start.6 = (bf16[128,1024]{1,0:T(8,128)(2,1)S(1)}, bf16[128,1024]{1,0:T(8,128)(2,1)S(1)}, u32[]{:S(2)}, u32[]{:S(2)}) collective-permute-start(bf16[128,1024]{1,0:T(8,128)(2,1)S(1)} %stack.3.refs_0_), channel_id=1, source_target_pairs={{0,16},{8,24},{16,0},{24,8},{1,17},{9,25},{17,1},{25,9},{2,18},{10... | collective-permute-start | bytes 786440 | tf_op jit(solution)/shard_map/gather_middle_panel/ppermute | solution.py:436
  28.1 12.7 %collective-permute-start.5 = (bf16[128,1024]{1,0:T(8,128)(2,1)S(1)}, bf16[128,1024]{1,0:T(8,128)(2,1)S(1)}, u32[]{:S(2)}, u32[]{:S(2)}) collective-permute-start(bf16[128,1024]{1,0:T(8,128)(2,1)S(1)} %stack.3.refs_0_), channel_id=1, source_target_pairs={{0,8},{8,0},{16,24},{24,16},{1,9},{9,1},{17,25},{25,17},{2,10},{10... | collective-permute-start | bytes 786440 | tf_op jit(solution)/shard_map/gather_middle_panel/ppermute | solution.py:436
  43.5 10.4 %collective-permute-start.11 = (bf16[512,1024]{1,0:T(8,128)(2,1)S(1)}, bf16[512,1024]{1,0:T(8,128)(2,1)S(1)}, u32[]{:S(2)}, u32[]{:S(2)}) collective-permute-start(bf16[512,1024]{1,0:T(8,128)(2,1)S(1)} %stack.4.own), channel_id=1, source_target_pairs={{0,1},{1,0},{2,3},{3,2},{4,5},{5,4},{6,7},{7,6},{8,9},{9,8},{10,11... | collective-permute-start | bytes 3145736 | tf_op jit(solution)/shard_map/gather_middle_panel/ppermute | solution.py:436
  48.0 5.9 %collective-permute-start.12 = (bf16[256,256]{1,0:T(8,128)(2,1)S(1)}, bf16[256,256]{1,0:T(8,128)(2,1)S(1)}, u32[]{:S(2)}, u32[]{:S(2)}) collective-permute-start(bf16[256,256]{1,0:T(8,128)(2,1)S(1)} %get-tuple-element.63.refs_0_), channel_id=1, source_target_pairs={{0,2},{1,3},{2,0},{3,1},{4,6},{5,7},{6,4},{7,5},{8,10},{9,11},{10,... | collective-permute-start | bytes 393224 | tf_op jit(solution)/shard_map/sum_group_over_pos/ppermute | solution.py:436
  48.9 5.8 %collective-permute-start.8 = (bf16[256,256]{1,0:T(8,128)(2,1)S(1)}, bf16[256,256]{1,0:T(8,128)(2,1)S(1)}, u32[]{:S(2)}, u32[]{:S(2)}) collective-permute-start(bf16[256,256]{1,0:T(8,128)(2,1)S(1)} %get-tuple-element.59), channel_id=1, source_target_pairs={{0,8},{8,0},{16,24},{24,16},{1,9},{9,1},{17,25},{25,17},{2,10},{10... | collective-permute-start | bytes 393224 | tf_op jit(solution)/shard_map/sum_over_leaf/ppermute | solution.py:436
  50.7 6.5 %collective-permute-start.9 = (bf16[256,256]{1,0:T(8,128)(2,1)S(1)}, bf16[256,256]{1,0:T(8,128)(2,1)S(1)}, u32[]{:S(2)}, u32[]{:S(2)}) collective-permute-start(bf16[256,256]{1,0:T(8,128)(2,1)S(1)} %get-tuple-element.60), channel_id=1, source_target_pairs={{0,16},{8,24},{16,0},{24,8},{1,17},{9,25},{17,1},{25,9},{2,18},{10... | collective-permute-start | bytes 393224 | tf_op jit(solution)/shard_map/sum_over_leaf/ppermute | solution.py:436
  51.5 7.2 %collective-permute-start.10 = (bf16[256,256]{1,0:T(8,128)(2,1)S(1)}, bf16[256,256]{1,0:T(8,128)(2,1)S(1)}, u32[]{:S(2)}, u32[]{:S(2)}) collective-permute-start(bf16[256,256]{1,0:T(8,128)(2,1)S(1)} %get-tuple-element.61), channel_id=1, source_target_pairs={{0,24},{8,16},{16,8},{24,0},{1,25},{9,17},{17,9},{25,1},{2,26},{10... | collective-permute-start | bytes 393224 | tf_op jit(solution)/shard_map/sum_over_leaf/ppermute | solution.py:436
  54.1 31.7 %copy-start.2 = (bf16[1024,1024]{1,0:T(8,128)(2,1)S(1)}, bf16[1024,1024]{1,0:T(8,128)(2,1)}, u32[]{:S(2)}) copy-start(bf16[1024,1024]{1,0:T(8,128)(2,1)} %inv_mid.1) | copy-start | bytes 6291460
  58.8 24.7 %collective-permute-start.18 = (bf16[4,256,512]{2,1,0:T(8,128)(2,1)S(1)}, bf16[4,256,512]{2,1,0:T(8,128)(2,1)S(1)}, u32[]{:S(2)}, u32[]{:S(2)}) collective-permute-start(bf16[4,256,512]{2,1,0:T(8,128)(2,1)S(1)} %copy-done), channel_id=1, source_target_pairs={{0,1},{1,0},{2,3},{3,2},{4,5},{5,4},{6,7},{7,6},{8,9},{9,8},{10,11... | collective-permute-start | bytes 3145736 | tf_op jit(solution)/shard_map/swap_group_panel/ppermute | solution.py:436
  58.9 5.9 %collective-permute-start.13 = (bf16[256,256]{1,0:T(8,128)(2,1)S(1)}, bf16[256,256]{1,0:T(8,128)(2,1)S(1)}, u32[]{:S(2)}, u32[]{:S(2)}) collective-permute-start(bf16[256,256]{1,0:T(8,128)(2,1)S(1)} %sum.4.refs_0_), channel_id=1, source_target_pairs={{0,2},{1,3},{2,0},{3,1},{4,6},{5,7},{6,4},{7,5},{8,10},{9,11},{10,... | collective-permute-start | bytes 393224 | tf_op jit(solution)/shard_map/sum_over_pos/ppermute | solution.py:436
  64.9 9.4 %collective-permute-start.14 = (bf16[256,256]{1,0:T(8,128)(2,1)S(1)}, bf16[256,256]{1,0:T(8,128)(2,1)S(1)}, u32[]{:S(2)}, u32[]{:S(2)}) collective-permute-start(bf16[256,256]{1,0:T(8,128)(2,1)S(1)} %sum.5.refs_0_), channel_id=1, source_target_pairs={{0,4},{1,5},{2,6},{3,7},{4,0},{5,1},{6,2},{7,3},{8,12},{9,13},{10,... | collective-permute-start | bytes 393224 | tf_op jit(solution)/shard_map/sum_over_pos/ppermute | solution.py:436
  74.3 8.0 %collective-permute-start.19 = (bf16[256,256]{1,0:T(8,128)(2,1)S(1)}, bf16[256,256]{1,0:T(8,128)(2,1)S(1)}, u32[]{:S(2)}, u32[]{:S(2)}) collective-permute-start(bf16[256,256]{1,0:T(8,128)(2,1)S(1)} %sum.3.refs_0_), channel_id=1, source_target_pairs={{0,4},{1,5},{2,6},{3,7},{4,0},{5,1},{6,2},{7,3},{8,12},{9,13},{10,... | collective-permute-start | bytes 393224 | tf_op jit(solution)/shard_map/sum_group_over_pos/ppermute | solution.py:436
  74.5 7.9 %collective-permute-start.17 = (bf16[256,256]{1,0:T(8,128)(2,1)S(1)}, bf16[256,256]{1,0:T(8,128)(2,1)S(1)}, u32[]{:S(2)}, u32[]{:S(2)}) collective-permute-start(bf16[256,256]{1,0:T(8,128)(2,1)S(1)} %residual.2.refs_0_), channel_id=1, source_target_pairs={{0,24},{8,16},{16,8},{24,0},{1,25},{9,17},{17,9},{25,1},{2,26},{10... | collective-permute-start | bytes 393224 | tf_op jit(solution)/shard_map/gather_leaf/ppermute | solution.py:436
  75.9 7.6 %collective-permute-start.16 = (bf16[256,256]{1,0:T(8,128)(2,1)S(1)}, bf16[256,256]{1,0:T(8,128)(2,1)S(1)}, u32[]{:S(2)}, u32[]{:S(2)}) collective-permute-start(bf16[256,256]{1,0:T(8,128)(2,1)S(1)} %residual.2.refs_0_), channel_id=1, source_target_pairs={{0,16},{8,24},{16,0},{24,8},{1,17},{9,25},{17,1},{25,9},{2,18},{10... | collective-permute-start | bytes 393224 | tf_op jit(solution)/shard_map/gather_leaf/ppermute | solution.py:436
  76.4 7.2 %collective-permute-start.15 = (bf16[256,256]{1,0:T(8,128)(2,1)S(1)}, bf16[256,256]{1,0:T(8,128)(2,1)S(1)}, u32[]{:S(2)}, u32[]{:S(2)}) collective-permute-start(bf16[256,256]{1,0:T(8,128)(2,1)S(1)} %residual.2.refs_0_), channel_id=1, source_target_pairs={{0,8},{8,0},{16,24},{24,16},{1,9},{9,1},{17,25},{25,17},{2,10},{10... | collective-permute-start | bytes 393224 | tf_op jit(solution)/shard_map/gather_leaf/ppermute | solution.py:436
  83.6 2.2 %collective-permute-start.20 = (bf16[1280,256]{1,0:T(8,128)(2,1)S(1)}, bf16[1280,256]{1,0:T(8,128)(2,1)S(1)}, u32[]{:S(2)}, u32[]{:S(2)}) collective-permute-start(bf16[1280,256]{1,0:T(8,128)(2,1)S(1)} %stack.5.mine), channel_id=1, source_target_pairs={{0,1},{1,0},{2,3},{3,2},{4,5},{5,4},{6,7},{7,6},{8,9},{9,8},{10,11... | collective-permute-start | bytes 1966088 | tf_op jit(solution)/shard_map/gather_cores/ppermute | solution.py:436
  (12 other events, 36.8 us)
Sparse Core Ops, SparseCore 0:
  9.6 30.6 all-gather.1

commit v9 on v6

--- a/solution.py
+++ b/solution.py
@@ -56,8 +56,12 @@
     rhs_hbm,
     inv_hbm,
     tiles_hbm,
+    inv_group_hbm,
+    rhs_group_hbm,
     keep,
     send,
+    inv_group,
+    rhs_group,
     solved_hbm,
     dense_hbm,
     count,
@@ -73,6 +77,7 @@
     in_sems,
     tile_sems,
     out_sems,
+    pass_sems,
 ):
     slots, block, _ = tiles.shape
     supernodes = inv.shape[0]
@@ -97,6 +102,10 @@
         load.start()
     for k in range(chunks):
         tile_copy(k).start()
+    pairs = ((inv_group_hbm, inv_group), (rhs_group_hbm, rhs_group))
+    passes = [pltpu.make_async_copy(a, b, pass_sems.at[i]) for i, (a, b) in enumerate(pairs)]
+    for copy in passes:
+        copy.start()
 
     acc[...] = jnp.zeros_like(acc)
     for load in loads:
@@ -150,11 +159,14 @@
                 stage[(section % 2) ^ core, begin : begin + sec, :] = total[q : q + sec, :]
     keep[...] = stage[0]
     send[...] = stage[1]
-    for store in stores:
-        store.wait()
-
-
-def leaf_forward(rhs, inverse, tiles, cols, tgts, count, sec, group_cols, upper_cols):
+    for copy in passes + stores:
+        copy.wait()
+
+
+def leaf_forward(
+    rhs, inverse, tiles, cols, tgts, count, inv_group, rhs_group, sec, upper_cols
+):
+    group_cols = rhs_group.shape[0]
     slots, block, _ = tiles.shape
     supernodes = inverse.shape[0]
     targets = (group_cols + upper_cols) // block
@@ -165,11 +177,13 @@
         out_shape=(
             pltpu.VMEM((half, width), BF),
             pltpu.VMEM((half, width), BF),
+            pltpu.VMEM(inv_group.shape, BF),
+            pltpu.VMEM(rhs_group.shape, F32),
             pltpu.HBM((supernodes * block, width), BF),
             pltpu.HBM((targets * block, supernodes * block), BF),
         ),
-        in_specs=[HBM] * 6,
-        out_specs=(VMEM, VMEM, HBM, HBM),
+        in_specs=[HBM] * 8,
+        out_specs=(VMEM,) * 4 + (HBM,) * 2,
         scratch_shapes=[
             pltpu.SMEM(count.shape, count.dtype),
             pltpu.SMEM(cols.shape, cols.dtype),
@@ -184,6 +198,7 @@
             pltpu.SemaphoreType.DMA((5,)),
             pltpu.SemaphoreType.DMA((CHUNKS,)),
             pltpu.SemaphoreType.DMA((1 + targets * block // group_cols,)),
+            pltpu.SemaphoreType.DMA((2,)),
         ],
         compiler_params=pltpu.CompilerParams(vmem_limit_bytes=BIG),
         cost_estimate=pl.CostEstimate(
@@ -192,7 +207,7 @@
             transcendentals=0,
         ),
         name="leaf_forward",
-    )(count, *in_hbm(cols, tgts, rhs, inverse, tiles))
+    )(count, *in_hbm(cols, tgts, rhs, inverse, tiles, inv_group, rhs_group))
 
 
 def total_of(refs):
@@ -202,13 +217,8 @@
     return total
 
 
-def fold_kernel(n_leaf, n_pos, keep, recv, inv, rhs, panel_hbm, *refs):
-    parts, group, (gsum, stage, panel, sems) = refs[:n_leaf], refs[n_leaf], refs[n_leaf + 1 :]
-    loads = [
-        pltpu.make_async_copy(panel_hbm.at[p], panel.at[p], sems.at[p]) for p in range(n_pos)
-    ]
-    for load in loads:
-        load.start()
+def fold_kernel(n_leaf, n_pos, keep, recv, inv, rhs, panel, *refs):
+    parts, group, (gsum, stage) = refs[:n_leaf], refs[n_leaf], refs[n_leaf + 1 :]
     leaf, pos, core = place()
     group_cols = inv.shape[0]
     sec = panel.shape[1]
@@ -217,8 +227,6 @@
     gsum[...] = keep[0:group_cols, :].astype(F32) + recv[0:group_cols, :].astype(F32)
     residual = rhs[...] * (1.0 / n_pos) - gsum[...]
     solved = dot(inv[...], residual.astype(BF)).astype(BF)
-    for load in loads:
-        load.wait()
     for k in range(n_pos):
         p = pos ^ k
         rows = pl.ds(pl.multiple_of(group_cols + p * sec, sec), sec)
@@ -236,21 +244,17 @@
     width = rhs.shape[-1]
     n_pos, sec, _ = panel.shape
     part = (n_pos * sec // n_leaf, width)
-    outs = pl.pallas_call(
+    outs = small(
         functools.partial(fold_kernel, n_leaf, n_pos),
-        out_shape=[pltpu.VMEM(part, BF)] * n_leaf
-        + [pltpu.VMEM((inverse.shape[0] // 2, width), BF)],
-        in_specs=[VMEM] * 4 + [HBM],
-        out_specs=[VMEM] * (n_leaf + 1),
-        scratch_shapes=[
-            pltpu.VMEM(rhs.shape, F32),
-            pltpu.VMEM((n_leaf,) + part, BF),
-            pltpu.VMEM(panel.shape, BF),
-            pltpu.SemaphoreType.DMA((n_pos,)),
-        ],
-        compiler_params=pltpu.CompilerParams(vmem_limit_bytes=SMALL),
-        name="fold_group",
-    )(*in_vmem(keep, recv, inverse, rhs), *in_hbm(panel))
+        "fold_group",
+        [part] * n_leaf + [(inverse.shape[0] // 2, width)],
+        [pltpu.VMEM(rhs.shape, F32), pltpu.VMEM((n_leaf,) + part, BF)],
+        keep,
+        recv,
+        inverse,
+        rhs,
+        panel,
+    )
     return list(outs[:n_leaf]), outs[n_leaf]
 
 
@@ -327,6 +331,24 @@
     shape = (2 * own.shape[0], own.shape[1])
     kernel = functools.partial(weave_kernel, n_leaf, n_pos)
     return small(kernel, "weave", [shape], [], own, other)[0]
+
+
+def lower_dot(lower, x):
+    n = lower.shape[0]
+    step = n // 4
+    parts = []
+    for i in range(0, n, step):
+        parts.append(dot(lower[i : i + step, 0 : i + step], x[0 : i + step, :]))
+    return jnp.concatenate(parts, axis=0)
+
+
+def dot_lower(x, lower):
+    n = lower.shape[0]
+    step = n // 4
+    parts = []
+    for i in range(0, n, step):
+        parts.append(dot(x[:, i:], lower[i:, i : i + step]))
+    return jnp.concatenate(parts, axis=1)
 
 
 def backward_kernel(
@@ -398,17 +420,17 @@
             begin = n_leaf * n_pos * q + kz * gq
             residual[pl.ds(pl.multiple_of(row, gq), gq), :] = got[begin : begin + gq, :]
 
-    mid_solved = dot(inv_mid[...], upper[0:mid_rows, :]).astype(BF)
+    mid_solved = lower_dot(inv_mid, upper[0:mid_rows, :]).astype(BF)
     top_residual = upper[mid_rows:, :].astype(F32) - dot(panel_mid[...], mid_solved)
     loads[0].wait()
-    top_solved = dot(inv_top[...], top_residual.astype(BF))
-    top_t = dot(top_solved.T.astype(BF), inv_top[...])
+    top_solved = lower_dot(inv_top, top_residual.astype(BF))
+    top_t = dot_lower(top_solved.T.astype(BF), inv_top)
     above[:, top_cols] = top_t.astype(BF)
     top_out[...] = top_t.T
     stores = [pltpu.make_async_copy(top_out, top_hbm, out_sems.at[0])]
     stores[0].start()
     mid_back = mid_solved.astype(F32).T - dot(above[:, top_cols], panel_mid[...])
-    mid_t = dot(mid_back.astype(BF), inv_mid[...])
+    mid_t = dot_lower(mid_back.astype(BF), inv_mid)
     above[:, mid_cols] = mid_t.astype(BF)
     mid_out[...] = mid_t.T
     stores.append(pltpu.make_async_copy(mid_out, mid_hbm, out_sems.at[1]))
@@ -519,15 +541,16 @@
     rhs_mine = jnp.where(begin < mid_cols, low, high)
     group_begin = (group_cols // 2) * core + gq * pos
     group_mine = lax.dynamic_slice_in_dim(rhs_group[0], group_begin, gq, 0)
-    keep, send, leaf_solved, dense = leaf_forward(
+    keep, send, inv_here, rhs_here, leaf_solved, dense = leaf_forward(
         rhs_leaf[0],
         inv_leaf[0],
         leaf_tiles[0],
         tile_column,
         tile_target,
         tile_count,
+        inv_group[0],
+        rhs_group[0],
         sec,
-        group_cols,
         upper_cols,
     )
     with jax.named_scope("swap_cores"):
@@ -537,9 +560,9 @@
     with jax.named_scope("gather_middle_panel"):
         if by_parts:
             middles = swaps(stack(after(middles, send)), "leaf", n_leaf)
-            recv = after(recv, (middles, rhs_mine, group_mine))
-            middle = stack(middles)
-    parts, group = fold(keep, recv, inv_group[0], rhs_group[0], panel, n_leaf)
+            recv = after(recv, middles)
+            middle = stack(after(middles, (rhs_mine, group_mine)))
+    parts, group = fold(keep, recv, inv_here, rhs_here, panel, n_leaf)
     with jax.named_scope("sum_over_leaf"):
         parts = parts[:1] + [swap(parts[k], "leaf", n_leaf, k) for k in range(1, n_leaf)]
     with jax.named_scope("gather_middle_panel"):

time: 103 us -> 102 us (level)
  Pallas kernels: 25 us -> 22.9 us
  local copies, waits for them, and re-layouts: 1.9 us -> 3.13 us
    pallas_call x1 -> x0, Pallas kernels: 3.19 us -> none  [fold(): pl.pallas_call(functools.partial(fold_kernel, n_leaf, n_pos), out_shape=[...]
    pallas_call x7 -> x8, Pallas kernels: 0.4 us -> 2.53 us  [small(): pl.pallas_call(kernel, out_shape=[pltpu.VMEM(shape, BF) for shape in shap...]
    pallas_call x1, Pallas kernels: 12 us -> 10.4 us  [backward(): pl.pallas_call(functools.partial(backward_kernel, n_leaf, n_pos), out_sha...]
    unnamed x8 -> x12, local copies, waits for them, and re-layouts: 1.06 us -> 2.29 us
  transfers between devices with their start and end apart: 23 -> 23, of which waited for: 14 -> 14; matrix products, arithmetic and copies ran while one was open for 2% -> 2% of each run, Pallas kernels for 13% -> 12%
where the time goes in v9:
time: 102 us
  waiting for transfers between devices  33.5 us (33%)
  starting transfers between devices  26.6 us (26%)
  Pallas kernels  22.9 us (22%)
  between operations  14.8 us (15%)
  local copies, waits for them, and re-layouts  3.13 us (3%)
    ppermute x22, waiting for transfers between devices, swap(): return lax.ppermute(x, axis, [(i, i ^ bits) for i in range(size)])  31.7 us
    ppermute x22, starting transfers between devices, swap(): return lax.ppermute(x, axis, [(i, i ^ bits) for i in range(size)])  26.6 us
    pallas_call x1, Pallas kernels, backward(): pl.pallas_call(functools.partial(backward_kernel, n_leaf, n_pos), out_sha...  10.4 us
    pallas_call x1, Pallas kernels, leaf_forward(): pl.pallas_call(functools.partial(forward_kernel, sec, group_cols), out_sh...  9.93 us
    pallas_call x8, Pallas kernels, small(): pl.pallas_call(kernel, out_shape=[pltpu.VMEM(shape, BF) for shape in shap...  2.53 us
    unnamed x12, local copies, waits for them, and re-layouts  2.29 us
  transfers between devices with their start and end apart: 23, of which 14 were waited for; matrix products, arithmetic and copies ran while one was open for 2% of the time, Pallas kernels for 12%

profile of v9, /device:TPU:0, one launch (start us, length us, event | category | flops | bytes accessed | tf_op | source)
XLA Modules:
  0.0 101.9 jit_solution(1183861323358867281)
XLA Ops:
  7.9 5.1 %collective-permute-start.2 = (bf16[32,1024]{1,0:T(8,128)(2,1)}, bf16[32,1024]{1,0:T(8,128)(2,1)S(1)}, u32[]{:S(2)}, u32[]{:S(2)}) collective-permute-start(bf16[32,1024]{1,0:T(8,128)(2,1)} %refs_0_), channel_id=1, source_target_pairs={{0,6},{1,7},{2,4},{3,5},{4,2},{5,3},{6,0},{7,1},{8,14},{9,15},{10,... | collective-permute-start | bytes 196616 | tf_op jit(solution)/shard_map/gather_middle_panel/ppermute | solution.py:492
  14.3 9.9 %leaf_forward.1 = (bf16[1536,256]{1,0:T(8,128)(2,1)S(1)}, bf16[1536,256]{1,0:T(8,128)(2,1)}, bf16[512,512]{1,0:T(8,128)(2,1)S(1)}, f32[512,256]{1,0:T(8,128)S(1)...) custom-call(s32[1,1]{1,0:T(1,128)S(6)} %copy.18.count_hbm, s32[1,256]{1,0:T(1,128)} %cols_hbm.1, ...), custom_call_target="tpu_custom_call" | custom-call | flops 1342177280 | bytes 9437184 | tf_op jit(solution)/shard_map/leaf_forward/pallas_call | solution.py:175
  24.3 2.6 %collective-permute-start.6 = (bf16[128,1024]{1,0:T(8,128)(2,1)S(1)}, bf16[128,1024]{1,0:T(8,128)(2,1)S(1)}, u32[]{:S(2)}, u32[]{:S(2)}) collective-permute-start(bf16[128,1024]{1,0:T(8,128)(2,1)S(1)} %stack.3.refs_0_), channel_id=1, source_target_pairs={{0,24},{8,16},{16,8},{24,0},{1,25},{9,17},{17,9},{25,1},{2,26},{10... | collective-permute-start | bytes 786440 | tf_op jit(solution)/shard_map/gather_middle_panel/ppermute | solution.py:492
  29.9 4.7 %collective-permute-done.6.refs_3_ = bf16[128,1024]{1,0:T(8,128)(2,1)S(1)} collective-permute-done((bf16[128,1024]{1,0:T(8,128)(2,1)S(1)}, bf16[128,1024]{1,0:T(8,128)(2,1)S(1)}, u32[]{:S(2)}, u32[]{:S(2)}) %collective-permute-start.6) | collective-permute-done | bytes 262176 | tf_op jit(solution)/shard_map/gather_middle_panel/ppermute | solution.py:492
  34.6 3.1 %collective-permute-done.5.refs_2_ = bf16[128,1024]{1,0:T(8,128)(2,1)S(1)} collective-permute-done((bf16[128,1024]{1,0:T(8,128)(2,1)S(1)}, bf16[128,1024]{1,0:T(8,128)(2,1)S(1)}, u32[]{:S(2)}, u32[]{:S(2)}) %collective-permute-start.5) | collective-permute-done | bytes 262176 | tf_op jit(solution)/shard_map/gather_middle_panel/ppermute | solution.py:492
  40.2 2.9 %collective-permute-done.3.recv = bf16[1536,256]{1,0:T(8,128)(2,1)} collective-permute-done((bf16[1536,256]{1,0:T(8,128)(2,1)}, bf16[1536,256]{1,0:T(8,128)(2,1)}, u32[]{:S(2)}, u32[]{:S(2)}) %collective-permute-start.3) | collective-permute-done | bytes 786464 | tf_op jit(solution)/shard_map/swap_cores/ppermute | solution.py:492
  45.4 2.1 %fold_group.1 = (bf16[256,256]{1,0:T(8,128)(2,1)S(1)}, bf16[256,256]{1,0:T(8,128)(2,1)S(1)}, bf16[256,256]{1,0:T(8,128)(2,1)S(1)}, bf16[256,256]{1,0:T(8,128)(2,1)S(1)}, bf16[256,256]{1,0:T(8,128)(2,1)S(1)}) custom-call(bf16[1536,256]{1,0:T(8,128)(2,1)S(1)} %get-tuple-element.43.keep, bf16[1536,256]{1,0:T(8,128)(2,1)} %collective-permute-done.3.recv, ...), custom_call_target="tpu_custom_call" | custom-call | tf_op jit(solution)/shard_map/fold_group/pallas_call | solution.py:30
  47.9 1.2 %collective-permute-start.8 = (bf16[256,256]{1,0:T(8,128)(2,1)S(1)}, bf16[256,256]{1,0:T(8,128)(2,1)S(1)}, u32[]{:S(2)}, u32[]{:S(2)}) collective-permute-start(bf16[256,256]{1,0:T(8,128)(2,1)S(1)} %get-tuple-element.55), channel_id=1, source_target_pairs={{0,16},{8,24},{16,0},{24,8},{1,17},{9,25},{17,1},{25,9},{2,18},{10... | collective-permute-start | bytes 393224 | tf_op jit(solution)/shard_map/sum_over_leaf/ppermute | solution.py:492
  49.1 1.9 %collective-permute-start.9 = (bf16[256,256]{1,0:T(8,128)(2,1)S(1)}, bf16[256,256]{1,0:T(8,128)(2,1)S(1)}, u32[]{:S(2)}, u32[]{:S(2)}) collective-permute-start(bf16[256,256]{1,0:T(8,128)(2,1)S(1)} %get-tuple-element.56), channel_id=1, source_target_pairs={{0,24},{8,16},{16,8},{24,0},{1,25},{9,17},{17,9},{25,1},{2,26},{10... | collective-permute-start | bytes 393224 | tf_op jit(solution)/shard_map/sum_over_leaf/ppermute | solution.py:492
  51.2 2.7 %collective-permute-done.7.refs_1_ = bf16[256,256]{1,0:T(8,128)(2,1)S(1)} collective-permute-done((bf16[256,256]{1,0:T(8,128)(2,1)S(1)}, bf16[256,256]{1,0:T(8,128)(2,1)S(1)}, u32[]{:S(2)}, u32[]{:S(2)}) %collective-permute-start.7) | collective-permute-done | bytes 131104 | tf_op jit(solution)/shard_map/sum_over_leaf/ppermute | solution.py:492
  53.9 2.6 %collective-permute-done.9.refs_3_ = bf16[256,256]{1,0:T(8,128)(2,1)S(1)} collective-permute-done((bf16[256,256]{1,0:T(8,128)(2,1)S(1)}, bf16[256,256]{1,0:T(8,128)(2,1)S(1)}, u32[]{:S(2)}, u32[]{:S(2)}) %collective-permute-start.9) | collective-permute-done | bytes 131104 | tf_op jit(solution)/shard_map/sum_over_leaf/ppermute | solution.py:492
  56.6 1.4 %collective-permute-start.11 = (bf16[128,256]{1,0:T(8,128)(2,1)S(1)}, bf16[128,256]{1,0:T(8,128)(2,1)S(1)}, u32[]{:S(2)}, u32[]{:S(2)}) collective-permute-start(bf16[128,256]{1,0:T(8,128)(2,1)S(1)} %get-tuple-element.67), channel_id=1, source_target_pairs={{0,2},{1,3},{2,0},{3,1},{4,6},{5,7},{6,4},{7,5},{8,10},{9,11},{10,... | collective-permute-start | bytes 196616 | tf_op jit(solution)/shard_map/sum_over_pos/ppermute | solution.py:492
  57.9 3.4 %collective-permute-start.12 = (bf16[128,256]{1,0:T(8,128)(2,1)S(1)}, bf16[128,256]{1,0:T(8,128)(2,1)S(1)}, u32[]{:S(2)}, u32[]{:S(2)}) collective-permute-start(bf16[128,256]{1,0:T(8,128)(2,1)S(1)} %get-tuple-element.68), channel_id=1, source_target_pairs={{0,4},{1,5},{2,6},{3,7},{4,0},{5,1},{6,2},{7,3},{8,12},{9,13},{10,... | collective-permute-start | bytes 196616 | tf_op jit(solution)/shard_map/sum_over_pos/ppermute | solution.py:492
  61.4 4.1 %collective-permute-done.12.refs_2_ = bf16[128,256]{1,0:T(8,128)(2,1)S(1)} collective-permute-done((bf16[128,256]{1,0:T(8,128)(2,1)S(1)}, bf16[128,256]{1,0:T(8,128)(2,1)S(1)}, u32[]{:S(2)}, u32[]{:S(2)}) %collective-permute-start.12) | collective-permute-done | bytes 65568 | tf_op jit(solution)/shard_map/sum_over_pos/ppermute | solution.py:492
  65.5 1.9 %collective-permute-done.13.refs_3_ = bf16[128,256]{1,0:T(8,128)(2,1)S(1)} collective-permute-done((bf16[128,256]{1,0:T(8,128)(2,1)S(1)}, bf16[128,256]{1,0:T(8,128)(2,1)S(1)}, u32[]{:S(2)}, u32[]{:S(2)}) %collective-permute-start.13) | collective-permute-done | bytes 65568 | tf_op jit(solution)/shard_map/sum_over_pos/ppermute | solution.py:492
  67.5 1.4 %collective-permute-start.16 = (bf16[128,256]{1,0:T(8,128)(2,1)S(1)}, bf16[128,256]{1,0:T(8,128)(2,1)S(1)}, u32[]{:S(2)}, u32[]{:S(2)}) collective-permute-start(bf16[128,256]{1,0:T(8,128)(2,1)S(1)} %sum_pos.1.refs_0_), channel_id=1, source_target_pairs={{0,6},{1,7},{2,4},{3,5},{4,2},{5,3},{6,0},{7,1},{8,14},{9,15},{10,... | collective-permute-start | bytes 196616 | tf_op jit(solution)/shard_map/gather_pos/ppermute | solution.py:492
  68.9 3.0 %collective-permute-start.14 = (bf16[128,256]{1,0:T(8,128)(2,1)S(1)}, bf16[128,256]{1,0:T(8,128)(2,1)S(1)}, u32[]{:S(2)}, u32[]{:S(2)}) collective-permute-start(bf16[128,256]{1,0:T(8,128)(2,1)S(1)} %sum_pos.1.refs_0_), channel_id=1, source_target_pairs={{0,2},{1,3},{2,0},{3,1},{4,6},{5,7},{6,4},{7,5},{8,10},{9,11},{10,... | collective-permute-start | bytes 196616 | tf_op jit(solution)/shard_map/gather_pos/ppermute | solution.py:492
  71.9 1.7 %collective-permute-done.16.refs_3_ = bf16[128,256]{1,0:T(8,128)(2,1)S(1)} collective-permute-done((bf16[128,256]{1,0:T(8,128)(2,1)S(1)}, bf16[128,256]{1,0:T(8,128)(2,1)S(1)}, u32[]{:S(2)}, u32[]{:S(2)}) %collective-permute-start.16) | collective-permute-done | bytes 65568 | tf_op jit(solution)/shard_map/gather_pos/ppermute | solution.py:492
  73.7 1.4 %collective-permute-done.15.refs_2_ = bf16[128,256]{1,0:T(8,128)(2,1)S(1)} collective-permute-done((bf16[128,256]{1,0:T(8,128)(2,1)S(1)}, bf16[128,256]{1,0:T(8,128)(2,1)S(1)}, u32[]{:S(2)}, u32[]{:S(2)}) %collective-permute-start.15) | collective-permute-done | bytes 65568 | tf_op jit(solution)/shard_map/gather_pos/ppermute | solution.py:492
  75.0 1.5 %collective-permute-start.19 = (bf16[256,256]{1,0:T(8,128)(2,1)S(1)}, bf16[256,256]{1,0:T(8,128)(2,1)S(1)}, u32[]{:S(2)}, u32[]{:S(2)}) collective-permute-start(bf16[256,256]{1,0:T(8,128)(2,1)S(1)} %get-tuple-element.71.refs_0_), channel_id=1, source_target_pairs={{0,24},{8,16},{16,8},{24,0},{1,25},{9,17},{17,9},{25,1},{2,26},{10... | collective-permute-start | bytes 393224 | tf_op jit(solution)/shard_map/gather_leaf/ppermute | solution.py:492
  78.6 2.5 %collective-permute-done.19.refs_3_ = bf16[256,256]{1,0:T(8,128)(2,1)S(1)} collective-permute-done((bf16[256,256]{1,0:T(8,128)(2,1)S(1)}, bf16[256,256]{1,0:T(8,128)(2,1)S(1)}, u32[]{:S(2)}, u32[]{:S(2)}) %collective-permute-start.19) | collective-permute-done | bytes 131104 | tf_op jit(solution)/shard_map/gather_leaf/ppermute | solution.py:492
  81.1 1.3 %collective-permute-done.18.refs_2_ = bf16[256,256]{1,0:T(8,128)(2,1)S(1)} collective-permute-done((bf16[256,256]{1,0:T(8,128)(2,1)S(1)}, bf16[256,256]{1,0:T(8,128)(2,1)S(1)}, u32[]{:S(2)}, u32[]{:S(2)}) %collective-permute-start.18) | collective-permute-done | bytes 131104 | tf_op jit(solution)/shard_map/gather_leaf/ppermute | solution.py:492
  82.6 2.1 %collective-permute-done.21.theirs = bf16[1280,256]{1,0:T(8,128)(2,1)S(1)} collective-permute-done((bf16[1280,256]{1,0:T(8,128)(2,1)S(1)}, bf16[1280,256]{1,0:T(8,128)(2,1)S(1)}, u32[]{:S(2)}, u32[]{:S(2)}) %collective-permute-start.21) | collective-permute-done | bytes 655392 | tf_op jit(solution)/shard_map/gather_cores/ppermute | solution.py:492
  84.7 10.4 %backward.1 = (f32[1024,256]{1,0:T(8,128)}, f32[512,256]{1,0:T(8,128)}, f32[1024,256]{1,0:T(8,128)}, f32[1024,256]{1,0:T(8,128)}) custom-call(bf16[1280,256]{1,0:T(8,128)(2,1)S(1)} %stack.5.mine, bf16[1280,256]{1,0:T(8,128)(2,1)S(1)} %collective-permute-done.21.theirs, bf16[1024,1024]{1,0:T(8,128)(2,1)S(1)} %copy-done.1, ...), custom_call_target="tpu_custom_call" | custom-call | tf_op jit(solution)/shard_map/backward/pallas_call | solution.py:471
  (47 shorter events, 12.1 us)
Async XLA Ops:
  7.2 33.1 %all-gather.2.cloned.1.call-start = ((), (), s32[]{:S(2)}) async-start(), calls=%async_computation | async-start | bytes 1310720 | tf_op jit(solution)/shard_map/gather_group_panel/all_gather | solution.py:532
  7.9 16.4 %collective-permute-start.2 = (bf16[32,1024]{1,0:T(8,128)(2,1)}, bf16[32,1024]{1,0:T(8,128)(2,1)S(1)}, u32[]{:S(2)}, u32[]{:S(2)}) collective-permute-start(bf16[32,1024]{1,0:T(8,128)(2,1)} %refs_0_), channel_id=1, source_target_pairs={{0,6},{1,7},{2,4},{3,5},{4,2},{5,3},{6,0},{7,1},{8,14},{9,15},{10,... | collective-permute-start | bytes 196616 | tf_op jit(solution)/shard_map/gather_middle_panel/ppermute | solution.py:492
  13.0 11.3 %collective-permute-start.1 = (bf16[32,1024]{1,0:T(8,128)(2,1)}, bf16[32,1024]{1,0:T(8,128)(2,1)S(1)}, u32[]{:S(2)}, u32[]{:S(2)}) collective-permute-start(bf16[32,1024]{1,0:T(8,128)(2,1)} %refs_0_), channel_id=1, source_target_pairs={{0,4},{1,5},{2,6},{3,7},{4,0},{5,1},{6,2},{7,3},{8,12},{9,13},{10,... | collective-permute-start | bytes 196616 | tf_op jit(solution)/shard_map/gather_middle_panel/ppermute | solution.py:492
  13.0 11.3 %collective-permute-start = (bf16[32,1024]{1,0:T(8,128)(2,1)}, bf16[32,1024]{1,0:T(8,128)(2,1)S(1)}, u32[]{:S(2)}, u32[]{:S(2)}) collective-permute-start(bf16[32,1024]{1,0:T(8,128)(2,1)} %refs_0_), channel_id=1, source_target_pairs={{0,2},{1,3},{2,0},{3,1},{4,6},{5,7},{6,4},{7,5},{8,10},{9,11},{10,... | collective-permute-start | bytes 196616 | tf_op jit(solution)/shard_map/gather_middle_panel/ppermute | solution.py:492
  24.3 10.3 %collective-permute-start.6 = (bf16[128,1024]{1,0:T(8,128)(2,1)S(1)}, bf16[128,1024]{1,0:T(8,128)(2,1)S(1)}, u32[]{:S(2)}, u32[]{:S(2)}) collective-permute-start(bf16[128,1024]{1,0:T(8,128)(2,1)S(1)} %stack.3.refs_0_), channel_id=1, source_target_pairs={{0,24},{8,16},{16,8},{24,0},{1,25},{9,17},{17,9},{25,1},{2,26},{10... | collective-permute-start | bytes 786440 | tf_op jit(solution)/shard_map/gather_middle_panel/ppermute | solution.py:492
  26.9 10.7 %collective-permute-start.5 = (bf16[128,1024]{1,0:T(8,128)(2,1)S(1)}, bf16[128,1024]{1,0:T(8,128)(2,1)S(1)}, u32[]{:S(2)}, u32[]{:S(2)}) collective-permute-start(bf16[128,1024]{1,0:T(8,128)(2,1)S(1)} %stack.3.refs_0_), channel_id=1, source_target_pairs={{0,16},{8,24},{16,0},{24,8},{1,17},{9,25},{17,1},{25,9},{2,18},{10... | collective-permute-start | bytes 786440 | tf_op jit(solution)/shard_map/gather_middle_panel/ppermute | solution.py:492
  27.4 11.1 %collective-permute-start.4 = (bf16[128,1024]{1,0:T(8,128)(2,1)S(1)}, bf16[128,1024]{1,0:T(8,128)(2,1)S(1)}, u32[]{:S(2)}, u32[]{:S(2)}) collective-permute-start(bf16[128,1024]{1,0:T(8,128)(2,1)S(1)} %stack.3.refs_0_), channel_id=1, source_target_pairs={{0,8},{8,0},{16,24},{24,16},{1,9},{9,1},{17,25},{25,17},{2,10},{10... | collective-permute-start | bytes 786440 | tf_op jit(solution)/shard_map/gather_middle_panel/ppermute | solution.py:492
  38.5 12.6 %collective-permute-start.10 = (bf16[512,1024]{1,0:T(8,128)(2,1)S(1)}, bf16[512,1024]{1,0:T(8,128)(2,1)S(1)}, u32[]{:S(2)}, u32[]{:S(2)}) collective-permute-start(bf16[512,1024]{1,0:T(8,128)(2,1)S(1)} %stack.4.own), channel_id=1, source_target_pairs={{0,1},{1,0},{2,3},{3,2},{4,5},{5,4},{6,7},{7,6},{8,9},{9,8},{10,11... | collective-permute-start | bytes 3145736 | tf_op jit(solution)/shard_map/gather_middle_panel/ppermute | solution.py:492
  38.6 4.5 %collective-permute-start.3 = (bf16[1536,256]{1,0:T(8,128)(2,1)}, bf16[1536,256]{1,0:T(8,128)(2,1)}, u32[]{:S(2)}, u32[]{:S(2)}) collective-permute-start(bf16[1536,256]{1,0:T(8,128)(2,1)} %get-tuple-element.45), channel_id=1, source_target_pairs={{0,1},{1,0},{2,3},{3,2},{4,5},{5,4},{6,7},{7,6},{8,9},{9,8},{10,11... | collective-permute-start | bytes 2359304 | tf_op jit(solution)/shard_map/swap_cores/ppermute | solution.py:492
  40.2 42.2 %collective-permute-start.20 = (bf16[4,256,512]{2,1,0:T(8,128)(2,1)}, bf16[4,256,512]{2,1,0:T(8,128)(2,1)S(1)}, u32[]{:S(2)}, u32[]{:S(2)}) collective-permute-start(bf16[4,256,512]{2,1,0:T(8,128)(2,1)} %all-gather.2.cloned.1.call-done.panel.panel_own_hbm), channel_id=1, source_target_pairs={{0,1},{1,0},{2,3},{3,2},{4,5},{5,4},{6,7},{7,6},{8,9},{9,8},{10,11... | collective-permute-start | bytes 3145736 | tf_op jit(solution)/shard_map/swap_group_panel/ppermute | solution.py:492
  47.5 6.4 %collective-permute-start.7 = (bf16[256,256]{1,0:T(8,128)(2,1)S(1)}, bf16[256,256]{1,0:T(8,128)(2,1)S(1)}, u32[]{:S(2)}, u32[]{:S(2)}) collective-permute-start(bf16[256,256]{1,0:T(8,128)(2,1)S(1)} %get-tuple-element.54), channel_id=1, source_target_pairs={{0,8},{8,0},{16,24},{24,16},{1,9},{9,1},{17,25},{25,17},{2,10},{10... | collective-permute-start | bytes 393224 | tf_op jit(solution)/shard_map/sum_over_leaf/ppermute | solution.py:492
  47.9 6.0 %collective-permute-start.8 = (bf16[256,256]{1,0:T(8,128)(2,1)S(1)}, bf16[256,256]{1,0:T(8,128)(2,1)S(1)}, u32[]{:S(2)}, u32[]{:S(2)}) collective-permute-start(bf16[256,256]{1,0:T(8,128)(2,1)S(1)} %get-tuple-element.55), channel_id=1, source_target_pairs={{0,16},{8,24},{16,0},{24,8},{1,17},{9,25},{17,1},{25,9},{2,18},{10... | collective-permute-start | bytes 393224 | tf_op jit(solution)/shard_map/sum_over_leaf/ppermute | solution.py:492
  49.1 7.4 %collective-permute-start.9 = (bf16[256,256]{1,0:T(8,128)(2,1)S(1)}, bf16[256,256]{1,0:T(8,128)(2,1)S(1)}, u32[]{:S(2)}, u32[]{:S(2)}) collective-permute-start(bf16[256,256]{1,0:T(8,128)(2,1)S(1)} %get-tuple-element.56), channel_id=1, source_target_pairs={{0,24},{8,16},{16,8},{24,0},{1,25},{9,17},{17,9},{25,1},{2,26},{10... | collective-permute-start | bytes 393224 | tf_op jit(solution)/shard_map/sum_over_leaf/ppermute | solution.py:492
  51.2 33.4 %copy-start.1 = (bf16[1024,1024]{1,0:T(8,128)(2,1)S(1)}, bf16[1024,1024]{1,0:T(8,128)(2,1)}, u32[]{:S(2)}) copy-start(bf16[1024,1024]{1,0:T(8,128)(2,1)} %inv_mid.1) | copy-start | bytes 6291460
  56.6 4.8 %collective-permute-start.11 = (bf16[128,256]{1,0:T(8,128)(2,1)S(1)}, bf16[128,256]{1,0:T(8,128)(2,1)S(1)}, u32[]{:S(2)}, u32[]{:S(2)}) collective-permute-start(bf16[128,256]{1,0:T(8,128)(2,1)S(1)} %get-tuple-element.67), channel_id=1, source_target_pairs={{0,2},{1,3},{2,0},{3,1},{4,6},{5,7},{6,4},{7,5},{8,10},{9,11},{10,... | collective-permute-start | bytes 196616 | tf_op jit(solution)/shard_map/sum_over_pos/ppermute | solution.py:492
  57.9 7.6 %collective-permute-start.12 = (bf16[128,256]{1,0:T(8,128)(2,1)S(1)}, bf16[128,256]{1,0:T(8,128)(2,1)S(1)}, u32[]{:S(2)}, u32[]{:S(2)}) collective-permute-start(bf16[128,256]{1,0:T(8,128)(2,1)S(1)} %get-tuple-element.68), channel_id=1, source_target_pairs={{0,4},{1,5},{2,6},{3,7},{4,0},{5,1},{6,2},{7,3},{8,12},{9,13},{10,... | collective-permute-start | bytes 196616 | tf_op jit(solution)/shard_map/sum_over_pos/ppermute | solution.py:492
  61.4 6.1 %collective-permute-start.13 = (bf16[128,256]{1,0:T(8,128)(2,1)S(1)}, bf16[128,256]{1,0:T(8,128)(2,1)S(1)}, u32[]{:S(2)}, u32[]{:S(2)}) collective-permute-start(bf16[128,256]{1,0:T(8,128)(2,1)S(1)} %get-tuple-element.69), channel_id=1, source_target_pairs={{0,6},{1,7},{2,4},{3,5},{4,2},{5,3},{6,0},{7,1},{8,14},{9,15},{10,... | collective-permute-start | bytes 196616 | tf_op jit(solution)/shard_map/sum_over_pos/ppermute | solution.py:492
  67.5 6.2 %collective-permute-start.16 = (bf16[128,256]{1,0:T(8,128)(2,1)S(1)}, bf16[128,256]{1,0:T(8,128)(2,1)S(1)}, u32[]{:S(2)}, u32[]{:S(2)}) collective-permute-start(bf16[128,256]{1,0:T(8,128)(2,1)S(1)} %sum_pos.1.refs_0_), channel_id=1, source_target_pairs={{0,6},{1,7},{2,4},{3,5},{4,2},{5,3},{6,0},{7,1},{8,14},{9,15},{10,... | collective-permute-start | bytes 196616 | tf_op jit(solution)/shard_map/gather_pos/ppermute | solution.py:492
  68.9 6.1 %collective-permute-start.15 = (bf16[128,256]{1,0:T(8,128)(2,1)S(1)}, bf16[128,256]{1,0:T(8,128)(2,1)S(1)}, u32[]{:S(2)}, u32[]{:S(2)}) collective-permute-start(bf16[128,256]{1,0:T(8,128)(2,1)S(1)} %sum_pos.1.refs_0_), channel_id=1, source_target_pairs={{0,4},{1,5},{2,6},{3,7},{4,0},{5,1},{6,2},{7,3},{8,12},{9,13},{10,... | collective-permute-start | bytes 196616 | tf_op jit(solution)/shard_map/gather_pos/ppermute | solution.py:492
  68.9 6.1 %collective-permute-start.14 = (bf16[128,256]{1,0:T(8,128)(2,1)S(1)}, bf16[128,256]{1,0:T(8,128)(2,1)S(1)}, u32[]{:S(2)}, u32[]{:S(2)}) collective-permute-start(bf16[128,256]{1,0:T(8,128)(2,1)S(1)} %sum_pos.1.refs_0_), channel_id=1, source_target_pairs={{0,2},{1,3},{2,0},{3,1},{4,6},{5,7},{6,4},{7,5},{8,10},{9,11},{10,... | collective-permute-start | bytes 196616 | tf_op jit(solution)/shard_map/gather_pos/ppermute | solution.py:492
  75.0 6.0 %collective-permute-start.19 = (bf16[256,256]{1,0:T(8,128)(2,1)S(1)}, bf16[256,256]{1,0:T(8,128)(2,1)S(1)}, u32[]{:S(2)}, u32[]{:S(2)}) collective-permute-start(bf16[256,256]{1,0:T(8,128)(2,1)S(1)} %get-tuple-element.71.refs_0_), channel_id=1, source_target_pairs={{0,24},{8,16},{16,8},{24,0},{1,25},{9,17},{17,9},{25,1},{2,26},{10... | collective-permute-start | bytes 393224 | tf_op jit(solution)/shard_map/gather_leaf/ppermute | solution.py:492
  76.5 5.8 %collective-permute-start.18 = (bf16[256,256]{1,0:T(8,128)(2,1)S(1)}, bf16[256,256]{1,0:T(8,128)(2,1)S(1)}, u32[]{:S(2)}, u32[]{:S(2)}) collective-permute-start(bf16[256,256]{1,0:T(8,128)(2,1)S(1)} %get-tuple-element.71.refs_0_), channel_id=1, source_target_pairs={{0,16},{8,24},{16,0},{24,8},{1,17},{9,25},{17,1},{25,9},{2,18},{10... | collective-permute-start | bytes 393224 | tf_op jit(solution)/shard_map/gather_leaf/ppermute | solution.py:492
  77.5 5.0 %collective-permute-start.17 = (bf16[256,256]{1,0:T(8,128)(2,1)S(1)}, bf16[256,256]{1,0:T(8,128)(2,1)S(1)}, u32[]{:S(2)}, u32[]{:S(2)}) collective-permute-start(bf16[256,256]{1,0:T(8,128)(2,1)S(1)} %get-tuple-element.71.refs_0_), channel_id=1, source_target_pairs={{0,8},{8,0},{16,24},{24,16},{1,9},{9,1},{17,25},{25,17},{2,10},{10... | collective-permute-start | bytes 393224 | tf_op jit(solution)/shard_map/gather_leaf/ppermute | solution.py:492
  82.5 2.2 %collective-permute-start.21 = (bf16[1280,256]{1,0:T(8,128)(2,1)S(1)}, bf16[1280,256]{1,0:T(8,128)(2,1)S(1)}, u32[]{:S(2)}, u32[]{:S(2)}) collective-permute-start(bf16[1280,256]{1,0:T(8,128)(2,1)S(1)} %stack.5.mine), channel_id=1, source_target_pairs={{0,1},{1,0},{2,3},{3,2},{4,5},{5,4},{6,7},{7,6},{8,9},{9,8},{10,11... | collective-permute-start | bytes 1966088 | tf_op jit(solution)/shard_map/gather_cores/ppermute | solution.py:492
  (5 other events, 17.2 us)
Sparse Core Ops, SparseCore 0:
  9.6 30.6 all-gather.1

commit v10 on v9

--- a/solution.py
+++ b/solution.py
@@ -48,6 +48,7 @@
 
 
 def forward_kernel(
+    n_pos,
     sec,
     group_cols,
     count_hbm,
@@ -59,9 +60,9 @@
     inv_group_hbm,
     rhs_group_hbm,
     keep,
-    send,
+    send_low,
+    send_high,
     inv_group,
-    rhs_group,
     solved_hbm,
     dense_hbm,
     count,
@@ -74,6 +75,7 @@
     stage,
     solved,
     dense,
+    rhs_group,
     in_sems,
     tile_sems,
     out_sems,
@@ -148,18 +150,24 @@
         rows = pl.ds(i * span, span)
         stores.append(pltpu.make_async_copy(dense.at[rows], dense_hbm.at[rows], out_sems.at[1 + i]))
         stores[-1].start()
-        total = dot(dense[rows, :], solved[...]).astype(BF)
+        total = dot(dense[rows, :], solved[...])
         if i == 0:
+            passes[1].wait()
+            share = jnp.where(core == 0, 1.0 / n_pos, 0.0)
+            total = (total - rhs_group[...] * share).astype(BF)
             stage[0, 0:span, :] = total
             stage[1, 0:span, :] = total
         else:
+            total = total.astype(BF)
             for q in range(0, span, sec):
                 section = ((i - 1) * span + q) // sec
                 begin = group_cols + (section // 2) * sec
                 stage[(section % 2) ^ core, begin : begin + sec, :] = total[q : q + sec, :]
     keep[...] = stage[0]
-    send[...] = stage[1]
-    for copy in passes + stores:
+    cut = send_low.shape[0]
+    send_low[...] = stage[1, 0:cut, :]
+    send_high[...] = stage[1, cut:, :]
+    for copy in passes[:1] + stores:
         copy.wait()
 
 
@@ -173,12 +181,12 @@
     width = rhs.shape[-1]
     half = group_cols + upper_cols // 2
     return pl.pallas_call(
-        functools.partial(forward_kernel, sec, group_cols),
+        functools.partial(forward_kernel, upper_cols // (2 * sec), sec, group_cols),
         out_shape=(
             pltpu.VMEM((half, width), BF),
-            pltpu.VMEM((half, width), BF),
+            pltpu.VMEM((half // 2, width), BF),
+            pltpu.VMEM((half // 2, width), BF),
             pltpu.VMEM(inv_group.shape, BF),
-            pltpu.VMEM(rhs_group.shape, F32),
             pltpu.HBM((supernodes * block, width), BF),
             pltpu.HBM((targets * block, supernodes * block), BF),
         ),
@@ -195,6 +203,7 @@
             pltpu.VMEM((2, half, width), BF),
             pltpu.VMEM((supernodes * block, width), BF),
             pltpu.VMEM((targets * block, supernodes * block), BF),
+            pltpu.VMEM(rhs_group.shape, F32),
             pltpu.SemaphoreType.DMA((5,)),
             pltpu.SemaphoreType.DMA((CHUNKS,)),
             pltpu.SemaphoreType.DMA((1 + targets * block // group_cols,)),
@@ -217,21 +226,22 @@
     return total
 
 
-def fold_kernel(n_leaf, n_pos, keep, recv, inv, rhs, panel, *refs):
-    parts, group, (gsum, stage) = refs[:n_leaf], refs[n_leaf], refs[n_leaf + 1 :]
+def fold_kernel(n_leaf, n_pos, keep, low, high, inv, panel, *refs):
+    parts, group, (gsum, base, stage) = refs[:n_leaf], refs[n_leaf], refs[n_leaf + 1 :]
     leaf, pos, core = place()
     group_cols = inv.shape[0]
     sec = panel.shape[1]
     q = sec // n_leaf
     gq = group_cols // (2 * n_pos)
-    gsum[...] = keep[0:group_cols, :].astype(F32) + recv[0:group_cols, :].astype(F32)
-    residual = rhs[...] * (1.0 / n_pos) - gsum[...]
-    solved = dot(inv[...], residual.astype(BF)).astype(BF)
+    cut = low.shape[0]
+    gsum[...] = keep[0:group_cols, :].astype(F32) + low[0:group_cols, :].astype(F32)
+    base[0 : cut - group_cols, :] = keep[group_cols:cut, :].astype(F32) + low[group_cols:, :].astype(F32)
+    base[cut - group_cols :, :] = keep[cut:, :].astype(F32) + high[...].astype(F32)
+    solved = dot(inv[...], (-gsum[...]).astype(BF)).astype(BF)
     for k in range(n_pos):
         p = pos ^ k
-        rows = pl.ds(pl.multiple_of(group_cols + p * sec, sec), sec)
-        terms = dot(panel[p], solved)
-        terms = (terms + (keep[rows, :].astype(F32) + recv[rows, :].astype(F32))).astype(BF)
+        rows = pl.ds(pl.multiple_of(p * sec, sec), sec)
+        terms = (dot(panel[p], solved) + base[rows, :]).astype(BF)
         for j in range(n_leaf):
             stage[j ^ leaf, k * q : (k + 1) * q, :] = terms[j * q : (j + 1) * q, :]
         begin = pl.multiple_of(core * (group_cols // 2) + p * gq, gq)
@@ -240,19 +250,22 @@
         parts[k][...] = stage[k]
 
 
-def fold(keep, recv, inverse, rhs, panel, n_leaf):
-    width = rhs.shape[-1]
+def fold(keep, recv, inverse, panel, n_leaf):
+    width = keep.shape[-1]
     n_pos, sec, _ = panel.shape
     part = (n_pos * sec // n_leaf, width)
     outs = small(
         functools.partial(fold_kernel, n_leaf, n_pos),
         "fold_group",
         [part] * n_leaf + [(inverse.shape[0] // 2, width)],
-        [pltpu.VMEM(rhs.shape, F32), pltpu.VMEM((n_leaf,) + part, BF)],
+        [
+            pltpu.VMEM((inverse.shape[0], width), F32),
+            pltpu.VMEM((n_pos * sec, width), F32),
+            pltpu.VMEM((n_leaf,) + part, BF),
+        ],
         keep,
-        recv,
+        *recv,
         inverse,
-        rhs,
         panel,
     )
     return list(outs[:n_leaf]), outs[n_leaf]
@@ -276,16 +289,16 @@
     return list(small(kernel, "sum_leaf", shapes, [], *parts, group))
 
 
-def sum_pos_kernel(high, group, *refs):
+def sum_pos_kernel(high, *refs):
     parts, out = refs[:-1], refs[-1]
     q = high.shape[0]
     total = total_of(parts)
     out[0:q, :] = (high[...] - total[0:q, :]).astype(BF)
-    out[q:, :] = (group[...] - total[q:, :]).astype(BF)
-
-
-def sum_pos(high, group, parts):
-    return small(sum_pos_kernel, "sum_pos", [parts[0].shape], [], high, group, *parts)[0]
+    out[q:, :] = (-total[q:, :]).astype(BF)
+
+
+def sum_pos(high, parts):
+    return small(sum_pos_kernel, "sum_pos", [parts[0].shape], [], high, *parts)[0]
 
 
 def stack_pos_kernel(q, *refs):
@@ -539,9 +552,7 @@
     low = lax.dynamic_slice_in_dim(rhs_middle, jnp.minimum(begin, mid_cols - q), q, 0)
     high = lax.dynamic_slice_in_dim(rhs_top, jnp.maximum(begin - mid_cols, 0), q, 0)
     rhs_mine = jnp.where(begin < mid_cols, low, high)
-    group_begin = (group_cols // 2) * core + gq * pos
-    group_mine = lax.dynamic_slice_in_dim(rhs_group[0], group_begin, gq, 0)
-    keep, send, inv_here, rhs_here, leaf_solved, dense = leaf_forward(
+    keep, *send, inv_here, leaf_solved, dense = leaf_forward(
         rhs_leaf[0],
         inv_leaf[0],
         leaf_tiles[0],
@@ -556,30 +567,31 @@
     with jax.named_scope("swap_cores"):
         if by_parts:
             send = after(send, middles)
-        recv = swap(send, "grp", n_grp, 1)
+        recv = [swap(x, "grp", n_grp, 1) for x in send]
     with jax.named_scope("gather_middle_panel"):
         if by_parts:
             middles = swaps(stack(after(middles, send)), "leaf", n_leaf)
             recv = after(recv, middles)
-            middle = stack(after(middles, (rhs_mine, group_mine)))
-    parts, group = fold(keep, recv, inv_here, rhs_here, panel, n_leaf)
+            middle = stack(after(middles, rhs_mine))
+    parts, group = fold(keep, recv, inv_here, panel, n_leaf)
     with jax.named_scope("sum_over_leaf"):
         parts = parts[:1] + [swap(parts[k], "leaf", n_leaf, k) for k in range(1, n_leaf)]
     with jax.named_scope("gather_middle_panel"):
         if by_parts:
-            middle = weave(middle, swap(middle, "grp", n_grp, 1), n_leaf, n_pos)
-    sends = sum_leaf(after(parts, middle), group, n_pos)
+            other = swap(after(middle, group), "grp", n_grp, 1)
+            middle = weave(middle, other, n_leaf, n_pos)
+    sends = sum_leaf(parts, group, n_pos)
     with jax.named_scope("sum_over_pos"):
         got = sends[:1] + [swap(sends[k], "grp", n_grp, 2 * k) for k in range(1, n_pos)]
     with jax.named_scope("swap_group_panel"):
-        panel_other = swap(panel, "grp", n_grp, 1)
-    residual = sum_pos(rhs_mine, group_mine, got)
+        panel_other = swap(after(panel, sends), "grp", n_grp, 1)
+    residual = sum_pos(rhs_mine, got)
     with jax.named_scope("gather_pos"):
         uppers, groups = stack_pos(swaps(residual, "grp", n_grp, 2), q)
     with jax.named_scope("gather_leaf"):
         stacks = swaps(uppers, "leaf", n_leaf)
     with jax.named_scope("gather_cores"):
-        mine = stack(after(stacks, panel_other) + [groups])
+        mine = stack(after(stacks, (panel_other, middle)) + [groups])
         theirs = swap(mine, "grp", n_grp, 1)
     leaf_out, group_out, mid_out, top_out = backward(
         (mine, theirs, inv_middle, middle),

time: 102 us -> 100 us (0.980)
  Pallas kernels: 22.9 us -> 21.5 us
  waiting for transfers between devices: 33.5 us -> 34.8 us
  local copies, waits for them, and re-layouts: 3.13 us -> 1.9 us
    ppermute x22 -> x23, waiting for transfers between devices: 31.7 us -> 33.2 us  [swap(): return lax.ppermute(x, axis, [(i, i ^ bits) for i in range(size)])]
    unnamed x12 -> x14, local copies, waits for them, and re-layouts: 2.29 us -> 1.9 us
    ppermute x22 -> x23, starting transfers between devices: 26.6 us -> 26.2 us  [swap(): return lax.ppermute(x, axis, [(i, i ^ bits) for i in range(size)])]
  transfers between devices with their start and end apart: 23 -> 24, of which waited for: 14 -> 14; matrix products, arithmetic and copies ran while one was open for 2% -> 1% of each run, Pallas kernels for 12% -> 9%
where the time goes in v10:
time: 100 us
  waiting for transfers between devices  34.8 us (35%)
  starting transfers between devices  26.3 us (26%)
  Pallas kernels  21.5 us (22%)
  between operations  14.9 us (15%)
  local copies, waits for them, and re-layouts  1.9 us (2%)
    ppermute x23, waiting for transfers between devices, swap(): return lax.ppermute(x, axis, [(i, i ^ bits) for i in range(size)])  33.2 us
    ppermute x23, starting transfers between devices, swap(): return lax.ppermute(x, axis, [(i, i ^ bits) for i in range(size)])  26.2 us
    pallas_call x1, Pallas kernels, backward(): pl.pallas_call(functools.partial(backward_kernel, n_leaf, n_pos), out_sha...  10.4 us
    pallas_call x1, Pallas kernels, leaf_forward(): pl.pallas_call(functools.partial(forward_kernel, upper_cols // (2 * sec),...  8.96 us
    pallas_call x8, Pallas kernels, small(): pl.pallas_call(kernel, out_shape=[pltpu.VMEM(shape, BF) for shape in shap...  2.1 us
  transfers between devices with their start and end apart: 24, of which 14 were waited for; matrix products, arithmetic and copies ran while one was open for 1% of the time, Pallas kernels for 9%

profile of v10, /device:TPU:0, one launch (start us, length us, event | category | flops | bytes accessed | tf_op | source)
XLA Modules:
  0.0 100.2 jit_solution(6049180496040450139)
XLA Ops:
  7.9 5.1 %collective-permute-start.2 = (bf16[32,1024]{1,0:T(8,128)(2,1)}, bf16[32,1024]{1,0:T(8,128)(2,1)S(1)}, u32[]{:S(2)}, u32[]{:S(2)}) collective-permute-start(bf16[32,1024]{1,0:T(8,128)(2,1)} %refs_0_), channel_id=1, source_target_pairs={{0,6},{1,7},{2,4},{3,5},{4,2},{5,3},{6,0},{7,1},{8,14},{9,15},{10,... | collective-permute-start | bytes 196616 | tf_op jit(solution)/shard_map/gather_middle_panel/ppermute | solution.py:505
  14.3 9.0 %leaf_forward.1 = (bf16[1536,256]{1,0:T(8,128)(2,1)S(1)}, bf16[768,256]{1,0:T(8,128)(2,1)S(1)}, bf16[768,256]{1,0:T(8,128)(2,1)S(1)}, bf16[512,512]{1,0:T(8,128)...) custom-call(s32[1,1]{1,0:T(1,128)S(6)} %copy.18.count_hbm, s32[1,256]{1,0:T(1,128)} %cols_hbm.1, ...), custom_call_target="tpu_custom_call" | custom-call | flops 1342177280 | bytes 9437184 | tf_op jit(solution)/shard_map/leaf_forward/pallas_call | solution.py:183
  23.9 3.1 %collective-permute-start.7 = (bf16[128,1024]{1,0:T(8,128)(2,1)S(1)}, bf16[128,1024]{1,0:T(8,128)(2,1)S(1)}, u32[]{:S(2)}, u32[]{:S(2)}) collective-permute-start(bf16[128,1024]{1,0:T(8,128)(2,1)S(1)} %stack.3.refs_0_), channel_id=1, source_target_pairs={{0,24},{8,16},{16,8},{24,0},{1,25},{9,17},{17,9},{25,1},{2,26},{10... | collective-permute-start | bytes 786440 | tf_op jit(solution)/shard_map/gather_middle_panel/ppermute | solution.py:505
  27.7 6.5 %collective-permute-done.7.refs_3_ = bf16[128,1024]{1,0:T(8,128)(2,1)S(1)} collective-permute-done((bf16[128,1024]{1,0:T(8,128)(2,1)S(1)}, bf16[128,1024]{1,0:T(8,128)(2,1)S(1)}, u32[]{:S(2)}, u32[]{:S(2)}) %collective-permute-start.7) | collective-permute-done | bytes 262176 | tf_op jit(solution)/shard_map/gather_middle_panel/ppermute | solution.py:505
  34.2 5.0 %collective-permute-done.6.refs_2_ = bf16[128,1024]{1,0:T(8,128)(2,1)S(1)} collective-permute-done((bf16[128,1024]{1,0:T(8,128)(2,1)S(1)}, bf16[128,1024]{1,0:T(8,128)(2,1)S(1)}, u32[]{:S(2)}, u32[]{:S(2)}) %collective-permute-start.6) | collective-permute-done | bytes 262176 | tf_op jit(solution)/shard_map/gather_middle_panel/ppermute | solution.py:505
  40.2 1.2 %copy-done = bf16[4,256,512]{2,1,0:T(8,128)(2,1)S(1)} copy-done((bf16[4,256,512]{2,1,0:T(8,128)(2,1)S(1)}, bf16[4,256,512]{2,1,0:T(8,128)(2,1)}, u32[]{:S(2)}) %copy-start) | copy-done | bytes 1048600
  41.5 1.7 %fold_group.1 = (bf16[256,256]{1,0:T(8,128)(2,1)S(1)}, bf16[256,256]{1,0:T(8,128)(2,1)}, bf16[256,256]{1,0:T(8,128)(2,1)}, bf16[256,256]{1,0:T(8,128)(2,1)}, bf16[256,256]{1,0:T(8,128)(2,1)S(1)}) custom-call(bf16[1536,256]{1,0:T(8,128)(2,1)S(1)} %get-tuple-element.43.keep, bf16[768,256]{1,0:T(8,128)(2,1)S(1)} %collective-permute-done.3.low, ...), custom_call_target="tpu_custom_call" | custom-call | tf_op jit(solution)/shard_map/fold_group/pallas_call | solution.py:30
  43.8 1.5 %collective-permute-start.8 = (bf16[256,256]{1,0:T(8,128)(2,1)}, bf16[256,256]{1,0:T(8,128)(2,1)S(1)}, u32[]{:S(2)}, u32[]{:S(2)}) collective-permute-start(bf16[256,256]{1,0:T(8,128)(2,1)} %get-tuple-element.56), channel_id=1, source_target_pairs={{0,8},{8,0},{16,24},{24,16},{1,9},{9,1},{17,25},{25,17},{2,10},{10... | collective-permute-start | bytes 393224 | tf_op jit(solution)/shard_map/sum_over_leaf/ppermute | solution.py:505
  45.3 1.5 %collective-permute-start.9 = (bf16[256,256]{1,0:T(8,128)(2,1)}, bf16[256,256]{1,0:T(8,128)(2,1)S(1)}, u32[]{:S(2)}, u32[]{:S(2)}) collective-permute-start(bf16[256,256]{1,0:T(8,128)(2,1)} %get-tuple-element.57), channel_id=1, source_target_pairs={{0,16},{8,24},{16,0},{24,8},{1,17},{9,25},{17,1},{25,9},{2,18},{10... | collective-permute-start | bytes 393224 | tf_op jit(solution)/shard_map/sum_over_leaf/ppermute | solution.py:505
  48.4 1.1 %collective-permute-done.8.refs_1_ = bf16[256,256]{1,0:T(8,128)(2,1)S(1)} collective-permute-done((bf16[256,256]{1,0:T(8,128)(2,1)}, bf16[256,256]{1,0:T(8,128)(2,1)S(1)}, u32[]{:S(2)}, u32[]{:S(2)}) %collective-permute-start.8) | collective-permute-done | bytes 131104 | tf_op jit(solution)/shard_map/sum_over_leaf/ppermute | solution.py:505
  49.5 3.7 %collective-permute-done.9.refs_2_ = bf16[256,256]{1,0:T(8,128)(2,1)S(1)} collective-permute-done((bf16[256,256]{1,0:T(8,128)(2,1)}, bf16[256,256]{1,0:T(8,128)(2,1)S(1)}, u32[]{:S(2)}, u32[]{:S(2)}) %collective-permute-start.9) | collective-permute-done | bytes 131104 | tf_op jit(solution)/shard_map/sum_over_leaf/ppermute | solution.py:505
  53.4 1.5 %collective-permute-start.11 = (bf16[128,256]{1,0:T(8,128)(2,1)S(1)}, bf16[128,256]{1,0:T(8,128)(2,1)S(1)}, u32[]{:S(2)}, u32[]{:S(2)}) collective-permute-start(bf16[128,256]{1,0:T(8,128)(2,1)S(1)} %get-tuple-element.61), channel_id=1, source_target_pairs={{0,2},{1,3},{2,0},{3,1},{4,6},{5,7},{6,4},{7,5},{8,10},{9,11},{10,... | collective-permute-start | bytes 196616 | tf_op jit(solution)/shard_map/sum_over_pos/ppermute | solution.py:505
  55.0 1.4 %collective-permute-start.12 = (bf16[128,256]{1,0:T(8,128)(2,1)S(1)}, bf16[128,256]{1,0:T(8,128)(2,1)S(1)}, u32[]{:S(2)}, u32[]{:S(2)}) collective-permute-start(bf16[128,256]{1,0:T(8,128)(2,1)S(1)} %get-tuple-element.62), channel_id=1, source_target_pairs={{0,4},{1,5},{2,6},{3,7},{4,0},{5,1},{6,2},{7,3},{8,12},{9,13},{10,... | collective-permute-start | bytes 196616 | tf_op jit(solution)/shard_map/sum_over_pos/ppermute | solution.py:505
  56.4 1.5 %collective-permute-start.13 = (bf16[128,256]{1,0:T(8,128)(2,1)S(1)}, bf16[128,256]{1,0:T(8,128)(2,1)S(1)}, u32[]{:S(2)}, u32[]{:S(2)}) collective-permute-start(bf16[128,256]{1,0:T(8,128)(2,1)S(1)} %get-tuple-element.63), channel_id=1, source_target_pairs={{0,6},{1,7},{2,4},{3,5},{4,2},{5,3},{6,0},{7,1},{8,14},{9,15},{10,... | collective-permute-start | bytes 196616 | tf_op jit(solution)/shard_map/sum_over_pos/ppermute | solution.py:505
  57.9 5.4 %collective-permute-done.12.refs_2_ = bf16[128,256]{1,0:T(8,128)(2,1)S(1)} collective-permute-done((bf16[128,256]{1,0:T(8,128)(2,1)S(1)}, bf16[128,256]{1,0:T(8,128)(2,1)S(1)}, u32[]{:S(2)}, u32[]{:S(2)}) %collective-permute-start.12) | collective-permute-done | bytes 65568 | tf_op jit(solution)/shard_map/sum_over_pos/ppermute | solution.py:505
  63.4 2.0 %collective-permute-start.16 = (bf16[128,256]{1,0:T(8,128)(2,1)S(1)}, bf16[128,256]{1,0:T(8,128)(2,1)S(1)}, u32[]{:S(2)}, u32[]{:S(2)}) collective-permute-start(bf16[128,256]{1,0:T(8,128)(2,1)S(1)} %sum_pos.1.refs_0_), channel_id=1, source_target_pairs={{0,6},{1,7},{2,4},{3,5},{4,2},{5,3},{6,0},{7,1},{8,14},{9,15},{10,... | collective-permute-start | bytes 196616 | tf_op jit(solution)/shard_map/gather_pos/ppermute | solution.py:505
  66.4 1.4 %collective-permute-start.14 = (bf16[128,256]{1,0:T(8,128)(2,1)S(1)}, bf16[128,256]{1,0:T(8,128)(2,1)S(1)}, u32[]{:S(2)}, u32[]{:S(2)}) collective-permute-start(bf16[128,256]{1,0:T(8,128)(2,1)S(1)} %sum_pos.1.refs_0_), channel_id=1, source_target_pairs={{0,2},{1,3},{2,0},{3,1},{4,6},{5,7},{6,4},{7,5},{8,10},{9,11},{10,... | collective-permute-start | bytes 196616 | tf_op jit(solution)/shard_map/gather_pos/ppermute | solution.py:505
  67.8 2.4 %collective-permute-done.16.refs_3_ = bf16[128,256]{1,0:T(8,128)(2,1)S(1)} collective-permute-done((bf16[128,256]{1,0:T(8,128)(2,1)S(1)}, bf16[128,256]{1,0:T(8,128)(2,1)S(1)}, u32[]{:S(2)}, u32[]{:S(2)}) %collective-permute-start.16) | collective-permute-done | bytes 65568 | tf_op jit(solution)/shard_map/gather_pos/ppermute | solution.py:505
  70.2 1.7 %collective-permute-done.15.refs_2_ = bf16[128,256]{1,0:T(8,128)(2,1)S(1)} collective-permute-done((bf16[128,256]{1,0:T(8,128)(2,1)S(1)}, bf16[128,256]{1,0:T(8,128)(2,1)S(1)}, u32[]{:S(2)}, u32[]{:S(2)}) %collective-permute-start.15) | collective-permute-done | bytes 65568 | tf_op jit(solution)/shard_map/gather_pos/ppermute | solution.py:505
  71.9 1.5 %collective-permute-start.19 = (bf16[256,256]{1,0:T(8,128)(2,1)S(1)}, bf16[256,256]{1,0:T(8,128)(2,1)S(1)}, u32[]{:S(2)}, u32[]{:S(2)}) collective-permute-start(bf16[256,256]{1,0:T(8,128)(2,1)S(1)} %get-tuple-element.71.refs_0_), channel_id=1, source_target_pairs={{0,24},{8,16},{16,8},{24,0},{1,25},{9,17},{17,9},{25,1},{2,26},{10... | collective-permute-start | bytes 393224 | tf_op jit(solution)/shard_map/gather_leaf/ppermute | solution.py:505
  73.5 1.2 %collective-permute-start.18 = (bf16[256,256]{1,0:T(8,128)(2,1)S(1)}, bf16[256,256]{1,0:T(8,128)(2,1)S(1)}, u32[]{:S(2)}, u32[]{:S(2)}) collective-permute-start(bf16[256,256]{1,0:T(8,128)(2,1)S(1)} %get-tuple-element.71.refs_0_), channel_id=1, source_target_pairs={{0,16},{8,24},{16,0},{24,8},{1,17},{9,25},{17,1},{25,9},{2,18},{10... | collective-permute-start | bytes 393224 | tf_op jit(solution)/shard_map/gather_leaf/ppermute | solution.py:505
  75.6 3.6 %collective-permute-done.19.refs_3_ = bf16[256,256]{1,0:T(8,128)(2,1)S(1)} collective-permute-done((bf16[256,256]{1,0:T(8,128)(2,1)S(1)}, bf16[256,256]{1,0:T(8,128)(2,1)S(1)}, u32[]{:S(2)}, u32[]{:S(2)}) %collective-permute-start.19) | collective-permute-done | bytes 131104 | tf_op jit(solution)/shard_map/gather_leaf/ppermute | solution.py:505
  80.8 2.1 %collective-permute-done.22.theirs = bf16[1280,256]{1,0:T(8,128)(2,1)S(1)} collective-permute-done((bf16[1280,256]{1,0:T(8,128)(2,1)S(1)}, bf16[1280,256]{1,0:T(8,128)(2,1)S(1)}, u32[]{:S(2)}, u32[]{:S(2)}) %collective-permute-start.22) | collective-permute-done | bytes 655392 | tf_op jit(solution)/shard_map/gather_cores/ppermute | solution.py:505
  82.9 10.4 %backward.1 = (f32[1024,256]{1,0:T(8,128)}, f32[512,256]{1,0:T(8,128)}, f32[1024,256]{1,0:T(8,128)}, f32[1024,256]{1,0:T(8,128)}) custom-call(bf16[1280,256]{1,0:T(8,128)(2,1)S(1)} %stack.5.mine, bf16[1280,256]{1,0:T(8,128)(2,1)S(1)} %collective-permute-done.22.theirs, bf16[1024,1024]{1,0:T(8,128)(2,1)S(1)} %copy-done.2, ...), custom_call_target="tpu_custom_call" | custom-call | tf_op jit(solution)/shard_map/backward/pallas_call | solution.py:484
  (50 shorter events, 9.7 us)
Async XLA Ops:
  7.2 33.1 %all-gather.2.cloned.1.call-start = ((), (), s32[]{:S(2)}) async-start(), calls=%async_computation | async-start | bytes 1310720 | tf_op jit(solution)/shard_map/gather_group_panel/all_gather | solution.py:545
  7.9 15.4 %collective-permute-start.2 = (bf16[32,1024]{1,0:T(8,128)(2,1)}, bf16[32,1024]{1,0:T(8,128)(2,1)S(1)}, u32[]{:S(2)}, u32[]{:S(2)}) collective-permute-start(bf16[32,1024]{1,0:T(8,128)(2,1)} %refs_0_), channel_id=1, source_target_pairs={{0,6},{1,7},{2,4},{3,5},{4,2},{5,3},{6,0},{7,1},{8,14},{9,15},{10,... | collective-permute-start | bytes 196616 | tf_op jit(solution)/shard_map/gather_middle_panel/ppermute | solution.py:505
  13.0 10.3 %collective-permute-start.1 = (bf16[32,1024]{1,0:T(8,128)(2,1)}, bf16[32,1024]{1,0:T(8,128)(2,1)S(1)}, u32[]{:S(2)}, u32[]{:S(2)}) collective-permute-start(bf16[32,1024]{1,0:T(8,128)(2,1)} %refs_0_), channel_id=1, source_target_pairs={{0,4},{1,5},{2,6},{3,7},{4,0},{5,1},{6,2},{7,3},{8,12},{9,13},{10,... | collective-permute-start | bytes 196616 | tf_op jit(solution)/shard_map/gather_middle_panel/ppermute | solution.py:505
  13.0 10.3 %collective-permute-start = (bf16[32,1024]{1,0:T(8,128)(2,1)}, bf16[32,1024]{1,0:T(8,128)(2,1)S(1)}, u32[]{:S(2)}, u32[]{:S(2)}) collective-permute-start(bf16[32,1024]{1,0:T(8,128)(2,1)} %refs_0_), channel_id=1, source_target_pairs={{0,2},{1,3},{2,0},{3,1},{4,6},{5,7},{6,4},{7,5},{8,10},{9,11},{10,... | collective-permute-start | bytes 196616 | tf_op jit(solution)/shard_map/gather_middle_panel/ppermute | solution.py:505
  23.3 16.0 %collective-permute-start.3 = (bf16[768,256]{1,0:T(8,128)(2,1)S(1)}, bf16[768,256]{1,0:T(8,128)(2,1)S(1)}, u32[]{:S(2)}, u32[]{:S(2)}) collective-permute-start(bf16[768,256]{1,0:T(8,128)(2,1)S(1)} %get-tuple-element.46), channel_id=1, source_target_pairs={{0,1},{1,0},{2,3},{3,2},{4,5},{5,4},{6,7},{7,6},{8,9},{9,8},{10,11... | collective-permute-start | bytes 1179656 | tf_op jit(solution)/shard_map/swap_cores/ppermute | solution.py:505
  23.4 15.9 %collective-permute-start.4 = (bf16[768,256]{1,0:T(8,128)(2,1)S(1)}, bf16[768,256]{1,0:T(8,128)(2,1)S(1)}, u32[]{:S(2)}, u32[]{:S(2)}) collective-permute-start(bf16[768,256]{1,0:T(8,128)(2,1)S(1)} %get-tuple-element.47), channel_id=1, source_target_pairs={{0,1},{1,0},{2,3},{3,2},{4,5},{5,4},{6,7},{7,6},{8,9},{9,8},{10,11... | collective-permute-start | bytes 1179656 | tf_op jit(solution)/shard_map/swap_cores/ppermute | solution.py:505
  23.9 10.2 %collective-permute-start.7 = (bf16[128,1024]{1,0:T(8,128)(2,1)S(1)}, bf16[128,1024]{1,0:T(8,128)(2,1)S(1)}, u32[]{:S(2)}, u32[]{:S(2)}) collective-permute-start(bf16[128,1024]{1,0:T(8,128)(2,1)S(1)} %stack.3.refs_0_), channel_id=1, source_target_pairs={{0,24},{8,16},{16,8},{24,0},{1,25},{9,17},{17,9},{25,1},{2,26},{10... | collective-permute-start | bytes 786440 | tf_op jit(solution)/shard_map/gather_middle_panel/ppermute | solution.py:505
  27.0 12.2 %collective-permute-start.6 = (bf16[128,1024]{1,0:T(8,128)(2,1)S(1)}, bf16[128,1024]{1,0:T(8,128)(2,1)S(1)}, u32[]{:S(2)}, u32[]{:S(2)}) collective-permute-start(bf16[128,1024]{1,0:T(8,128)(2,1)S(1)} %stack.3.refs_0_), channel_id=1, source_target_pairs={{0,16},{8,24},{16,0},{24,8},{1,17},{9,25},{17,1},{25,9},{2,18},{10... | collective-permute-start | bytes 786440 | tf_op jit(solution)/shard_map/gather_middle_panel/ppermute | solution.py:505
  27.6 11.7 %collective-permute-start.5 = (bf16[128,1024]{1,0:T(8,128)(2,1)S(1)}, bf16[128,1024]{1,0:T(8,128)(2,1)S(1)}, u32[]{:S(2)}, u32[]{:S(2)}) collective-permute-start(bf16[128,1024]{1,0:T(8,128)(2,1)S(1)} %stack.3.refs_0_), channel_id=1, source_target_pairs={{0,8},{8,0},{16,24},{24,16},{1,9},{9,1},{17,25},{25,17},{2,10},{10... | collective-permute-start | bytes 786440 | tf_op jit(solution)/shard_map/gather_middle_panel/ppermute | solution.py:505
  43.8 5.7 %collective-permute-start.8 = (bf16[256,256]{1,0:T(8,128)(2,1)}, bf16[256,256]{1,0:T(8,128)(2,1)S(1)}, u32[]{:S(2)}, u32[]{:S(2)}) collective-permute-start(bf16[256,256]{1,0:T(8,128)(2,1)} %get-tuple-element.56), channel_id=1, source_target_pairs={{0,8},{8,0},{16,24},{24,16},{1,9},{9,1},{17,25},{25,17},{2,10},{10... | collective-permute-start | bytes 393224 | tf_op jit(solution)/shard_map/sum_over_leaf/ppermute | solution.py:505
  45.3 8.0 %collective-permute-start.9 = (bf16[256,256]{1,0:T(8,128)(2,1)}, bf16[256,256]{1,0:T(8,128)(2,1)S(1)}, u32[]{:S(2)}, u32[]{:S(2)}) collective-permute-start(bf16[256,256]{1,0:T(8,128)(2,1)} %get-tuple-element.57), channel_id=1, source_target_pairs={{0,16},{8,24},{16,0},{24,8},{1,17},{9,25},{17,1},{25,9},{2,18},{10... | collective-permute-start | bytes 393224 | tf_op jit(solution)/shard_map/sum_over_leaf/ppermute | solution.py:505
  46.8 6.5 %collective-permute-start.10 = (bf16[256,256]{1,0:T(8,128)(2,1)}, bf16[256,256]{1,0:T(8,128)(2,1)S(1)}, u32[]{:S(2)}, u32[]{:S(2)}) collective-permute-start(bf16[256,256]{1,0:T(8,128)(2,1)} %get-tuple-element.58), channel_id=1, source_target_pairs={{0,24},{8,16},{16,8},{24,0},{1,25},{9,17},{17,9},{25,1},{2,26},{10... | collective-permute-start | bytes 393224 | tf_op jit(solution)/shard_map/sum_over_leaf/ppermute | solution.py:505
  48.3 27.1 %collective-permute-start.21 = (bf16[512,1024]{1,0:T(8,128)(2,1)S(1)}, bf16[512,1024]{1,0:T(8,128)(2,1)S(1)}, u32[]{:S(2)}, u32[]{:S(2)}) collective-permute-start(bf16[512,1024]{1,0:T(8,128)(2,1)S(1)} %stack.4.own), channel_id=1, source_target_pairs={{0,1},{1,0},{2,3},{3,2},{4,5},{5,4},{6,7},{7,6},{8,9},{9,8},{10,11... | collective-permute-start | bytes 3145736 | tf_op jit(solution)/shard_map/gather_middle_panel/ppermute | solution.py:505
  53.4 27.3 %collective-permute-start.20 = (bf16[4,256,512]{2,1,0:T(8,128)(2,1)S(1)}, bf16[4,256,512]{2,1,0:T(8,128)(2,1)S(1)}, u32[]{:S(2)}, u32[]{:S(2)}) collective-permute-start(bf16[4,256,512]{2,1,0:T(8,128)(2,1)S(1)} %copy-done.1), channel_id=1, source_target_pairs={{0,1},{1,0},{2,3},{3,2},{4,5},{5,4},{6,7},{7,6},{8,9},{9,8},{10,11... | collective-permute-start | bytes 3145736 | tf_op jit(solution)/shard_map/swap_group_panel/ppermute | solution.py:505
  53.4 4.5 %collective-permute-start.11 = (bf16[128,256]{1,0:T(8,128)(2,1)S(1)}, bf16[128,256]{1,0:T(8,128)(2,1)S(1)}, u32[]{:S(2)}, u32[]{:S(2)}) collective-permute-start(bf16[128,256]{1,0:T(8,128)(2,1)S(1)} %get-tuple-element.61), channel_id=1, source_target_pairs={{0,2},{1,3},{2,0},{3,1},{4,6},{5,7},{6,4},{7,5},{8,10},{9,11},{10,... | collective-permute-start | bytes 196616 | tf_op jit(solution)/shard_map/sum_over_pos/ppermute | solution.py:505
  55.0 8.4 %collective-permute-start.12 = (bf16[128,256]{1,0:T(8,128)(2,1)S(1)}, bf16[128,256]{1,0:T(8,128)(2,1)S(1)}, u32[]{:S(2)}, u32[]{:S(2)}) collective-permute-start(bf16[128,256]{1,0:T(8,128)(2,1)S(1)} %get-tuple-element.62), channel_id=1, source_target_pairs={{0,4},{1,5},{2,6},{3,7},{4,0},{5,1},{6,2},{7,3},{8,12},{9,13},{10,... | collective-permute-start | bytes 196616 | tf_op jit(solution)/shard_map/sum_over_pos/ppermute | solution.py:505
  56.4 7.0 %collective-permute-start.13 = (bf16[128,256]{1,0:T(8,128)(2,1)S(1)}, bf16[128,256]{1,0:T(8,128)(2,1)S(1)}, u32[]{:S(2)}, u32[]{:S(2)}) collective-permute-start(bf16[128,256]{1,0:T(8,128)(2,1)S(1)} %get-tuple-element.63), channel_id=1, source_target_pairs={{0,6},{1,7},{2,4},{3,5},{4,2},{5,3},{6,0},{7,1},{8,14},{9,15},{10,... | collective-permute-start | bytes 196616 | tf_op jit(solution)/shard_map/sum_over_pos/ppermute | solution.py:505
  63.4 6.8 %collective-permute-start.16 = (bf16[128,256]{1,0:T(8,128)(2,1)S(1)}, bf16[128,256]{1,0:T(8,128)(2,1)S(1)}, u32[]{:S(2)}, u32[]{:S(2)}) collective-permute-start(bf16[128,256]{1,0:T(8,128)(2,1)S(1)} %sum_pos.1.refs_0_), channel_id=1, source_target_pairs={{0,6},{1,7},{2,4},{3,5},{4,2},{5,3},{6,0},{7,1},{8,14},{9,15},{10,... | collective-permute-start | bytes 196616 | tf_op jit(solution)/shard_map/gather_pos/ppermute | solution.py:505
  65.4 6.5 %collective-permute-start.15 = (bf16[128,256]{1,0:T(8,128)(2,1)S(1)}, bf16[128,256]{1,0:T(8,128)(2,1)S(1)}, u32[]{:S(2)}, u32[]{:S(2)}) collective-permute-start(bf16[128,256]{1,0:T(8,128)(2,1)S(1)} %sum_pos.1.refs_0_), channel_id=1, source_target_pairs={{0,4},{1,5},{2,6},{3,7},{4,0},{5,1},{6,2},{7,3},{8,12},{9,13},{10,... | collective-permute-start | bytes 196616 | tf_op jit(solution)/shard_map/gather_pos/ppermute | solution.py:505
  66.4 5.5 %collective-permute-start.14 = (bf16[128,256]{1,0:T(8,128)(2,1)S(1)}, bf16[128,256]{1,0:T(8,128)(2,1)S(1)}, u32[]{:S(2)}, u32[]{:S(2)}) collective-permute-start(bf16[128,256]{1,0:T(8,128)(2,1)S(1)} %sum_pos.1.refs_0_), channel_id=1, source_target_pairs={{0,2},{1,3},{2,0},{3,1},{4,6},{5,7},{6,4},{7,5},{8,10},{9,11},{10,... | collective-permute-start | bytes 196616 | tf_op jit(solution)/shard_map/gather_pos/ppermute | solution.py:505
  71.9 7.3 %collective-permute-start.19 = (bf16[256,256]{1,0:T(8,128)(2,1)S(1)}, bf16[256,256]{1,0:T(8,128)(2,1)S(1)}, u32[]{:S(2)}, u32[]{:S(2)}) collective-permute-start(bf16[256,256]{1,0:T(8,128)(2,1)S(1)} %get-tuple-element.71.refs_0_), channel_id=1, source_target_pairs={{0,24},{8,16},{16,8},{24,0},{1,25},{9,17},{17,9},{25,1},{2,26},{10... | collective-permute-start | bytes 393224 | tf_op jit(solution)/shard_map/gather_leaf/ppermute | solution.py:505
  73.5 6.1 %collective-permute-start.18 = (bf16[256,256]{1,0:T(8,128)(2,1)S(1)}, bf16[256,256]{1,0:T(8,128)(2,1)S(1)}, u32[]{:S(2)}, u32[]{:S(2)}) collective-permute-start(bf16[256,256]{1,0:T(8,128)(2,1)S(1)} %get-tuple-element.71.refs_0_), channel_id=1, source_target_pairs={{0,16},{8,24},{16,0},{24,8},{1,17},{9,25},{17,1},{25,9},{2,18},{10... | collective-permute-start | bytes 393224 | tf_op jit(solution)/shard_map/gather_leaf/ppermute | solution.py:505
  74.6 6.0 %collective-permute-start.17 = (bf16[256,256]{1,0:T(8,128)(2,1)S(1)}, bf16[256,256]{1,0:T(8,128)(2,1)S(1)}, u32[]{:S(2)}, u32[]{:S(2)}) collective-permute-start(bf16[256,256]{1,0:T(8,128)(2,1)S(1)} %get-tuple-element.71.refs_0_), channel_id=1, source_target_pairs={{0,8},{8,0},{16,24},{24,16},{1,9},{9,1},{17,25},{25,17},{2,10},{10... | collective-permute-start | bytes 393224 | tf_op jit(solution)/shard_map/gather_leaf/ppermute | solution.py:505
  80.7 2.2 %collective-permute-start.22 = (bf16[1280,256]{1,0:T(8,128)(2,1)S(1)}, bf16[1280,256]{1,0:T(8,128)(2,1)S(1)}, u32[]{:S(2)}, u32[]{:S(2)}) collective-permute-start(bf16[1280,256]{1,0:T(8,128)(2,1)S(1)} %stack.5.mine), channel_id=1, source_target_pairs={{0,1},{1,0},{2,3},{3,2},{4,5},{5,4},{6,7},{7,6},{8,9},{9,8},{10,11... | collective-permute-start | bytes 1966088 | tf_op jit(solution)/shard_map/gather_cores/ppermute | solution.py:505
  (7 other events, 43.7 us)
Sparse Core Ops, SparseCore 0:
  9.6 30.6 all-gather.1

commit v11 on v10

--- a/solution.py
+++ b/solution.py
@@ -226,11 +226,13 @@
     return total
 
 
-def fold_kernel(n_leaf, n_pos, keep, low, high, inv, panel, *refs):
+def fold_kernel(n_leaf, n_pos, keep, low, high, inv, late, *refs):
+    early, refs = refs[:n_pos], refs[n_pos:]
     parts, group, (gsum, base, stage) = refs[:n_leaf], refs[n_leaf], refs[n_leaf + 1 :]
     leaf, pos, core = place()
     group_cols = inv.shape[0]
-    sec = panel.shape[1]
+    first = early[0].shape[0]
+    sec = first + late.shape[1]
     q = sec // n_leaf
     gq = group_cols // (2 * n_pos)
     cut = low.shape[0]
@@ -240,19 +242,22 @@
     solved = dot(inv[...], (-gsum[...]).astype(BF)).astype(BF)
     for k in range(n_pos):
         p = pos ^ k
-        rows = pl.ds(pl.multiple_of(p * sec, sec), sec)
-        terms = (dot(panel[p], solved) + base[rows, :]).astype(BF)
-        for j in range(n_leaf):
-            stage[j ^ leaf, k * q : (k + 1) * q, :] = terms[j * q : (j + 1) * q, :]
+        for begin, panel in ((0, early[k]), (first, late.at[2 * p + core])):
+            span = panel.shape[0]
+            rows = pl.ds(pl.multiple_of(p * sec + begin, first), span)
+            terms = (dot(panel[...], solved) + base[rows, :]).astype(BF)
+            for j in range(begin // q, (begin + span) // q):
+                stage[j ^ leaf, k * q : (k + 1) * q, :] = terms[j * q - begin : (j + 1) * q - begin, :]
         begin = pl.multiple_of(core * (group_cols // 2) + p * gq, gq)
         group[k * gq : (k + 1) * gq, :] = gsum[pl.ds(begin, gq), :].astype(BF)
     for k in range(n_leaf):
         parts[k][...] = stage[k]
 
 
-def fold(keep, recv, inverse, panel, n_leaf):
+def fold(keep, recv, inverse, early, late, n_leaf):
     width = keep.shape[-1]
-    n_pos, sec, _ = panel.shape
+    n_pos = len(early)
+    sec = early[0].shape[0] + late.shape[1]
     part = (n_pos * sec // n_leaf, width)
     outs = small(
         functools.partial(fold_kernel, n_leaf, n_pos),
@@ -266,7 +271,8 @@
         keep,
         *recv,
         inverse,
-        panel,
+        late,
+        *early,
     )
     return list(outs[:n_leaf]), outs[n_leaf]
 
@@ -328,22 +334,34 @@
     return small(stack_kernel, "stack", [(rows, parts[0].shape[1])], [], *parts)[0]
 
 
-def weave_kernel(n_leaf, n_pos, own, other, out):
-    leaf, pos, core = place()
-    rows = own.shape[0] // (n_leaf * n_pos)
-    for kc, part in enumerate((own, other)):
-        for kl in range(n_leaf):
-            for k in range(n_pos):
-                block = (leaf ^ kl) * (2 * n_pos) + 2 * (pos ^ k) + (core ^ kc)
-                span = pl.ds(pl.multiple_of(block * rows, rows), rows)
-                begin = (kl * n_pos + k) * rows
-                out[span, :] = part[begin : begin + rows, :]
-
-
-def weave(own, other, n_leaf, n_pos):
-    shape = (2 * own.shape[0], own.shape[1])
-    kernel = functools.partial(weave_kernel, n_leaf, n_pos)
-    return small(kernel, "weave", [shape], [], own, other)[0]
+def weave_kernel(n_leaf, gathered, out, sems):
+    leaf, _, _ = place()
+    n_grp = gathered.shape[0]
+    rows = gathered.shape[1] // n_leaf
+    loads = []
+    for g in range(n_grp):
+        for k in range(n_leaf):
+            begin = pl.multiple_of(((leaf ^ k) * n_grp + g) * rows, rows)
+            got = gathered.at[g, pl.ds(k * rows, rows)]
+            target = out.at[pl.ds(begin, rows)]
+            loads.append(pltpu.make_async_copy(got, target, sems.at[g * n_leaf + k]))
+    for load in loads:
+        load.start()
+    for load in loads:
+        load.wait()
+
+
+def weave(gathered, n_leaf):
+    n_grp, rows, cols = gathered.shape
+    return pl.pallas_call(
+        functools.partial(weave_kernel, n_leaf),
+        out_shape=pltpu.VMEM((n_grp * rows, cols), BF),
+        in_specs=[HBM],
+        out_specs=VMEM,
+        scratch_shapes=[pltpu.SemaphoreType.DMA((n_grp * n_leaf,))],
+        compiler_params=pltpu.CompilerParams(vmem_limit_bytes=SMALL),
+        name="weave",
+    )(*in_hbm(gathered))
 
 
 def lower_dot(lower, x):
@@ -375,6 +393,7 @@
     inv_group_hbm,
     panel_own_hbm,
     panel_other_hbm,
+    panel_late_hbm,
     leaf_solved_hbm,
     inv_leaf_hbm,
     dense_hbm,
@@ -408,11 +427,23 @@
         (dense_hbm, dense),
     )
     loads = [pltpu.make_async_copy(a, b, sems.at[i]) for i, (a, b) in enumerate(pairs)]
+    first = panel_own_hbm.shape[0] // n_pos
+    panel_loads = []
     for kc, got in enumerate((panel_own_hbm, panel_other_hbm)):
-        target = panel_group.at[:, core ^ kc]
-        loads.append(pltpu.make_async_copy(got, target, panel_sems.at[kc]))
-    for i in (0, 1, 5, 6, 2, 3, 4):
-        loads[i].start()
+        for k in range(n_pos):
+            target = panel_group.at[pos ^ k, core ^ kc, pl.ds(0, first)]
+            sem = panel_sems.at[kc * n_pos + k]
+            rows = pl.ds(k * first, first)
+            panel_loads.append(pltpu.make_async_copy(got.at[rows], target, sem))
+    for p in range(n_pos):
+        for c in range(2):
+            got = panel_late_hbm.at[2 * p + c]
+            target = panel_group.at[p, c, pl.ds(first, got.shape[0])]
+            sem = panel_sems.at[2 * n_pos + 2 * p + c]
+            panel_loads.append(pltpu.make_async_copy(got, target, sem))
+    for load in loads[:2] + panel_loads + loads[2:]:
+        load.start()
+    loads = loads + panel_loads
     mid_rows = inv_mid.shape[0]
     top_rows = inv_top.shape[0]
     group_rows = inv_group.shape[0]
@@ -471,9 +502,10 @@
 
 def backward(close, far, n_leaf, n_pos):
     mine, _, inv_mid, _ = close
-    inv_top, inv_group, panel, _, leaf_solved, inv_leaf, dense = far
+    inv_top, inv_group, panel, _, late, leaf_solved, inv_leaf, dense = far
+    sec = panel.shape[0] // n_pos + late.shape[1]
     width = mine.shape[-1]
-    held = (inv_top.shape, inv_group.shape, (n_pos, 2) + panel.shape[1:])
+    held = (inv_top.shape, inv_group.shape, (n_pos, 2, sec, late.shape[2]))
     held += (leaf_solved.shape, inv_leaf.shape, dense.shape)
     outs = (
         leaf_solved.shape,
@@ -493,7 +525,7 @@
             pltpu.VMEM((inv_group.shape[0], width), BF),
             pltpu.VMEM((width, dense.shape[0]), BF),
             pltpu.SemaphoreType.DMA((5,)),
-            pltpu.SemaphoreType.DMA((2,)),
+            pltpu.SemaphoreType.DMA((4 * n_pos,)),
             pltpu.SemaphoreType.DMA((len(outs),)),
         ],
         compiler_params=pltpu.CompilerParams(vmem_limit_bytes=BIG),
@@ -540,12 +572,13 @@
     gq = group_cols // n_grp
     leaf, pos, core = place()
     by_parts = middle_panel.shape[0] % 16 == 0
-    pos_groups = [[2 * p + c for p in range(n_pos)] for c in range(2)]
+    first = sec // 2
     with jax.named_scope("gather_group_panel"):
-        panel = lax.all_gather(group_panel[0], "grp", axis_index_groups=pos_groups)
+        late = lax.all_gather(group_panel[0, first:], "grp")
+        early = swaps(group_panel[0, :first], "grp", n_grp, 2)
     with jax.named_scope("gather_middle_panel"):
         if by_parts:
-            middles = swaps(middle_panel, "grp", n_grp, 2)
+            middles = swaps(middle_panel, "leaf", n_leaf)
         else:
             middle = lax.all_gather(middle_panel, ("leaf", "grp"), axis=0, tiled=True)
     begin = sec * lax.axis_index("grp") + q * leaf
@@ -565,37 +598,33 @@
         upper_cols,
     )
     with jax.named_scope("swap_cores"):
-        if by_parts:
-            send = after(send, middles)
         recv = [swap(x, "grp", n_grp, 1) for x in send]
     with jax.named_scope("gather_middle_panel"):
         if by_parts:
-            middles = swaps(stack(after(middles, send)), "leaf", n_leaf)
-            recv = after(recv, middles)
-            middle = stack(after(middles, rhs_mine))
-    parts, group = fold(keep, recv, inv_here, panel, n_leaf)
+            middle = stack(after(middles, (keep, early)))
+            middle = lax.all_gather(middle, "grp")
+    parts, group = fold(keep, recv, inv_here, after(early, rhs_mine), late, n_leaf)
     with jax.named_scope("sum_over_leaf"):
         parts = parts[:1] + [swap(parts[k], "leaf", n_leaf, k) for k in range(1, n_leaf)]
-    with jax.named_scope("gather_middle_panel"):
-        if by_parts:
-            other = swap(after(middle, group), "grp", n_grp, 1)
-            middle = weave(middle, other, n_leaf, n_pos)
     sends = sum_leaf(parts, group, n_pos)
     with jax.named_scope("sum_over_pos"):
         got = sends[:1] + [swap(sends[k], "grp", n_grp, 2 * k) for k in range(1, n_pos)]
     with jax.named_scope("swap_group_panel"):
-        panel_other = swap(after(panel, sends), "grp", n_grp, 1)
+        early = stack(after(early, sends))
+        early_other = swap(early, "grp", n_grp, 1)
     residual = sum_pos(rhs_mine, got)
     with jax.named_scope("gather_pos"):
         uppers, groups = stack_pos(swaps(residual, "grp", n_grp, 2), q)
     with jax.named_scope("gather_leaf"):
         stacks = swaps(uppers, "leaf", n_leaf)
     with jax.named_scope("gather_cores"):
-        mine = stack(after(stacks, (panel_other, middle)) + [groups])
+        if by_parts:
+            middle = weave(middle, n_leaf)
+        mine = stack(after(stacks, (early_other, middle)) + [groups])
         theirs = swap(mine, "grp", n_grp, 1)
     leaf_out, group_out, mid_out, top_out = backward(
         (mine, theirs, inv_middle, middle),
-        (inv_top, inv_group[0], panel, panel_other, leaf_solved, inv_leaf[0], dense),
+        (inv_top, inv_group[0], early, early_other, late, leaf_solved, inv_leaf[0], dense),
         n_leaf,
         n_pos,
     )

time: 100 us -> 107 us (1.070)
  starting transfers between devices: 26.3 us -> 30.2 us
  Pallas kernels: 21.5 us -> 23.3 us
    ppermute x23 -> x22, starting transfers between devices: 26.2 us -> 30.1 us  [swap(): return lax.ppermute(x, axis, [(i, i ^ bits) for i in range(size)])]
    pallas_call x0 -> x1, Pallas kernels: none -> 1.97 us  [weave(): pl.pallas_call(functools.partial(weave_kernel, n_leaf), out_shape=pltpu.V...]
    squeeze x0 -> x1, local copies, waits for them, and re-layouts: none -> 1.64 us  [body(): early = swaps(group_panel[0, :first], 'grp', n_grp, 2)]
    ppermute x23 -> x22, waiting for transfers between devices: 33.2 us -> 33.2 us  [swap(): return lax.ppermute(x, axis, [(i, i ^ bits) for i in range(size)])]
  transfers between devices with their start and end apart: 24 -> 24, of which waited for: 14 -> 13; matrix products, arithmetic and copies ran while one was open for 1% -> 1% of each run, Pallas kernels for 9% -> 12%
where the time goes in v11:
time: 107 us
  waiting for transfers between devices  34.5 us (32%)
  starting transfers between devices  30.2 us (28%)
  Pallas kernels  23.3 us (22%)
  between operations  14.9 us (14%)
  local copies, waits for them, and re-layouts  2.88 us (3%)
    ppermute x22, waiting for transfers between devices, swap(): return lax.ppermute(x, axis, [(i, i ^ bits) for i in range(size)])  33.2 us
    ppermute x22, starting transfers between devices, swap(): return lax.ppermute(x, axis, [(i, i ^ bits) for i in range(size)])  30.1 us
    pallas_call x1, Pallas kernels, backward(): pl.pallas_call(functools.partial(backward_kernel, n_leaf, n_pos), out_sha...  10.9 us
    pallas_call x1, Pallas kernels, leaf_forward(): pl.pallas_call(functools.partial(forward_kernel, upper_cols // (2 * sec),...  8.47 us
  transfers between devices with their start and end apart: 24, of which 13 were waited for; matrix products, arithmetic and copies ran while one was open for 1% of the time, Pallas kernels for 12%

profile of v11, /device:TPU:0, one launch (start us, length us, event | category | flops | bytes accessed | tf_op | source)
XLA Modules:
  0.0 106.6 jit_solution(6346367374924840900)
XLA Ops:
  7.2 1.6 %slice_bitcast_fusion = (bf16[128,512]{1,0:T(8,128)(2,1)S(1)}, bf16[1,128,512]{2,1,0:T(8,128)(2,1)}) fusion(bf16[1,256,512]{2,1,0:T(8,128)(2,1)} %param.26), kind=kLoop, calls=%fused_computation | loop fusion | bytes 524288 | tf_op jit(solution)/shard_map/gather_group_panel/squeeze | solution.py:578
  8.9 3.0 %collective-permute-start.19 = (bf16[32,1024]{1,0:T(8,128)(2,1)}, bf16[32,1024]{1,0:T(8,128)(2,1)S(1)}, u32[]{:S(2)}, u32[]{:S(2)}) collective-permute-start(bf16[32,1024]{1,0:T(8,128)(2,1)} %refs_0_), channel_id=1, source_target_pairs={{0,16},{8,24},{16,0},{24,8},{1,17},{9,25},{17,1},{25,9},{2,18},{10... | collective-permute-start | bytes 196616 | tf_op jit(solution)/shard_map/gather_middle_panel/ppermute | solution.py:537
  12.0 3.6 %collective-permute-start.4 = (bf16[128,512]{1,0:T(8,128)(2,1)S(1)}, bf16[128,512]{1,0:T(8,128)(2,1)S(1)}, u32[]{:S(2)}, u32[]{:S(2)}) collective-permute-start(bf16[128,512]{1,0:T(8,128)(2,1)S(1)} %get-tuple-element.59.refs_0_), channel_id=1, source_target_pairs={{0,6},{1,7},{2,4},{3,5},{4,2},{5,3},{6,0},{7,1},{8,14},{9,15},{10,... | collective-permute-start | bytes 393224 | tf_op jit(solution)/shard_map/gather_group_panel/ppermute | solution.py:537
  16.3 1.5 %collective-permute-start.18 = (bf16[32,1024]{1,0:T(8,128)(2,1)}, bf16[32,1024]{1,0:T(8,128)(2,1)S(1)}, u32[]{:S(2)}, u32[]{:S(2)}) collective-permute-start(bf16[32,1024]{1,0:T(8,128)(2,1)} %refs_0_), channel_id=1, source_target_pairs={{0,8},{8,0},{16,24},{24,16},{1,9},{9,1},{17,25},{25,17},{2,10},{10... | collective-permute-start | bytes 196616 | tf_op jit(solution)/shard_map/gather_middle_panel/ppermute | solution.py:537
  18.8 8.5 %leaf_forward.1 = (bf16[1536,256]{1,0:T(8,128)(2,1)S(1)}, bf16[768,256]{1,0:T(8,128)(2,1)S(1)}, bf16[768,256]{1,0:T(8,128)(2,1)S(1)}, bf16[512,512]{1,0:T(8,128)...) custom-call(s32[1,1]{1,0:T(1,128)S(6)} %copy.18.count_hbm, s32[1,256]{1,0:T(1,128)} %cols_hbm.1, ...), custom_call_target="tpu_custom_call" | custom-call | flops 1342177280 | bytes 9437184 | tf_op jit(solution)/shard_map/leaf_forward/pallas_call | solution.py:183
  27.3 5.3 %collective-permute-done.3.refs_2_ = bf16[128,512]{1,0:T(8,128)(2,1)S(1)} collective-permute-done((bf16[128,512]{1,0:T(8,128)(2,1)S(1)}, bf16[128,512]{1,0:T(8,128)(2,1)S(1)}, u32[]{:S(2)}, u32[]{:S(2)}) %collective-permute-start.3) | collective-permute-done | bytes 131104 | tf_op jit(solution)/shard_map/gather_group_panel/ppermute | solution.py:537
  35.8 1.2 %all-gather.4.cloned.1.call-done.late.panel_late_hbm = bf16[8,128,512]{2,1,0:T(8,128)(2,1)} async-done(((bf16[1,128,512]{2,1,0:T(8,128)(2,1)}), bf16[8,128,512]{2,1,0:T(8,128)(2,1)}) %all-gather.4.cloned.1.call-update) | async-done | bytes 1048592 | tf_op jit(solution)/shard_map/gather_group_panel/all_gather | solution.py:577
  37.0 1.2 %copy-done = bf16[8,128,512]{2,1,0:T(8,128)(2,1)S(1)} copy-done((bf16[8,128,512]{2,1,0:T(8,128)(2,1)S(1)}, bf16[8,128,512]{2,1,0:T(8,128)(2,1)}, u32[]{:S(2)}) %copy-start) | copy-done | bytes 1048600
  39.2 1.5 %collective-permute-start.5 = (bf16[256,256]{1,0:T(8,128)(2,1)S(1)}, bf16[256,256]{1,0:T(8,128)(2,1)S(1)}, u32[]{:S(2)}, u32[]{:S(2)}) collective-permute-start(bf16[256,256]{1,0:T(8,128)(2,1)S(1)} %get-tuple-element.50), channel_id=1, source_target_pairs={{0,8},{8,0},{16,24},{24,16},{1,9},{9,1},{17,25},{25,17},{2,10},{10... | collective-permute-start | bytes 393224 | tf_op jit(solution)/shard_map/sum_over_leaf/ppermute | solution.py:537
  41.1 1.7 %collective-permute-start.7 = (bf16[256,256]{1,0:T(8,128)(2,1)S(1)}, bf16[256,256]{1,0:T(8,128)(2,1)S(1)}, u32[]{:S(2)}, u32[]{:S(2)}) collective-permute-start(bf16[256,256]{1,0:T(8,128)(2,1)S(1)} %get-tuple-element.52), channel_id=1, source_target_pairs={{0,24},{8,16},{16,8},{24,0},{1,25},{9,17},{17,9},{25,1},{2,26},{10... | collective-permute-start | bytes 393224 | tf_op jit(solution)/shard_map/sum_over_leaf/ppermute | solution.py:537
  42.8 2.5 %collective-permute-done.5.refs_1_ = bf16[256,256]{1,0:T(8,128)(2,1)S(1)} collective-permute-done((bf16[256,256]{1,0:T(8,128)(2,1)S(1)}, bf16[256,256]{1,0:T(8,128)(2,1)S(1)}, u32[]{:S(2)}, u32[]{:S(2)}) %collective-permute-start.5) | collective-permute-done | bytes 131104 | tf_op jit(solution)/shard_map/sum_over_leaf/ppermute | solution.py:537
  45.3 3.6 %collective-permute-done.6.refs_2_ = bf16[256,256]{1,0:T(8,128)(2,1)S(1)} collective-permute-done((bf16[256,256]{1,0:T(8,128)(2,1)S(1)}, bf16[256,256]{1,0:T(8,128)(2,1)S(1)}, u32[]{:S(2)}, u32[]{:S(2)}) %collective-permute-start.6) | collective-permute-done | bytes 131104 | tf_op jit(solution)/shard_map/sum_over_leaf/ppermute | solution.py:537
  50.1 2.4 %collective-permute-start.9 = (bf16[128,256]{1,0:T(8,128)(2,1)S(1)}, bf16[128,256]{1,0:T(8,128)(2,1)S(1)}, u32[]{:S(2)}, u32[]{:S(2)}) collective-permute-start(bf16[128,256]{1,0:T(8,128)(2,1)S(1)} %get-tuple-element.56), channel_id=1, source_target_pairs={{0,4},{1,5},{2,6},{3,7},{4,0},{5,1},{6,2},{7,3},{8,12},{9,13},{10,... | collective-permute-start | bytes 196616 | tf_op jit(solution)/shard_map/sum_over_pos/ppermute | solution.py:537
  53.6 5.0 %collective-permute-done.8.refs_1_ = bf16[128,256]{1,0:T(8,128)(2,1)S(1)} collective-permute-done((bf16[128,256]{1,0:T(8,128)(2,1)S(1)}, bf16[128,256]{1,0:T(8,128)(2,1)S(1)}, u32[]{:S(2)}, u32[]{:S(2)}) %collective-permute-start.8) | collective-permute-done | bytes 65568 | tf_op jit(solution)/shard_map/sum_over_pos/ppermute | solution.py:537
  58.6 3.0 %collective-permute-done.9.refs_2_ = bf16[128,256]{1,0:T(8,128)(2,1)S(1)} collective-permute-done((bf16[128,256]{1,0:T(8,128)(2,1)S(1)}, bf16[128,256]{1,0:T(8,128)(2,1)S(1)}, u32[]{:S(2)}, u32[]{:S(2)}) %collective-permute-start.9) | collective-permute-done | bytes 65568 | tf_op jit(solution)/shard_map/sum_over_pos/ppermute | solution.py:537
  62.1 2.5 %collective-permute-start.13 = (bf16[128,256]{1,0:T(8,128)(2,1)S(1)}, bf16[128,256]{1,0:T(8,128)(2,1)S(1)}, u32[]{:S(2)}, u32[]{:S(2)}) collective-permute-start(bf16[128,256]{1,0:T(8,128)(2,1)S(1)} %sum_pos.1.refs_0_), channel_id=1, source_target_pairs={{0,6},{1,7},{2,4},{3,5},{4,2},{5,3},{6,0},{7,1},{8,14},{9,15},{10,... | collective-permute-start | bytes 196616 | tf_op jit(solution)/shard_map/gather_pos/ppermute | solution.py:537
  64.6 5.6 %collective-permute-start.12 = (bf16[128,256]{1,0:T(8,128)(2,1)S(1)}, bf16[128,256]{1,0:T(8,128)(2,1)S(1)}, u32[]{:S(2)}, u32[]{:S(2)}) collective-permute-start(bf16[128,256]{1,0:T(8,128)(2,1)S(1)} %sum_pos.1.refs_0_), channel_id=1, source_target_pairs={{0,4},{1,5},{2,6},{3,7},{4,0},{5,1},{6,2},{7,3},{8,12},{9,13},{10,... | collective-permute-start | bytes 196616 | tf_op jit(solution)/shard_map/gather_pos/ppermute | solution.py:537
  70.7 6.9 %collective-permute-done.12.refs_2_ = bf16[128,256]{1,0:T(8,128)(2,1)S(1)} collective-permute-done((bf16[128,256]{1,0:T(8,128)(2,1)S(1)}, bf16[128,256]{1,0:T(8,128)(2,1)S(1)}, u32[]{:S(2)}, u32[]{:S(2)}) %collective-permute-start.12) | collective-permute-done | bytes 65568 | tf_op jit(solution)/shard_map/gather_pos/ppermute | solution.py:537
  77.7 2.4 %collective-permute-start.16 = (bf16[256,256]{1,0:T(8,128)(2,1)S(1)}, bf16[256,256]{1,0:T(8,128)(2,1)S(1)}, u32[]{:S(2)}, u32[]{:S(2)}) collective-permute-start(bf16[256,256]{1,0:T(8,128)(2,1)S(1)} %get-tuple-element.67.refs_0_), channel_id=1, source_target_pairs={{0,24},{8,16},{16,8},{24,0},{1,25},{9,17},{17,9},{25,1},{2,26},{10... | collective-permute-start | bytes 393224 | tf_op jit(solution)/shard_map/gather_leaf/ppermute | solution.py:537
  81.2 2.0 %weave.1.panel_mid = bf16[1024,1024]{1,0:T(8,128)(2,1)S(1)} custom-call(bf16[8,128,1024]{2,1,0:T(8,128)(2,1)} %bitcast.13), custom_call_target="tpu_custom_call" | custom-call | tf_op jit(solution)/shard_map/gather_cores/weave/pallas_call | solution.py:356
  83.2 1.3 %collective-permute-done.16.refs_3_ = bf16[256,256]{1,0:T(8,128)(2,1)S(1)} collective-permute-done((bf16[256,256]{1,0:T(8,128)(2,1)S(1)}, bf16[256,256]{1,0:T(8,128)(2,1)S(1)}, u32[]{:S(2)}, u32[]{:S(2)}) %collective-permute-start.16) | collective-permute-done | bytes 131104 | tf_op jit(solution)/shard_map/gather_leaf/ppermute | solution.py:537
  84.5 2.1 %collective-permute-done.15.refs_2_ = bf16[256,256]{1,0:T(8,128)(2,1)S(1)} collective-permute-done((bf16[256,256]{1,0:T(8,128)(2,1)S(1)}, bf16[256,256]{1,0:T(8,128)(2,1)S(1)}, u32[]{:S(2)}, u32[]{:S(2)}) %collective-permute-start.15) | collective-permute-done | bytes 131104 | tf_op jit(solution)/shard_map/gather_leaf/ppermute | solution.py:537
  86.7 2.1 %collective-permute-done.21.theirs = bf16[1280,256]{1,0:T(8,128)(2,1)S(1)} collective-permute-done((bf16[1280,256]{1,0:T(8,128)(2,1)S(1)}, bf16[1280,256]{1,0:T(8,128)(2,1)S(1)}, u32[]{:S(2)}, u32[]{:S(2)}) %collective-permute-start.21) | collective-permute-done | bytes 655392 | tf_op jit(solution)/shard_map/gather_cores/ppermute | solution.py:537
  88.8 10.9 %backward.1 = (f32[1024,256]{1,0:T(8,128)}, f32[512,256]{1,0:T(8,128)}, f32[1024,256]{1,0:T(8,128)}, f32[1024,256]{1,0:T(8,128)}) custom-call(bf16[1280,256]{1,0:T(8,128)(2,1)S(1)} %stack.5.mine, bf16[1280,256]{1,0:T(8,128)(2,1)S(1)} %collective-permute-done.21.theirs, bf16[1024,1024]{1,0:T(8,128)(2,1)S(1)} %copy-done.2, ...), custom_call_target="tpu_custom_call" | custom-call | tf_op jit(solution)/shard_map/backward/pallas_call | solution.py:516
  (48 shorter events, 10.2 us)
Async XLA Ops:
  7.2 29.8 %all-gather.4.cloned.1.call-start = ((), (), s32[]{:S(2)}) async-start(), calls=%async_computation | async-start | bytes 1179648 | tf_op jit(solution)/shard_map/gather_group_panel/all_gather | solution.py:577
  8.9 72.3 %all-gather.6.cloned.1.call-start = ((), (), s32[]{:S(2)}) async-start(), calls=%async_computation.1 | async-start | bytes 2359296 | tf_op jit(solution)/shard_map/gather_middle_panel/all_gather | solution.py:605
  8.9 9.6 %collective-permute-start.19 = (bf16[32,1024]{1,0:T(8,128)(2,1)}, bf16[32,1024]{1,0:T(8,128)(2,1)S(1)}, u32[]{:S(2)}, u32[]{:S(2)}) collective-permute-start(bf16[32,1024]{1,0:T(8,128)(2,1)} %refs_0_), channel_id=1, source_target_pairs={{0,16},{8,24},{16,0},{24,8},{1,17},{9,25},{17,1},{25,9},{2,18},{10... | collective-permute-start | bytes 196616 | tf_op jit(solution)/shard_map/gather_middle_panel/ppermute | solution.py:537
  12.0 15.4 %collective-permute-start.4 = (bf16[128,512]{1,0:T(8,128)(2,1)S(1)}, bf16[128,512]{1,0:T(8,128)(2,1)S(1)}, u32[]{:S(2)}, u32[]{:S(2)}) collective-permute-start(bf16[128,512]{1,0:T(8,128)(2,1)S(1)} %get-tuple-element.59.refs_0_), channel_id=1, source_target_pairs={{0,6},{1,7},{2,4},{3,5},{4,2},{5,3},{6,0},{7,1},{8,14},{9,15},{10,... | collective-permute-start | bytes 393224 | tf_op jit(solution)/shard_map/gather_group_panel/ppermute | solution.py:537
  15.6 17.0 %collective-permute-start.3 = (bf16[128,512]{1,0:T(8,128)(2,1)S(1)}, bf16[128,512]{1,0:T(8,128)(2,1)S(1)}, u32[]{:S(2)}, u32[]{:S(2)}) collective-permute-start(bf16[128,512]{1,0:T(8,128)(2,1)S(1)} %get-tuple-element.59.refs_0_), channel_id=1, source_target_pairs={{0,4},{1,5},{2,6},{3,7},{4,0},{5,1},{6,2},{7,3},{8,12},{9,13},{10,... | collective-permute-start | bytes 393224 | tf_op jit(solution)/shard_map/gather_group_panel/ppermute | solution.py:537
  15.6 17.0 %collective-permute-start.2 = (bf16[128,512]{1,0:T(8,128)(2,1)S(1)}, bf16[128,512]{1,0:T(8,128)(2,1)S(1)}, u32[]{:S(2)}, u32[]{:S(2)}) collective-permute-start(bf16[128,512]{1,0:T(8,128)(2,1)S(1)} %get-tuple-element.59.refs_0_), channel_id=1, source_target_pairs={{0,2},{1,3},{2,0},{3,1},{4,6},{5,7},{6,4},{7,5},{8,10},{9,11},{10,... | collective-permute-start | bytes 393224 | tf_op jit(solution)/shard_map/gather_group_panel/ppermute | solution.py:537
  16.3 11.0 %collective-permute-start.18 = (bf16[32,1024]{1,0:T(8,128)(2,1)}, bf16[32,1024]{1,0:T(8,128)(2,1)S(1)}, u32[]{:S(2)}, u32[]{:S(2)}) collective-permute-start(bf16[32,1024]{1,0:T(8,128)(2,1)} %refs_0_), channel_id=1, source_target_pairs={{0,8},{8,0},{16,24},{24,16},{1,9},{9,1},{17,25},{25,17},{2,10},{10... | collective-permute-start | bytes 196616 | tf_op jit(solution)/shard_map/gather_middle_panel/ppermute | solution.py:537
  18.5 8.8 %collective-permute-start.20 = (bf16[32,1024]{1,0:T(8,128)(2,1)}, bf16[32,1024]{1,0:T(8,128)(2,1)S(1)}, u32[]{:S(2)}, u32[]{:S(2)}) collective-permute-start(bf16[32,1024]{1,0:T(8,128)(2,1)} %refs_0_), channel_id=1, source_target_pairs={{0,24},{8,16},{16,8},{24,0},{1,25},{9,17},{17,9},{25,1},{2,26},{10... | collective-permute-start | bytes 196616 | tf_op jit(solution)/shard_map/gather_middle_panel/ppermute | solution.py:537
  33.3 1.8 %collective-permute-start = (bf16[768,256]{1,0:T(8,128)(2,1)S(1)}, bf16[768,256]{1,0:T(8,128)(2,1)S(1)}, u32[]{:S(2)}, u32[]{:S(2)}) collective-permute-start(bf16[768,256]{1,0:T(8,128)(2,1)S(1)} %get-tuple-element.42), channel_id=1, source_target_pairs={{0,1},{1,0},{2,3},{3,2},{4,5},{5,4},{6,7},{7,6},{8,9},{9,8},{10,11... | collective-permute-start | bytes 1179656 | tf_op jit(solution)/shard_map/swap_cores/ppermute | solution.py:537
  33.4 2.3 %collective-permute-start.1 = (bf16[768,256]{1,0:T(8,128)(2,1)S(1)}, bf16[768,256]{1,0:T(8,128)(2,1)S(1)}, u32[]{:S(2)}, u32[]{:S(2)}) collective-permute-start(bf16[768,256]{1,0:T(8,128)(2,1)S(1)} %get-tuple-element.43), channel_id=1, source_target_pairs={{0,1},{1,0},{2,3},{3,2},{4,5},{5,4},{6,7},{7,6},{8,9},{9,8},{10,11... | collective-permute-start | bytes 1179656 | tf_op jit(solution)/shard_map/swap_cores/ppermute | solution.py:537
  39.2 6.1 %collective-permute-start.5 = (bf16[256,256]{1,0:T(8,128)(2,1)S(1)}, bf16[256,256]{1,0:T(8,128)(2,1)S(1)}, u32[]{:S(2)}, u32[]{:S(2)}) collective-permute-start(bf16[256,256]{1,0:T(8,128)(2,1)S(1)} %get-tuple-element.50), channel_id=1, source_target_pairs={{0,8},{8,0},{16,24},{24,16},{1,9},{9,1},{17,25},{25,17},{2,10},{10... | collective-permute-start | bytes 393224 | tf_op jit(solution)/shard_map/sum_over_leaf/ppermute | solution.py:537
  40.8 8.2 %collective-permute-start.6 = (bf16[256,256]{1,0:T(8,128)(2,1)S(1)}, bf16[256,256]{1,0:T(8,128)(2,1)S(1)}, u32[]{:S(2)}, u32[]{:S(2)}) collective-permute-start(bf16[256,256]{1,0:T(8,128)(2,1)S(1)} %get-tuple-element.51), channel_id=1, source_target_pairs={{0,16},{8,24},{16,0},{24,8},{1,17},{9,25},{17,1},{25,9},{2,18},{10... | collective-permute-start | bytes 393224 | tf_op jit(solution)/shard_map/sum_over_leaf/ppermute | solution.py:537
  41.1 7.8 %collective-permute-start.7 = (bf16[256,256]{1,0:T(8,128)(2,1)S(1)}, bf16[256,256]{1,0:T(8,128)(2,1)S(1)}, u32[]{:S(2)}, u32[]{:S(2)}) collective-permute-start(bf16[256,256]{1,0:T(8,128)(2,1)S(1)} %get-tuple-element.52), channel_id=1, source_target_pairs={{0,24},{8,16},{16,8},{24,0},{1,25},{9,17},{17,9},{25,1},{2,26},{10... | collective-permute-start | bytes 393224 | tf_op jit(solution)/shard_map/sum_over_leaf/ppermute | solution.py:537
  49.0 37.6 %collective-permute-start.17 = (bf16[512,512]{1,0:T(8,128)(2,1)S(1)}, bf16[512,512]{1,0:T(8,128)(2,1)S(1)}, u32[]{:S(2)}, u32[]{:S(2)}) collective-permute-start(bf16[512,512]{1,0:T(8,128)(2,1)S(1)} %stack.3.panel_own_hbm), channel_id=1, source_target_pairs={{0,1},{1,0},{2,3},{3,2},{4,5},{5,4},{6,7},{7,6},{8,9},{9,8},{10,11... | collective-permute-start | bytes 1572872 | tf_op jit(solution)/shard_map/swap_group_panel/ppermute | solution.py:537
  49.1 9.4 %collective-permute-start.8 = (bf16[128,256]{1,0:T(8,128)(2,1)S(1)}, bf16[128,256]{1,0:T(8,128)(2,1)S(1)}, u32[]{:S(2)}, u32[]{:S(2)}) collective-permute-start(bf16[128,256]{1,0:T(8,128)(2,1)S(1)} %get-tuple-element.55), channel_id=1, source_target_pairs={{0,2},{1,3},{2,0},{3,1},{4,6},{5,7},{6,4},{7,5},{8,10},{9,11},{10,... | collective-permute-start | bytes 196616 | tf_op jit(solution)/shard_map/sum_over_pos/ppermute | solution.py:537
  50.1 11.5 %collective-permute-start.9 = (bf16[128,256]{1,0:T(8,128)(2,1)S(1)}, bf16[128,256]{1,0:T(8,128)(2,1)S(1)}, u32[]{:S(2)}, u32[]{:S(2)}) collective-permute-start(bf16[128,256]{1,0:T(8,128)(2,1)S(1)} %get-tuple-element.56), channel_id=1, source_target_pairs={{0,4},{1,5},{2,6},{3,7},{4,0},{5,1},{6,2},{7,3},{8,12},{9,13},{10,... | collective-permute-start | bytes 196616 | tf_op jit(solution)/shard_map/sum_over_pos/ppermute | solution.py:537
  52.5 9.6 %collective-permute-start.10 = (bf16[128,256]{1,0:T(8,128)(2,1)S(1)}, bf16[128,256]{1,0:T(8,128)(2,1)S(1)}, u32[]{:S(2)}, u32[]{:S(2)}) collective-permute-start(bf16[128,256]{1,0:T(8,128)(2,1)S(1)} %get-tuple-element.57), channel_id=1, source_target_pairs={{0,6},{1,7},{2,4},{3,5},{4,2},{5,3},{6,0},{7,1},{8,14},{9,15},{10,... | collective-permute-start | bytes 196616 | tf_op jit(solution)/shard_map/sum_over_pos/ppermute | solution.py:537
  62.1 8.6 %collective-permute-start.13 = (bf16[128,256]{1,0:T(8,128)(2,1)S(1)}, bf16[128,256]{1,0:T(8,128)(2,1)S(1)}, u32[]{:S(2)}, u32[]{:S(2)}) collective-permute-start(bf16[128,256]{1,0:T(8,128)(2,1)S(1)} %sum_pos.1.refs_0_), channel_id=1, source_target_pairs={{0,6},{1,7},{2,4},{3,5},{4,2},{5,3},{6,0},{7,1},{8,14},{9,15},{10,... | collective-permute-start | bytes 196616 | tf_op jit(solution)/shard_map/gather_pos/ppermute | solution.py:537
  64.6 13.1 %collective-permute-start.12 = (bf16[128,256]{1,0:T(8,128)(2,1)S(1)}, bf16[128,256]{1,0:T(8,128)(2,1)S(1)}, u32[]{:S(2)}, u32[]{:S(2)}) collective-permute-start(bf16[128,256]{1,0:T(8,128)(2,1)S(1)} %sum_pos.1.refs_0_), channel_id=1, source_target_pairs={{0,4},{1,5},{2,6},{3,7},{4,0},{5,1},{6,2},{7,3},{8,12},{9,13},{10,... | collective-permute-start | bytes 196616 | tf_op jit(solution)/shard_map/gather_pos/ppermute | solution.py:537
  70.2 7.4 %collective-permute-start.11 = (bf16[128,256]{1,0:T(8,128)(2,1)S(1)}, bf16[128,256]{1,0:T(8,128)(2,1)S(1)}, u32[]{:S(2)}, u32[]{:S(2)}) collective-permute-start(bf16[128,256]{1,0:T(8,128)(2,1)S(1)} %sum_pos.1.refs_0_), channel_id=1, source_target_pairs={{0,2},{1,3},{2,0},{3,1},{4,6},{5,7},{6,4},{7,5},{8,10},{9,11},{10,... | collective-permute-start | bytes 196616 | tf_op jit(solution)/shard_map/gather_pos/ppermute | solution.py:537
  77.7 6.9 %collective-permute-start.16 = (bf16[256,256]{1,0:T(8,128)(2,1)S(1)}, bf16[256,256]{1,0:T(8,128)(2,1)S(1)}, u32[]{:S(2)}, u32[]{:S(2)}) collective-permute-start(bf16[256,256]{1,0:T(8,128)(2,1)S(1)} %get-tuple-element.67.refs_0_), channel_id=1, source_target_pairs={{0,24},{8,16},{16,8},{24,0},{1,25},{9,17},{17,9},{25,1},{2,26},{10... | collective-permute-start | bytes 393224 | tf_op jit(solution)/shard_map/gather_leaf/ppermute | solution.py:537
  80.1 6.5 %collective-permute-start.15 = (bf16[256,256]{1,0:T(8,128)(2,1)S(1)}, bf16[256,256]{1,0:T(8,128)(2,1)S(1)}, u32[]{:S(2)}, u32[]{:S(2)}) collective-permute-start(bf16[256,256]{1,0:T(8,128)(2,1)S(1)} %get-tuple-element.67.refs_0_), channel_id=1, source_target_pairs={{0,16},{8,24},{16,0},{24,8},{1,17},{9,25},{17,1},{25,9},{2,18},{10... | collective-permute-start | bytes 393224 | tf_op jit(solution)/shard_map/gather_leaf/ppermute | solution.py:537
  80.7 6.0 %collective-permute-start.14 = (bf16[256,256]{1,0:T(8,128)(2,1)S(1)}, bf16[256,256]{1,0:T(8,128)(2,1)S(1)}, u32[]{:S(2)}, u32[]{:S(2)}) collective-permute-start(bf16[256,256]{1,0:T(8,128)(2,1)S(1)} %get-tuple-element.67.refs_0_), channel_id=1, source_target_pairs={{0,8},{8,0},{16,24},{24,16},{1,9},{9,1},{17,25},{25,17},{2,10},{10... | collective-permute-start | bytes 393224 | tf_op jit(solution)/shard_map/gather_leaf/ppermute | solution.py:537
  86.7 2.2 %collective-permute-start.21 = (bf16[1280,256]{1,0:T(8,128)(2,1)S(1)}, bf16[1280,256]{1,0:T(8,128)(2,1)S(1)}, u32[]{:S(2)}, u32[]{:S(2)}) collective-permute-start(bf16[1280,256]{1,0:T(8,128)(2,1)S(1)} %stack.5.mine), channel_id=1, source_target_pairs={{0,1},{1,0},{2,3},{3,2},{4,5},{5,4},{6,7},{7,6},{8,9},{9,8},{10,11... | collective-permute-start | bytes 1966088 | tf_op jit(solution)/shard_map/gather_cores/ppermute | solution.py:537
  (5 other events, 59.0 us)
Sparse Core Ops, SparseCore 0:
  10.2 26.7 all-gather.3
  39.2 39.5 all-gather.5

commit v12 on v10

--- a/solution.py
+++ b/solution.py
@@ -348,7 +348,7 @@
 
 def lower_dot(lower, x):
     n = lower.shape[0]
-    step = n // 4
+    step = min(n, max(n // 4, 256))
     parts = []
     for i in range(0, n, step):
         parts.append(dot(lower[i : i + step, 0 : i + step], x[0 : i + step, :]))
@@ -357,7 +357,7 @@
 
 def dot_lower(x, lower):
     n = lower.shape[0]
-    step = n // 4
+    step = min(n, max(n // 4, 256))
     parts = []
     for i in range(0, n, step):
         parts.append(dot(x[:, i:], lower[i:, i : i + step]))
@@ -450,21 +450,26 @@
     stores[1].start()
     for load in loads[1:]:
         load.wait()
-    group_solved = dot(inv_group[...], residual[...]).astype(BF).astype(F32).T
+    group_solved = lower_dot(inv_group, residual).astype(BF).astype(F32).T
     panel = panel_group[...].reshape(mid_rows + top_rows, group_rows)
     group_back = group_solved - dot(above[:, upper_cols], panel)
-    group_t = dot(group_back.astype(BF), inv_group[...])
+    group_t = dot_lower(group_back.astype(BF), inv_group)
     above[:, 0:group_rows] = group_t.astype(BF)
     group_out[...] = group_t.T
     stores.append(pltpu.make_async_copy(group_out, group_hbm, out_sems.at[2]))
     stores[2].start()
-    for s in range(supernodes):
-        cols = pl.ds(s * block, block)
+    pair = 2 * block
+    for i in range(supernodes // 2):
+        cols = pl.ds(i * pair, pair)
         terms = dot(above[...], dense[:, cols])
         back = (leaf_solved[cols, :].astype(F32).T - terms).astype(BF)
-        leaf_out[cols, :] = dot(back, inv_leaf[s]).T
-    stores.append(pltpu.make_async_copy(leaf_out, leaf_hbm, out_sems.at[3]))
-    stores[3].start()
+        for j in range(2):
+            span = pl.ds(i * pair + j * block, block)
+            out = dot(back[:, j * block : (j + 1) * block], inv_leaf[2 * i + j])
+            leaf_out[span, :] = out.T
+        sem = out_sems.at[3 + i]
+        stores.append(pltpu.make_async_copy(leaf_out.at[cols], leaf_hbm.at[cols], sem))
+        stores[-1].start()
     for store in stores:
         store.wait()
 
@@ -494,7 +499,7 @@
             pltpu.VMEM((width, dense.shape[0]), BF),
             pltpu.SemaphoreType.DMA((5,)),
             pltpu.SemaphoreType.DMA((2,)),
-            pltpu.SemaphoreType.DMA((len(outs),)),
+            pltpu.SemaphoreType.DMA((3 + leaf_solved.shape[0] // (2 * inv_leaf.shape[1]),)),
         ],
         compiler_params=pltpu.CompilerParams(vmem_limit_bytes=BIG),
         name="backward",

time: 100 us -> 99.4 us (level)
  transfers between devices with their start and end apart: 24 -> 24, of which waited for: 14 -> 13; matrix products, arithmetic and copies ran while one was open for 1% -> 1% of each run, Pallas kernels for 9% -> 10%
where the time goes in v12:
time: 99.4 us; the launch traced here: 99.2 us
  waiting for transfers between devices  34.8 us (35%)
  starting transfers between devices  26.1 us (26%)
  Pallas kernels  20.7 us (21%)
  between operations  14.9 us (15%)
  local copies, waits for them, and re-layouts  1.9 us (2%)
    ppermute x23, waiting for transfers between devices, swap(): return lax.ppermute(x, axis, [(i, i ^ bits) for i in range(size)])  32.8 us
    ppermute x23, starting transfers between devices, swap(): return lax.ppermute(x, axis, [(i, i ^ bits) for i in range(size)])  26 us
    pallas_call x1, Pallas kernels, backward(): pl.pallas_call(functools.partial(backward_kernel, n_leaf, n_pos), out_sha...  9.48 us
    pallas_call x1, Pallas kernels, leaf_forward(): pl.pallas_call(functools.partial(forward_kernel, upper_cols // (2 * sec),...  9.09 us
    pallas_call x8, Pallas kernels, small(): pl.pallas_call(kernel, out_shape=[pltpu.VMEM(shape, BF) for shape in shap...  2.1 us
  transfers between devices with their start and end apart: 24, of which 13 were waited for; matrix products, arithmetic and copies ran while one was open for 1% of the time, Pallas kernels for 10%

profile of v12, /device:TPU:0, one launch (start us, length us, event | category | flops | bytes accessed | tf_op | source)
XLA Modules:
  0.0 99.2 jit_solution(4819619395741109913)
XLA Ops:
  7.9 5.1 %collective-permute-start.2 = (bf16[32,1024]{1,0:T(8,128)(2,1)}, bf16[32,1024]{1,0:T(8,128)(2,1)S(1)}, u32[]{:S(2)}, u32[]{:S(2)}) collective-permute-start(bf16[32,1024]{1,0:T(8,128)(2,1)} %refs_0_), channel_id=1, source_target_pairs={{0,6},{1,7},{2,4},{3,5},{4,2},{5,3},{6,0},{7,1},{8,14},{9,15},{10,... | collective-permute-start | bytes 196616 | tf_op jit(solution)/shard_map/gather_middle_panel/ppermute | solution.py:510
  14.3 9.1 %leaf_forward.1 = (bf16[1536,256]{1,0:T(8,128)(2,1)S(1)}, bf16[768,256]{1,0:T(8,128)(2,1)S(1)}, bf16[768,256]{1,0:T(8,128)(2,1)S(1)}, bf16[512,512]{1,0:T(8,128)...) custom-call(s32[1,1]{1,0:T(1,128)S(6)} %copy.18.count_hbm, s32[1,256]{1,0:T(1,128)} %cols_hbm.1, ...), custom_call_target="tpu_custom_call" | custom-call | flops 1342177280 | bytes 9437184 | tf_op jit(solution)/shard_map/leaf_forward/pallas_call | solution.py:183
  24.1 2.7 %collective-permute-start.7 = (bf16[128,1024]{1,0:T(8,128)(2,1)S(1)}, bf16[128,1024]{1,0:T(8,128)(2,1)S(1)}, u32[]{:S(2)}, u32[]{:S(2)}) collective-permute-start(bf16[128,1024]{1,0:T(8,128)(2,1)S(1)} %stack.3.refs_0_), channel_id=1, source_target_pairs={{0,24},{8,16},{16,8},{24,0},{1,25},{9,17},{17,9},{25,1},{2,26},{10... | collective-permute-start | bytes 786440 | tf_op jit(solution)/shard_map/gather_middle_panel/ppermute | solution.py:510
  27.6 6.6 %collective-permute-done.7.refs_3_ = bf16[128,1024]{1,0:T(8,128)(2,1)S(1)} collective-permute-done((bf16[128,1024]{1,0:T(8,128)(2,1)S(1)}, bf16[128,1024]{1,0:T(8,128)(2,1)S(1)}, u32[]{:S(2)}, u32[]{:S(2)}) %collective-permute-start.7) | collective-permute-done | bytes 262176 | tf_op jit(solution)/shard_map/gather_middle_panel/ppermute | solution.py:510
  34.2 4.7 %collective-permute-done.6.refs_2_ = bf16[128,1024]{1,0:T(8,128)(2,1)S(1)} collective-permute-done((bf16[128,1024]{1,0:T(8,128)(2,1)S(1)}, bf16[128,1024]{1,0:T(8,128)(2,1)S(1)}, u32[]{:S(2)}, u32[]{:S(2)}) %collective-permute-start.6) | collective-permute-done | bytes 262176 | tf_op jit(solution)/shard_map/gather_middle_panel/ppermute | solution.py:510
  38.9 1.3 %all-gather.2.cloned.1.call-done.panel.panel_own_hbm = bf16[4,256,512]{2,1,0:T(8,128)(2,1)} async-done(((bf16[1,256,512]{2,1,0:T(8,128)(2,1)}), bf16[4,256,512]{2,1,0:T(8,128)(2,1)}) %all-gather.2.cloned.1.call-update) | async-done | bytes 1048592 | tf_op jit(solution)/shard_map/gather_group_panel/all_gather | solution.py:550
  40.2 1.2 %copy-done = bf16[4,256,512]{2,1,0:T(8,128)(2,1)S(1)} copy-done((bf16[4,256,512]{2,1,0:T(8,128)(2,1)S(1)}, bf16[4,256,512]{2,1,0:T(8,128)(2,1)}, u32[]{:S(2)}) %copy-start) | copy-done | bytes 1048600
  41.5 1.7 %fold_group.1 = (bf16[256,256]{1,0:T(8,128)(2,1)S(1)}, bf16[256,256]{1,0:T(8,128)(2,1)}, bf16[256,256]{1,0:T(8,128)(2,1)}, bf16[256,256]{1,0:T(8,128)(2,1)}, bf16[256,256]{1,0:T(8,128)(2,1)S(1)}) custom-call(bf16[1536,256]{1,0:T(8,128)(2,1)S(1)} %get-tuple-element.43.keep, bf16[768,256]{1,0:T(8,128)(2,1)S(1)} %collective-permute-done.3.low, ...), custom_call_target="tpu_custom_call" | custom-call | tf_op jit(solution)/shard_map/fold_group/pallas_call | solution.py:30
  43.8 1.5 %collective-permute-start.8 = (bf16[256,256]{1,0:T(8,128)(2,1)}, bf16[256,256]{1,0:T(8,128)(2,1)S(1)}, u32[]{:S(2)}, u32[]{:S(2)}) collective-permute-start(bf16[256,256]{1,0:T(8,128)(2,1)} %get-tuple-element.56), channel_id=1, source_target_pairs={{0,8},{8,0},{16,24},{24,16},{1,9},{9,1},{17,25},{25,17},{2,10},{10... | collective-permute-start | bytes 393224 | tf_op jit(solution)/shard_map/sum_over_leaf/ppermute | solution.py:510
  45.3 1.5 %collective-permute-start.9 = (bf16[256,256]{1,0:T(8,128)(2,1)}, bf16[256,256]{1,0:T(8,128)(2,1)S(1)}, u32[]{:S(2)}, u32[]{:S(2)}) collective-permute-start(bf16[256,256]{1,0:T(8,128)(2,1)} %get-tuple-element.57), channel_id=1, source_target_pairs={{0,16},{8,24},{16,0},{24,8},{1,17},{9,25},{17,1},{25,9},{2,18},{10... | collective-permute-start | bytes 393224 | tf_op jit(solution)/shard_map/sum_over_leaf/ppermute | solution.py:510
  49.5 3.7 %collective-permute-done.9.refs_2_ = bf16[256,256]{1,0:T(8,128)(2,1)S(1)} collective-permute-done((bf16[256,256]{1,0:T(8,128)(2,1)}, bf16[256,256]{1,0:T(8,128)(2,1)S(1)}, u32[]{:S(2)}, u32[]{:S(2)}) %collective-permute-start.9) | collective-permute-done | bytes 131104 | tf_op jit(solution)/shard_map/sum_over_leaf/ppermute | solution.py:510
  53.4 1.5 %collective-permute-start.11 = (bf16[128,256]{1,0:T(8,128)(2,1)S(1)}, bf16[128,256]{1,0:T(8,128)(2,1)S(1)}, u32[]{:S(2)}, u32[]{:S(2)}) collective-permute-start(bf16[128,256]{1,0:T(8,128)(2,1)S(1)} %get-tuple-element.61), channel_id=1, source_target_pairs={{0,2},{1,3},{2,0},{3,1},{4,6},{5,7},{6,4},{7,5},{8,10},{9,11},{10,... | collective-permute-start | bytes 196616 | tf_op jit(solution)/shard_map/sum_over_pos/ppermute | solution.py:510
  55.0 1.8 %collective-permute-start.12 = (bf16[128,256]{1,0:T(8,128)(2,1)S(1)}, bf16[128,256]{1,0:T(8,128)(2,1)S(1)}, u32[]{:S(2)}, u32[]{:S(2)}) collective-permute-start(bf16[128,256]{1,0:T(8,128)(2,1)S(1)} %get-tuple-element.62), channel_id=1, source_target_pairs={{0,4},{1,5},{2,6},{3,7},{4,0},{5,1},{6,2},{7,3},{8,12},{9,13},{10,... | collective-permute-start | bytes 196616 | tf_op jit(solution)/shard_map/sum_over_pos/ppermute | solution.py:510
  56.7 1.1 %collective-permute-start.13 = (bf16[128,256]{1,0:T(8,128)(2,1)S(1)}, bf16[128,256]{1,0:T(8,128)(2,1)S(1)}, u32[]{:S(2)}, u32[]{:S(2)}) collective-permute-start(bf16[128,256]{1,0:T(8,128)(2,1)S(1)} %get-tuple-element.63), channel_id=1, source_target_pairs={{0,6},{1,7},{2,4},{3,5},{4,2},{5,3},{6,0},{7,1},{8,14},{9,15},{10,... | collective-permute-start | bytes 196616 | tf_op jit(solution)/shard_map/sum_over_pos/ppermute | solution.py:510
  57.9 5.4 %collective-permute-done.12.refs_2_ = bf16[128,256]{1,0:T(8,128)(2,1)S(1)} collective-permute-done((bf16[128,256]{1,0:T(8,128)(2,1)S(1)}, bf16[128,256]{1,0:T(8,128)(2,1)S(1)}, u32[]{:S(2)}, u32[]{:S(2)}) %collective-permute-start.12) | collective-permute-done | bytes 65568 | tf_op jit(solution)/shard_map/sum_over_pos/ppermute | solution.py:510
  63.4 2.2 %collective-permute-start.16 = (bf16[128,256]{1,0:T(8,128)(2,1)S(1)}, bf16[128,256]{1,0:T(8,128)(2,1)S(1)}, u32[]{:S(2)}, u32[]{:S(2)}) collective-permute-start(bf16[128,256]{1,0:T(8,128)(2,1)S(1)} %sum_pos.1.refs_0_), channel_id=1, source_target_pairs={{0,6},{1,7},{2,4},{3,5},{4,2},{5,3},{6,0},{7,1},{8,14},{9,15},{10,... | collective-permute-start | bytes 196616 | tf_op jit(solution)/shard_map/gather_pos/ppermute | solution.py:510
  66.4 1.4 %collective-permute-start.14 = (bf16[128,256]{1,0:T(8,128)(2,1)S(1)}, bf16[128,256]{1,0:T(8,128)(2,1)S(1)}, u32[]{:S(2)}, u32[]{:S(2)}) collective-permute-start(bf16[128,256]{1,0:T(8,128)(2,1)S(1)} %sum_pos.1.refs_0_), channel_id=1, source_target_pairs={{0,2},{1,3},{2,0},{3,1},{4,6},{5,7},{6,4},{7,5},{8,10},{9,11},{10,... | collective-permute-start | bytes 196616 | tf_op jit(solution)/shard_map/gather_pos/ppermute | solution.py:510
  67.8 1.9 %collective-permute-done.16.refs_3_ = bf16[128,256]{1,0:T(8,128)(2,1)S(1)} collective-permute-done((bf16[128,256]{1,0:T(8,128)(2,1)S(1)}, bf16[128,256]{1,0:T(8,128)(2,1)S(1)}, u32[]{:S(2)}, u32[]{:S(2)}) %collective-permute-start.16) | collective-permute-done | bytes 65568 | tf_op jit(solution)/shard_map/gather_pos/ppermute | solution.py:510
  69.7 1.9 %collective-permute-done.15.refs_2_ = bf16[128,256]{1,0:T(8,128)(2,1)S(1)} collective-permute-done((bf16[128,256]{1,0:T(8,128)(2,1)S(1)}, bf16[128,256]{1,0:T(8,128)(2,1)S(1)}, u32[]{:S(2)}, u32[]{:S(2)}) %collective-permute-start.15) | collective-permute-done | bytes 65568 | tf_op jit(solution)/shard_map/gather_pos/ppermute | solution.py:510
  71.7 1.8 %collective-permute-start.19 = (bf16[256,256]{1,0:T(8,128)(2,1)S(1)}, bf16[256,256]{1,0:T(8,128)(2,1)S(1)}, u32[]{:S(2)}, u32[]{:S(2)}) collective-permute-start(bf16[256,256]{1,0:T(8,128)(2,1)S(1)} %get-tuple-element.71.refs_0_), channel_id=1, source_target_pairs={{0,24},{8,16},{16,8},{24,0},{1,25},{9,17},{17,9},{25,1},{2,26},{10... | collective-permute-start | bytes 393224 | tf_op jit(solution)/shard_map/gather_leaf/ppermute | solution.py:510
  73.5 1.2 %collective-permute-start.18 = (bf16[256,256]{1,0:T(8,128)(2,1)S(1)}, bf16[256,256]{1,0:T(8,128)(2,1)S(1)}, u32[]{:S(2)}, u32[]{:S(2)}) collective-permute-start(bf16[256,256]{1,0:T(8,128)(2,1)S(1)} %get-tuple-element.71.refs_0_), channel_id=1, source_target_pairs={{0,16},{8,24},{16,0},{24,8},{1,17},{9,25},{17,1},{25,9},{2,18},{10... | collective-permute-start | bytes 393224 | tf_op jit(solution)/shard_map/gather_leaf/ppermute | solution.py:510
  75.4 3.4 %collective-permute-done.19.refs_3_ = bf16[256,256]{1,0:T(8,128)(2,1)S(1)} collective-permute-done((bf16[256,256]{1,0:T(8,128)(2,1)S(1)}, bf16[256,256]{1,0:T(8,128)(2,1)S(1)}, u32[]{:S(2)}, u32[]{:S(2)}) %collective-permute-start.19) | collective-permute-done | bytes 131104 | tf_op jit(solution)/shard_map/gather_leaf/ppermute | solution.py:510
  80.8 2.1 %collective-permute-done.22.theirs = bf16[1280,256]{1,0:T(8,128)(2,1)S(1)} collective-permute-done((bf16[1280,256]{1,0:T(8,128)(2,1)S(1)}, bf16[1280,256]{1,0:T(8,128)(2,1)S(1)}, u32[]{:S(2)}, u32[]{:S(2)}) %collective-permute-start.22) | collective-permute-done | bytes 655392 | tf_op jit(solution)/shard_map/gather_cores/ppermute | solution.py:510
  82.9 9.5 %backward.1 = (f32[1024,256]{1,0:T(8,128)}, f32[512,256]{1,0:T(8,128)}, f32[1024,256]{1,0:T(8,128)}, f32[1024,256]{1,0:T(8,128)}) custom-call(bf16[1280,256]{1,0:T(8,128)(2,1)S(1)} %stack.5.mine, bf16[1280,256]{1,0:T(8,128)(2,1)S(1)} %collective-permute-done.22.theirs, bf16[1024,1024]{1,0:T(8,128)(2,1)S(1)} %copy-done.2, ...), custom_call_target="tpu_custom_call" | custom-call | tf_op jit(solution)/shard_map/backward/pallas_call | solution.py:489
  (50 shorter events, 10.0 us)
Async XLA Ops:
  7.2 33.1 %all-gather.2.cloned.1.call-start = ((), (), s32[]{:S(2)}) async-start(), calls=%async_computation | async-start | bytes 1310720 | tf_op jit(solution)/shard_map/gather_group_panel/all_gather | solution.py:550
  7.9 15.5 %collective-permute-start.2 = (bf16[32,1024]{1,0:T(8,128)(2,1)}, bf16[32,1024]{1,0:T(8,128)(2,1)S(1)}, u32[]{:S(2)}, u32[]{:S(2)}) collective-permute-start(bf16[32,1024]{1,0:T(8,128)(2,1)} %refs_0_), channel_id=1, source_target_pairs={{0,6},{1,7},{2,4},{3,5},{4,2},{5,3},{6,0},{7,1},{8,14},{9,15},{10,... | collective-permute-start | bytes 196616 | tf_op jit(solution)/shard_map/gather_middle_panel/ppermute | solution.py:510
  13.0 10.4 %collective-permute-start.1 = (bf16[32,1024]{1,0:T(8,128)(2,1)}, bf16[32,1024]{1,0:T(8,128)(2,1)S(1)}, u32[]{:S(2)}, u32[]{:S(2)}) collective-permute-start(bf16[32,1024]{1,0:T(8,128)(2,1)} %refs_0_), channel_id=1, source_target_pairs={{0,4},{1,5},{2,6},{3,7},{4,0},{5,1},{6,2},{7,3},{8,12},{9,13},{10,... | collective-permute-start | bytes 196616 | tf_op jit(solution)/shard_map/gather_middle_panel/ppermute | solution.py:510
  13.0 10.4 %collective-permute-start = (bf16[32,1024]{1,0:T(8,128)(2,1)}, bf16[32,1024]{1,0:T(8,128)(2,1)S(1)}, u32[]{:S(2)}, u32[]{:S(2)}) collective-permute-start(bf16[32,1024]{1,0:T(8,128)(2,1)} %refs_0_), channel_id=1, source_target_pairs={{0,2},{1,3},{2,0},{3,1},{4,6},{5,7},{6,4},{7,5},{8,10},{9,11},{10,... | collective-permute-start | bytes 196616 | tf_op jit(solution)/shard_map/gather_middle_panel/ppermute | solution.py:510
  23.5 15.5 %collective-permute-start.3 = (bf16[768,256]{1,0:T(8,128)(2,1)S(1)}, bf16[768,256]{1,0:T(8,128)(2,1)S(1)}, u32[]{:S(2)}, u32[]{:S(2)}) collective-permute-start(bf16[768,256]{1,0:T(8,128)(2,1)S(1)} %get-tuple-element.46), channel_id=1, source_target_pairs={{0,1},{1,0},{2,3},{3,2},{4,5},{5,4},{6,7},{7,6},{8,9},{9,8},{10,11... | collective-permute-start | bytes 1179656 | tf_op jit(solution)/shard_map/swap_cores/ppermute | solution.py:510
  23.5 15.4 %collective-permute-start.4 = (bf16[768,256]{1,0:T(8,128)(2,1)S(1)}, bf16[768,256]{1,0:T(8,128)(2,1)S(1)}, u32[]{:S(2)}, u32[]{:S(2)}) collective-permute-start(bf16[768,256]{1,0:T(8,128)(2,1)S(1)} %get-tuple-element.47), channel_id=1, source_target_pairs={{0,1},{1,0},{2,3},{3,2},{4,5},{5,4},{6,7},{7,6},{8,9},{9,8},{10,11... | collective-permute-start | bytes 1179656 | tf_op jit(solution)/shard_map/swap_cores/ppermute | solution.py:510
  24.1 10.2 %collective-permute-start.7 = (bf16[128,1024]{1,0:T(8,128)(2,1)S(1)}, bf16[128,1024]{1,0:T(8,128)(2,1)S(1)}, u32[]{:S(2)}, u32[]{:S(2)}) collective-permute-start(bf16[128,1024]{1,0:T(8,128)(2,1)S(1)} %stack.3.refs_0_), channel_id=1, source_target_pairs={{0,24},{8,16},{16,8},{24,0},{1,25},{9,17},{17,9},{25,1},{2,26},{10... | collective-permute-start | bytes 786440 | tf_op jit(solution)/shard_map/gather_middle_panel/ppermute | solution.py:510
  26.7 12.2 %collective-permute-start.6 = (bf16[128,1024]{1,0:T(8,128)(2,1)S(1)}, bf16[128,1024]{1,0:T(8,128)(2,1)S(1)}, u32[]{:S(2)}, u32[]{:S(2)}) collective-permute-start(bf16[128,1024]{1,0:T(8,128)(2,1)S(1)} %stack.3.refs_0_), channel_id=1, source_target_pairs={{0,16},{8,24},{16,0},{24,8},{1,17},{9,25},{17,1},{25,9},{2,18},{10... | collective-permute-start | bytes 786440 | tf_op jit(solution)/shard_map/gather_middle_panel/ppermute | solution.py:510
  27.6 11.4 %collective-permute-start.5 = (bf16[128,1024]{1,0:T(8,128)(2,1)S(1)}, bf16[128,1024]{1,0:T(8,128)(2,1)S(1)}, u32[]{:S(2)}, u32[]{:S(2)}) collective-permute-start(bf16[128,1024]{1,0:T(8,128)(2,1)S(1)} %stack.3.refs_0_), channel_id=1, source_target_pairs={{0,8},{8,0},{16,24},{24,16},{1,9},{9,1},{17,25},{25,17},{2,10},{10... | collective-permute-start | bytes 786440 | tf_op jit(solution)/shard_map/gather_middle_panel/ppermute | solution.py:510
  43.8 5.7 %collective-permute-start.8 = (bf16[256,256]{1,0:T(8,128)(2,1)}, bf16[256,256]{1,0:T(8,128)(2,1)S(1)}, u32[]{:S(2)}, u32[]{:S(2)}) collective-permute-start(bf16[256,256]{1,0:T(8,128)(2,1)} %get-tuple-element.56), channel_id=1, source_target_pairs={{0,8},{8,0},{16,24},{24,16},{1,9},{9,1},{17,25},{25,17},{2,10},{10... | collective-permute-start | bytes 393224 | tf_op jit(solution)/shard_map/sum_over_leaf/ppermute | solution.py:510
  45.3 8.0 %collective-permute-start.9 = (bf16[256,256]{1,0:T(8,128)(2,1)}, bf16[256,256]{1,0:T(8,128)(2,1)S(1)}, u32[]{:S(2)}, u32[]{:S(2)}) collective-permute-start(bf16[256,256]{1,0:T(8,128)(2,1)} %get-tuple-element.57), channel_id=1, source_target_pairs={{0,16},{8,24},{16,0},{24,8},{1,17},{9,25},{17,1},{25,9},{2,18},{10... | collective-permute-start | bytes 393224 | tf_op jit(solution)/shard_map/sum_over_leaf/ppermute | solution.py:510
  46.8 6.5 %collective-permute-start.10 = (bf16[256,256]{1,0:T(8,128)(2,1)}, bf16[256,256]{1,0:T(8,128)(2,1)S(1)}, u32[]{:S(2)}, u32[]{:S(2)}) collective-permute-start(bf16[256,256]{1,0:T(8,128)(2,1)} %get-tuple-element.58), channel_id=1, source_target_pairs={{0,24},{8,16},{16,8},{24,0},{1,25},{9,17},{17,9},{25,1},{2,26},{10... | collective-permute-start | bytes 393224 | tf_op jit(solution)/shard_map/sum_over_leaf/ppermute | solution.py:510
  48.3 26.9 %collective-permute-start.21 = (bf16[512,1024]{1,0:T(8,128)(2,1)S(1)}, bf16[512,1024]{1,0:T(8,128)(2,1)S(1)}, u32[]{:S(2)}, u32[]{:S(2)}) collective-permute-start(bf16[512,1024]{1,0:T(8,128)(2,1)S(1)} %stack.4.own), channel_id=1, source_target_pairs={{0,1},{1,0},{2,3},{3,2},{4,5},{5,4},{6,7},{7,6},{8,9},{9,8},{10,11... | collective-permute-start | bytes 3145736 | tf_op jit(solution)/shard_map/gather_middle_panel/ppermute | solution.py:510
  53.4 27.3 %collective-permute-start.20 = (bf16[4,256,512]{2,1,0:T(8,128)(2,1)S(1)}, bf16[4,256,512]{2,1,0:T(8,128)(2,1)S(1)}, u32[]{:S(2)}, u32[]{:S(2)}) collective-permute-start(bf16[4,256,512]{2,1,0:T(8,128)(2,1)S(1)} %copy-done.1), channel_id=1, source_target_pairs={{0,1},{1,0},{2,3},{3,2},{4,5},{5,4},{6,7},{7,6},{8,9},{9,8},{10,11... | collective-permute-start | bytes 3145736 | tf_op jit(solution)/shard_map/swap_group_panel/ppermute | solution.py:510
  53.4 4.5 %collective-permute-start.11 = (bf16[128,256]{1,0:T(8,128)(2,1)S(1)}, bf16[128,256]{1,0:T(8,128)(2,1)S(1)}, u32[]{:S(2)}, u32[]{:S(2)}) collective-permute-start(bf16[128,256]{1,0:T(8,128)(2,1)S(1)} %get-tuple-element.61), channel_id=1, source_target_pairs={{0,2},{1,3},{2,0},{3,1},{4,6},{5,7},{6,4},{7,5},{8,10},{9,11},{10,... | collective-permute-start | bytes 196616 | tf_op jit(solution)/shard_map/sum_over_pos/ppermute | solution.py:510
  55.0 8.4 %collective-permute-start.12 = (bf16[128,256]{1,0:T(8,128)(2,1)S(1)}, bf16[128,256]{1,0:T(8,128)(2,1)S(1)}, u32[]{:S(2)}, u32[]{:S(2)}) collective-permute-start(bf16[128,256]{1,0:T(8,128)(2,1)S(1)} %get-tuple-element.62), channel_id=1, source_target_pairs={{0,4},{1,5},{2,6},{3,7},{4,0},{5,1},{6,2},{7,3},{8,12},{9,13},{10,... | collective-permute-start | bytes 196616 | tf_op jit(solution)/shard_map/sum_over_pos/ppermute | solution.py:510
  56.7 6.6 %collective-permute-start.13 = (bf16[128,256]{1,0:T(8,128)(2,1)S(1)}, bf16[128,256]{1,0:T(8,128)(2,1)S(1)}, u32[]{:S(2)}, u32[]{:S(2)}) collective-permute-start(bf16[128,256]{1,0:T(8,128)(2,1)S(1)} %get-tuple-element.63), channel_id=1, source_target_pairs={{0,6},{1,7},{2,4},{3,5},{4,2},{5,3},{6,0},{7,1},{8,14},{9,15},{10,... | collective-permute-start | bytes 196616 | tf_op jit(solution)/shard_map/sum_over_pos/ppermute | solution.py:510
  63.4 6.4 %collective-permute-start.16 = (bf16[128,256]{1,0:T(8,128)(2,1)S(1)}, bf16[128,256]{1,0:T(8,128)(2,1)S(1)}, u32[]{:S(2)}, u32[]{:S(2)}) collective-permute-start(bf16[128,256]{1,0:T(8,128)(2,1)S(1)} %sum_pos.1.refs_0_), channel_id=1, source_target_pairs={{0,6},{1,7},{2,4},{3,5},{4,2},{5,3},{6,0},{7,1},{8,14},{9,15},{10,... | collective-permute-start | bytes 196616 | tf_op jit(solution)/shard_map/gather_pos/ppermute | solution.py:510
  65.6 6.1 %collective-permute-start.15 = (bf16[128,256]{1,0:T(8,128)(2,1)S(1)}, bf16[128,256]{1,0:T(8,128)(2,1)S(1)}, u32[]{:S(2)}, u32[]{:S(2)}) collective-permute-start(bf16[128,256]{1,0:T(8,128)(2,1)S(1)} %sum_pos.1.refs_0_), channel_id=1, source_target_pairs={{0,4},{1,5},{2,6},{3,7},{4,0},{5,1},{6,2},{7,3},{8,12},{9,13},{10,... | collective-permute-start | bytes 196616 | tf_op jit(solution)/shard_map/gather_pos/ppermute | solution.py:510
  66.4 5.3 %collective-permute-start.14 = (bf16[128,256]{1,0:T(8,128)(2,1)S(1)}, bf16[128,256]{1,0:T(8,128)(2,1)S(1)}, u32[]{:S(2)}, u32[]{:S(2)}) collective-permute-start(bf16[128,256]{1,0:T(8,128)(2,1)S(1)} %sum_pos.1.refs_0_), channel_id=1, source_target_pairs={{0,2},{1,3},{2,0},{3,1},{4,6},{5,7},{6,4},{7,5},{8,10},{9,11},{10,... | collective-permute-start | bytes 196616 | tf_op jit(solution)/shard_map/gather_pos/ppermute | solution.py:510
  71.7 7.1 %collective-permute-start.19 = (bf16[256,256]{1,0:T(8,128)(2,1)S(1)}, bf16[256,256]{1,0:T(8,128)(2,1)S(1)}, u32[]{:S(2)}, u32[]{:S(2)}) collective-permute-start(bf16[256,256]{1,0:T(8,128)(2,1)S(1)} %get-tuple-element.71.refs_0_), channel_id=1, source_target_pairs={{0,24},{8,16},{16,8},{24,0},{1,25},{9,17},{17,9},{25,1},{2,26},{10... | collective-permute-start | bytes 393224 | tf_op jit(solution)/shard_map/gather_leaf/ppermute | solution.py:510
  73.5 6.2 %collective-permute-start.18 = (bf16[256,256]{1,0:T(8,128)(2,1)S(1)}, bf16[256,256]{1,0:T(8,128)(2,1)S(1)}, u32[]{:S(2)}, u32[]{:S(2)}) collective-permute-start(bf16[256,256]{1,0:T(8,128)(2,1)S(1)} %get-tuple-element.71.refs_0_), channel_id=1, source_target_pairs={{0,16},{8,24},{16,0},{24,8},{1,17},{9,25},{17,1},{25,9},{2,18},{10... | collective-permute-start | bytes 393224 | tf_op jit(solution)/shard_map/gather_leaf/ppermute | solution.py:510
  74.6 6.0 %collective-permute-start.17 = (bf16[256,256]{1,0:T(8,128)(2,1)S(1)}, bf16[256,256]{1,0:T(8,128)(2,1)S(1)}, u32[]{:S(2)}, u32[]{:S(2)}) collective-permute-start(bf16[256,256]{1,0:T(8,128)(2,1)S(1)} %get-tuple-element.71.refs_0_), channel_id=1, source_target_pairs={{0,8},{8,0},{16,24},{24,16},{1,9},{9,1},{17,25},{25,17},{2,10},{10... | collective-permute-start | bytes 393224 | tf_op jit(solution)/shard_map/gather_leaf/ppermute | solution.py:510
  80.7 2.2 %collective-permute-start.22 = (bf16[1280,256]{1,0:T(8,128)(2,1)S(1)}, bf16[1280,256]{1,0:T(8,128)(2,1)S(1)}, u32[]{:S(2)}, u32[]{:S(2)}) collective-permute-start(bf16[1280,256]{1,0:T(8,128)(2,1)S(1)} %stack.5.mine), channel_id=1, source_target_pairs={{0,1},{1,0},{2,3},{3,2},{4,5},{5,4},{6,7},{7,6},{8,9},{9,8},{10,11... | collective-permute-start | bytes 1966088 | tf_op jit(solution)/shard_map/gather_cores/ppermute | solution.py:510
  (7 other events, 44.0 us)
Sparse Core Ops, SparseCore 0:
  9.6 30.6 all-gather.1

commit v13 on v12

--- a/solution.py
+++ b/solution.py
@@ -226,9 +226,14 @@
     return total
 
 
-def fold_kernel(n_leaf, n_pos, keep, low, high, inv, panel, *refs):
-    parts, group, (gsum, base, stage) = refs[:n_leaf], refs[n_leaf], refs[n_leaf + 1 :]
+def fold_kernel(n_leaf, n_pos, keep, low, high, inv, panel_hbm, *refs):
+    parts, group, (gsum, base, stage, panel, sems) = refs[:n_leaf], refs[n_leaf], refs[n_leaf + 1 :]
     leaf, pos, core = place()
+    loads = [
+        pltpu.make_async_copy(panel_hbm.at[pos ^ k], panel.at[k], sems.at[k]) for k in range(n_pos)
+    ]
+    for load in loads:
+        load.start()
     group_cols = inv.shape[0]
     sec = panel.shape[1]
     q = sec // n_leaf
@@ -241,7 +246,8 @@
     for k in range(n_pos):
         p = pos ^ k
         rows = pl.ds(pl.multiple_of(p * sec, sec), sec)
-        terms = (dot(panel[p], solved) + base[rows, :]).astype(BF)
+        loads[k].wait()
+        terms = (dot(panel[k], solved) + base[rows, :]).astype(BF)
         for j in range(n_leaf):
             stage[j ^ leaf, k * q : (k + 1) * q, :] = terms[j * q : (j + 1) * q, :]
         begin = pl.multiple_of(core * (group_cols // 2) + p * gq, gq)
@@ -254,20 +260,22 @@
     width = keep.shape[-1]
     n_pos, sec, _ = panel.shape
     part = (n_pos * sec // n_leaf, width)
-    outs = small(
+    outs = pl.pallas_call(
         functools.partial(fold_kernel, n_leaf, n_pos),
-        "fold_group",
-        [part] * n_leaf + [(inverse.shape[0] // 2, width)],
-        [
+        out_shape=[pltpu.VMEM(part, BF)] * n_leaf
+        + [pltpu.VMEM((inverse.shape[0] // 2, width), BF)],
+        in_specs=[VMEM] * 4 + [HBM],
+        out_specs=[VMEM] * (n_leaf + 1),
+        scratch_shapes=[
             pltpu.VMEM((inverse.shape[0], width), F32),
             pltpu.VMEM((n_pos * sec, width), F32),
             pltpu.VMEM((n_leaf,) + part, BF),
+            pltpu.VMEM(panel.shape, BF),
+            pltpu.SemaphoreType.DMA((n_pos,)),
         ],
-        keep,
-        *recv,
-        inverse,
-        panel,
-    )
+        compiler_params=pltpu.CompilerParams(vmem_limit_bytes=SMALL),
+        name="fold_group",
+    )(*in_vmem(keep, *recv, inverse), *in_hbm(panel))
     return list(outs[:n_leaf]), outs[n_leaf]
 
 

time: 99.4 us -> 99.1 us (level)
  local copies, waits for them, and re-layouts: 1.9 us -> 0.02 us
  Pallas kernels: 20.7 us -> 21.7 us
    pallas_call x0 -> x1, Pallas kernels: none -> 3.23 us  [fold(): pl.pallas_call(functools.partial(fold_kernel, n_leaf, n_pos), out_shape=[...]
    unnamed x14 -> x8, local copies, waits for them, and re-layouts: 1.9 us -> 0.02 us
    pallas_call x8 -> x7, Pallas kernels: 2.1 us -> 0.41 us  [small(): pl.pallas_call(kernel, out_shape=[pltpu.VMEM(shape, BF) for shape in shap...]
  transfers between devices with their start and end apart: 24 -> 24, of which waited for: 13 -> 14; matrix products, arithmetic and copies ran while one was open for 1% -> 1% of each run, Pallas kernels for 10% -> 9%
where the time goes in v13:
time: 99.1 us; the launch traced here: 99 us
  waiting for transfers between devices  35 us (35%)
  starting transfers between devices  26.4 us (27%)
  Pallas kernels  21.7 us (22%)
  between operations  14.9 us (15%)
    ppermute x23, waiting for transfers between devices, swap(): return lax.ppermute(x, axis, [(i, i ^ bits) for i in range(size)])  33.3 us
    ppermute x23, starting transfers between devices, swap(): return lax.ppermute(x, axis, [(i, i ^ bits) for i in range(size)])  26.4 us
    pallas_call x1, Pallas kernels, backward(): pl.pallas_call(functools.partial(backward_kernel, n_leaf, n_pos), out_sha...  9.48 us
    pallas_call x1, Pallas kernels, leaf_forward(): pl.pallas_call(functools.partial(forward_kernel, upper_cols // (2 * sec),...  8.59 us
    pallas_call x1, Pallas kernels, fold(): pl.pallas_call(functools.partial(fold_kernel, n_leaf, n_pos), out_shape=[...  3.23 us
  transfers between devices with their start and end apart: 24, of which 14 were waited for; matrix products, arithmetic and copies ran while one was open for 1% of the time, Pallas kernels for 9%

profile of v13, /device:TPU:0, one launch (start us, length us, event | category | flops | bytes accessed | tf_op | source)
XLA Modules:
  0.0 99.0 jit_solution(14522793791916339166)
XLA Ops:
  7.9 5.1 %collective-permute-start.2 = (bf16[32,1024]{1,0:T(8,128)(2,1)}, bf16[32,1024]{1,0:T(8,128)(2,1)S(1)}, u32[]{:S(2)}, u32[]{:S(2)}) collective-permute-start(bf16[32,1024]{1,0:T(8,128)(2,1)} %refs_0_), channel_id=1, source_target_pairs={{0,6},{1,7},{2,4},{3,5},{4,2},{5,3},{6,0},{7,1},{8,14},{9,15},{10,... | collective-permute-start | bytes 196616 | tf_op jit(solution)/shard_map/gather_middle_panel/ppermute | solution.py:518
  14.3 8.6 %leaf_forward.1 = (bf16[1536,256]{1,0:T(8,128)(2,1)S(1)}, bf16[768,256]{1,0:T(8,128)(2,1)S(1)}, bf16[768,256]{1,0:T(8,128)(2,1)S(1)}, bf16[512,512]{1,0:T(8,128)...) custom-call(s32[1,1]{1,0:T(1,128)S(6)} %copy.18.count_hbm, s32[1,256]{1,0:T(1,128)} %cols_hbm.1, ...), custom_call_target="tpu_custom_call" | custom-call | flops 1342177280 | bytes 9437184 | tf_op jit(solution)/shard_map/leaf_forward/pallas_call | solution.py:183
  23.5 2.8 %collective-permute-start.7 = (bf16[128,1024]{1,0:T(8,128)(2,1)S(1)}, bf16[128,1024]{1,0:T(8,128)(2,1)S(1)}, u32[]{:S(2)}, u32[]{:S(2)}) collective-permute-start(bf16[128,1024]{1,0:T(8,128)(2,1)S(1)} %stack.3.refs_0_), channel_id=1, source_target_pairs={{0,24},{8,16},{16,8},{24,0},{1,25},{9,17},{17,9},{25,1},{2,26},{10... | collective-permute-start | bytes 786440 | tf_op jit(solution)/shard_map/gather_middle_panel/ppermute | solution.py:518
  26.3 1.1 %collective-permute-start.6 = (bf16[128,1024]{1,0:T(8,128)(2,1)S(1)}, bf16[128,1024]{1,0:T(8,128)(2,1)S(1)}, u32[]{:S(2)}, u32[]{:S(2)}) collective-permute-start(bf16[128,1024]{1,0:T(8,128)(2,1)S(1)} %stack.3.refs_0_), channel_id=1, source_target_pairs={{0,16},{8,24},{16,0},{24,8},{1,17},{9,25},{17,1},{25,9},{2,18},{10... | collective-permute-start | bytes 786440 | tf_op jit(solution)/shard_map/gather_middle_panel/ppermute | solution.py:518
  27.4 6.3 %collective-permute-done.7.refs_3_ = bf16[128,1024]{1,0:T(8,128)(2,1)S(1)} collective-permute-done((bf16[128,1024]{1,0:T(8,128)(2,1)S(1)}, bf16[128,1024]{1,0:T(8,128)(2,1)S(1)}, u32[]{:S(2)}, u32[]{:S(2)}) %collective-permute-start.7) | collective-permute-done | bytes 262176 | tf_op jit(solution)/shard_map/gather_middle_panel/ppermute | solution.py:518
  33.7 4.8 %collective-permute-done.6.refs_2_ = bf16[128,1024]{1,0:T(8,128)(2,1)S(1)} collective-permute-done((bf16[128,1024]{1,0:T(8,128)(2,1)S(1)}, bf16[128,1024]{1,0:T(8,128)(2,1)S(1)}, u32[]{:S(2)}, u32[]{:S(2)}) %collective-permute-start.6) | collective-permute-done | bytes 262176 | tf_op jit(solution)/shard_map/gather_middle_panel/ppermute | solution.py:518
  40.2 3.2 %fold_group.1 = (bf16[256,256]{1,0:T(8,128)(2,1)S(1)}, bf16[256,256]{1,0:T(8,128)(2,1)}, bf16[256,256]{1,0:T(8,128)(2,1)}, bf16[256,256]{1,0:T(8,128)(2,1)S(1)}, bf16[256,256]{1,0:T(8,128)(2,1)S(1)}) custom-call(bf16[1536,256]{1,0:T(8,128)(2,1)S(1)} %get-tuple-element.43.keep, bf16[768,256]{1,0:T(8,128)(2,1)S(1)} %collective-permute-done.3.low, ...), custom_call_target="tpu_custom_call" | custom-call | tf_op jit(solution)/shard_map/fold_group/pallas_call | solution.py:263
  43.5 1.5 %collective-permute-start.8 = (bf16[256,256]{1,0:T(8,128)(2,1)}, bf16[256,256]{1,0:T(8,128)(2,1)S(1)}, u32[]{:S(2)}, u32[]{:S(2)}) collective-permute-start(bf16[256,256]{1,0:T(8,128)(2,1)} %get-tuple-element.56), channel_id=1, source_target_pairs={{0,8},{8,0},{16,24},{24,16},{1,9},{9,1},{17,25},{25,17},{2,10},{10... | collective-permute-start | bytes 393224 | tf_op jit(solution)/shard_map/sum_over_leaf/ppermute | solution.py:518
  45.0 1.5 %collective-permute-start.9 = (bf16[256,256]{1,0:T(8,128)(2,1)}, bf16[256,256]{1,0:T(8,128)(2,1)S(1)}, u32[]{:S(2)}, u32[]{:S(2)}) collective-permute-start(bf16[256,256]{1,0:T(8,128)(2,1)} %get-tuple-element.57), channel_id=1, source_target_pairs={{0,16},{8,24},{16,0},{24,8},{1,17},{9,25},{17,1},{25,9},{2,18},{10... | collective-permute-start | bytes 393224 | tf_op jit(solution)/shard_map/sum_over_leaf/ppermute | solution.py:518
  48.1 1.4 %collective-permute-done.8.refs_1_ = bf16[256,256]{1,0:T(8,128)(2,1)S(1)} collective-permute-done((bf16[256,256]{1,0:T(8,128)(2,1)}, bf16[256,256]{1,0:T(8,128)(2,1)S(1)}, u32[]{:S(2)}, u32[]{:S(2)}) %collective-permute-start.8) | collective-permute-done | bytes 131104 | tf_op jit(solution)/shard_map/sum_over_leaf/ppermute | solution.py:518
  49.5 3.5 %collective-permute-done.9.refs_2_ = bf16[256,256]{1,0:T(8,128)(2,1)S(1)} collective-permute-done((bf16[256,256]{1,0:T(8,128)(2,1)}, bf16[256,256]{1,0:T(8,128)(2,1)S(1)}, u32[]{:S(2)}, u32[]{:S(2)}) %collective-permute-start.9) | collective-permute-done | bytes 131104 | tf_op jit(solution)/shard_map/sum_over_leaf/ppermute | solution.py:518
  53.2 1.5 %collective-permute-start.11 = (bf16[128,256]{1,0:T(8,128)(2,1)S(1)}, bf16[128,256]{1,0:T(8,128)(2,1)S(1)}, u32[]{:S(2)}, u32[]{:S(2)}) collective-permute-start(bf16[128,256]{1,0:T(8,128)(2,1)S(1)} %get-tuple-element.61), channel_id=1, source_target_pairs={{0,2},{1,3},{2,0},{3,1},{4,6},{5,7},{6,4},{7,5},{8,10},{9,11},{10,... | collective-permute-start | bytes 196616 | tf_op jit(solution)/shard_map/sum_over_pos/ppermute | solution.py:518
  54.7 1.8 %collective-permute-start.12 = (bf16[128,256]{1,0:T(8,128)(2,1)S(1)}, bf16[128,256]{1,0:T(8,128)(2,1)S(1)}, u32[]{:S(2)}, u32[]{:S(2)}) collective-permute-start(bf16[128,256]{1,0:T(8,128)(2,1)S(1)} %get-tuple-element.62), channel_id=1, source_target_pairs={{0,4},{1,5},{2,6},{3,7},{4,0},{5,1},{6,2},{7,3},{8,12},{9,13},{10,... | collective-permute-start | bytes 196616 | tf_op jit(solution)/shard_map/sum_over_pos/ppermute | solution.py:518
  56.5 1.1 %collective-permute-start.13 = (bf16[128,256]{1,0:T(8,128)(2,1)S(1)}, bf16[128,256]{1,0:T(8,128)(2,1)S(1)}, u32[]{:S(2)}, u32[]{:S(2)}) collective-permute-start(bf16[128,256]{1,0:T(8,128)(2,1)S(1)} %get-tuple-element.63), channel_id=1, source_target_pairs={{0,6},{1,7},{2,4},{3,5},{4,2},{5,3},{6,0},{7,1},{8,14},{9,15},{10,... | collective-permute-start | bytes 196616 | tf_op jit(solution)/shard_map/sum_over_pos/ppermute | solution.py:518
  57.7 5.4 %collective-permute-done.12.refs_2_ = bf16[128,256]{1,0:T(8,128)(2,1)S(1)} collective-permute-done((bf16[128,256]{1,0:T(8,128)(2,1)S(1)}, bf16[128,256]{1,0:T(8,128)(2,1)S(1)}, u32[]{:S(2)}, u32[]{:S(2)}) %collective-permute-start.12) | collective-permute-done | bytes 65568 | tf_op jit(solution)/shard_map/sum_over_pos/ppermute | solution.py:518
  63.1 2.2 %collective-permute-start.16 = (bf16[128,256]{1,0:T(8,128)(2,1)S(1)}, bf16[128,256]{1,0:T(8,128)(2,1)S(1)}, u32[]{:S(2)}, u32[]{:S(2)}) collective-permute-start(bf16[128,256]{1,0:T(8,128)(2,1)S(1)} %sum_pos.1.refs_0_), channel_id=1, source_target_pairs={{0,6},{1,7},{2,4},{3,5},{4,2},{5,3},{6,0},{7,1},{8,14},{9,15},{10,... | collective-permute-start | bytes 196616 | tf_op jit(solution)/shard_map/gather_pos/ppermute | solution.py:518
  66.1 1.4 %collective-permute-start.14 = (bf16[128,256]{1,0:T(8,128)(2,1)S(1)}, bf16[128,256]{1,0:T(8,128)(2,1)S(1)}, u32[]{:S(2)}, u32[]{:S(2)}) collective-permute-start(bf16[128,256]{1,0:T(8,128)(2,1)S(1)} %sum_pos.1.refs_0_), channel_id=1, source_target_pairs={{0,2},{1,3},{2,0},{3,1},{4,6},{5,7},{6,4},{7,5},{8,10},{9,11},{10,... | collective-permute-start | bytes 196616 | tf_op jit(solution)/shard_map/gather_pos/ppermute | solution.py:518
  67.5 1.9 %collective-permute-done.16.refs_3_ = bf16[128,256]{1,0:T(8,128)(2,1)S(1)} collective-permute-done((bf16[128,256]{1,0:T(8,128)(2,1)S(1)}, bf16[128,256]{1,0:T(8,128)(2,1)S(1)}, u32[]{:S(2)}, u32[]{:S(2)}) %collective-permute-start.16) | collective-permute-done | bytes 65568 | tf_op jit(solution)/shard_map/gather_pos/ppermute | solution.py:518
  69.5 2.0 %collective-permute-done.15.refs_2_ = bf16[128,256]{1,0:T(8,128)(2,1)S(1)} collective-permute-done((bf16[128,256]{1,0:T(8,128)(2,1)S(1)}, bf16[128,256]{1,0:T(8,128)(2,1)S(1)}, u32[]{:S(2)}, u32[]{:S(2)}) %collective-permute-start.15) | collective-permute-done | bytes 65568 | tf_op jit(solution)/shard_map/gather_pos/ppermute | solution.py:518
  71.5 1.7 %collective-permute-start.19 = (bf16[256,256]{1,0:T(8,128)(2,1)S(1)}, bf16[256,256]{1,0:T(8,128)(2,1)S(1)}, u32[]{:S(2)}, u32[]{:S(2)}) collective-permute-start(bf16[256,256]{1,0:T(8,128)(2,1)S(1)} %get-tuple-element.71.refs_0_), channel_id=1, source_target_pairs={{0,24},{8,16},{16,8},{24,0},{1,25},{9,17},{17,9},{25,1},{2,26},{10... | collective-permute-start | bytes 393224 | tf_op jit(solution)/shard_map/gather_leaf/ppermute | solution.py:518
  73.1 1.2 %collective-permute-start.18 = (bf16[256,256]{1,0:T(8,128)(2,1)S(1)}, bf16[256,256]{1,0:T(8,128)(2,1)S(1)}, u32[]{:S(2)}, u32[]{:S(2)}) collective-permute-start(bf16[256,256]{1,0:T(8,128)(2,1)S(1)} %get-tuple-element.71.refs_0_), channel_id=1, source_target_pairs={{0,16},{8,24},{16,0},{24,8},{1,17},{9,25},{17,1},{25,9},{2,18},{10... | collective-permute-start | bytes 393224 | tf_op jit(solution)/shard_map/gather_leaf/ppermute | solution.py:518
  75.2 3.6 %collective-permute-done.19.refs_3_ = bf16[256,256]{1,0:T(8,128)(2,1)S(1)} collective-permute-done((bf16[256,256]{1,0:T(8,128)(2,1)S(1)}, bf16[256,256]{1,0:T(8,128)(2,1)S(1)}, u32[]{:S(2)}, u32[]{:S(2)}) %collective-permute-start.19) | collective-permute-done | bytes 131104 | tf_op jit(solution)/shard_map/gather_leaf/ppermute | solution.py:518
  80.5 2.1 %collective-permute-done.22.theirs = bf16[1280,256]{1,0:T(8,128)(2,1)S(1)} collective-permute-done((bf16[1280,256]{1,0:T(8,128)(2,1)S(1)}, bf16[1280,256]{1,0:T(8,128)(2,1)S(1)}, u32[]{:S(2)}, u32[]{:S(2)}) %collective-permute-start.22) | collective-permute-done | bytes 655392 | tf_op jit(solution)/shard_map/gather_cores/ppermute | solution.py:518
  82.6 9.5 %backward.1 = (f32[1024,256]{1,0:T(8,128)}, f32[512,256]{1,0:T(8,128)}, f32[1024,256]{1,0:T(8,128)}, f32[1024,256]{1,0:T(8,128)}) custom-call(bf16[1280,256]{1,0:T(8,128)(2,1)S(1)} %stack.5.mine, bf16[1280,256]{1,0:T(8,128)(2,1)S(1)} %collective-permute-done.22.theirs, bf16[1024,1024]{1,0:T(8,128)(2,1)S(1)} %copy-done, ...), custom_call_target="tpu_custom_call" | custom-call | tf_op jit(solution)/shard_map/backward/pallas_call | solution.py:497
  (44 shorter events, 8.9 us)
Async XLA Ops:
  7.2 33.1 %all-gather.2.cloned.1.call-start = ((), (), s32[]{:S(2)}) async-start(), calls=%async_computation | async-start | bytes 1310720 | tf_op jit(solution)/shard_map/gather_group_panel/all_gather | solution.py:558
  7.9 15.0 %collective-permute-start.2 = (bf16[32,1024]{1,0:T(8,128)(2,1)}, bf16[32,1024]{1,0:T(8,128)(2,1)S(1)}, u32[]{:S(2)}, u32[]{:S(2)}) collective-permute-start(bf16[32,1024]{1,0:T(8,128)(2,1)} %refs_0_), channel_id=1, source_target_pairs={{0,6},{1,7},{2,4},{3,5},{4,2},{5,3},{6,0},{7,1},{8,14},{9,15},{10,... | collective-permute-start | bytes 196616 | tf_op jit(solution)/shard_map/gather_middle_panel/ppermute | solution.py:518
  13.0 9.9 %collective-permute-start.1 = (bf16[32,1024]{1,0:T(8,128)(2,1)}, bf16[32,1024]{1,0:T(8,128)(2,1)S(1)}, u32[]{:S(2)}, u32[]{:S(2)}) collective-permute-start(bf16[32,1024]{1,0:T(8,128)(2,1)} %refs_0_), channel_id=1, source_target_pairs={{0,4},{1,5},{2,6},{3,7},{4,0},{5,1},{6,2},{7,3},{8,12},{9,13},{10,... | collective-permute-start | bytes 196616 | tf_op jit(solution)/shard_map/gather_middle_panel/ppermute | solution.py:518
  13.0 9.9 %collective-permute-start = (bf16[32,1024]{1,0:T(8,128)(2,1)}, bf16[32,1024]{1,0:T(8,128)(2,1)S(1)}, u32[]{:S(2)}, u32[]{:S(2)}) collective-permute-start(bf16[32,1024]{1,0:T(8,128)(2,1)} %refs_0_), channel_id=1, source_target_pairs={{0,2},{1,3},{2,0},{3,1},{4,6},{5,7},{6,4},{7,5},{8,10},{9,11},{10,... | collective-permute-start | bytes 196616 | tf_op jit(solution)/shard_map/gather_middle_panel/ppermute | solution.py:518
  22.9 16.3 %collective-permute-start.3 = (bf16[768,256]{1,0:T(8,128)(2,1)S(1)}, bf16[768,256]{1,0:T(8,128)(2,1)S(1)}, u32[]{:S(2)}, u32[]{:S(2)}) collective-permute-start(bf16[768,256]{1,0:T(8,128)(2,1)S(1)} %get-tuple-element.46), channel_id=1, source_target_pairs={{0,1},{1,0},{2,3},{3,2},{4,5},{5,4},{6,7},{7,6},{8,9},{9,8},{10,11... | collective-permute-start | bytes 1179656 | tf_op jit(solution)/shard_map/swap_cores/ppermute | solution.py:518
  23.0 16.2 %collective-permute-start.4 = (bf16[768,256]{1,0:T(8,128)(2,1)S(1)}, bf16[768,256]{1,0:T(8,128)(2,1)S(1)}, u32[]{:S(2)}, u32[]{:S(2)}) collective-permute-start(bf16[768,256]{1,0:T(8,128)(2,1)S(1)} %get-tuple-element.47), channel_id=1, source_target_pairs={{0,1},{1,0},{2,3},{3,2},{4,5},{5,4},{6,7},{7,6},{8,9},{9,8},{10,11... | collective-permute-start | bytes 1179656 | tf_op jit(solution)/shard_map/swap_cores/ppermute | solution.py:518
  23.5 10.2 %collective-permute-start.7 = (bf16[128,1024]{1,0:T(8,128)(2,1)S(1)}, bf16[128,1024]{1,0:T(8,128)(2,1)S(1)}, u32[]{:S(2)}, u32[]{:S(2)}) collective-permute-start(bf16[128,1024]{1,0:T(8,128)(2,1)S(1)} %stack.3.refs_0_), channel_id=1, source_target_pairs={{0,24},{8,16},{16,8},{24,0},{1,25},{9,17},{17,9},{25,1},{2,26},{10... | collective-permute-start | bytes 786440 | tf_op jit(solution)/shard_map/gather_middle_panel/ppermute | solution.py:518
  26.3 12.2 %collective-permute-start.6 = (bf16[128,1024]{1,0:T(8,128)(2,1)S(1)}, bf16[128,1024]{1,0:T(8,128)(2,1)S(1)}, u32[]{:S(2)}, u32[]{:S(2)}) collective-permute-start(bf16[128,1024]{1,0:T(8,128)(2,1)S(1)} %stack.3.refs_0_), channel_id=1, source_target_pairs={{0,16},{8,24},{16,0},{24,8},{1,17},{9,25},{17,1},{25,9},{2,18},{10... | collective-permute-start | bytes 786440 | tf_op jit(solution)/shard_map/gather_middle_panel/ppermute | solution.py:518
  27.4 11.8 %collective-permute-start.5 = (bf16[128,1024]{1,0:T(8,128)(2,1)S(1)}, bf16[128,1024]{1,0:T(8,128)(2,1)S(1)}, u32[]{:S(2)}, u32[]{:S(2)}) collective-permute-start(bf16[128,1024]{1,0:T(8,128)(2,1)S(1)} %stack.3.refs_0_), channel_id=1, source_target_pairs={{0,8},{8,0},{16,24},{24,16},{1,9},{9,1},{17,25},{25,17},{2,10},{10... | collective-permute-start | bytes 786440 | tf_op jit(solution)/shard_map/gather_middle_panel/ppermute | solution.py:518
  43.5 6.0 %collective-permute-start.8 = (bf16[256,256]{1,0:T(8,128)(2,1)}, bf16[256,256]{1,0:T(8,128)(2,1)S(1)}, u32[]{:S(2)}, u32[]{:S(2)}) collective-permute-start(bf16[256,256]{1,0:T(8,128)(2,1)} %get-tuple-element.56), channel_id=1, source_target_pairs={{0,8},{8,0},{16,24},{24,16},{1,9},{9,1},{17,25},{25,17},{2,10},{10... | collective-permute-start | bytes 393224 | tf_op jit(solution)/shard_map/sum_over_leaf/ppermute | solution.py:518
  45.0 8.0 %collective-permute-start.9 = (bf16[256,256]{1,0:T(8,128)(2,1)}, bf16[256,256]{1,0:T(8,128)(2,1)S(1)}, u32[]{:S(2)}, u32[]{:S(2)}) collective-permute-start(bf16[256,256]{1,0:T(8,128)(2,1)} %get-tuple-element.57), channel_id=1, source_target_pairs={{0,16},{8,24},{16,0},{24,8},{1,17},{9,25},{17,1},{25,9},{2,18},{10... | collective-permute-start | bytes 393224 | tf_op jit(solution)/shard_map/sum_over_leaf/ppermute | solution.py:518
  46.5 6.5 %collective-permute-start.10 = (bf16[256,256]{1,0:T(8,128)(2,1)S(1)}, bf16[256,256]{1,0:T(8,128)(2,1)S(1)}, u32[]{:S(2)}, u32[]{:S(2)}) collective-permute-start(bf16[256,256]{1,0:T(8,128)(2,1)S(1)} %get-tuple-element.58), channel_id=1, source_target_pairs={{0,24},{8,16},{16,8},{24,0},{1,25},{9,17},{17,9},{25,1},{2,26},{10... | collective-permute-start | bytes 393224 | tf_op jit(solution)/shard_map/sum_over_leaf/ppermute | solution.py:518
  48.1 27.0 %collective-permute-start.21 = (bf16[512,1024]{1,0:T(8,128)(2,1)S(1)}, bf16[512,1024]{1,0:T(8,128)(2,1)S(1)}, u32[]{:S(2)}, u32[]{:S(2)}) collective-permute-start(bf16[512,1024]{1,0:T(8,128)(2,1)S(1)} %stack.4.own), channel_id=1, source_target_pairs={{0,1},{1,0},{2,3},{3,2},{4,5},{5,4},{6,7},{7,6},{8,9},{9,8},{10,11... | collective-permute-start | bytes 3145736 | tf_op jit(solution)/shard_map/gather_middle_panel/ppermute | solution.py:518
  53.1 27.3 %collective-permute-start.20 = (bf16[4,256,512]{2,1,0:T(8,128)(2,1)S(1)}, bf16[4,256,512]{2,1,0:T(8,128)(2,1)S(1)}, u32[]{:S(2)}, u32[]{:S(2)}) collective-permute-start(bf16[4,256,512]{2,1,0:T(8,128)(2,1)S(1)} %copy-done.2), channel_id=1, source_target_pairs={{0,1},{1,0},{2,3},{3,2},{4,5},{5,4},{6,7},{7,6},{8,9},{9,8},{10,11... | collective-permute-start | bytes 3145736 | tf_op jit(solution)/shard_map/swap_group_panel/ppermute | solution.py:518
  53.2 4.5 %collective-permute-start.11 = (bf16[128,256]{1,0:T(8,128)(2,1)S(1)}, bf16[128,256]{1,0:T(8,128)(2,1)S(1)}, u32[]{:S(2)}, u32[]{:S(2)}) collective-permute-start(bf16[128,256]{1,0:T(8,128)(2,1)S(1)} %get-tuple-element.61), channel_id=1, source_target_pairs={{0,2},{1,3},{2,0},{3,1},{4,6},{5,7},{6,4},{7,5},{8,10},{9,11},{10,... | collective-permute-start | bytes 196616 | tf_op jit(solution)/shard_map/sum_over_pos/ppermute | solution.py:518
  54.7 8.4 %collective-permute-start.12 = (bf16[128,256]{1,0:T(8,128)(2,1)S(1)}, bf16[128,256]{1,0:T(8,128)(2,1)S(1)}, u32[]{:S(2)}, u32[]{:S(2)}) collective-permute-start(bf16[128,256]{1,0:T(8,128)(2,1)S(1)} %get-tuple-element.62), channel_id=1, source_target_pairs={{0,4},{1,5},{2,6},{3,7},{4,0},{5,1},{6,2},{7,3},{8,12},{9,13},{10,... | collective-permute-start | bytes 196616 | tf_op jit(solution)/shard_map/sum_over_pos/ppermute | solution.py:518
  56.5 6.5 %collective-permute-start.13 = (bf16[128,256]{1,0:T(8,128)(2,1)S(1)}, bf16[128,256]{1,0:T(8,128)(2,1)S(1)}, u32[]{:S(2)}, u32[]{:S(2)}) collective-permute-start(bf16[128,256]{1,0:T(8,128)(2,1)S(1)} %get-tuple-element.63), channel_id=1, source_target_pairs={{0,6},{1,7},{2,4},{3,5},{4,2},{5,3},{6,0},{7,1},{8,14},{9,15},{10,... | collective-permute-start | bytes 196616 | tf_op jit(solution)/shard_map/sum_over_pos/ppermute | solution.py:518
  63.1 6.4 %collective-permute-start.16 = (bf16[128,256]{1,0:T(8,128)(2,1)S(1)}, bf16[128,256]{1,0:T(8,128)(2,1)S(1)}, u32[]{:S(2)}, u32[]{:S(2)}) collective-permute-start(bf16[128,256]{1,0:T(8,128)(2,1)S(1)} %sum_pos.1.refs_0_), channel_id=1, source_target_pairs={{0,6},{1,7},{2,4},{3,5},{4,2},{5,3},{6,0},{7,1},{8,14},{9,15},{10,... | collective-permute-start | bytes 196616 | tf_op jit(solution)/shard_map/gather_pos/ppermute | solution.py:518
  65.3 6.1 %collective-permute-start.15 = (bf16[128,256]{1,0:T(8,128)(2,1)S(1)}, bf16[128,256]{1,0:T(8,128)(2,1)S(1)}, u32[]{:S(2)}, u32[]{:S(2)}) collective-permute-start(bf16[128,256]{1,0:T(8,128)(2,1)S(1)} %sum_pos.1.refs_0_), channel_id=1, source_target_pairs={{0,4},{1,5},{2,6},{3,7},{4,0},{5,1},{6,2},{7,3},{8,12},{9,13},{10,... | collective-permute-start | bytes 196616 | tf_op jit(solution)/shard_map/gather_pos/ppermute | solution.py:518
  66.1 5.3 %collective-permute-start.14 = (bf16[128,256]{1,0:T(8,128)(2,1)S(1)}, bf16[128,256]{1,0:T(8,128)(2,1)S(1)}, u32[]{:S(2)}, u32[]{:S(2)}) collective-permute-start(bf16[128,256]{1,0:T(8,128)(2,1)S(1)} %sum_pos.1.refs_0_), channel_id=1, source_target_pairs={{0,2},{1,3},{2,0},{3,1},{4,6},{5,7},{6,4},{7,5},{8,10},{9,11},{10,... | collective-permute-start | bytes 196616 | tf_op jit(solution)/shard_map/gather_pos/ppermute | solution.py:518
  71.5 7.4 %collective-permute-start.19 = (bf16[256,256]{1,0:T(8,128)(2,1)S(1)}, bf16[256,256]{1,0:T(8,128)(2,1)S(1)}, u32[]{:S(2)}, u32[]{:S(2)}) collective-permute-start(bf16[256,256]{1,0:T(8,128)(2,1)S(1)} %get-tuple-element.71.refs_0_), channel_id=1, source_target_pairs={{0,24},{8,16},{16,8},{24,0},{1,25},{9,17},{17,9},{25,1},{2,26},{10... | collective-permute-start | bytes 393224 | tf_op jit(solution)/shard_map/gather_leaf/ppermute | solution.py:518
  73.1 6.3 %collective-permute-start.18 = (bf16[256,256]{1,0:T(8,128)(2,1)S(1)}, bf16[256,256]{1,0:T(8,128)(2,1)S(1)}, u32[]{:S(2)}, u32[]{:S(2)}) collective-permute-start(bf16[256,256]{1,0:T(8,128)(2,1)S(1)} %get-tuple-element.71.refs_0_), channel_id=1, source_target_pairs={{0,16},{8,24},{16,0},{24,8},{1,17},{9,25},{17,1},{25,9},{2,18},{10... | collective-permute-start | bytes 393224 | tf_op jit(solution)/shard_map/gather_leaf/ppermute | solution.py:518
  74.4 6.0 %collective-permute-start.17 = (bf16[256,256]{1,0:T(8,128)(2,1)S(1)}, bf16[256,256]{1,0:T(8,128)(2,1)S(1)}, u32[]{:S(2)}, u32[]{:S(2)}) collective-permute-start(bf16[256,256]{1,0:T(8,128)(2,1)S(1)} %get-tuple-element.71.refs_0_), channel_id=1, source_target_pairs={{0,8},{8,0},{16,24},{24,16},{1,9},{9,1},{17,25},{25,17},{2,10},{10... | collective-permute-start | bytes 393224 | tf_op jit(solution)/shard_map/gather_leaf/ppermute | solution.py:518
  80.4 2.2 %collective-permute-start.22 = (bf16[1280,256]{1,0:T(8,128)(2,1)S(1)}, bf16[1280,256]{1,0:T(8,128)(2,1)S(1)}, u32[]{:S(2)}, u32[]{:S(2)}) collective-permute-start(bf16[1280,256]{1,0:T(8,128)(2,1)S(1)} %stack.5.mine), channel_id=1, source_target_pairs={{0,1},{1,0},{2,3},{3,2},{4,5},{5,4},{6,7},{7,6},{8,9},{9,8},{10,11... | collective-permute-start | bytes 1966088 | tf_op jit(solution)/shard_map/gather_cores/ppermute | solution.py:518
  (4 other events, 32.2 us)
Sparse Core Ops, SparseCore 0:
  9.6 30.6 all-gather.1

commit v14 on v13

--- a/solution.py
+++ b/solution.py
@@ -596,15 +596,15 @@
     sends = sum_leaf(parts, group, n_pos)
     with jax.named_scope("sum_over_pos"):
         got = sends[:1] + [swap(sends[k], "grp", n_grp, 2 * k) for k in range(1, n_pos)]
-    with jax.named_scope("swap_group_panel"):
-        panel_other = swap(after(panel, sends), "grp", n_grp, 1)
     residual = sum_pos(rhs_mine, got)
     with jax.named_scope("gather_pos"):
         uppers, groups = stack_pos(swaps(residual, "grp", n_grp, 2), q)
+    with jax.named_scope("swap_group_panel"):
+        panel_other = swap(after(panel, uppers), "grp", n_grp, 1)
     with jax.named_scope("gather_leaf"):
         stacks = swaps(uppers, "leaf", n_leaf)
     with jax.named_scope("gather_cores"):
-        mine = stack(after(stacks, (panel_other, middle)) + [groups])
+        mine = stack(after(stacks, middle) + [groups])
         theirs = swap(mine, "grp", n_grp, 1)
     leaf_out, group_out, mid_out, top_out = backward(
         (mine, theirs, inv_middle, middle),

time: 99.1 us -> 103 us (1.039)
  local copies, waits for them, and re-layouts: 0.02 us -> 4.98 us
  waiting for transfers between devices: 35 us -> 33.6 us
    unnamed x8 -> x20, local copies, waits for them, and re-layouts: 0.02 us -> 4.98 us
  transfers between devices with their start and end apart: 24 -> 24, of which waited for: 14 -> 11; matrix products, arithmetic and copies ran while one was open for 1% -> 1% of each run, Pallas kernels for 9% -> 9%
where the time goes in v14:
time: 103 us
  waiting for transfers between devices  33.6 us (33%)
  starting transfers between devices  27.3 us (27%)
  Pallas kernels  21.2 us (21%)
  between operations  14.9 us (14%)
  local copies, waits for them, and re-layouts  4.98 us (5%)
    ppermute x23, waiting for transfers between devices, swap(): return lax.ppermute(x, axis, [(i, i ^ bits) for i in range(size)])  32.9 us
    ppermute x23, starting transfers between devices, swap(): return lax.ppermute(x, axis, [(i, i ^ bits) for i in range(size)])  27.3 us
    pallas_call x1, Pallas kernels, backward(): pl.pallas_call(functools.partial(backward_kernel, n_leaf, n_pos), out_sha...  9.48 us
    pallas_call x1, Pallas kernels, leaf_forward(): pl.pallas_call(functools.partial(forward_kernel, upper_cols // (2 * sec),...  8.93 us
    unnamed x20, local copies, waits for them, and re-layouts  4.98 us
    pallas_call x1, Pallas kernels, fold(): pl.pallas_call(functools.partial(fold_kernel, n_leaf, n_pos), out_shape=[...  2.35 us
  transfers between devices with their start and end apart: 24, of which 11 were waited for; matrix products, arithmetic and copies ran while one was open for 1% of the time, Pallas kernels for 9%

profile of v14, /device:TPU:0, one launch (start us, length us, event | category | flops | bytes accessed | tf_op | source)
XLA Modules:
  0.0 102.9 jit_solution(16477944201095711421)
XLA Ops:
  7.9 5.1 %collective-permute-start.2 = (bf16[32,1024]{1,0:T(8,128)(2,1)}, bf16[32,1024]{1,0:T(8,128)(2,1)S(1)}, u32[]{:S(2)}, u32[]{:S(2)}) collective-permute-start(bf16[32,1024]{1,0:T(8,128)(2,1)} %refs_0_), channel_id=1, source_target_pairs={{0,6},{1,7},{2,4},{3,5},{4,2},{5,3},{6,0},{7,1},{8,14},{9,15},{10,... | collective-permute-start | bytes 196616 | tf_op jit(solution)/shard_map/gather_middle_panel/ppermute | solution.py:518
  14.3 8.9 %leaf_forward.1 = (bf16[1536,256]{1,0:T(8,128)(2,1)S(1)}, bf16[768,256]{1,0:T(8,128)(2,1)}, bf16[768,256]{1,0:T(8,128)(2,1)}, bf16[512,512]{1,0:T(8,128)(2,1)S(1...) custom-call(s32[1,1]{1,0:T(1,128)S(6)} %copy.18.count_hbm, s32[1,256]{1,0:T(1,128)} %cols_hbm.1, ...), custom_call_target="tpu_custom_call" | custom-call | flops 1342177280 | bytes 9437184 | tf_op jit(solution)/shard_map/leaf_forward/pallas_call | solution.py:183
  23.9 3.9 %collective-permute-start.7 = (bf16[128,1024]{1,0:T(8,128)(2,1)S(1)}, bf16[128,1024]{1,0:T(8,128)(2,1)S(1)}, u32[]{:S(2)}, u32[]{:S(2)}) collective-permute-start(bf16[128,1024]{1,0:T(8,128)(2,1)S(1)} %stack.3.refs_0_), channel_id=1, source_target_pairs={{0,24},{8,16},{16,8},{24,0},{1,25},{9,17},{17,9},{25,1},{2,26},{10... | collective-permute-start | bytes 786440 | tf_op jit(solution)/shard_map/gather_middle_panel/ppermute | solution.py:518
  29.4 5.6 %collective-permute-done.7.refs_3_ = bf16[128,1024]{1,0:T(8,128)(2,1)S(1)} collective-permute-done((bf16[128,1024]{1,0:T(8,128)(2,1)S(1)}, bf16[128,1024]{1,0:T(8,128)(2,1)S(1)}, u32[]{:S(2)}, u32[]{:S(2)}) %collective-permute-start.7) | collective-permute-done | bytes 262176 | tf_op jit(solution)/shard_map/gather_middle_panel/ppermute | solution.py:518
  35.7 4.3 %collective-permute-done.6.refs_2_ = bf16[128,1024]{1,0:T(8,128)(2,1)S(1)} collective-permute-done((bf16[128,1024]{1,0:T(8,128)(2,1)S(1)}, bf16[128,1024]{1,0:T(8,128)(2,1)S(1)}, u32[]{:S(2)}, u32[]{:S(2)}) %collective-permute-start.6) | collective-permute-done | bytes 262176 | tf_op jit(solution)/shard_map/gather_middle_panel/ppermute | solution.py:518
  44.4 2.4 %fold_group.1 = (bf16[256,256]{1,0:T(8,128)(2,1)S(1)}, bf16[256,256]{1,0:T(8,128)(2,1)S(1)}, bf16[256,256]{1,0:T(8,128)(2,1)S(1)}, bf16[256,256]{1,0:T(8,128)(2,1)S(1)}, bf16[256,256]{1,0:T(8,128)(2,1)S(1)}) custom-call(bf16[1536,256]{1,0:T(8,128)(2,1)S(1)} %get-tuple-element.43.keep, bf16[768,256]{1,0:T(8,128)(2,1)S(1)} %collective-permute-done.3.low, ...), custom_call_target="tpu_custom_call" | custom-call | tf_op jit(solution)/shard_map/fold_group/pallas_call | solution.py:263
  46.9 1.0 %collective-permute-start.8 = (bf16[256,256]{1,0:T(8,128)(2,1)S(1)}, bf16[256,256]{1,0:T(8,128)(2,1)S(1)}, u32[]{:S(2)}, u32[]{:S(2)}) collective-permute-start(bf16[256,256]{1,0:T(8,128)(2,1)S(1)} %get-tuple-element.56), channel_id=1, source_target_pairs={{0,8},{8,0},{16,24},{24,16},{1,9},{9,1},{17,25},{25,17},{2,10},{10... | collective-permute-start | bytes 393224 | tf_op jit(solution)/shard_map/sum_over_leaf/ppermute | solution.py:518
  47.9 1.3 %collective-permute-start.9 = (bf16[256,256]{1,0:T(8,128)(2,1)S(1)}, bf16[256,256]{1,0:T(8,128)(2,1)S(1)}, u32[]{:S(2)}, u32[]{:S(2)}) collective-permute-start(bf16[256,256]{1,0:T(8,128)(2,1)S(1)} %get-tuple-element.57), channel_id=1, source_target_pairs={{0,16},{8,24},{16,0},{24,8},{1,17},{9,25},{17,1},{25,9},{2,18},{10... | collective-permute-start | bytes 393224 | tf_op jit(solution)/shard_map/sum_over_leaf/ppermute | solution.py:518
  49.2 1.2 %collective-permute-start.10 = (bf16[256,256]{1,0:T(8,128)(2,1)S(1)}, bf16[256,256]{1,0:T(8,128)(2,1)S(1)}, u32[]{:S(2)}, u32[]{:S(2)}) collective-permute-start(bf16[256,256]{1,0:T(8,128)(2,1)S(1)} %get-tuple-element.58), channel_id=1, source_target_pairs={{0,24},{8,16},{16,8},{24,0},{1,25},{9,17},{17,9},{25,1},{2,26},{10... | collective-permute-start | bytes 393224 | tf_op jit(solution)/shard_map/sum_over_leaf/ppermute | solution.py:518
  50.4 2.8 %collective-permute-done.8.refs_1_ = bf16[256,256]{1,0:T(8,128)(2,1)S(1)} collective-permute-done((bf16[256,256]{1,0:T(8,128)(2,1)S(1)}, bf16[256,256]{1,0:T(8,128)(2,1)S(1)}, u32[]{:S(2)}, u32[]{:S(2)}) %collective-permute-start.8) | collective-permute-done | bytes 131104 | tf_op jit(solution)/shard_map/sum_over_leaf/ppermute | solution.py:518
  53.2 3.1 %collective-permute-done.9.refs_2_ = bf16[256,256]{1,0:T(8,128)(2,1)S(1)} collective-permute-done((bf16[256,256]{1,0:T(8,128)(2,1)S(1)}, bf16[256,256]{1,0:T(8,128)(2,1)S(1)}, u32[]{:S(2)}, u32[]{:S(2)}) %collective-permute-start.9) | collective-permute-done | bytes 131104 | tf_op jit(solution)/shard_map/sum_over_leaf/ppermute | solution.py:518
  57.3 3.7 %collective-permute-start.12 = (bf16[128,256]{1,0:T(8,128)(2,1)S(1)}, bf16[128,256]{1,0:T(8,128)(2,1)S(1)}, u32[]{:S(2)}, u32[]{:S(2)}) collective-permute-start(bf16[128,256]{1,0:T(8,128)(2,1)S(1)} %get-tuple-element.62), channel_id=1, source_target_pairs={{0,4},{1,5},{2,6},{3,7},{4,0},{5,1},{6,2},{7,3},{8,12},{9,13},{10,... | collective-permute-start | bytes 196616 | tf_op jit(solution)/shard_map/sum_over_pos/ppermute | solution.py:518
  61.0 3.9 %collective-permute-done.12.refs_2_ = bf16[128,256]{1,0:T(8,128)(2,1)S(1)} collective-permute-done((bf16[128,256]{1,0:T(8,128)(2,1)S(1)}, bf16[128,256]{1,0:T(8,128)(2,1)S(1)}, u32[]{:S(2)}, u32[]{:S(2)}) %collective-permute-start.12) | collective-permute-done | bytes 65568 | tf_op jit(solution)/shard_map/sum_over_pos/ppermute | solution.py:518
  64.9 2.3 %collective-permute-done.13.refs_3_ = bf16[128,256]{1,0:T(8,128)(2,1)S(1)} collective-permute-done((bf16[128,256]{1,0:T(8,128)(2,1)S(1)}, bf16[128,256]{1,0:T(8,128)(2,1)S(1)}, u32[]{:S(2)}, u32[]{:S(2)}) %collective-permute-start.13) | collective-permute-done | bytes 65568 | tf_op jit(solution)/shard_map/sum_over_pos/ppermute | solution.py:518
  67.2 1.0 collective-permute-start.16
  68.1 3.5 %collective-permute-start.14 = (bf16[128,256]{1,0:T(8,128)(2,1)S(1)}, bf16[128,256]{1,0:T(8,128)(2,1)S(1)}, u32[]{:S(2)}, u32[]{:S(2)}) collective-permute-start(bf16[128,256]{1,0:T(8,128)(2,1)S(1)} %sum_pos.1.refs_0_), channel_id=1, source_target_pairs={{0,2},{1,3},{2,0},{3,1},{4,6},{5,7},{6,4},{7,5},{8,10},{9,11},{10,... | collective-permute-start | bytes 196616 | tf_op jit(solution)/shard_map/gather_pos/ppermute | solution.py:518
  71.6 1.8 %collective-permute-done.16.refs_3_ = bf16[128,256]{1,0:T(8,128)(2,1)S(1)} collective-permute-done((bf16[128,256]{1,0:T(8,128)(2,1)S(1)}, bf16[128,256]{1,0:T(8,128)(2,1)S(1)}, u32[]{:S(2)}, u32[]{:S(2)}) %collective-permute-start.16) | collective-permute-done | bytes 65568 | tf_op jit(solution)/shard_map/gather_pos/ppermute | solution.py:518
  73.4 1.3 %collective-permute-done.15.refs_2_ = bf16[128,256]{1,0:T(8,128)(2,1)S(1)} collective-permute-done((bf16[128,256]{1,0:T(8,128)(2,1)S(1)}, bf16[128,256]{1,0:T(8,128)(2,1)S(1)}, u32[]{:S(2)}, u32[]{:S(2)}) %collective-permute-start.15) | collective-permute-done | bytes 65568 | tf_op jit(solution)/shard_map/gather_pos/ppermute | solution.py:518
  74.8 1.1 %collective-permute-start.19 = (bf16[256,256]{1,0:T(8,128)(2,1)S(1)}, bf16[256,256]{1,0:T(8,128)(2,1)S(1)}, u32[]{:S(2)}, u32[]{:S(2)}) collective-permute-start(bf16[256,256]{1,0:T(8,128)(2,1)S(1)} %get-tuple-element.70.refs_0_), channel_id=1, source_target_pairs={{0,24},{8,16},{16,8},{24,0},{1,25},{9,17},{17,9},{25,1},{2,26},{10... | collective-permute-start | bytes 393224 | tf_op jit(solution)/shard_map/gather_leaf/ppermute | solution.py:518
  76.5 1.9 %collective-permute-start.17 = (bf16[256,256]{1,0:T(8,128)(2,1)S(1)}, bf16[256,256]{1,0:T(8,128)(2,1)S(1)}, u32[]{:S(2)}, u32[]{:S(2)}) collective-permute-start(bf16[256,256]{1,0:T(8,128)(2,1)S(1)} %get-tuple-element.70.refs_0_), channel_id=1, source_target_pairs={{0,8},{8,0},{16,24},{24,16},{1,9},{9,1},{17,25},{25,17},{2,10},{10... | collective-permute-start | bytes 393224 | tf_op jit(solution)/shard_map/gather_leaf/ppermute | solution.py:518
  78.5 3.6 %collective-permute-done.19.refs_3_ = bf16[256,256]{1,0:T(8,128)(2,1)S(1)} collective-permute-done((bf16[256,256]{1,0:T(8,128)(2,1)S(1)}, bf16[256,256]{1,0:T(8,128)(2,1)S(1)}, u32[]{:S(2)}, u32[]{:S(2)}) %collective-permute-start.19) | collective-permute-done | bytes 131104 | tf_op jit(solution)/shard_map/gather_leaf/ppermute | solution.py:518
  82.1 2.2 %collective-permute-done.18.refs_2_ = bf16[256,256]{1,0:T(8,128)(2,1)S(1)} collective-permute-done((bf16[256,256]{1,0:T(8,128)(2,1)S(1)}, bf16[256,256]{1,0:T(8,128)(2,1)S(1)}, u32[]{:S(2)}, u32[]{:S(2)}) %collective-permute-start.18) | collective-permute-done | bytes 131104 | tf_op jit(solution)/shard_map/gather_leaf/ppermute | solution.py:518
  84.5 2.1 %collective-permute-done.21.theirs = bf16[1280,256]{1,0:T(8,128)(2,1)S(1)} collective-permute-done((bf16[1280,256]{1,0:T(8,128)(2,1)S(1)}, bf16[1280,256]{1,0:T(8,128)(2,1)S(1)}, u32[]{:S(2)}, u32[]{:S(2)}) %collective-permute-start.21) | collective-permute-done | bytes 655392 | tf_op jit(solution)/shard_map/gather_cores/ppermute | solution.py:518
  86.6 9.5 %backward.1 = (f32[1024,256]{1,0:T(8,128)}, f32[512,256]{1,0:T(8,128)}, f32[1024,256]{1,0:T(8,128)}, f32[1024,256]{1,0:T(8,128)}) custom-call(bf16[1280,256]{1,0:T(8,128)(2,1)S(1)} %stack.5.mine, bf16[1280,256]{1,0:T(8,128)(2,1)S(1)} %collective-permute-done.21.theirs, bf16[1024,1024]{1,0:T(8,128)(2,1)S(1)} %copy-done, ...), custom_call_target="tpu_custom_call" | custom-call | tf_op jit(solution)/shard_map/backward/pallas_call | solution.py:497
  (56 shorter events, 10.7 us)
Async XLA Ops:
  7.2 37.2 %all-gather.2.cloned.1.call-start = ((), (), s32[]{:S(2)}) async-start(), calls=%async_computation | async-start | bytes 1310720 | tf_op jit(solution)/shard_map/gather_group_panel/all_gather | solution.py:558
  7.9 15.4 %collective-permute-start.2 = (bf16[32,1024]{1,0:T(8,128)(2,1)}, bf16[32,1024]{1,0:T(8,128)(2,1)S(1)}, u32[]{:S(2)}, u32[]{:S(2)}) collective-permute-start(bf16[32,1024]{1,0:T(8,128)(2,1)} %refs_0_), channel_id=1, source_target_pairs={{0,6},{1,7},{2,4},{3,5},{4,2},{5,3},{6,0},{7,1},{8,14},{9,15},{10,... | collective-permute-start | bytes 196616 | tf_op jit(solution)/shard_map/gather_middle_panel/ppermute | solution.py:518
  13.0 10.3 %collective-permute-start.1 = (bf16[32,1024]{1,0:T(8,128)(2,1)}, bf16[32,1024]{1,0:T(8,128)(2,1)S(1)}, u32[]{:S(2)}, u32[]{:S(2)}) collective-permute-start(bf16[32,1024]{1,0:T(8,128)(2,1)} %refs_0_), channel_id=1, source_target_pairs={{0,4},{1,5},{2,6},{3,7},{4,0},{5,1},{6,2},{7,3},{8,12},{9,13},{10,... | collective-permute-start | bytes 196616 | tf_op jit(solution)/shard_map/gather_middle_panel/ppermute | solution.py:518
  13.0 10.3 %collective-permute-start = (bf16[32,1024]{1,0:T(8,128)(2,1)}, bf16[32,1024]{1,0:T(8,128)(2,1)S(1)}, u32[]{:S(2)}, u32[]{:S(2)}) collective-permute-start(bf16[32,1024]{1,0:T(8,128)(2,1)} %refs_0_), channel_id=1, source_target_pairs={{0,2},{1,3},{2,0},{3,1},{4,6},{5,7},{6,4},{7,5},{8,10},{9,11},{10,... | collective-permute-start | bytes 196616 | tf_op jit(solution)/shard_map/gather_middle_panel/ppermute | solution.py:518
  23.3 21.0 %collective-permute-start.3 = (bf16[768,256]{1,0:T(8,128)(2,1)}, bf16[768,256]{1,0:T(8,128)(2,1)S(1)}, u32[]{:S(2)}, u32[]{:S(2)}) collective-permute-start(bf16[768,256]{1,0:T(8,128)(2,1)} %get-tuple-element.46), channel_id=1, source_target_pairs={{0,1},{1,0},{2,3},{3,2},{4,5},{5,4},{6,7},{7,6},{8,9},{9,8},{10,11... | collective-permute-start | bytes 1179656 | tf_op jit(solution)/shard_map/swap_cores/ppermute | solution.py:518
  23.4 21.0 %collective-permute-start.4 = (bf16[768,256]{1,0:T(8,128)(2,1)}, bf16[768,256]{1,0:T(8,128)(2,1)S(1)}, u32[]{:S(2)}, u32[]{:S(2)}) collective-permute-start(bf16[768,256]{1,0:T(8,128)(2,1)} %get-tuple-element.47), channel_id=1, source_target_pairs={{0,1},{1,0},{2,3},{3,2},{4,5},{5,4},{6,7},{7,6},{8,9},{9,8},{10,11... | collective-permute-start | bytes 1179656 | tf_op jit(solution)/shard_map/swap_cores/ppermute | solution.py:518
  23.9 11.1 %collective-permute-start.7 = (bf16[128,1024]{1,0:T(8,128)(2,1)S(1)}, bf16[128,1024]{1,0:T(8,128)(2,1)S(1)}, u32[]{:S(2)}, u32[]{:S(2)}) collective-permute-start(bf16[128,1024]{1,0:T(8,128)(2,1)S(1)} %stack.3.refs_0_), channel_id=1, source_target_pairs={{0,24},{8,16},{16,8},{24,0},{1,25},{9,17},{17,9},{25,1},{2,26},{10... | collective-permute-start | bytes 786440 | tf_op jit(solution)/shard_map/gather_middle_panel/ppermute | solution.py:518
  27.8 12.2 %collective-permute-start.6 = (bf16[128,1024]{1,0:T(8,128)(2,1)S(1)}, bf16[128,1024]{1,0:T(8,128)(2,1)S(1)}, u32[]{:S(2)}, u32[]{:S(2)}) collective-permute-start(bf16[128,1024]{1,0:T(8,128)(2,1)S(1)} %stack.3.refs_0_), channel_id=1, source_target_pairs={{0,16},{8,24},{16,0},{24,8},{1,17},{9,25},{17,1},{25,9},{2,18},{10... | collective-permute-start | bytes 786440 | tf_op jit(solution)/shard_map/gather_middle_panel/ppermute | solution.py:518
  27.8 12.9 %collective-permute-start.5 = (bf16[128,1024]{1,0:T(8,128)(2,1)S(1)}, bf16[128,1024]{1,0:T(8,128)(2,1)S(1)}, u32[]{:S(2)}, u32[]{:S(2)}) collective-permute-start(bf16[128,1024]{1,0:T(8,128)(2,1)S(1)} %stack.3.refs_0_), channel_id=1, source_target_pairs={{0,8},{8,0},{16,24},{24,16},{1,9},{9,1},{17,25},{25,17},{2,10},{10... | collective-permute-start | bytes 786440 | tf_op jit(solution)/shard_map/gather_middle_panel/ppermute | solution.py:518
  46.7 31.7 %collective-permute-start.20 = (bf16[512,1024]{1,0:T(8,128)(2,1)S(1)}, bf16[512,1024]{1,0:T(8,128)(2,1)S(1)}, u32[]{:S(2)}, u32[]{:S(2)}) collective-permute-start(bf16[512,1024]{1,0:T(8,128)(2,1)S(1)} %stack.4.own), channel_id=1, source_target_pairs={{0,1},{1,0},{2,3},{3,2},{4,5},{5,4},{6,7},{7,6},{8,9},{9,8},{10,11... | collective-permute-start | bytes 3145736 | tf_op jit(solution)/shard_map/gather_middle_panel/ppermute | solution.py:518
  46.9 6.3 %collective-permute-start.8 = (bf16[256,256]{1,0:T(8,128)(2,1)S(1)}, bf16[256,256]{1,0:T(8,128)(2,1)S(1)}, u32[]{:S(2)}, u32[]{:S(2)}) collective-permute-start(bf16[256,256]{1,0:T(8,128)(2,1)S(1)} %get-tuple-element.56), channel_id=1, source_target_pairs={{0,8},{8,0},{16,24},{24,16},{1,9},{9,1},{17,25},{25,17},{2,10},{10... | collective-permute-start | bytes 393224 | tf_op jit(solution)/shard_map/sum_over_leaf/ppermute | solution.py:518
  47.9 8.4 %collective-permute-start.9 = (bf16[256,256]{1,0:T(8,128)(2,1)S(1)}, bf16[256,256]{1,0:T(8,128)(2,1)S(1)}, u32[]{:S(2)}, u32[]{:S(2)}) collective-permute-start(bf16[256,256]{1,0:T(8,128)(2,1)S(1)} %get-tuple-element.57), channel_id=1, source_target_pairs={{0,16},{8,24},{16,0},{24,8},{1,17},{9,25},{17,1},{25,9},{2,18},{10... | collective-permute-start | bytes 393224 | tf_op jit(solution)/shard_map/sum_over_leaf/ppermute | solution.py:518
  49.2 7.1 %collective-permute-start.10 = (bf16[256,256]{1,0:T(8,128)(2,1)S(1)}, bf16[256,256]{1,0:T(8,128)(2,1)S(1)}, u32[]{:S(2)}, u32[]{:S(2)}) collective-permute-start(bf16[256,256]{1,0:T(8,128)(2,1)S(1)} %get-tuple-element.58), channel_id=1, source_target_pairs={{0,24},{8,16},{16,8},{24,0},{1,25},{9,17},{17,9},{25,1},{2,26},{10... | collective-permute-start | bytes 393224 | tf_op jit(solution)/shard_map/sum_over_leaf/ppermute | solution.py:518
  56.4 4.6 %collective-permute-start.11 = (bf16[128,256]{1,0:T(8,128)(2,1)S(1)}, bf16[128,256]{1,0:T(8,128)(2,1)S(1)}, u32[]{:S(2)}, u32[]{:S(2)}) collective-permute-start(bf16[128,256]{1,0:T(8,128)(2,1)S(1)} %get-tuple-element.61), channel_id=1, source_target_pairs={{0,2},{1,3},{2,0},{3,1},{4,6},{5,7},{6,4},{7,5},{8,10},{9,11},{10,... | collective-permute-start | bytes 196616 | tf_op jit(solution)/shard_map/sum_over_pos/ppermute | solution.py:518
  57.3 7.6 %collective-permute-start.12 = (bf16[128,256]{1,0:T(8,128)(2,1)S(1)}, bf16[128,256]{1,0:T(8,128)(2,1)S(1)}, u32[]{:S(2)}, u32[]{:S(2)}) collective-permute-start(bf16[128,256]{1,0:T(8,128)(2,1)S(1)} %get-tuple-element.62), channel_id=1, source_target_pairs={{0,4},{1,5},{2,6},{3,7},{4,0},{5,1},{6,2},{7,3},{8,12},{9,13},{10,... | collective-permute-start | bytes 196616 | tf_op jit(solution)/shard_map/sum_over_pos/ppermute | solution.py:518
  61.0 6.2 %collective-permute-start.13 = (bf16[128,256]{1,0:T(8,128)(2,1)S(1)}, bf16[128,256]{1,0:T(8,128)(2,1)S(1)}, u32[]{:S(2)}, u32[]{:S(2)}) collective-permute-start(bf16[128,256]{1,0:T(8,128)(2,1)S(1)} %get-tuple-element.63), channel_id=1, source_target_pairs={{0,6},{1,7},{2,4},{3,5},{4,2},{5,3},{6,0},{7,1},{8,14},{9,15},{10,... | collective-permute-start | bytes 196616 | tf_op jit(solution)/shard_map/sum_over_pos/ppermute | solution.py:518
  67.2 6.3 %collective-permute-start.16 = (bf16[128,256]{1,0:T(8,128)(2,1)S(1)}, bf16[128,256]{1,0:T(8,128)(2,1)S(1)}, u32[]{:S(2)}, u32[]{:S(2)}) collective-permute-start(bf16[128,256]{1,0:T(8,128)(2,1)S(1)} %sum_pos.1.refs_0_), channel_id=1, source_target_pairs={{0,6},{1,7},{2,4},{3,5},{4,2},{5,3},{6,0},{7,1},{8,14},{9,15},{10,... | collective-permute-start | bytes 196616 | tf_op jit(solution)/shard_map/gather_pos/ppermute | solution.py:518
  68.1 6.6 %collective-permute-start.15 = (bf16[128,256]{1,0:T(8,128)(2,1)S(1)}, bf16[128,256]{1,0:T(8,128)(2,1)S(1)}, u32[]{:S(2)}, u32[]{:S(2)}) collective-permute-start(bf16[128,256]{1,0:T(8,128)(2,1)S(1)} %sum_pos.1.refs_0_), channel_id=1, source_target_pairs={{0,4},{1,5},{2,6},{3,7},{4,0},{5,1},{6,2},{7,3},{8,12},{9,13},{10,... | collective-permute-start | bytes 196616 | tf_op jit(solution)/shard_map/gather_pos/ppermute | solution.py:518
  68.1 6.6 %collective-permute-start.14 = (bf16[128,256]{1,0:T(8,128)(2,1)S(1)}, bf16[128,256]{1,0:T(8,128)(2,1)S(1)}, u32[]{:S(2)}, u32[]{:S(2)}) collective-permute-start(bf16[128,256]{1,0:T(8,128)(2,1)S(1)} %sum_pos.1.refs_0_), channel_id=1, source_target_pairs={{0,2},{1,3},{2,0},{3,1},{4,6},{5,7},{6,4},{7,5},{8,10},{9,11},{10,... | collective-permute-start | bytes 196616 | tf_op jit(solution)/shard_map/gather_pos/ppermute | solution.py:518
  74.7 9.7 %collective-permute-start.22 = (bf16[4,256,512]{2,1,0:T(8,128)(2,1)S(1)}, bf16[4,256,512]{2,1,0:T(8,128)(2,1)S(1)}, u32[]{:S(2)}, u32[]{:S(2)}) collective-permute-start(bf16[4,256,512]{2,1,0:T(8,128)(2,1)S(1)} %copy-done.8), channel_id=1, source_target_pairs={{0,1},{1,0},{2,3},{3,2},{4,5},{5,4},{6,7},{7,6},{8,9},{9,8},{10,11... | collective-permute-start | bytes 3145736 | tf_op jit(solution)/shard_map/swap_group_panel/ppermute | solution.py:518
  74.8 7.3 %collective-permute-start.19 = (bf16[256,256]{1,0:T(8,128)(2,1)S(1)}, bf16[256,256]{1,0:T(8,128)(2,1)S(1)}, u32[]{:S(2)}, u32[]{:S(2)}) collective-permute-start(bf16[256,256]{1,0:T(8,128)(2,1)S(1)} %get-tuple-element.70.refs_0_), channel_id=1, source_target_pairs={{0,24},{8,16},{16,8},{24,0},{1,25},{9,17},{17,9},{25,1},{2,26},{10... | collective-permute-start | bytes 393224 | tf_op jit(solution)/shard_map/gather_leaf/ppermute | solution.py:518
  76.0 8.4 %collective-permute-start.18 = (bf16[256,256]{1,0:T(8,128)(2,1)S(1)}, bf16[256,256]{1,0:T(8,128)(2,1)S(1)}, u32[]{:S(2)}, u32[]{:S(2)}) collective-permute-start(bf16[256,256]{1,0:T(8,128)(2,1)S(1)} %get-tuple-element.70.refs_0_), channel_id=1, source_target_pairs={{0,16},{8,24},{16,0},{24,8},{1,17},{9,25},{17,1},{25,9},{2,18},{10... | collective-permute-start | bytes 393224 | tf_op jit(solution)/shard_map/gather_leaf/ppermute | solution.py:518
  76.5 7.8 %collective-permute-start.17 = (bf16[256,256]{1,0:T(8,128)(2,1)S(1)}, bf16[256,256]{1,0:T(8,128)(2,1)S(1)}, u32[]{:S(2)}, u32[]{:S(2)}) collective-permute-start(bf16[256,256]{1,0:T(8,128)(2,1)S(1)} %get-tuple-element.70.refs_0_), channel_id=1, source_target_pairs={{0,8},{8,0},{16,24},{24,16},{1,9},{9,1},{17,25},{25,17},{2,10},{10... | collective-permute-start | bytes 393224 | tf_op jit(solution)/shard_map/gather_leaf/ppermute | solution.py:518
  84.4 2.2 %collective-permute-start.21 = (bf16[1280,256]{1,0:T(8,128)(2,1)S(1)}, bf16[1280,256]{1,0:T(8,128)(2,1)S(1)}, u32[]{:S(2)}, u32[]{:S(2)}) collective-permute-start(bf16[1280,256]{1,0:T(8,128)(2,1)S(1)} %stack.5.mine), channel_id=1, source_target_pairs={{0,1},{1,0},{2,3},{3,2},{4,5},{5,4},{6,7},{7,6},{8,9},{9,8},{10,11... | collective-permute-start | bytes 1966088 | tf_op jit(solution)/shard_map/gather_cores/ppermute | solution.py:518
  (10 other events, 58.8 us)
Sparse Core Ops, SparseCore 0:
  9.6 30.6 all-gather.1
